TPU v7x, 32 devices: a whole 2x2x4 slice. The times are simulated.
32 devices in a mesh: tensor: 16 (over z, x, core), rep: 2 (over y).
Axes of the slice: x: 2, y: 2, z: 4, core: 2. Of those that a mesh axis runs over, the one named last changes fastest.
Arguments:
- amplitudes: float32 [8, 16384, 1024], P('rep', 'tensor'), may hold values from -6 to 6
- integrals: float32 [1024, 8, 16384], P(None, 'rep', 'tensor'), may hold values from -0.078125 to 0.078125
- row_count: int32 [8], replicated, may hold values from 1 to 1024, 6400 in all
- pair_count: int32 [8], replicated, may hold values from 1 to 16384, 80000 in all
- col_count: int32 [8], replicated, may hold values from 1 to 1024, 6400 in all
Outputs:
- cycle_term: float32 [1024, 8, 1024], P('tensor', None, 'rep')
Inputs may be any that keep to these rules, and one draw needn't show every extreme that they name: row_count[h] is the number of (i, a) pairs with irrep product h for 8 occupied i; the counts sum to 6400 and one equals 1024. pair_count[h] is the number of (k, c) pairs with irrep product h; the counts sum to 80000 and one equals 16384. col_count[h] is the number of (j, b) pairs with irrep product h for 8 occupied j; the counts sum to 6400 and one equals 1024.
All inputs are finite; a program needn't handle non-finite values.
Results may differ from a plain program's by a relative error of at most 0.0003.
Values sent between devices are 32-bit elements; how exact they have to be, the bound alone decides.
No kernel may reach another device: no remote copies, remote signals or barrier semaphores. Data moves between devices by JAX's collectives and lax.ppermute only.
A program may use at most 128 MiB of HBM per device.

v0:
```python
import jax
import jax.numpy as jnp
from jax import lax
from jax.sharding import PartitionSpec as P

ROW_CAP = 1024
COL_CAP = 1024


def local(amplitudes, integrals, row_count, pair_count, col_count):
    block_local = amplitudes.shape[0]
    pair_local = amplitudes.shape[1]
    col_local = COL_CAP // lax.axis_size("tensor")
    row_local = ROW_CAP // lax.axis_size("rep")
    block_start = lax.axis_index("rep") * block_local
    pairs_here = lax.dynamic_slice_in_dim(pair_count, block_start, block_local)
    pair_index = lax.axis_index("tensor") * pair_local + lax.broadcasted_iota(
        jnp.int32, (1, pair_local, 1), 1
    )
    masked = jnp.where(pair_index < pairs_here[:, None, None], amplitudes, jnp.float32(0.0))
    partial_sums = jnp.einsum(
        "chk,hkr->chr",
        integrals,
        masked,
        precision=lax.Precision.HIGHEST,
        preferred_element_type=jnp.float32,
    )
    summed = lax.psum_scatter(partial_sums, "tensor", scatter_dimension=0, tiled=True)
    arranged = lax.all_to_all(summed, "rep", split_axis=2, concat_axis=1, tiled=True)
    col_index = lax.axis_index("tensor") * col_local + lax.broadcasted_iota(
        jnp.int32, (col_local, 1, 1), 0
    )
    row_index = lax.axis_index("rep") * row_local + lax.broadcasted_iota(
        jnp.int32, (1, 1, row_local), 2
    )
    keep = (col_index < col_count[None, :, None]) & (row_index < row_count[None, :, None])
    return jnp.where(keep, arranged, jnp.float32(0.0))


def solution(mesh):
    in_specs = (P("rep", "tensor", None), P(None, "rep", "tensor"), P(), P(), P())
    out_specs = P("tensor", None, "rep")
    return jax.shard_map(local, mesh=mesh, in_specs=in_specs, out_specs=out_specs, check_vma=False)
```

profile of v0, /device:TPU:0, one launch (start us, length us, event | category | flops | bytes accessed | tf_op | source)
XLA Modules:
  0.0 488.2 jit_solution(14435926594990211834)
XLA Ops:
  6.5 0.0 all-reduce.3.cloned.1.call-start
  6.5 0.7 dynamic_slice.3
  7.3 0.1 broadcast_compare_fusion.1
  7.3 121.2 %fusion.3 = f32[1024,4,1024]{0,2,1:T(8,128)} fusion(f32[1024,4,1024]{2,1,0:T(4,128)} %param.6, f32[4,1024,1024]{2,1,0:T(8,128)} %param.5, pred[4,1024]{1,0:T(4,128)(4,1)S(1)} %broadcast_compare_fusion.1), kind=kOutput, calls=%fused_computation.3 | convolution fusion | flops 51543801856 | bytes 50335744 | tf_op jit(solution)/shard_map/chk,hkr->chr/dot_general | solution.py:21
  128.6 20.2 %copy.11 = f32[1024,4,1024]{2,1,0:T(4,128)} copy(f32[1024,4,1024]{0,2,1:T(8,128)} %fusion.3) | data formatting | bytes 33554432 | tf_op jit(solution)/shard_map/chk,hkr->chr/transpose | solution.py:21
  148.7 0.0 all-reduce.3.cloned.1.call-update
  148.8 0.6 copy-done.2
  149.4 0.6 dynamic-slice
  150.6 299.2 %all-reduce.3.cloned.1.call-done = f32[1024,4,1024]{2,1,0:T(4,128)} async-done(((f32[1024,4,1024]{2,1,0:T(4,128)}), f32[1024,4,1024]{2,1,0:T(4,128)}) %all-reduce.3.cloned.1.call-update) | async-done | bytes 16777232
  449.9 1.3 constant_dynamic-slice_fusion
  451.2 0.9 copy.12
  452.1 2.8 reshape.111
  454.9 3.6 all-to-all-start
  458.5 0.0 copy-done.1
  458.5 0.1 broadcast_compare_fusion.2
  458.6 0.0 copy-done
  458.6 0.1 broadcast_compare_fusion
  458.6 14.0 %all-to-all-done = f32[2,1,131072]{2,1,0:T(1,128)S(1)} async-done(((f32[2,1,131072]{2,1,0:T(1,128)}), f32[2,1,131072]{2,1,0:T(1,128)S(1)}, u32[]{:S(2)}, u32[]{:S(2)}) %all-to-all-start) | async-done | bytes 1048608 | tf_op jit(solution)/shard_map/all_to_all | solution.py:29
  472.6 0.5 broadcast.82
  473.1 4.0 reduce
  477.1 1.7 reshape.112
  478.9 0.9 copy.13
  479.8 0.4 all_to_all.16
  480.2 1.1 and_select_fusion
  (6 shorter events, 0.0 us)
Async XLA Ops:
  6.5 443.3 %all-reduce.3.cloned.1.call-start = ((), (), s32[]{:S(2)}) async-start(), calls=%async_computation.1 | async-start | bytes 33554432
  148.7 0.7 copy-start.2
  148.7 309.7 %copy-start.1 = (s32[8]{0:T(128)S(1)}, s32[8]{0:T(128)}, u32[]{:S(2)}) copy-start(s32[8]{0:T(128)} %param.7) | copy-start | bytes 100
  148.7 309.8 %copy-start = (s32[8]{0:T(128)S(1)}, s32[8]{0:T(128)}, u32[]{:S(2)}) copy-start(s32[8]{0:T(128)} %param.9) | copy-start | bytes 100
  454.9 17.7 %all-to-all-start = ((f32[2,1,131072]{2,1,0:T(1,128)}), f32[2,1,131072]{2,1,0:T(1,128)S(1)}, u32[]{:S(2)}, u32[]{:S(2)}) async-start(f32[2,1,131072]{2,1,0:T(1,128)} %reshape.111), calls=%async_computation | async-start | bytes 2097152 | tf_op jit(solution)/shard_map/all_to_all | solution.py:29
Sparse Core Ops, SparseCore 0:
  148.9 300.9 all-reduce.2
where the time goes:
time: 489 us; the launch traced here: 488 us
  waiting for transfers between devices  313 us (64%)
  matrix products  121 us (25%)
  local copies, waits for them, and re-layouts  30.6 us (6%)
  between operations  14.1 us (3%)
  other arithmetic  5.41 us (1%)
    unnamed x2, waiting for transfers between devices  299 us
    dot_general x1, matrix products, local(): jnp.einsum('chk,hkr->chr', integrals, masked, precision=lax.Precision.HIG...  121 us
    transpose x1, local copies, waits for them, and re-layouts, local(): jnp.einsum('chk,hkr->chr', integrals, masked, precision=lax.Precision.HIG...  20.2 us
    all_to_all x1, waiting for transfers between devices, local(): lax.all_to_all(summed, 'rep', split_axis=2, concat_axis=1, tiled=True)  14 us
  transfers between devices with their start and end apart: 2, of which 2 were waited for; matrix products, arithmetic and copies ran while one was open for 0% of the time, Pallas kernels for 0%

commit v1 on v0

v1 whole, which is shorter than its diff:
```python
import functools

import jax
import jax.numpy as jnp
from jax import lax
from jax.experimental import pallas as pl
from jax.experimental.pallas import tpu as pltpu
from jax.sharding import PartitionSpec as P

OUTER = 4
CORES = 2
VMEM_BYTES = 56 * 1024 * 1024
F32 = jnp.float32
BF16 = jnp.bfloat16


def split(value):
    high = value.astype(BF16)
    return high, (value - high.astype(F32)).astype(BF16)


def prep_kernel(place, limit, b_ref, high_ref, low_ref):
    blocks, depth = b_ref.shape[1], b_ref.shape[2]
    pair = lax.broadcasted_iota(jnp.int32, (1, depth), 1)
    for h in range(blocks):
        value = jnp.where(pair < limit[h], b_ref[:, h, :], F32(0.0))
        high, low = split(value)
        high_ref[h, 0, 0] = high
        low_ref[h, 0, 0] = low


def prepare(integrals, place, limit, inner, cols):
    _, blocks, depth = integrals.shape
    groups = inner * OUTER

    def source(c, g, place, limit):
        return (((g // inner) * inner + g % inner) * CORES + c, 0, 0)

    def target(c, g, place, limit):
        z = lax.rem(g // inner - place[0] + OUTER, OUTER)
        x = lax.rem(g % inner - place[1] + inner, inner)
        core = lax.rem(c - place[2] + CORES, CORES)
        return (0, core, x * OUTER + z, 0, 0)

    shape = jax.ShapeDtypeStruct((blocks, CORES, groups, cols, depth), BF16)
    spec = pl.BlockSpec((blocks, 1, 1, cols, depth), target)
    return pl.pallas_call(
        prep_kernel,
        grid_spec=pltpu.PrefetchScalarGridSpec(
            num_scalar_prefetch=2,
            grid=(CORES, groups),
            in_specs=[pl.BlockSpec((cols, blocks, depth), source)],
            out_specs=[spec, spec],
        ),
        out_shape=[shape, shape],
        compiler_params=pltpu.CompilerParams(vmem_limit_bytes=VMEM_BYTES),
        name="prepare",
    )(place, limit, integrals)


def product(b_high, b_low, a_high, a_low):
    dot = functools.partial(jnp.dot, preferred_element_type=F32)
    return dot(b_high, a_high) + (dot(b_high, a_low) + dot(b_low, a_high))


def first_kernel(rows_live, b_high, b_low, a_ref, out, a_high, a_low):
    tile = a_ref.shape[2]
    groups, cols, depth = b_high.shape[2:]
    high, low = split(a_ref[0])
    a_high[...] = high
    a_low[...] = low
    live = pl.program_id(0) * tile < rows_live[0]

    @pl.when(live)
    def _():
        left = (r[0, 0].reshape(groups * cols, depth) for r in (b_high, b_low))
        out[...] = product(*left, high, low)

    @pl.when(jnp.logical_not(live))
    def _():
        out[...] = jnp.zeros_like(out)


def second_kernel(rows_live, b_high, b_low, a_high, a_low, received, *outs):
    tile = a_high.shape[1]
    groups, cols, depth = b_high.shape[2:]
    size = outs[0].shape[0]
    live = pl.program_id(0) * tile < rows_live[0]

    @pl.when(live)
    def _():
        left = (r[0, 0].reshape(groups * cols, depth) for r in (b_high, b_low))
        total = received[...] + product(*left, a_high[...], a_low[...])
        for i, out in enumerate(outs):
            out[...] = total[i * size:(i + 1) * size]

    @pl.when(jnp.logical_not(live))
    def _():
        for i, out in enumerate(outs):
            out[...] = received[i * size:(i + 1) * size, :]


def cost(m, k, n):
    return pl.CostEstimate(
        flops=6 * m * k * n, bytes_accessed=4 * (m * k + k * n + m * n), transcendentals=0
    )


def first_half(h, rows_live, b_high, b_low, amplitudes):
    _, _, groups, cols, depth = b_high.shape
    rows = amplitudes.shape[2]
    tile = min(rows, 256)
    left = pl.BlockSpec((1, 1, groups, cols, depth), lambda n, s: (h, 1, 0, 0, 0))
    wide = pl.BlockSpec((depth, tile), lambda n, s: (0, n))
    return pl.pallas_call(
        first_kernel,
        grid_spec=pltpu.PrefetchScalarGridSpec(
            num_scalar_prefetch=1,
            grid=(rows // tile,),
            in_specs=[left, left, pl.BlockSpec((1, depth, tile), lambda n, s: (h, 0, n))],
            out_specs=[pl.BlockSpec((groups * cols, tile), lambda n, s: (0, n)), wide, wide],
        ),
        out_shape=[
            jax.ShapeDtypeStruct((groups * cols, rows), F32),
            jax.ShapeDtypeStruct((depth, rows), BF16),
            jax.ShapeDtypeStruct((depth, rows), BF16),
        ],
        cost_estimate=cost(groups * cols, depth, rows),
        compiler_params=pltpu.CompilerParams(vmem_limit_bytes=VMEM_BYTES),
        name="first_half",
    )(rows_live, b_high, b_low, amplitudes)


def second_half(h, rows_live, b_high, b_low, a_high, a_low, received, inner):
    _, _, groups, cols, depth = b_high.shape
    rows = a_high.shape[1]
    tile = min(rows, 256)
    size = groups * cols // inner
    left = pl.BlockSpec((1, 1, groups, cols, depth), lambda n, s: (h, 0, 0, 0, 0))
    wide = pl.BlockSpec((depth, tile), lambda n, s: (0, n))
    return pl.pallas_call(
        second_kernel,
        grid_spec=pltpu.PrefetchScalarGridSpec(
            num_scalar_prefetch=1,
            grid=(rows // tile,),
            in_specs=[left, left, wide, wide,
                      pl.BlockSpec((groups * cols, tile), lambda n, s: (0, n))],
            out_specs=[pl.BlockSpec((size, tile), lambda n, s: (0, n))] * inner,
        ),
        out_shape=[jax.ShapeDtypeStruct((size, rows), F32)] * inner,
        cost_estimate=cost(groups * cols, depth, rows),
        compiler_params=pltpu.CompilerParams(vmem_limit_bytes=VMEM_BYTES),
        name="second_half",
    )(rows_live, b_high, b_low, a_high, a_low, received)


def line_sum(shards, pairs_of):
    n = len(shards)
    if n == 2:
        return shards[0] + lax.ppermute(shards[1], "tensor", pairs_of([(0, 1), (1, 0)]))
    up = down = None
    for step in range(1, n):
        reach = n - step
        send_up, send_down = shards[reach], shards[step]
        if up is not None:
            send_up, send_down = send_up + up, send_down + down
        up = lax.ppermute(send_up, "tensor", pairs_of([(i, i + 1) for i in range(step)]))
        down = lax.ppermute(
            send_down, "tensor", pairs_of([(i, i - 1) for i in range(reach, n)])
        )
    return shards[0] + up + down


def local(inner, amplitudes, integrals, row_count, pair_count, col_count):
    blocks, depth, rows = amplitudes.shape
    all_cols = integrals.shape[0]
    tensor, rep = lax.axis_size("tensor"), lax.axis_size("rep")
    cols, row_local = all_cols // tensor, rows // rep
    me, side = lax.axis_index("tensor"), lax.axis_index("rep")
    z, x, core = me // (inner * CORES), me // CORES % inner, me % CORES
    place = jnp.stack([z, x, core]).astype(jnp.int32)

    pairs_here = lax.dynamic_slice_in_dim(pair_count, side * blocks, blocks) - me * depth
    rows_here = lax.dynamic_slice_in_dim(row_count, side * blocks, blocks)
    rows_here = jnp.where(pairs_here > 0, rows_here, 0)
    b_high, b_low = prepare(integrals, place, pairs_here, inner, cols)

    def index(z, x, core):
        return (z * inner + x) * CORES + core

    across = [(index(z, x, c), index(z, x, 1 - c))
              for z in range(OUTER) for x in range(inner) for c in range(CORES)]

    def along_inner(moves):
        return [(index(z, a, c), index(z, b, c))
                for z in range(OUTER) for c in range(CORES) for a, b in moves]

    def along_outer(moves):
        return [(index(a, x, c), index(b, x, c))
                for x in range(inner) for c in range(CORES) for a, b in moves]

    halves = []
    for h in range(blocks):
        live = rows_here[h:h + 1]
        sent, a_high, a_low = first_half(h, live, b_high, b_low, amplitudes)
        received = lax.ppermute(sent, "tensor", across)
        halves.append((live, a_high, a_low, received))
    mine, other = [], []
    for h in range(blocks):
        live, a_high, a_low, received = halves[h]
        shards = second_half(h, live, b_high, b_low, a_high, a_low, received, inner)
        summed = line_sum(shards, along_inner)
        total = line_sum([summed[j * cols:(j + 1) * cols] for j in range(OUTER)], along_outer)
        if rep == 2:
            mine.append(lax.dynamic_slice_in_dim(total, side * row_local, row_local, 1))
            away = lax.dynamic_slice_in_dim(total, (1 - side) * row_local, row_local, 1)
            other.append(lax.ppermute(away, "rep", [(0, 1), (1, 0)]))
        else:
            mine.append(total)
    if rep == 2:
        swap = side == 1
        low = [jnp.where(swap, b, a) for a, b in zip(mine, other)]
        high = [jnp.where(swap, a, b) for a, b in zip(mine, other)]
        arranged = jnp.stack(low + high, axis=1)
    else:
        arranged = lax.all_to_all(
            jnp.stack(mine, axis=1), "rep", split_axis=2, concat_axis=1, tiled=True
        )
    col_index = me * cols + lax.broadcasted_iota(jnp.int32, (cols, 1, 1), 0)
    row_index = side * row_local + lax.broadcasted_iota(jnp.int32, (1, 1, row_local), 2)
    keep = (col_index < col_count[None, :, None]) & (row_index < row_count[None, :, None])
    return jnp.where(keep, arranged, F32(0.0))


def solution(mesh):
    inner = mesh.shape["tensor"] // (OUTER * CORES)
    in_specs = (P("rep", "tensor", None), P(None, "rep", "tensor"), P(), P(), P())
    out_specs = P("tensor", None, "rep")
    return jax.shard_map(
        functools.partial(local, inner), mesh=mesh, in_specs=in_specs, out_specs=out_specs,
        check_vma=False,
    )
```

time: 489 us -> 234 us (0.48)
  waiting for transfers between devices: 313 us -> 66.9 us
  matrix products: 121 us -> 0 us
  Pallas kernels: 0 us -> 85.7 us
  starting transfers between devices: 3.58 us -> 71.6 us
  local copies, waits for them, and re-layouts: 30.6 us -> 3.83 us
  between operations: 14.1 us -> 0.65 us
    unnamed x2 -> x0, waiting for transfers between devices: 299 us -> none
    dot_general x1 -> x0, matrix products: 121 us -> none  [local(): jnp.einsum('chk,hkr->chr', integrals, masked, precision=lax.Precision.HIG...]
    pallas_call x0 -> x9, Pallas kernels: none -> 85.7 us  [the longest x4 34.3 us: first_half(): pl.pallas_call(first_kernel, grid_spec=pltpu.PrefetchScalarGridSpec(num_s...]
    ppermute x0 -> x36, starting transfers between devices: none -> 71.6 us  [the longest x12 41.6 us: line_sum(): lax.ppermute(send_up, 'tensor', pairs_of([(i, i + 1) for i in range(step)]))]
    ppermute x0 -> x36, waiting for transfers between devices: none -> 66.9 us  [the longest x4 59.1 us: line_sum(): lax.ppermute(shards[1], 'tensor', pairs_of([(0, 1), (1, 0)]))]
    transpose x1 -> x0, local copies, waits for them, and re-layouts: 20.2 us -> none  [local(): jnp.einsum('chk,hkr->chr', integrals, masked, precision=lax.Precision.HIG...]
    all_to_all x1 -> x0, waiting for transfers between devices: 14 us -> none  [local(): lax.all_to_all(summed, 'rep', split_axis=2, concat_axis=1, tiled=True)]
    unnamed x10 -> x14, local copies, waits for them, and re-layouts: 7.01 us -> 1.39 us
  transfers between devices with their start and end apart: 2 -> 36, of which waited for: 2 -> 6; matrix products, arithmetic and copies ran while one was open for 0% -> 1% of each run, Pallas kernels for 0% -> 24%
where the time goes in v1:
time: 234 us; the launch traced here: 232 us
  Pallas kernels  85.7 us (37%)
  starting transfers between devices  71.6 us (31%)
  waiting for transfers between devices  66.9 us (29%)
  local copies, waits for them, and re-layouts  3.83 us (2%)
  other arithmetic  3.69 us (2%)
    ppermute x4, waiting for transfers between devices, line_sum(): lax.ppermute(shards[1], 'tensor', pairs_of([(0, 1), (1, 0)]))  59.1 us
    ppermute x12, starting transfers between devices, line_sum(): lax.ppermute(send_up, 'tensor', pairs_of([(i, i + 1) for i in range(step)]))  41.6 us
    pallas_call x4, Pallas kernels, first_half(): pl.pallas_call(first_kernel, grid_spec=pltpu.PrefetchScalarGridSpec(num_s...  34.3 us
    pallas_call x4, Pallas kernels, second_half(): pl.pallas_call(second_kernel, grid_spec=pltpu.PrefetchScalarGridSpec(num_...  31.2 us
    pallas_call x1, Pallas kernels, prepare(): pl.pallas_call(prep_kernel, grid_spec=pltpu.PrefetchScalarGridSpec(num_sc...  20.2 us
    ppermute x4, starting transfers between devices, local(): other.append(lax.ppermute(away, 'rep', [(0, 1), (1, 0)]))  13.5 us
    ppermute x12, starting transfers between devices, line_sum(): lax.ppermute(send_down, 'tensor', pairs_of([(i, i - 1) for i in range(rea...  10.6 us
    ppermute x4, waiting for transfers between devices, local(): other.append(lax.ppermute(away, 'rep', [(0, 1), (1, 0)]))  5.38 us
  transfers between devices with their start and end apart: 36, of which 6 were waited for; matrix products, arithmetic and copies ran while one was open for 1% of the time, Pallas kernels for 24%

profile of v1, /device:TPU:0, one launch (start us, length us, event | category | flops | bytes accessed | tf_op | source)
XLA Modules:
  0.0 232.4 jit_solution(5287760223915768837)
XLA Ops:
  2.5 20.2 %prepare.1 = (bf16[4,2,8,64,1024]{4,3,2,1,0:T(8,128)(2,1)}, bf16[4,2,8,64,1024]{4,3,2,1,0:T(8,128)(2,1)}) custom-call(s32[3]{0:T(128)} %pad_add_fusion.place, s32[4]{0:T(128)} %get-tuple-element.50.limit, f32[1024,4,1024]{2,1,0:T(4,128)} %b_ref.1), custom_call_target="tpu_custom_call" | custom-call | tf_op jit(solution)/shard_map/prepare/pallas_call | solution.py:47
  22.8 9.2 %first_half.7 = (f32[512,1024]{1,0:T(8,128)}, bf16[1024,1024]{1,0:T(8,128)(2,1)}, bf16[1024,1024]{1,0:T(8,128)(2,1)}) custom-call(s32[1]{0:T(128)} %get-tuple-element.75.rows_live, bf16[4,2,8,64,1024]{4,3,2,1,0:T(8,128)(2,1)} %get-tuple-element.27.b_high, bf16[4,2,8,64,1024]{4,3,2,1,0:T(8,128)(2,1)} %get-tuple-element.28.b_low, f32[4,1024,1024]{2,1,0:T(8,128)} %a_ref.7), custom_call_target="tpu_custom_call" | custom-call | flops 3221225472 | bytes 8388608 | tf_op jit(solution)/shard_map/first_half/pallas_call | solution.py:115
  32.3 8.4 %first_half.6 = (f32[512,1024]{1,0:T(8,128)}, bf16[1024,1024]{1,0:T(8,128)(2,1)}, bf16[1024,1024]{1,0:T(8,128)(2,1)}) custom-call(s32[1]{0:T(128)} %get-tuple-element.76.rows_live, bf16[4,2,8,64,1024]{4,3,2,1,0:T(8,128)(2,1)} %get-tuple-element.27.b_high, bf16[4,2,8,64,1024]{4,3,2,1,0:T(8,128)(2,1)} %get-tuple-element.28.b_low, f32[4,1024,1024]{2,1,0:T(8,128)} %a_ref.7), custom_call_target="tpu_custom_call" | custom-call | flops 3221225472 | bytes 8388608 | tf_op jit(solution)/shard_map/first_half/pallas_call | solution.py:115
  40.8 8.4 %first_half.5 = (f32[512,1024]{1,0:T(8,128)}, bf16[1024,1024]{1,0:T(8,128)(2,1)}, bf16[1024,1024]{1,0:T(8,128)(2,1)}) custom-call(s32[1]{0:T(128)} %get-tuple-element.77.rows_live, bf16[4,2,8,64,1024]{4,3,2,1,0:T(8,128)(2,1)} %get-tuple-element.27.b_high, bf16[4,2,8,64,1024]{4,3,2,1,0:T(8,128)(2,1)} %get-tuple-element.28.b_low, f32[4,1024,1024]{2,1,0:T(8,128)} %a_ref.7), custom_call_target="tpu_custom_call" | custom-call | flops 3221225472 | bytes 8388608 | tf_op jit(solution)/shard_map/first_half/pallas_call | solution.py:115
  49.7 8.3 %first_half.4 = (f32[512,1024]{1,0:T(8,128)}, bf16[1024,1024]{1,0:T(8,128)(2,1)}, bf16[1024,1024]{1,0:T(8,128)(2,1)}) custom-call(s32[1]{0:T(128)} %get-tuple-element.78.rows_live, bf16[4,2,8,64,1024]{4,3,2,1,0:T(8,128)(2,1)} %get-tuple-element.27.b_high, bf16[4,2,8,64,1024]{4,3,2,1,0:T(8,128)(2,1)} %get-tuple-element.28.b_low, f32[4,1024,1024]{2,1,0:T(8,128)} %a_ref.7), custom_call_target="tpu_custom_call" | custom-call | flops 3221225472 | bytes 8388608 | tf_op jit(solution)/shard_map/first_half/pallas_call | solution.py:115
  58.2 8.4 %second_half.7 = (f32[256,1024]{1,0:T(8,128)}, f32[256,1024]{1,0:T(8,128)}) custom-call(s32[1]{0:T(128)} %get-tuple-element.75.rows_live, bf16[4,2,8,64,1024]{4,3,2,1,0:T(8,128)(2,1)} %get-tuple-element.27.b_high, bf16[4,2,8,64,1024]{4,3,2,1,0:T(8,128)(2,1)} %get-tuple-element.28.b_low, bf16[1024,1024]{1,0:T(8,128)(2,1)} %get-tuple-element.44.a_high, ...), custom_call_target="tpu_custom_call" | custom-call | flops 3221225472 | bytes 8388608 | tf_op jit(solution)/shard_map/second_half/pallas_call | solution.py:141
  66.6 2.9 %collective-permute-start.28 = (f32[256,1024]{1,0:T(8,128)}, f32[256,1024]{1,0:T(8,128)S(1)}, u32[]{:S(2)}, u32[]{:S(2)}) collective-permute-start(f32[256,1024]{1,0:T(8,128)} %get-tuple-element.48), channel_id=1, source_target_pairs={{0,4},{4,0},{2,6},{6,2},{8,12},{12,8},{10,14},{14,10},{16,20},{20,... | collective-permute-start | bytes 3145736 | tf_op jit(solution)/shard_map/ppermute | solution.py:160
  69.5 7.5 %second_half.6 = (f32[256,1024]{1,0:T(8,128)}, f32[256,1024]{1,0:T(8,128)}) custom-call(s32[1]{0:T(128)} %get-tuple-element.76.rows_live, bf16[4,2,8,64,1024]{4,3,2,1,0:T(8,128)(2,1)} %get-tuple-element.27.b_high, bf16[4,2,8,64,1024]{4,3,2,1,0:T(8,128)(2,1)} %get-tuple-element.28.b_low, bf16[1024,1024]{1,0:T(8,128)(2,1)} %get-tuple-element.39.a_high, ...), custom_call_target="tpu_custom_call" | custom-call | flops 3221225472 | bytes 8388608 | tf_op jit(solution)/shard_map/second_half/pallas_call | solution.py:141
  77.0 7.4 %second_half.5 = (f32[256,1024]{1,0:T(8,128)}, f32[256,1024]{1,0:T(8,128)}) custom-call(s32[1]{0:T(128)} %get-tuple-element.77.rows_live, bf16[4,2,8,64,1024]{4,3,2,1,0:T(8,128)(2,1)} %get-tuple-element.27.b_high, bf16[4,2,8,64,1024]{4,3,2,1,0:T(8,128)(2,1)} %get-tuple-element.28.b_low, bf16[1024,1024]{1,0:T(8,128)(2,1)} %get-tuple-element.34.a_high, ...), custom_call_target="tpu_custom_call" | custom-call | flops 3221225472 | bytes 8388608 | tf_op jit(solution)/shard_map/second_half/pallas_call | solution.py:141
  87.8 7.9 %second_half.4 = (f32[256,1024]{1,0:T(8,128)}, f32[256,1024]{1,0:T(8,128)}) custom-call(s32[1]{0:T(128)} %get-tuple-element.78.rows_live, bf16[4,2,8,64,1024]{4,3,2,1,0:T(8,128)(2,1)} %get-tuple-element.27.b_high, bf16[4,2,8,64,1024]{4,3,2,1,0:T(8,128)(2,1)} %get-tuple-element.28.b_low, bf16[1024,1024]{1,0:T(8,128)(2,1)} %get-tuple-element.29.a_high, ...), custom_call_target="tpu_custom_call" | custom-call | flops 3221225472 | bytes 8388608 | tf_op jit(solution)/shard_map/second_half/pallas_call | solution.py:141
  98.1 18.2 %collective-permute-done.19 = f32[256,1024]{1,0:T(8,128)S(1)} collective-permute-done((f32[256,1024]{1,0:T(8,128)}, f32[256,1024]{1,0:T(8,128)S(1)}, u32[]{:S(2)}, u32[]{:S(2)}) %collective-permute-start.19) | collective-permute-done | bytes 1048608 | tf_op jit(solution)/shard_map/ppermute | solution.py:160
  117.9 20.8 %collective-permute-done.10 = f32[256,1024]{1,0:T(8,128)S(1)} collective-permute-done((f32[256,1024]{1,0:T(8,128)}, f32[256,1024]{1,0:T(8,128)S(1)}, u32[]{:S(2)}, u32[]{:S(2)}) %collective-permute-start.10) | collective-permute-done | bytes 1048608 | tf_op jit(solution)/shard_map/ppermute | solution.py:160
  139.6 20.1 %collective-permute-done.1 = f32[256,1024]{1,0:T(8,128)S(1)} collective-permute-done((f32[256,1024]{1,0:T(8,128)}, f32[256,1024]{1,0:T(8,128)S(1)}, u32[]{:S(2)}, u32[]{:S(2)}) %collective-permute-start.1) | collective-permute-done | bytes 1048608 | tf_op jit(solution)/shard_map/ppermute | solution.py:160
  165.4 2.3 collective-permute-done.11
  168.4 5.0 %collective-permute-start.21 = (f32[64,1024]{1,0:T(8,128)S(1)}, f32[64,1024]{1,0:T(8,128)S(1)}, u32[]{:S(2)}, u32[]{:S(2)}) collective-permute-start(f32[64,1024]{1,0:T(8,128)S(1)} %get-tuple-element.59), channel_id=1, source_target_pairs={{0,8},{8,16},{2,10},{10,18},{4,12},{12,20},{6,14},{14,22},{1,9},{9... | collective-permute-start | bytes 786440 | tf_op jit(solution)/shard_map/ppermute | solution.py:167
  174.2 5.2 %collective-permute-start.12 = (f32[64,1024]{1,0:T(8,128)S(1)}, f32[64,1024]{1,0:T(8,128)S(1)}, u32[]{:S(2)}, u32[]{:S(2)}) collective-permute-start(f32[64,1024]{1,0:T(8,128)S(1)} %get-tuple-element.65), channel_id=1, source_target_pairs={{0,8},{8,16},{2,10},{10,18},{4,12},{12,20},{6,14},{14,22},{1,9},{9... | collective-permute-start | bytes 786440 | tf_op jit(solution)/shard_map/ppermute | solution.py:167
  180.2 5.2 %collective-permute-start.3 = (f32[64,1024]{1,0:T(8,128)S(1)}, f32[64,1024]{1,0:T(8,128)S(1)}, u32[]{:S(2)}, u32[]{:S(2)}) collective-permute-start(f32[64,1024]{1,0:T(8,128)S(1)} %get-tuple-element.71), channel_id=1, source_target_pairs={{0,8},{8,16},{2,10},{10,18},{4,12},{12,20},{6,14},{14,22},{1,9},{9... | collective-permute-start | bytes 786440 | tf_op jit(solution)/shard_map/ppermute | solution.py:167
  186.1 5.2 %collective-permute-start.31 = (f32[64,1024]{1,0:T(8,128)S(1)}, f32[64,1024]{1,0:T(8,128)S(1)}, u32[]{:S(2)}, u32[]{:S(2)}) collective-permute-start(f32[64,1024]{1,0:T(8,128)S(1)} %get-tuple-element.51), channel_id=1, source_target_pairs={{0,8},{8,16},{16,24},{2,10},{10,18},{18,26},{4,12},{12,20},{20,28}... | collective-permute-start | bytes 786440 | tf_op jit(solution)/shard_map/ppermute | solution.py:167
  192.7 5.2 %collective-permute-start.22 = (f32[64,1024]{1,0:T(8,128)S(1)}, f32[64,1024]{1,0:T(8,128)S(1)}, u32[]{:S(2)}, u32[]{:S(2)}) collective-permute-start(f32[64,1024]{1,0:T(8,128)S(1)} %get-tuple-element.57), channel_id=1, source_target_pairs={{0,8},{8,16},{16,24},{2,10},{10,18},{18,26},{4,12},{12,20},{20,28}... | collective-permute-start | bytes 786440 | tf_op jit(solution)/shard_map/ppermute | solution.py:167
  199.3 4.6 %collective-permute-start.13 = (f32[64,1024]{1,0:T(8,128)S(1)}, f32[64,1024]{1,0:T(8,128)S(1)}, u32[]{:S(2)}, u32[]{:S(2)}) collective-permute-start(f32[64,1024]{1,0:T(8,128)S(1)} %get-tuple-element.63), channel_id=1, source_target_pairs={{0,8},{8,16},{16,24},{2,10},{10,18},{18,26},{4,12},{12,20},{20,28}... | collective-permute-start | bytes 786440 | tf_op jit(solution)/shard_map/ppermute | solution.py:167
  205.2 4.6 %collective-permute-start.4 = (f32[64,1024]{1,0:T(8,128)S(1)}, f32[64,1024]{1,0:T(8,128)S(1)}, u32[]{:S(2)}, u32[]{:S(2)}) collective-permute-start(f32[64,1024]{1,0:T(8,128)S(1)} %get-tuple-element.69), channel_id=1, source_target_pairs={{0,8},{8,16},{16,24},{2,10},{10,18},{18,26},{4,12},{12,20},{20,28}... | collective-permute-start | bytes 786440 | tf_op jit(solution)/shard_map/ppermute | solution.py:167
  211.2 6.3 %collective-permute-start.35 = (f32[64,512]{1,0:T(8,128)S(1)}, f32[64,512]{1,0:T(8,128)S(1)}, u32[]{:S(2)}, u32[]{:S(2)}) collective-permute-start(f32[64,512]{1,0:T(8,128)S(1)} %constant_dynamic-slice_fusion), channel_id=1, source_target_pairs={{0,1},{1,0},{2,3},{3,2},{4,5},{5,4},{6,7},{7,6},{8,9},{9,8},{10,11... | collective-permute-start | bytes 393224 | tf_op jit(solution)/shard_map/ppermute | solution.py:217
  217.6 5.0 %collective-permute-start.26 = (f32[64,512]{1,0:T(8,128)S(1)}, f32[64,512]{1,0:T(8,128)S(1)}, u32[]{:S(2)}, u32[]{:S(2)}) collective-permute-start(f32[64,512]{1,0:T(8,128)S(1)} %constant_dynamic-slice_fusion.1), channel_id=1, source_target_pairs={{0,1},{1,0},{2,3},{3,2},{4,5},{5,4},{6,7},{7,6},{8,9},{9,8},{10,11... | collective-permute-start | bytes 393224 | tf_op jit(solution)/shard_map/ppermute | solution.py:217
  225.0 4.0 %collective-permute-done.8 = f32[64,512]{1,0:T(8,128)S(1)} collective-permute-done((f32[64,512]{1,0:T(8,128)S(1)}, f32[64,512]{1,0:T(8,128)S(1)}, u32[]{:S(2)}, u32[]{:S(2)}) %collective-permute-start.8) | collective-permute-done | bytes 131104 | tf_op jit(solution)/shard_map/ppermute | solution.py:217
  (112 shorter events, 31.5 us)
Async XLA Ops:
  31.9 26.3 %collective-permute-start.27 = (f32[512,1024]{1,0:T(8,128)}, f32[512,1024]{1,0:T(8,128)}, u32[]{:S(2)}, u32[]{:S(2)}) collective-permute-start(f32[512,1024]{1,0:T(8,128)} %get-tuple-element.46), channel_id=1, source_target_pairs={{0,2},{2,0},{4,6},{6,4},{8,10},{10,8},{12,14},{14,12},{16,18},{18,... | collective-permute-start | bytes 6291464 | tf_op jit(solution)/shard_map/ppermute | solution.py:206
  40.8 28.7 %collective-permute-start.18 = (f32[512,1024]{1,0:T(8,128)}, f32[512,1024]{1,0:T(8,128)}, u32[]{:S(2)}, u32[]{:S(2)}) collective-permute-start(f32[512,1024]{1,0:T(8,128)} %get-tuple-element.41), channel_id=1, source_target_pairs={{0,2},{2,0},{4,6},{6,4},{8,10},{10,8},{12,14},{14,12},{16,18},{18,... | collective-permute-start | bytes 6291464 | tf_op jit(solution)/shard_map/ppermute | solution.py:206
  49.2 27.7 %collective-permute-start.9 = (f32[512,1024]{1,0:T(8,128)}, f32[512,1024]{1,0:T(8,128)}, u32[]{:S(2)}, u32[]{:S(2)}) collective-permute-start(f32[512,1024]{1,0:T(8,128)} %get-tuple-element.36), channel_id=1, source_target_pairs={{0,2},{2,0},{4,6},{6,4},{8,10},{10,8},{12,14},{14,12},{16,18},{18,... | collective-permute-start | bytes 6291464 | tf_op jit(solution)/shard_map/ppermute | solution.py:206
  58.0 28.4 %collective-permute-start = (f32[512,1024]{1,0:T(8,128)}, f32[512,1024]{1,0:T(8,128)S(1)}, u32[]{:S(2)}, u32[]{:S(2)}) collective-permute-start(f32[512,1024]{1,0:T(8,128)} %get-tuple-element.31), channel_id=1, source_target_pairs={{0,2},{2,0},{4,6},{6,4},{8,10},{10,8},{12,14},{14,12},{16,18},{18,... | collective-permute-start | bytes 6291464 | tf_op jit(solution)/shard_map/ppermute | solution.py:206
  66.6 29.2 %collective-permute-start.28 = (f32[256,1024]{1,0:T(8,128)}, f32[256,1024]{1,0:T(8,128)S(1)}, u32[]{:S(2)}, u32[]{:S(2)}) collective-permute-start(f32[256,1024]{1,0:T(8,128)} %get-tuple-element.48), channel_id=1, source_target_pairs={{0,4},{4,0},{2,6},{6,2},{8,12},{12,8},{10,14},{14,10},{16,20},{20,... | collective-permute-start | bytes 3145736 | tf_op jit(solution)/shard_map/ppermute | solution.py:160
  77.0 39.3 %collective-permute-start.19 = (f32[256,1024]{1,0:T(8,128)}, f32[256,1024]{1,0:T(8,128)S(1)}, u32[]{:S(2)}, u32[]{:S(2)}) collective-permute-start(f32[256,1024]{1,0:T(8,128)} %get-tuple-element.43), channel_id=1, source_target_pairs={{0,4},{4,0},{2,6},{6,2},{8,12},{12,8},{10,14},{14,10},{16,20},{20,... | collective-permute-start | bytes 3145736 | tf_op jit(solution)/shard_map/ppermute | solution.py:160
  84.4 54.3 %collective-permute-start.10 = (f32[256,1024]{1,0:T(8,128)}, f32[256,1024]{1,0:T(8,128)S(1)}, u32[]{:S(2)}, u32[]{:S(2)}) collective-permute-start(f32[256,1024]{1,0:T(8,128)} %get-tuple-element.38), channel_id=1, source_target_pairs={{0,4},{4,0},{2,6},{6,2},{8,12},{12,8},{10,14},{14,10},{16,20},{20,... | collective-permute-start | bytes 3145736 | tf_op jit(solution)/shard_map/ppermute | solution.py:160
  95.7 64.1 %collective-permute-start.1 = (f32[256,1024]{1,0:T(8,128)}, f32[256,1024]{1,0:T(8,128)S(1)}, u32[]{:S(2)}, u32[]{:S(2)}) collective-permute-start(f32[256,1024]{1,0:T(8,128)} %get-tuple-element.33), channel_id=1, source_target_pairs={{0,4},{4,0},{2,6},{6,2},{8,12},{12,8},{10,14},{14,10},{16,20},{20,... | collective-permute-start | bytes 3145736 | tf_op jit(solution)/shard_map/ppermute | solution.py:160
  96.0 65.3 %collective-permute-start.29 = (f32[64,1024]{1,0:T(8,128)S(1)}, f32[64,1024]{1,0:T(8,128)S(1)}, u32[]{:S(2)}, u32[]{:S(2)}) collective-permute-start(f32[64,1024]{1,0:T(8,128)S(1)} %get-tuple-element.55), channel_id=1, source_target_pairs={{0,8},{2,10},{4,12},{6,14},{1,9},{3,11},{5,13},{7,15}} | collective-permute-start | bytes 786440 | tf_op jit(solution)/shard_map/ppermute | solution.py:167
  97.4 64.6 %collective-permute-start.32 = (f32[64,1024]{1,0:T(8,128)S(1)}, f32[64,1024]{1,0:T(8,128)S(1)}, u32[]{:S(2)}, u32[]{:S(2)}) collective-permute-start(f32[64,1024]{1,0:T(8,128)S(1)} %get-tuple-element.56), channel_id=1, source_target_pairs={{24,16},{26,18},{28,20},{30,22},{25,17},{27,19},{29,21},{31,23}} | collective-permute-start | bytes 786440 | tf_op jit(solution)/shard_map/ppermute | solution.py:168
  116.5 46.9 %collective-permute-start.20 = (f32[64,1024]{1,0:T(8,128)S(1)}, f32[64,1024]{1,0:T(8,128)S(1)}, u32[]{:S(2)}, u32[]{:S(2)}) collective-permute-start(f32[64,1024]{1,0:T(8,128)S(1)} %get-tuple-element.61), channel_id=1, source_target_pairs={{0,8},{2,10},{4,12},{6,14},{1,9},{3,11},{5,13},{7,15}} | collective-permute-start | bytes 786440 | tf_op jit(solution)/shard_map/ppermute | solution.py:167
  138.7 25.3 %collective-permute-start.23 = (f32[64,1024]{1,0:T(8,128)S(1)}, f32[64,1024]{1,0:T(8,128)S(1)}, u32[]{:S(2)}, u32[]{:S(2)}) collective-permute-start(f32[64,1024]{1,0:T(8,128)S(1)} %get-tuple-element.62), channel_id=1, source_target_pairs={{24,16},{26,18},{28,20},{30,22},{25,17},{27,19},{29,21},{31,23}} | collective-permute-start | bytes 786440 | tf_op jit(solution)/shard_map/ppermute | solution.py:168
  164.0 15.4 %collective-permute-start.30 = (f32[64,1024]{1,0:T(8,128)S(1)}, f32[64,1024]{1,0:T(8,128)S(1)}, u32[]{:S(2)}, u32[]{:S(2)}) collective-permute-start(f32[64,1024]{1,0:T(8,128)S(1)} %get-tuple-element.53), channel_id=1, source_target_pairs={{0,8},{8,16},{2,10},{10,18},{4,12},{12,20},{6,14},{14,22},{1,9},{9... | collective-permute-start | bytes 786440 | tf_op jit(solution)/shard_map/ppermute | solution.py:167
  168.4 17.0 %collective-permute-start.21 = (f32[64,1024]{1,0:T(8,128)S(1)}, f32[64,1024]{1,0:T(8,128)S(1)}, u32[]{:S(2)}, u32[]{:S(2)}) collective-permute-start(f32[64,1024]{1,0:T(8,128)S(1)} %get-tuple-element.59), channel_id=1, source_target_pairs={{0,8},{8,16},{2,10},{10,18},{4,12},{12,20},{6,14},{14,22},{1,9},{9... | collective-permute-start | bytes 786440 | tf_op jit(solution)/shard_map/ppermute | solution.py:167
  174.2 17.1 %collective-permute-start.12 = (f32[64,1024]{1,0:T(8,128)S(1)}, f32[64,1024]{1,0:T(8,128)S(1)}, u32[]{:S(2)}, u32[]{:S(2)}) collective-permute-start(f32[64,1024]{1,0:T(8,128)S(1)} %get-tuple-element.65), channel_id=1, source_target_pairs={{0,8},{8,16},{2,10},{10,18},{4,12},{12,20},{6,14},{14,22},{1,9},{9... | collective-permute-start | bytes 786440 | tf_op jit(solution)/shard_map/ppermute | solution.py:167
  180.2 17.8 %collective-permute-start.3 = (f32[64,1024]{1,0:T(8,128)S(1)}, f32[64,1024]{1,0:T(8,128)S(1)}, u32[]{:S(2)}, u32[]{:S(2)}) collective-permute-start(f32[64,1024]{1,0:T(8,128)S(1)} %get-tuple-element.71), channel_id=1, source_target_pairs={{0,8},{8,16},{2,10},{10,18},{4,12},{12,20},{6,14},{14,22},{1,9},{9... | collective-permute-start | bytes 786440 | tf_op jit(solution)/shard_map/ppermute | solution.py:167
  185.4 13.8 %collective-permute-start.6 = (f32[64,1024]{1,0:T(8,128)S(1)}, f32[64,1024]{1,0:T(8,128)S(1)}, u32[]{:S(2)}, u32[]{:S(2)}) collective-permute-start(f32[64,1024]{1,0:T(8,128)S(1)} %get-tuple-element.72), channel_id=1, source_target_pairs={{16,8},{24,16},{18,10},{26,18},{20,12},{28,20},{22,14},{30,22},{17... | collective-permute-start | bytes 786440 | tf_op jit(solution)/shard_map/ppermute | solution.py:168
  186.1 17.8 %collective-permute-start.31 = (f32[64,1024]{1,0:T(8,128)S(1)}, f32[64,1024]{1,0:T(8,128)S(1)}, u32[]{:S(2)}, u32[]{:S(2)}) collective-permute-start(f32[64,1024]{1,0:T(8,128)S(1)} %get-tuple-element.51), channel_id=1, source_target_pairs={{0,8},{8,16},{16,24},{2,10},{10,18},{18,26},{4,12},{12,20},{20,28}... | collective-permute-start | bytes 786440 | tf_op jit(solution)/shard_map/ppermute | solution.py:167
  191.4 13.9 %collective-permute-start.34 = (f32[64,1024]{1,0:T(8,128)S(1)}, f32[64,1024]{1,0:T(8,128)S(1)}, u32[]{:S(2)}, u32[]{:S(2)}) collective-permute-start(f32[64,1024]{1,0:T(8,128)S(1)} %get-tuple-element.52), channel_id=1, source_target_pairs={{8,0},{16,8},{24,16},{10,2},{18,10},{26,18},{12,4},{20,12},{28,20}... | collective-permute-start | bytes 786440 | tf_op jit(solution)/shard_map/ppermute | solution.py:168
  192.7 17.2 %collective-permute-start.22 = (f32[64,1024]{1,0:T(8,128)S(1)}, f32[64,1024]{1,0:T(8,128)S(1)}, u32[]{:S(2)}, u32[]{:S(2)}) collective-permute-start(f32[64,1024]{1,0:T(8,128)S(1)} %get-tuple-element.57), channel_id=1, source_target_pairs={{0,8},{8,16},{16,24},{2,10},{10,18},{18,26},{4,12},{12,20},{20,28}... | collective-permute-start | bytes 786440 | tf_op jit(solution)/shard_map/ppermute | solution.py:167
  198.0 13.2 %collective-permute-start.25 = (f32[64,1024]{1,0:T(8,128)S(1)}, f32[64,1024]{1,0:T(8,128)S(1)}, u32[]{:S(2)}, u32[]{:S(2)}) collective-permute-start(f32[64,1024]{1,0:T(8,128)S(1)} %get-tuple-element.58), channel_id=1, source_target_pairs={{8,0},{16,8},{24,16},{10,2},{18,10},{26,18},{12,4},{20,12},{28,20}... | collective-permute-start | bytes 786440 | tf_op jit(solution)/shard_map/ppermute | solution.py:168
  199.3 25.3 %collective-permute-start.13 = (f32[64,1024]{1,0:T(8,128)S(1)}, f32[64,1024]{1,0:T(8,128)S(1)}, u32[]{:S(2)}, u32[]{:S(2)}) collective-permute-start(f32[64,1024]{1,0:T(8,128)S(1)} %get-tuple-element.63), channel_id=1, source_target_pairs={{0,8},{8,16},{16,24},{2,10},{10,18},{18,26},{4,12},{12,20},{20,28}... | collective-permute-start | bytes 786440 | tf_op jit(solution)/shard_map/ppermute | solution.py:167
  203.9 20.6 %collective-permute-start.16 = (f32[64,1024]{1,0:T(8,128)S(1)}, f32[64,1024]{1,0:T(8,128)S(1)}, u32[]{:S(2)}, u32[]{:S(2)}) collective-permute-start(f32[64,1024]{1,0:T(8,128)S(1)} %get-tuple-element.64), channel_id=1, source_target_pairs={{8,0},{16,8},{24,16},{10,2},{18,10},{26,18},{12,4},{20,12},{28,20}... | collective-permute-start | bytes 786440 | tf_op jit(solution)/shard_map/ppermute | solution.py:168
  211.2 19.2 %collective-permute-start.35 = (f32[64,512]{1,0:T(8,128)S(1)}, f32[64,512]{1,0:T(8,128)S(1)}, u32[]{:S(2)}, u32[]{:S(2)}) collective-permute-start(f32[64,512]{1,0:T(8,128)S(1)} %constant_dynamic-slice_fusion), channel_id=1, source_target_pairs={{0,1},{1,0},{2,3},{3,2},{4,5},{5,4},{6,7},{7,6},{8,9},{9,8},{10,11... | collective-permute-start | bytes 393224 | tf_op jit(solution)/shard_map/ppermute | solution.py:217
  (19 other events, 216.6 us)

commit v2 on v0

v2 whole, which is shorter than its diff:
```python
import functools

import jax
import jax.numpy as jnp
from jax import lax
from jax.experimental import pallas as pl
from jax.experimental.pallas import tpu as pltpu
from jax.sharding import PartitionSpec as P

OUTER = 4
CORES = 2
LANES = 128
TILE = 256
VMEM_BYTES = 40 * 1024 * 1024
F32 = jnp.float32
BF16 = jnp.bfloat16


def params():
    return pltpu.CompilerParams(vmem_limit_bytes=VMEM_BYTES)


def cost():
    return pl.CostEstimate(flops=1024, bytes_accessed=1024, transcendentals=0)


def split(value):
    high = value.astype(BF16)
    return high, (value - high.astype(F32)).astype(BF16)


def reversed_bits(value, count):
    result, bit = 0, 1
    while bit < count:
        result = 2 * result + (value // bit) % 2
        bit *= 2
    return result


def prep_kernel(place, limit, b_ref, high_ref, low_ref):
    blocks, _, _, cols, depth = high_ref.shape
    tiles = depth // LANES
    lane = lax.broadcasted_iota(jnp.int32, (1, LANES), 1)
    for h in range(blocks):
        for t in range(tiles):
            value = b_ref[pl.ds(t * blocks + h, cols, stride=tiles * blocks), :]
            value = jnp.where(lane < limit[h] - t * LANES, value, F32(0.0))
            high, low = split(value)
            high_ref[h, 0, 0, :, t * LANES:(t + 1) * LANES] = high
            low_ref[h, 0, 0, :, t * LANES:(t + 1) * LANES] = low


def prepare(rows_of_b, place, limit, shift, blocks, cols, depth, inner):
    size = cols * depth * blocks // LANES

    def source(g, place, limit):
        return (g * CORES + lax.rem(place[2] + shift, CORES), 0)

    def target(g, place, limit):
        z = reversed_bits((g // inner) ^ place[0], OUTER)
        x = reversed_bits((g % inner) ^ place[1], inner)
        return (0, x, z, 0, 0)

    shape = jax.ShapeDtypeStruct((blocks, inner, OUTER, cols, depth), BF16)
    spec = pl.BlockSpec((blocks, 1, 1, cols, depth), target)
    return pl.pallas_call(
        prep_kernel,
        grid_spec=pltpu.PrefetchScalarGridSpec(
            num_scalar_prefetch=2,
            grid=(inner * OUTER,),
            in_specs=[pl.BlockSpec((size, LANES), source)],
            out_specs=[spec, spec],
        ),
        out_shape=[shape, shape],
        cost_estimate=cost(),
        compiler_params=params(),
        name="prepare",
    )(place, limit, rows_of_b)


def product(b_high, b_low, a_ref):
    inner, outer, cols, depth = b_high.shape[1:]
    high, low = split(a_ref[0])
    left_high, left_low = (r[0].reshape(inner * outer * cols, depth) for r in (b_high, b_low))
    dot = functools.partial(jnp.dot, preferred_element_type=F32)
    return dot(left_high, high) + (dot(left_high, low) + dot(left_low, high))


def first_kernel(start, rows_live, b_high, b_low, a_ref, out):
    live = start + pl.program_id(0) * out.shape[1] < rows_live[0]

    @pl.when(live)
    def _():
        out[...] = product(b_high, b_low, a_ref)

    @pl.when(jnp.logical_not(live))
    def _():
        out[...] = jnp.zeros_like(out)


def second_kernel(start, outer_first, rows_live, b_high, b_low, a_ref, received, *outs):
    inner, outer, cols = b_high.shape[1:4]
    live = start + pl.program_id(0) * received.shape[1] < rows_live[0]

    def put(total):
        half = inner * outer // 2
        for x in range(inner):
            for z in range(outer):
                part = total[(x * outer + z) * cols:(x * outer + z + 1) * cols]
                place = z * inner + x if outer_first else x * outer + z
                row = place % half * cols
                outs[place // half][row:row + cols, :] = part

    @pl.when(live)
    def _():
        put(received[...] + product(b_high, b_low, a_ref))

    @pl.when(jnp.logical_not(live))
    def _():
        put(received[...])


def specs(h, start, b_high, amplitudes):
    inner, outer, cols, depth = b_high.shape[1:]
    tile = min(amplitudes.shape[2], TILE)
    left = pl.BlockSpec((1, inner, outer, cols, depth), lambda n, s: (h, 0, 0, 0, 0))
    right = pl.BlockSpec((1, depth, tile), lambda n, s: (h, 0, start // tile + n))
    return tile, inner * outer * cols, [left, left, right]


def first_half(h, start, rows, rows_live, b_high, b_low, amplitudes):
    tile, total, in_specs = specs(h, start, b_high, amplitudes)
    depth = amplitudes.shape[1]
    return pl.pallas_call(
        functools.partial(first_kernel, start),
        grid_spec=pltpu.PrefetchScalarGridSpec(
            num_scalar_prefetch=1,
            grid=(rows // tile,),
            in_specs=in_specs,
            out_specs=pl.BlockSpec((total, tile), lambda n, s: (0, n)),
        ),
        out_shape=jax.ShapeDtypeStruct((total, rows), F32),
        cost_estimate=cost(),
        compiler_params=params(),
        name="first_half",
    )(rows_live, b_high, b_low, amplitudes)


def second_half(h, start, rows, outer_first, rows_live, b_high, b_low, amplitudes, received):
    tile, total, in_specs = specs(h, start, b_high, amplitudes)
    depth = amplitudes.shape[1]
    part = total // 2
    return pl.pallas_call(
        functools.partial(second_kernel, start, outer_first),
        grid_spec=pltpu.PrefetchScalarGridSpec(
            num_scalar_prefetch=1,
            grid=(rows // tile,),
            in_specs=in_specs + [pl.BlockSpec((total, tile), lambda n, s: (0, n))],
            out_specs=[pl.BlockSpec((part, tile), lambda n, s: (0, n))] * 2,
        ),
        out_shape=[jax.ShapeDtypeStruct((part, rows), F32)] * 2,
        cost_estimate=cost(),
        compiler_params=params(),
        name="second_half",
    )(rows_live, b_high, b_low, amplitudes, received)


class Chain:
    def __init__(self):
        self.last = None

    def run(self, step, *args):
        if self.last is not None:
            args, _ = lax.optimization_barrier((args, self.last))
        result = step(*args)
        self.last = jax.tree.leaves(result)[0]
        return result


def local(inner, amplitudes, integrals, row_count, pair_count, col_count):
    blocks, depth, rows = amplitudes.shape
    all_cols = integrals.shape[0]
    tensor, rep = lax.axis_size("tensor"), lax.axis_size("rep")
    cols, row_local = all_cols // tensor, rows // rep
    me, side = lax.axis_index("tensor"), lax.axis_index("rep")
    z, x, core = me // (inner * CORES), me // CORES % inner, me % CORES
    place = jnp.stack([z, x, core]).astype(jnp.int32)

    pairs_here = lax.dynamic_slice_in_dim(pair_count, side * blocks, blocks) - me * depth
    rows_here = lax.dynamic_slice_in_dim(row_count, side * blocks, blocks)
    rows_here = jnp.where(pairs_here > 0, rows_here, 0)
    live = [rows_here[h:h + 1] for h in range(blocks)]
    rows_of_b = integrals.reshape(all_cols, blocks, depth // LANES, LANES)
    rows_of_b = rows_of_b.transpose(0, 2, 1, 3).reshape(-1, LANES)

    def index(z, x, core):
        return (z * inner + x) * CORES + core

    across = [(index(z, x, c), index(z, x, 1 - c))
              for z in range(OUTER) for x in range(inner) for c in range(CORES)]

    def along_inner(bit):
        return [(index(z, x, c), index(z, x ^ bit, c))
                for z in range(OUTER) for x in range(inner) for c in range(CORES)]

    def along_outer(bit):
        return [(index(z, x, c), index(z ^ bit, x, c))
                for z in range(OUTER) for x in range(inner) for c in range(CORES)]

    chain = Chain()
    left, totals = {}, {}

    def prep(shift):
        left[shift] = chain.run(
            lambda b: prepare(b, place, pairs_here, shift, blocks, cols, depth, inner), rows_of_b
        )

    def work(h, start, count, outer_first):
        sent = chain.run(
            functools.partial(first_half, h, start, count), live[h], *left[1], amplitudes
        )
        yield
        got = lax.ppermute(sent, "tensor", across)
        keep, send = chain.run(
            functools.partial(second_half, h, start, count, outer_first),
            live[h], *left[0], amplitudes, got,
        )
        yield
        steps = [along_inner(1 << i) for i in range(inner.bit_length() - 1)]
        more = [along_outer(1 << i) for i in range(OUTER.bit_length() - 1)]
        for pairs in more + steps if outer_first else steps + more:
            got = lax.ppermute(send, "tensor", pairs)
            half = keep.shape[0] // 2
            if half < cols:
                total = chain.run(jnp.add, keep, got)
            else:
                keep, send = chain.run(
                    lambda a, b: (a[:half] + b[:half], a[half:] + b[half:]), keep, got
                )
            yield
        totals[h, start] = total

    mine, other = {}, {}

    def exchange(h):
        for chunk in owned[h]:
            for _ in chunk:
                pass
        if rep != 2:
            mine[h] = totals[h, 0]
            return
        if (h, row_local) in totals:
            first, second = totals[h, 0], totals[h, row_local]
        else:
            first, second = totals[h, 0][:, :row_local], totals[h, 0][:, row_local:]
        mine[h], away = chain.run(
            lambda a, b: (jnp.where(side == 0, a, b), jnp.where(side == 0, b, a)), first, second
        )
        other[h] = lax.ppermute(away, "rep", [(0, 1), (1, 0)])

    prep(1)
    if inner == 2 and rep == 2 and blocks == 4:
        chunks = [work(0, 0, rows, False), work(1, 0, rows, False), work(2, 0, rows, False),
                  work(3, row_local, row_local, False), work(3, 0, row_local, True)]
        owned = [chunks[:1], chunks[1:2], chunks[2:3], chunks[3:]]
        plan = "0p044112240" + "3341" + "0420" + "a" + "131" + "b2323cd"
    else:
        chunks = [work(h, 0, rows, False) for h in range(blocks)]
        owned = [[chunk] for chunk in chunks]
        steps = 2 + (inner * OUTER).bit_length() - 1
        plan = "".join("0p" + "0" * (steps - 1) + "a" if h == 0 else
                       str(h) * steps + "abcdefgh"[h] for h in range(blocks))
    for move in plan:
        if move == "p":
            prep(0)
        elif move in "abcdefgh":
            exchange("abcdefgh".index(move))
        else:
            next(chunks[int(move)], None)

    if rep == 2:
        low = [jnp.where(side == 1, other[h], mine[h]) for h in range(blocks)]
        high = [jnp.where(side == 1, mine[h], other[h]) for h in range(blocks)]
        arranged = jnp.stack(low + high, axis=1)
    else:
        arranged = lax.all_to_all(
            jnp.stack([mine[h] for h in range(blocks)], axis=1), "rep",
            split_axis=2, concat_axis=1, tiled=True,
        )
    col_index = me * cols + lax.broadcasted_iota(jnp.int32, (cols, 1, 1), 0)
    row_index = side * row_local + lax.broadcasted_iota(jnp.int32, (1, 1, row_local), 2)
    keep = (col_index < col_count[None, :, None]) & (row_index < row_count[None, :, None])
    return jnp.where(keep, arranged, F32(0.0))


def solution(mesh):
    inner = mesh.shape["tensor"] // (OUTER * CORES)
    in_specs = (P("rep", "tensor", None), P(None, "rep", "tensor"), P(), P(), P())
    out_specs = P("tensor", None, "rep")
    return jax.shard_map(
        functools.partial(local, inner), mesh=mesh, in_specs=in_specs, out_specs=out_specs,
        check_vma=False,
    )
```

time: 489 us -> 222 us (0.45)
  waiting for transfers between devices: 313 us -> 91.3 us
  matrix products: 121 us -> 0 us
  Pallas kernels: 0 us -> 79.5 us
  starting transfers between devices: 3.58 us -> 26.8 us
  local copies, waits for them, and re-layouts: 30.6 us -> 7.7 us
  between operations: 14.1 us -> 0.34 us
  other arithmetic: 5.41 us -> 15.3 us
    unnamed x2 -> x0, waiting for transfers between devices: 299 us -> none
    dot_general x1 -> x0, matrix products: 121 us -> none  [local(): jnp.einsum('chk,hkr->chr', integrals, masked, precision=lax.Precision.HIG...]
    ppermute x0 -> x24, waiting for transfers between devices: none -> 91.3 us  [the longest x15 71 us: work(): got = lax.ppermute(send, 'tensor', pairs)]
    pallas_call x0 -> x12, Pallas kernels: none -> 79.5 us  [the longest x5 32 us: second_half(): pl.pallas_call(functools.partial(second_kernel, start, outer_first), grid...]
    ppermute x0 -> x24, starting transfers between devices: none -> 26.8 us  [the longest x15 19.3 us: work(): got = lax.ppermute(send, 'tensor', pairs)]
    transpose x1 -> x0, local copies, waits for them, and re-layouts: 20.2 us -> none  [local(): jnp.einsum('chk,hkr->chr', integrals, masked, precision=lax.Precision.HIG...]
    all_to_all x1 -> x0, waiting for transfers between devices: 14 us -> none  [local(): lax.all_to_all(summed, 'rep', split_axis=2, concat_axis=1, tiled=True)]
    add x3 -> x17, other arithmetic: 0.01 us -> 13.8 us  [the longest x10 13.7 us: work(): a[half:] + b[half:]]
  transfers between devices with their start and end apart: 2 -> 24, of which waited for: 2 -> 17; matrix products, arithmetic and copies ran while one was open for 0% -> 5% of each run, Pallas kernels for 0% -> 10%
where the time goes in v2:
time: 222 us; the launch traced here: 221 us
  waiting for transfers between devices  91.3 us (41%)
  Pallas kernels  79.5 us (36%)
  starting transfers between devices  26.8 us (12%)
  other arithmetic  15.3 us (7%)
  local copies, waits for them, and re-layouts  7.7 us (3%)
    ppermute x15, waiting for transfers between devices, work(): got = lax.ppermute(send, 'tensor', pairs)  71 us
    pallas_call x5, Pallas kernels, second_half(): pl.pallas_call(functools.partial(second_kernel, start, outer_first), grid...  32 us
    pallas_call x5, Pallas kernels, first_half(): pl.pallas_call(functools.partial(first_kernel, start), grid_spec=pltpu.Pr...  26.4 us
    pallas_call x2, Pallas kernels, prepare(): pl.pallas_call(prep_kernel, grid_spec=pltpu.PrefetchScalarGridSpec(num_sc...  21.1 us
    ppermute x15, starting transfers between devices, work(): got = lax.ppermute(send, 'tensor', pairs)  19.3 us
    add x10, other arithmetic, work(): a[half:] + b[half:]  13.7 us
    ppermute x4, waiting for transfers between devices, exchange(): other[h] = lax.ppermute(away, 'rep', [(0, 1), (1, 0)])  13.6 us
    ppermute x5, waiting for transfers between devices, work(): got = lax.ppermute(sent, 'tensor', across)  6.63 us
  transfers between devices with their start and end apart: 24, of which 17 were waited for; matrix products, arithmetic and copies ran while one was open for 5% of the time, Pallas kernels for 10%

profile of v2, /device:TPU:0, one launch (start us, length us, event | category | flops | bytes accessed | tf_op | source)
XLA Modules:
  0.0 220.9 jit_solution(9820420713721042632)
XLA Ops:
  1.5 10.6 %prepare.2 = (bf16[4,2,4,64,1024]{4,3,2,1,0:T(8,128)(2,1)S(1)}, bf16[4,2,4,64,1024]{4,3,2,1,0:T(8,128)(2,1)S(1)}) custom-call(s32[3]{0:T(128)S(1)} %pad_add_fusion.place, s32[4]{0:T(128)S(1)} %get-tuple-element.208.limit, f32[32768,128]{1,0:T(8,128)} %bitcast.24), custom_call_target="tpu_custom_call" | custom-call | flops 1024 | bytes 1024 | tf_op jit(solution)/shard_map/prepare/pallas_call | solution.py:66
  12.1 7.2 %first_half.5 = f32[512,1024]{1,0:T(8,128)S(1)} custom-call(s32[1]{0:T(128)} %get-tuple-element.112.rows_live, bf16[4,2,4,64,1024]{4,3,2,1,0:T(8,128)(2,1)S(1)} %get-tuple-element.156.b_high, bf16[4,2,4,64,1024]{4,3,2,1,0:T(8,128)(2,1)S(1)} %get-tuple-element.157.b_low, f32[4,1024,1024]{2,1,0:T(8,128)} %a_ref.9), custom_call_target="tpu_custom_call" | custom-call | flops 1024 | bytes 1024 | tf_op jit(solution)/shard_map/first_half/pallas_call | solution.py:134
  19.8 10.6 %prepare.3 = (bf16[4,2,4,64,1024]{4,3,2,1,0:T(8,128)(2,1)S(1)}, bf16[4,2,4,64,1024]{4,3,2,1,0:T(8,128)(2,1)S(1)}) custom-call(s32[3]{0:T(128)S(1)} %pad_add_fusion.place, s32[4]{0:T(128)S(1)} %get-tuple-element.208.limit, f32[32768,128]{1,0:T(8,128)} %bitcast.25), custom_call_target="tpu_custom_call" | custom-call | flops 1024 | bytes 1024 | tf_op jit(solution)/shard_map/prepare/pallas_call | solution.py:66
  30.4 10.3 %second_half.5 = (f32[256,1024]{1,0:T(8,128)S(1)}, f32[256,1024]{1,0:T(8,128)}) custom-call(s32[1]{0:T(128)} %get-tuple-element.112.rows_live, bf16[4,2,4,64,1024]{4,3,2,1,0:T(8,128)(2,1)S(1)} %get-tuple-element.160.b_high, bf16[4,2,4,64,1024]{4,3,2,1,0:T(8,128)(2,1)S(1)} %get-tuple-element.161.b_low, f32[4,1024,1024]{2,1,0:T(8,128)} %a_ref.9, ...), custom_call_target="tpu_custom_call" | custom-call | flops 1024 | bytes 1024 | tf_op jit(solution)/shard_map/second_half/pallas_call | solution.py:153
  40.8 4.0 %first_half.6 = f32[512,512]{1,0:T(8,128)S(1)} custom-call(s32[1]{0:T(128)} %get-tuple-element.159.rows_live, bf16[4,2,4,64,1024]{4,3,2,1,0:T(8,128)(2,1)S(1)} %copy-done.5, bf16[4,2,4,64,1024]{4,3,2,1,0:T(8,128)(2,1)S(1)} %copy-done.7, f32[4,1024,1024]{2,1,0:T(8,128)} %a_ref.9), custom_call_target="tpu_custom_call" | custom-call | flops 1024 | bytes 1024 | tf_op jit(solution)/shard_map/first_half/pallas_call | solution.py:134
  47.5 4.7 %second_half.6 = (f32[256,512]{1,0:T(8,128)S(1)}, f32[256,512]{1,0:T(8,128)}) custom-call(s32[1]{0:T(128)} %get-tuple-element.159.rows_live, bf16[4,2,4,64,1024]{4,3,2,1,0:T(8,128)(2,1)S(1)} %get-tuple-element.160.b_high, bf16[4,2,4,64,1024]{4,3,2,1,0:T(8,128)(2,1)S(1)} %get-tuple-element.161.b_low, f32[4,1024,1024]{2,1,0:T(8,128)} %a_ref.9, ...), custom_call_target="tpu_custom_call" | custom-call | flops 1024 | bytes 1024 | tf_op jit(solution)/shard_map/second_half/pallas_call | solution.py:153
  52.2 5.2 %first_half.7 = f32[512,1024]{1,0:T(8,128)S(1)} custom-call(s32[1]{0:T(128)} %get-tuple-element.134.rows_live, bf16[4,2,4,64,1024]{4,3,2,1,0:T(8,128)(2,1)S(1)} %copy-done.5, bf16[4,2,4,64,1024]{4,3,2,1,0:T(8,128)(2,1)S(1)} %copy-done.7, f32[4,1024,1024]{2,1,0:T(8,128)} %a_ref.9), custom_call_target="tpu_custom_call" | custom-call | flops 1024 | bytes 1024 | tf_op jit(solution)/shard_map/first_half/pallas_call | solution.py:134
  57.7 4.0 %collective-permute-done.4.received = f32[512,1024]{1,0:T(8,128)S(1)} collective-permute-done((f32[512,1024]{1,0:T(8,128)S(1)}, f32[512,1024]{1,0:T(8,128)S(1)}, u32[]{:S(2)}, u32[]{:S(2)}) %collective-permute-start.4) | collective-permute-done | bytes 2097184 | tf_op jit(solution)/shard_map/ppermute | solution.py:223
  61.7 6.1 %second_half.7 = (f32[256,1024]{1,0:T(8,128)S(1)}, f32[256,1024]{1,0:T(8,128)}) custom-call(s32[1]{0:T(128)} %get-tuple-element.134.rows_live, bf16[4,2,4,64,1024]{4,3,2,1,0:T(8,128)(2,1)S(1)} %get-tuple-element.160.b_high, bf16[4,2,4,64,1024]{4,3,2,1,0:T(8,128)(2,1)S(1)} %get-tuple-element.161.b_low, f32[4,1024,1024]{2,1,0:T(8,128)} %a_ref.9, ...), custom_call_target="tpu_custom_call" | custom-call | flops 1024 | bytes 1024 | tf_op jit(solution)/shard_map/second_half/pallas_call | solution.py:153
  68.7 5.2 %first_half.8 = f32[512,1024]{1,0:T(8,128)S(1)} custom-call(s32[1]{0:T(128)} %get-tuple-element.144.rows_live, bf16[4,2,4,64,1024]{4,3,2,1,0:T(8,128)(2,1)S(1)} %copy-done.5, bf16[4,2,4,64,1024]{4,3,2,1,0:T(8,128)(2,1)S(1)} %copy-done.7, f32[4,1024,1024]{2,1,0:T(8,128)} %a_ref.9), custom_call_target="tpu_custom_call" | custom-call | flops 1024 | bytes 1024 | tf_op jit(solution)/shard_map/first_half/pallas_call | solution.py:134
  78.3 6.1 %second_half.8 = (f32[256,1024]{1,0:T(8,128)S(1)}, f32[256,1024]{1,0:T(8,128)}) custom-call(s32[1]{0:T(128)} %get-tuple-element.144.rows_live, bf16[4,2,4,64,1024]{4,3,2,1,0:T(8,128)(2,1)S(1)} %get-tuple-element.160.b_high, bf16[4,2,4,64,1024]{4,3,2,1,0:T(8,128)(2,1)S(1)} %get-tuple-element.161.b_low, f32[4,1024,1024]{2,1,0:T(8,128)} %a_ref.9, ...), custom_call_target="tpu_custom_call" | custom-call | flops 1024 | bytes 1024 | tf_op jit(solution)/shard_map/second_half/pallas_call | solution.py:153
  84.4 6.6 %collective-permute-done.3 = f32[256,512]{1,0:T(8,128)} collective-permute-done((f32[256,512]{1,0:T(8,128)}, f32[256,512]{1,0:T(8,128)}, u32[]{:S(2)}, u32[]{:S(2)}) %collective-permute-start.3) | collective-permute-done | bytes 524320 | tf_op jit(solution)/shard_map/ppermute | solution.py:232
  92.8 8.0 %collective-permute-done.1 = f32[256,1024]{1,0:T(8,128)} collective-permute-done((f32[256,1024]{1,0:T(8,128)}, f32[256,1024]{1,0:T(8,128)}, u32[]{:S(2)}, u32[]{:S(2)}) %collective-permute-start.1) | collective-permute-done | bytes 1048608 | tf_op jit(solution)/shard_map/ppermute | solution.py:232
  103.0 4.7 %first_half.9 = f32[512,512]{1,0:T(8,128)} custom-call(s32[1]{0:T(128)} %get-tuple-element.159.rows_live, bf16[4,2,4,64,1024]{4,3,2,1,0:T(8,128)(2,1)S(1)} %copy-done.5, bf16[4,2,4,64,1024]{4,3,2,1,0:T(8,128)(2,1)S(1)} %copy-done.7, f32[4,1024,1024]{2,1,0:T(8,128)} %a_ref.9), custom_call_target="tpu_custom_call" | custom-call | flops 1024 | bytes 1024 | tf_op jit(solution)/shard_map/first_half/pallas_call | solution.py:134
  116.0 4.8 %second_half.9 = (f32[256,512]{1,0:T(8,128)S(1)}, f32[256,512]{1,0:T(8,128)}) custom-call(s32[1]{0:T(128)} %get-tuple-element.159.rows_live, bf16[4,2,4,64,1024]{4,3,2,1,0:T(8,128)(2,1)S(1)} %copy-done.1, bf16[4,2,4,64,1024]{4,3,2,1,0:T(8,128)(2,1)S(1)} %copy-done.3, f32[4,1024,1024]{2,1,0:T(8,128)} %a_ref.9, f32[512,512]{1,0:T(8,128)S(1)} %collective-permute-done.9.received), custom_call_target="tpu_custom_call" | custom-call | flops 1024 | bytes 1024 | tf_op jit(solution)/shard_map/second_half/pallas_call | solution.py:153
  120.8 4.2 %collective-permute-done.8 = f32[128,512]{1,0:T(8,128)} collective-permute-done((f32[128,512]{1,0:T(8,128)}, f32[128,512]{1,0:T(8,128)}, u32[]{:S(2)}, u32[]{:S(2)}) %collective-permute-start.8) | collective-permute-done | bytes 262176 | tf_op jit(solution)/shard_map/ppermute | solution.py:232
  125.9 8.1 %collective-permute-done.7 = f32[256,1024]{1,0:T(8,128)} collective-permute-done((f32[256,1024]{1,0:T(8,128)}, f32[256,1024]{1,0:T(8,128)}, u32[]{:S(2)}, u32[]{:S(2)}) %collective-permute-start.7) | collective-permute-done | bytes 1048608 | tf_op jit(solution)/shard_map/ppermute | solution.py:232
  140.7 18.1 %collective-permute-done.12 = f32[64,512]{1,0:T(8,128)S(1)} collective-permute-done((f32[64,512]{1,0:T(8,128)S(1)}, f32[64,512]{1,0:T(8,128)S(1)}, u32[]{:S(2)}, u32[]{:S(2)}) %collective-permute-start.12) | collective-permute-done | bytes 131104 | tf_op jit(solution)/shard_map/ppermute | solution.py:232
  170.2 7.3 %collective-permute-done.16 = f32[256,512]{1,0:T(8,128)} collective-permute-done((f32[256,512]{1,0:T(8,128)}, f32[256,512]{1,0:T(8,128)}, u32[]{:S(2)}, u32[]{:S(2)}) %collective-permute-start.16) | collective-permute-done | bytes 524320 | tf_op jit(solution)/shard_map/ppermute | solution.py:232
  178.7 3.9 %collective-permute-done.15 = f32[64,1024]{1,0:T(8,128)S(1)} collective-permute-done((f32[64,1024]{1,0:T(8,128)S(1)}, f32[64,1024]{1,0:T(8,128)S(1)}, u32[]{:S(2)}, u32[]{:S(2)}) %collective-permute-start.15) | collective-permute-done | bytes 262176 | tf_op jit(solution)/shard_map/ppermute | solution.py:232
  184.1 3.5 %collective-permute-done.17 = f32[64,512]{1,0:T(8,128)S(1)} collective-permute-done((f32[64,512]{1,0:T(8,128)S(1)}, f32[64,512]{1,0:T(8,128)S(1)}, u32[]{:S(2)}, u32[]{:S(2)}) %collective-permute-start.17) | collective-permute-done | bytes 131104 | tf_op jit(solution)/shard_map/ppermute | solution.py:259
  197.2 9.8 %collective-permute-done.19 = f32[64,1024]{1,0:T(8,128)S(1)} collective-permute-done((f32[64,1024]{1,0:T(8,128)S(1)}, f32[64,1024]{1,0:T(8,128)S(1)}, u32[]{:S(2)}, u32[]{:S(2)}) %collective-permute-start.19) | collective-permute-done | bytes 262176 | tf_op jit(solution)/shard_map/ppermute | solution.py:232
  209.7 4.2 %collective-permute-done.22 = f32[64,512]{1,0:T(8,128)S(1)} collective-permute-done((f32[64,512]{1,0:T(8,128)S(1)}, f32[64,512]{1,0:T(8,128)S(1)}, u32[]{:S(2)}, u32[]{:S(2)}) %collective-permute-start.22) | collective-permute-done | bytes 131104 | tf_op jit(solution)/shard_map/ppermute | solution.py:259
  215.0 4.0 %collective-permute-done.23 = f32[64,512]{1,0:T(8,128)S(1)} collective-permute-done((f32[64,512]{1,0:T(8,128)S(1)}, f32[64,512]{1,0:T(8,128)S(1)}, u32[]{:S(2)}, u32[]{:S(2)}) %collective-permute-start.23) | collective-permute-done | bytes 131104 | tf_op jit(solution)/shard_map/ppermute | solution.py:259
  (101 shorter events, 59.4 us)
Async XLA Ops:
  19.3 11.1 %collective-permute-start = (f32[512,1024]{1,0:T(8,128)S(1)}, f32[512,1024]{1,0:T(8,128)S(1)}, u32[]{:S(2)}, u32[]{:S(2)}) collective-permute-start(f32[512,1024]{1,0:T(8,128)S(1)} %first_half.5), channel_id=1, source_target_pairs={{0,2},{2,0},{4,6},{6,4},{8,10},{10,8},{12,14},{14,12},{16,18},{18,... | collective-permute-start | bytes 6291464 | tf_op jit(solution)/shard_map/ppermute | solution.py:223
  44.8 2.7 %collective-permute-start.2 = (f32[512,512]{1,0:T(8,128)S(1)}, f32[512,512]{1,0:T(8,128)S(1)}, u32[]{:S(2)}, u32[]{:S(2)}) collective-permute-start(f32[512,512]{1,0:T(8,128)S(1)} %first_half.6), channel_id=1, source_target_pairs={{0,2},{2,0},{4,6},{6,4},{8,10},{10,8},{12,14},{14,12},{16,18},{18,... | collective-permute-start | bytes 3145736 | tf_op jit(solution)/shard_map/ppermute | solution.py:223
  57.5 4.2 %collective-permute-start.4 = (f32[512,1024]{1,0:T(8,128)S(1)}, f32[512,1024]{1,0:T(8,128)S(1)}, u32[]{:S(2)}, u32[]{:S(2)}) collective-permute-start(f32[512,1024]{1,0:T(8,128)S(1)} %first_half.7), channel_id=1, source_target_pairs={{0,2},{2,0},{4,6},{6,4},{8,10},{10,8},{12,14},{14,12},{16,18},{18,... | collective-permute-start | bytes 6291464 | tf_op jit(solution)/shard_map/ppermute | solution.py:223
  74.0 4.4 %collective-permute-start.5 = (f32[512,1024]{1,0:T(8,128)S(1)}, f32[512,1024]{1,0:T(8,128)S(1)}, u32[]{:S(2)}, u32[]{:S(2)}) collective-permute-start(f32[512,1024]{1,0:T(8,128)S(1)} %first_half.8), channel_id=1, source_target_pairs={{0,2},{2,0},{4,6},{6,4},{8,10},{10,8},{12,14},{14,12},{16,18},{18,... | collective-permute-start | bytes 6291464 | tf_op jit(solution)/shard_map/ppermute | solution.py:223
  74.2 26.6 %collective-permute-start.1 = (f32[256,1024]{1,0:T(8,128)}, f32[256,1024]{1,0:T(8,128)}, u32[]{:S(2)}, u32[]{:S(2)}) collective-permute-start(f32[256,1024]{1,0:T(8,128)} %get-tuple-element.118), channel_id=1, source_target_pairs={{0,4},{2,6},{4,0},{6,2},{8,12},{10,14},{12,8},{14,10},{16,20},{18,... | collective-permute-start | bytes 3145736 | tf_op jit(solution)/shard_map/ppermute | solution.py:232
  77.0 14.0 %collective-permute-start.3 = (f32[256,512]{1,0:T(8,128)}, f32[256,512]{1,0:T(8,128)}, u32[]{:S(2)}, u32[]{:S(2)}) collective-permute-start(f32[256,512]{1,0:T(8,128)} %get-tuple-element.129), channel_id=1, source_target_pairs={{0,8},{2,10},{4,12},{6,14},{8,0},{10,2},{12,4},{14,6},{16,24},{18,... | collective-permute-start | bytes 1572872 | tf_op jit(solution)/shard_map/ppermute | solution.py:232
  107.7 3.9 %collective-permute-start.9 = (f32[512,512]{1,0:T(8,128)}, f32[512,512]{1,0:T(8,128)S(1)}, u32[]{:S(2)}, u32[]{:S(2)}) collective-permute-start(f32[512,512]{1,0:T(8,128)} %first_half.9), channel_id=1, source_target_pairs={{0,2},{2,0},{4,6},{6,4},{8,10},{10,8},{12,14},{14,12},{16,18},{18,... | collective-permute-start | bytes 3145736 | tf_op jit(solution)/shard_map/ppermute | solution.py:223
  107.7 26.3 %collective-permute-start.7 = (f32[256,1024]{1,0:T(8,128)}, f32[256,1024]{1,0:T(8,128)}, u32[]{:S(2)}, u32[]{:S(2)}) collective-permute-start(f32[256,1024]{1,0:T(8,128)} %get-tuple-element.154), channel_id=1, source_target_pairs={{0,4},{2,6},{4,0},{6,2},{8,12},{10,14},{12,8},{14,10},{16,20},{18,... | collective-permute-start | bytes 3145736 | tf_op jit(solution)/shard_map/ppermute | solution.py:232
  109.5 49.3 %collective-permute-start.11 = (f32[256,1024]{1,0:T(8,128)}, f32[256,1024]{1,0:T(8,128)}, u32[]{:S(2)}, u32[]{:S(2)}) collective-permute-start(f32[256,1024]{1,0:T(8,128)} %get-tuple-element.171), channel_id=1, source_target_pairs={{0,4},{2,6},{4,0},{6,2},{8,12},{10,14},{12,8},{14,10},{16,20},{18,... | collective-permute-start | bytes 3145736 | tf_op jit(solution)/shard_map/ppermute | solution.py:232
  109.7 15.2 %collective-permute-start.8 = (f32[128,512]{1,0:T(8,128)}, f32[128,512]{1,0:T(8,128)}, u32[]{:S(2)}, u32[]{:S(2)}) collective-permute-start(f32[128,512]{1,0:T(8,128)} %get-tuple-element.223), channel_id=1, source_target_pairs={{0,16},{2,18},{4,20},{6,22},{8,24},{10,26},{12,28},{14,30},{16,0},... | collective-permute-start | bytes 786440 | tf_op jit(solution)/shard_map/ppermute | solution.py:232
  109.7 26.4 %collective-permute-start.6 = (f32[128,1024]{1,0:T(8,128)S(1)}, f32[128,1024]{1,0:T(8,128)}, u32[]{:S(2)}, u32[]{:S(2)}) collective-permute-start(f32[128,1024]{1,0:T(8,128)S(1)} %get-tuple-element.213), channel_id=1, source_target_pairs={{0,8},{2,10},{4,12},{6,14},{8,0},{10,2},{12,4},{14,6},{16,24},{18,... | collective-permute-start | bytes 1572872 | tf_op jit(solution)/shard_map/ppermute | solution.py:232
  136.1 22.6 %collective-permute-start.12 = (f32[64,512]{1,0:T(8,128)S(1)}, f32[64,512]{1,0:T(8,128)S(1)}, u32[]{:S(2)}, u32[]{:S(2)}) collective-permute-start(f32[64,512]{1,0:T(8,128)S(1)} %get-tuple-element.227), channel_id=1, source_target_pairs={{0,4},{2,6},{4,0},{6,2},{8,12},{10,14},{12,8},{14,10},{16,20},{18,... | collective-permute-start | bytes 393224 | tf_op jit(solution)/shard_map/ppermute | solution.py:232
  139.0 22.0 %collective-permute-start.10 = (f32[64,1024]{1,0:T(8,128)S(1)}, f32[64,1024]{1,0:T(8,128)S(1)}, u32[]{:S(2)}, u32[]{:S(2)}) collective-permute-start(f32[64,1024]{1,0:T(8,128)S(1)} %get-tuple-element.221), channel_id=1, source_target_pairs={{0,16},{2,18},{4,20},{6,22},{8,24},{10,26},{12,28},{14,30},{16,0},... | collective-permute-start | bytes 786440 | tf_op jit(solution)/shard_map/ppermute | solution.py:232
  139.1 28.3 %collective-permute-start.14 = (f32[128,1024]{1,0:T(8,128)}, f32[128,1024]{1,0:T(8,128)}, u32[]{:S(2)}, u32[]{:S(2)}) collective-permute-start(f32[128,1024]{1,0:T(8,128)} %get-tuple-element.211), channel_id=1, source_target_pairs={{0,8},{2,10},{4,12},{6,14},{8,0},{10,2},{12,4},{14,6},{16,24},{18,... | collective-permute-start | bytes 1572872 | tf_op jit(solution)/shard_map/ppermute | solution.py:232
  161.0 6.3 %collective-permute-start.13 = (f32[64,512]{1,0:T(8,128)S(1)}, f32[64,512]{1,0:T(8,128)S(1)}, u32[]{:S(2)}, u32[]{:S(2)}) collective-permute-start(f32[64,512]{1,0:T(8,128)S(1)} %broadcast_select_fusion.7), channel_id=1, source_target_pairs={{0,1},{1,0},{2,3},{3,2},{4,5},{5,4},{6,7},{7,6},{8,9},{9,8},{10,11... | collective-permute-start | bytes 393224 | tf_op jit(solution)/shard_map/ppermute | solution.py:259
  163.9 13.6 %collective-permute-start.16 = (f32[256,512]{1,0:T(8,128)}, f32[256,512]{1,0:T(8,128)}, u32[]{:S(2)}, u32[]{:S(2)}) collective-permute-start(f32[256,512]{1,0:T(8,128)} %get-tuple-element.182), channel_id=1, source_target_pairs={{0,4},{2,6},{4,0},{6,2},{8,12},{10,14},{12,8},{14,10},{16,20},{18,... | collective-permute-start | bytes 1572872 | tf_op jit(solution)/shard_map/ppermute | solution.py:232
  168.5 14.1 %collective-permute-start.15 = (f32[64,1024]{1,0:T(8,128)S(1)}, f32[64,1024]{1,0:T(8,128)S(1)}, u32[]{:S(2)}, u32[]{:S(2)}) collective-permute-start(f32[64,1024]{1,0:T(8,128)S(1)} %get-tuple-element.219), channel_id=1, source_target_pairs={{0,16},{2,18},{4,20},{6,22},{8,24},{10,26},{12,28},{14,30},{16,0},... | collective-permute-start | bytes 786440 | tf_op jit(solution)/shard_map/ppermute | solution.py:232
  168.5 19.8 %collective-permute-start.18 = (f32[128,1024]{1,0:T(8,128)}, f32[128,1024]{1,0:T(8,128)}, u32[]{:S(2)}, u32[]{:S(2)}) collective-permute-start(f32[128,1024]{1,0:T(8,128)} %get-tuple-element.209), channel_id=1, source_target_pairs={{0,8},{2,10},{4,12},{6,14},{8,0},{10,2},{12,4},{14,6},{16,24},{18,... | collective-permute-start | bytes 1572872 | tf_op jit(solution)/shard_map/ppermute | solution.py:232
  182.6 5.0 %collective-permute-start.17 = (f32[64,512]{1,0:T(8,128)S(1)}, f32[64,512]{1,0:T(8,128)S(1)}, u32[]{:S(2)}, u32[]{:S(2)}) collective-permute-start(f32[64,512]{1,0:T(8,128)S(1)} %broadcast_select_fusion.5), channel_id=1, source_target_pairs={{0,1},{1,0},{2,3},{3,2},{4,5},{5,4},{6,7},{7,6},{8,9},{9,8},{10,11... | collective-permute-start | bytes 393224 | tf_op jit(solution)/shard_map/ppermute | solution.py:259
  184.1 11.8 %collective-permute-start.20 = (f32[128,512]{1,0:T(8,128)S(1)}, f32[128,512]{1,0:T(8,128)S(1)}, u32[]{:S(2)}, u32[]{:S(2)}) collective-permute-start(f32[128,512]{1,0:T(8,128)S(1)} %get-tuple-element.215), channel_id=1, source_target_pairs={{0,8},{2,10},{4,12},{6,14},{8,0},{10,2},{12,4},{14,6},{16,24},{18,... | collective-permute-start | bytes 786440 | tf_op jit(solution)/shard_map/ppermute | solution.py:232
  189.4 17.5 %collective-permute-start.19 = (f32[64,1024]{1,0:T(8,128)S(1)}, f32[64,1024]{1,0:T(8,128)S(1)}, u32[]{:S(2)}, u32[]{:S(2)}) collective-permute-start(f32[64,1024]{1,0:T(8,128)S(1)} %get-tuple-element.217), channel_id=1, source_target_pairs={{0,16},{2,18},{4,20},{6,22},{8,24},{10,26},{12,28},{14,30},{16,0},... | collective-permute-start | bytes 786440 | tf_op jit(solution)/shard_map/ppermute | solution.py:232
  195.9 12.4 %collective-permute-start.21 = (f32[64,512]{1,0:T(8,128)S(1)}, f32[64,512]{1,0:T(8,128)S(1)}, u32[]{:S(2)}, u32[]{:S(2)}) collective-permute-start(f32[64,512]{1,0:T(8,128)S(1)} %get-tuple-element.225), channel_id=1, source_target_pairs={{0,16},{2,18},{4,20},{6,22},{8,24},{10,26},{12,28},{14,30},{16,0},... | collective-permute-start | bytes 393224 | tf_op jit(solution)/shard_map/ppermute | solution.py:232
  208.4 5.5 %collective-permute-start.22 = (f32[64,512]{1,0:T(8,128)S(1)}, f32[64,512]{1,0:T(8,128)S(1)}, u32[]{:S(2)}, u32[]{:S(2)}) collective-permute-start(f32[64,512]{1,0:T(8,128)S(1)} %broadcast_select_fusion.3), channel_id=1, source_target_pairs={{0,1},{1,0},{2,3},{3,2},{4,5},{5,4},{6,7},{7,6},{8,9},{9,8},{10,11... | collective-permute-start | bytes 393224 | tf_op jit(solution)/shard_map/ppermute | solution.py:259
  214.0 5.0 %collective-permute-start.23 = (f32[64,512]{1,0:T(8,128)S(1)}, f32[64,512]{1,0:T(8,128)S(1)}, u32[]{:S(2)}, u32[]{:S(2)}) collective-permute-start(f32[64,512]{1,0:T(8,128)S(1)} %broadcast_select_fusion.1), channel_id=1, source_target_pairs={{0,1},{1,0},{2,3},{3,2},{4,5},{5,4},{6,7},{7,6},{8,9},{9,8},{10,11... | collective-permute-start | bytes 393224 | tf_op jit(solution)/shard_map/ppermute | solution.py:259
  (13 other events, 239.9 us)

commit v3 on v2

v3 whole, which is shorter than its diff:
```python
import functools

import jax
import jax.numpy as jnp
from jax import lax
from jax.experimental import pallas as pl
from jax.experimental.pallas import tpu as pltpu
from jax.sharding import PartitionSpec as P

OUTER = 4
CORES = 2
LANES = 128
TILE = 256
VMEM_BYTES = 40 * 1024 * 1024
F32 = jnp.float32
BF16 = jnp.bfloat16


def params():
    return pltpu.CompilerParams(vmem_limit_bytes=VMEM_BYTES)


def cost():
    return pl.CostEstimate(flops=1024, bytes_accessed=1024, transcendentals=0)


def split(value):
    high = value.astype(BF16)
    return high, (value - high.astype(F32)).astype(BF16)


def reversed_bits(value, count):
    result, bit = 0, 1
    while bit < count:
        result = 2 * result + (value // bit) % 2
        bit *= 2
    return result


def put_split(group, limit, first, b_ref, high_ref, low_ref, place):
    used = high_ref.shape[0]
    cols, depth = high_ref.shape[-2:]
    tiles = depth // LANES
    blocks = b_ref.shape[3] // tiles
    lane = lax.broadcasted_iota(jnp.int32, (1, LANES), 1)
    turned = jnp.swapaxes(b_ref[group, 0], 0, 1)
    for h in range(used):
        for t in range(tiles):
            value = turned[t * blocks + first + h]
            value = jnp.where(lane < limit[first + h] - t * LANES, value, F32(0.0))
            high, low = split(value)
            high_ref[(h, *place, slice(None), slice(t * LANES, (t + 1) * LANES))] = high
            low_ref[(h, *place, slice(None), slice(t * LANES, (t + 1) * LANES))] = low


def slot(group, place, inner):
    x = reversed_bits((group % inner) ^ place[1], inner)
    z = reversed_bits((group // inner) ^ place[0], OUTER)
    return x * OUTER + z


def prep_kernel(first, inner, place, limit, b_ref, high_ref, low_ref):
    put_split(0, limit, first, b_ref, high_ref, low_ref, (0,))


def prepare(parts_of_b, place, limit, first, shift, inner):
    groups, _, cols, rows, _ = parts_of_b.shape
    blocks = limit.shape[0]
    depth = rows * LANES // blocks

    def source(g, place, limit):
        return (g, lax.rem(place[2] + shift, CORES), 0, 0, 0)

    def target(g, place, limit):
        return (0, slot(g, place, inner), 0, 0)

    shape = jax.ShapeDtypeStruct((blocks - first, groups, cols, depth), BF16)
    spec = pl.BlockSpec((blocks - first, 1, cols, depth), target)
    return pl.pallas_call(
        functools.partial(prep_kernel, first, inner),
        grid_spec=pltpu.PrefetchScalarGridSpec(
            num_scalar_prefetch=2,
            grid=(groups,),
            in_specs=[pl.BlockSpec((1, 1, cols, rows, LANES), source)],
            out_specs=[spec, spec],
        ),
        out_shape=[shape, shape],
        cost_estimate=cost(),
        compiler_params=params(),
        name="prepare",
    )(place, limit, parts_of_b)


def halves_put(total, outs, inner, cols, outer_first):
    groups = total.shape[0] // cols
    for x in range(inner):
        for z in range(groups // inner):
            row = (x * OUTER + z) * cols
            place = z * inner + x if outer_first else x * OUTER + z
            at = place % (groups // 2) * cols
            outs[place // (groups // 2)][at:at + cols, :] = total[row:row + cols]


def both(refs):
    return jnp.concatenate([ref[...] for ref in refs], axis=0)


def dot3(left_high, left_low, a_ref):
    high, low = split(a_ref[0])
    dot = functools.partial(jnp.dot, preferred_element_type=F32)
    return dot(left_high, high) + (dot(left_high, low) + dot(left_low, high))


def whole_kernel(first, inner, step, chunks, adds, place, limit, rows_live, b_ref, a_ref, *refs):
    if adds:
        received, refs = refs[:2], refs[2:]
    *outs, high_ref, low_ref = refs
    tile = a_ref.shape[2]
    groups, cols, depth = high_ref.shape[1:]
    loads = groups // step
    now = pl.program_id(0)

    @pl.when(now < loads)
    def _():
        for i in range(step):
            group = now * step + i
            put_split(i, limit, first, b_ref, high_ref, low_ref, (slot(group, place, inner),))

    at = loads
    for i, (h, start, count) in enumerate(chunks):
        size = count // tile
        mine = (now >= at) & (now < at + size)
        live = start + (now - at) * tile < rows_live[h]

        @pl.when(mine & live)
        def _():
            total = dot3(*(r[h - first].reshape(groups * cols, depth) for r in (high_ref, low_ref)), a_ref)
            if adds:
                halves_put(total + both(received), outs, inner, cols, False)
            else:
                half = groups * cols // 2
                outs[2 * i][...] = total[:half]
                outs[2 * i + 1][...] = total[half:]

        @pl.when(mine & jnp.logical_not(live))
        def _():
            if adds:
                halves_put(both(received), outs, inner, cols, False)
            else:
                for out in outs[2 * i:2 * i + 2]:
                    out[...] = jnp.zeros_like(out)

        at += size


def whole_products(place, limit, rows_live, parts_of_b, amplitudes, chunks, shift, inner, received=None):
    groups, _, cols, rows_b, _ = parts_of_b.shape
    blocks, depth, rows = amplitudes.shape
    tile = min(rows, TILE)
    step = min(groups, 2)
    loads = groups // step
    first, last = chunks[0][0], chunks[-1][0]
    sizes = [count // tile for _, _, count in chunks]
    offset = chunks[0][1] // tile
    total = sum(sizes)
    per_block = rows // tile

    def b_map(n, place, *_):
        return (jnp.minimum(n, loads - 1), lax.rem(place[2] + shift, CORES), 0, 0, 0)

    def a_map(n, *_):
        t = jnp.maximum(n - loads, 0) + offset
        return (first + t // per_block, 0, t % per_block)

    def tile_map(at, size):
        return lambda n, *_: (0, jnp.clip(n - loads - at, 0, size - 1))

    in_specs = [pl.BlockSpec((step, 1, cols, rows_b, LANES), b_map),
                pl.BlockSpec((1, depth, tile), a_map)]
    operands = [parts_of_b, amplitudes]
    height = groups * cols
    if received is not None:
        in_specs += [pl.BlockSpec((height // 2, tile), tile_map(0, total))] * 2
        operands += received
        out_specs = [pl.BlockSpec((height // 2, tile), tile_map(0, total))] * 2
        shapes = [jax.ShapeDtypeStruct((height // 2, total * tile), F32)] * 2
    else:
        starts = [sum(sizes[:i]) for i in range(len(sizes))]
        out_specs = [pl.BlockSpec((height // 2, tile), tile_map(*x))
                     for x in zip(starts, sizes) for _ in range(2)]
        shapes = [jax.ShapeDtypeStruct((height // 2, size * tile), F32)
                  for size in sizes for _ in range(2)]
    part = pltpu.VMEM((last - first + 1, groups, cols, depth), BF16)
    return pl.pallas_call(
        functools.partial(whole_kernel, first, inner, step, chunks, received is not None),
        grid_spec=pltpu.PrefetchScalarGridSpec(
            num_scalar_prefetch=3,
            grid=(loads + total,),
            in_specs=in_specs,
            out_specs=out_specs,
            scratch_shapes=[part, part],
        ),
        out_shape=shapes,
        cost_estimate=cost(),
        compiler_params=params(),
        name="whole_products",
    )(place, limit, rows_live, *operands)


def second_kernel(h, start, inner, outer_first, rows_live, b_high, b_low, a_ref, *refs):
    received, outs = refs[:2], refs[2:]
    groups, cols, depth = b_high.shape[1:]
    live = start + pl.program_id(0) * a_ref.shape[2] < rows_live[h]

    @pl.when(live)
    def _():
        total = dot3(*(r[0].reshape(groups * cols, depth) for r in (b_high, b_low)), a_ref)
        halves_put(total + both(received), outs, inner, cols, outer_first)

    @pl.when(jnp.logical_not(live))
    def _():
        halves_put(both(received), outs, inner, cols, outer_first)


def second_half(h, start, count, first, inner, outer_first, rows_live, b_high, b_low, amplitudes, received):
    groups, cols, depth = b_high.shape[1:]
    tile = min(amplitudes.shape[2], TILE)
    height = groups * cols
    left = pl.BlockSpec((1, groups, cols, depth), lambda n, s: (h - first, 0, 0, 0))
    return pl.pallas_call(
        functools.partial(second_kernel, h, start, inner, outer_first),
        grid_spec=pltpu.PrefetchScalarGridSpec(
            num_scalar_prefetch=1,
            grid=(count // tile,),
            in_specs=[left, left,
                      pl.BlockSpec((1, depth, tile), lambda n, s: (h, 0, start // tile + n)),
                      *[pl.BlockSpec((height // 2, tile), lambda n, s: (0, n))] * 2],
            out_specs=[pl.BlockSpec((height // 2, tile), lambda n, s: (0, n))] * 2,
        ),
        out_shape=[jax.ShapeDtypeStruct((height // 2, count), F32)] * 2,
        cost_estimate=cost(),
        compiler_params=params(),
        name="second_half",
    )(rows_live, b_high, b_low, amplitudes, *received)


def place_kernel(side_ref, base, row_count, col_count, *refs):
    *parts, out_ref = refs
    side = side_ref[0]
    blocks = len(parts) // 2
    cols, rows = parts[0].shape
    col = base[0] + lax.broadcasted_iota(jnp.int32, (cols, rows), 0)
    row = base[1] + lax.broadcasted_iota(jnp.int32, (cols, rows), 1)
    for here in range(2):
        @pl.when(side == here)
        def _():
            order = parts[blocks:] + parts[:blocks] if here else parts
            kept = [
                jnp.where((col < col_count[h]) & (row < row_count[h]), part[...], F32(0.0))
                for h, part in enumerate(order)
            ]
            out_ref[...] = jnp.swapaxes(jnp.stack(kept), 0, 1)


def place_blocks(side, base, row_count, col_count, mine, other):
    cols, rows = mine[0].shape
    blocks = 2 * len(mine)
    vmem = pl.BlockSpec(memory_space=pltpu.VMEM)
    return pl.pallas_call(
        place_kernel,
        grid_spec=pltpu.PrefetchScalarGridSpec(
            num_scalar_prefetch=4, grid=(), in_specs=[vmem] * blocks, out_specs=vmem,
        ),
        out_shape=jax.ShapeDtypeStruct((cols, blocks, rows), F32),
        cost_estimate=cost(),
        compiler_params=params(),
        name="place_blocks",
    )(side, base, row_count, col_count, *mine, *other)


class Chain:
    def __init__(self):
        self.last = None

    def run(self, step, *args):
        if self.last is not None:
            args, _ = lax.optimization_barrier((args, self.last))
        result = step(*args)
        self.last = jax.tree.leaves(result)[0]
        return result


def local(inner, amplitudes, integrals, row_count, pair_count, col_count):
    blocks, depth, rows = amplitudes.shape
    all_cols = integrals.shape[0]
    tensor, rep = lax.axis_size("tensor"), lax.axis_size("rep")
    cols, row_local = all_cols // tensor, rows // rep
    me, side = lax.axis_index("tensor"), lax.axis_index("rep")
    z, x, core = me // (inner * CORES), me // CORES % inner, me % CORES
    place = jnp.stack([z, x, core]).astype(jnp.int32)

    pairs_here = lax.dynamic_slice_in_dim(pair_count, side * blocks, blocks) - me * depth
    rows_here = lax.dynamic_slice_in_dim(row_count, side * blocks, blocks)
    rows_here = jnp.where(pairs_here > 0, rows_here, 0)
    parts_of_b = integrals.reshape(all_cols, blocks, depth // LANES, LANES).transpose(0, 2, 1, 3)
    parts_of_b = parts_of_b.reshape(inner * OUTER, CORES, cols, blocks * depth // LANES, LANES)

    def index(z, x, core):
        return (z * inner + x) * CORES + core

    across = [(index(z, x, c), index(z, x, 1 - c))
              for z in range(OUTER) for x in range(inner) for c in range(CORES)]

    def along_inner(bit):
        return [(index(z, x, c), index(z, x ^ bit, c))
                for z in range(OUTER) for x in range(inner) for c in range(CORES)]

    def along_outer(bit):
        return [(index(z, x, c), index(z ^ bit, x, c))
                for z in range(OUTER) for x in range(inner) for c in range(CORES)]

    chain = Chain()
    received, totals = {}, {}

    def whole(chunks, shift, *got):
        return chain.run(
            lambda p, l, r, b, a, *g: whole_products(p, l, r, b, a, chunks, shift, inner, *g),
            place, pairs_here, rows_here, parts_of_b, amplitudes, *got,
        )

    def first_halves(chunks):
        sent = whole(chunks, 1)
        for i, (h, start, _) in enumerate(chunks):
            received[h, start] = [
                lax.ppermute(part, "tensor", across) for part in sent[2 * i:2 * i + 2]
            ]

    def work(h, start, count, outer_first=False):
        got = received[h, start]
        if h == 0:
            keep, send = whole([(h, start, count)], 0, got)
        else:
            keep, send = chain.run(
                functools.partial(second_half, h, start, count, 1, inner, outer_first),
                rows_here, *prepared, amplitudes, got,
            )
        yield
        steps = [along_inner(1 << i) for i in range(inner.bit_length() - 1)]
        more = [along_outer(1 << i) for i in range(OUTER.bit_length() - 1)]
        for pairs in more + steps if outer_first else steps + more:
            got = lax.ppermute(send, "tensor", pairs)
            half = keep.shape[0] // 2
            if half < cols:
                total = chain.run(jnp.add, keep, got)
            else:
                keep, send = chain.run(
                    lambda a, b: (a[:half] + b[:half], a[half:] + b[half:]), keep, got
                )
            yield
        totals[h, start] = total

    mine, other = {}, {}

    def exchange(h):
        for chunk in owned[h]:
            for _ in chunk:
                pass
        if rep != 2:
            mine[h] = totals[h, 0]
            return
        if (h, row_local) in totals:
            first, second = totals[h, 0], totals[h, row_local]
        else:
            first, second = totals[h, 0][:, :row_local], totals[h, 0][:, row_local:]
        mine[h], away = chain.run(
            lambda a, b: (jnp.where(side == 0, a, b), jnp.where(side == 0, b, a)), first, second
        )
        other[h] = lax.ppermute(away, "rep", [(0, 1), (1, 0)])

    first_halves([(0, 0, rows)])
    if inner == 2 and rep == 2 and blocks == 4:
        chunks = [work(0, 0, rows), work(1, 0, rows), work(2, 0, rows),
                  work(3, row_local, row_local), work(3, 0, row_local, True)]
        owned = [chunks[:1], chunks[1:2], chunks[2:3], chunks[3:]]
        later = [(1, 0, rows), (2, 0, rows), (3, 0, row_local), (3, row_local, row_local)]
        plan = "0p01024314a21A432bB3cCd"
    else:
        chunks = [work(h, 0, rows) for h in range(blocks)]
        owned = [[chunk] for chunk in chunks]
        later = [(h, 0, rows) for h in range(1, blocks)]
        plan = "0" + "p" * (blocks > 1) + "abcdefgh"[:blocks]
    for move in plan:
        if move == "p":
            first_halves(later)
            prepared = chain.run(
                lambda b: prepare(b, place, pairs_here, 1, 0, inner), parts_of_b
            )
        elif move in "ABCDEFGH":
            chain.last = chain.last, other["ABCDEFGH".index(move)]
        elif move in "abcdefgh":
            exchange("abcdefgh".index(move))
        else:
            next(chunks[int(move)], None)

    if rep == 2:
        base = jnp.stack([me * cols, side * row_local]).astype(jnp.int32)
        return place_blocks(
            jnp.reshape(side, (1,)).astype(jnp.int32), base, row_count, col_count,
            [mine[h] for h in range(blocks)], [other[h] for h in range(blocks)],
        )
    arranged = lax.all_to_all(
        jnp.stack([mine[h] for h in range(blocks)], axis=1), "rep",
        split_axis=2, concat_axis=1, tiled=True,
    )
    col_index = me * cols + lax.broadcasted_iota(jnp.int32, (cols, 1, 1), 0)
    row_index = side * row_local + lax.broadcasted_iota(jnp.int32, (1, 1, row_local), 2)
    keep = (col_index < col_count[None, :, None]) & (row_index < row_count[None, :, None])
    return jnp.where(keep, arranged, F32(0.0))


def solution(mesh):
    inner = mesh.shape["tensor"] // (OUTER * CORES)
    in_specs = (P("rep", "tensor", None), P(None, "rep", "tensor"), P(), P(), P())
    out_specs = P("tensor", None, "rep")
    return jax.shard_map(
        functools.partial(local, inner), mesh=mesh, in_specs=in_specs, out_specs=out_specs,
        check_vma=False,
    )
```

time: 222 us -> 174 us (0.78)
  waiting for transfers between devices: 91.3 us -> 72.5 us
  other arithmetic: 15.3 us -> 6.2 us
  starting transfers between devices: 26.8 us -> 18.5 us
  Pallas kernels: 79.5 us -> 73.3 us
  local copies, waits for them, and re-layouts: 7.7 us -> 2.8 us
    ppermute x15, waiting for transfers between devices: 71 us -> 60.6 us  [work(): got = lax.ppermute(send, 'tensor', pairs)]
    add x10, other arithmetic: 13.7 us -> 5.06 us  [work(): a[half:] + b[half:]]
    ppermute x15, starting transfers between devices: 19.3 us -> 12.2 us  [work(): got = lax.ppermute(send, 'tensor', pairs)]
    pallas_call x12 -> x9, Pallas kernels: 79.5 us -> 73.3 us  [the longest x3 41.1 us: whole_products(): pl.pallas_call(functools.partial(whole_kernel, first, inner, step, chunks...]
    ppermute x4, waiting for transfers between devices: 13.6 us -> 8.24 us  [exchange(): other[h] = lax.ppermute(away, 'rep', [(0, 1), (1, 0)])]
    ppermute x5 -> x10, waiting for transfers between devices: 6.63 us -> 3.73 us  [first_halves(): lax.ppermute(part, 'tensor', across)]
    unnamed x26 -> x20, local copies, waits for them, and re-layouts: 5.4 us -> 2.75 us
    ppermute x4, starting transfers between devices: 6.52 us -> 4.03 us  [exchange(): other[h] = lax.ppermute(away, 'rep', [(0, 1), (1, 0)])]
  transfers between devices with their start and end apart: 24 -> 29, of which waited for: 17 -> 14; matrix products, arithmetic and copies ran while one was open for 5% -> 3% of each run, Pallas kernels for 10% -> 30%
where the time goes in v3:
time: 174 us
  Pallas kernels  73.3 us (42%)
  waiting for transfers between devices  72.5 us (42%)
  starting transfers between devices  18.5 us (11%)
  other arithmetic  6.2 us (4%)
  local copies, waits for them, and re-layouts  2.8 us (2%)
    ppermute x15, waiting for transfers between devices, work(): got = lax.ppermute(send, 'tensor', pairs)  60.6 us
    pallas_call x3, Pallas kernels, whole_products(): pl.pallas_call(functools.partial(whole_kernel, first, inner, step, chunks...  41.1 us
    pallas_call x4, Pallas kernels, second_half(): pl.pallas_call(functools.partial(second_kernel, h, start, inner, outer_fi...  22 us
    ppermute x15, starting transfers between devices, work(): got = lax.ppermute(send, 'tensor', pairs)  12.2 us
    pallas_call x1, Pallas kernels, prepare(): pl.pallas_call(functools.partial(prep_kernel, first, inner), grid_spec=pl...  8.33 us
    ppermute x4, waiting for transfers between devices, exchange(): other[h] = lax.ppermute(away, 'rep', [(0, 1), (1, 0)])  8.24 us
    add x10, other arithmetic, work(): a[half:] + b[half:]  5.06 us
    ppermute x4, starting transfers between devices, exchange(): other[h] = lax.ppermute(away, 'rep', [(0, 1), (1, 0)])  4.03 us
  transfers between devices with their start and end apart: 29, of which 14 were waited for; matrix products, arithmetic and copies ran while one was open for 3% of the time, Pallas kernels for 30%

profile of v3, /device:TPU:0, one launch (start us, length us, event | category | flops | bytes accessed | tf_op | source)
XLA Modules:
  0.0 173.6 jit_solution(9615797388605945562)
XLA Ops:
  0.8 9.4 %whole_products.3 = (f32[256,1024]{1,0:T(8,128)S(1)}, f32[256,1024]{1,0:T(8,128)S(1)}) custom-call(s32[3]{0:T(128)S(1)} %pad_add_fusion.1.place, s32[4]{0:T(128)S(1)} %get-tuple-element.114.limit, s32[4]{0:T(128)S(1)} %get-tuple-element.156.rows_live, f32[8,2,64,32,128]{4,3,2,1,0:T(8,128)} %bitcast.11, f32[4,1024,1024]{2,1,0:T(8,128)} %a_ref.7), custom_call_target="tpu_custom_call" | custom-call | flops 1024 | bytes 1024 | tf_op jit(solution)/shard_map/whole_products/pallas_call | solution.py:194
  10.9 2.2 %collective-permute-done.refs_0_ = f32[256,1024]{1,0:T(8,128)S(1)} collective-permute-done((f32[256,1024]{1,0:T(8,128)S(1)}, f32[256,1024]{1,0:T(8,128)S(1)}, u32[]{:S(2)}, u32[]{:S(2)}) %collective-permute-start) | collective-permute-done | bytes 1048608 | tf_op jit(solution)/shard_map/ppermute | solution.py:335
  14.6 9.5 %whole_products.4 = (f32[256,1024]{1,0:T(8,128)S(1)}, f32[256,1024]{1,0:T(8,128)S(1)}) custom-call(s32[3]{0:T(128)S(1)} %pad_add_fusion.1.place, s32[4]{0:T(128)S(1)} %get-tuple-element.114.limit, s32[4]{0:T(128)S(1)} %get-tuple-element.156.rows_live, f32[8,2,64,32,128]{4,3,2,1,0:T(8,128)} %bitcast.12, f32[4,1024,1024]{2,1,0:T(8,128)} %a_ref.7, ...), custom_call_target="tpu_custom_call" | custom-call | flops 1024 | bytes 1024 | tf_op jit(solution)/shard_map/whole_products/pallas_call | solution.py:194
  24.0 2.9 %collective-permute-start.2 = (f32[256,1024]{1,0:T(8,128)S(1)}, f32[256,1024]{1,0:T(8,128)S(1)}, u32[]{:S(2)}, u32[]{:S(2)}) collective-permute-start(f32[256,1024]{1,0:T(8,128)S(1)} %get-tuple-element.112), channel_id=1, source_target_pairs={{0,4},{2,6},{4,0},{6,2},{8,12},{10,14},{12,8},{14,10},{16,20},{18,... | collective-permute-start | bytes 3145736 | tf_op jit(solution)/shard_map/ppermute | solution.py:351
  27.0 22.2 %whole_products.5 = (f32[256,1024]{1,0:T(8,128)S(1)}, f32[256,1024]{1,0:T(8,128)S(1)}, f32[256,1024]{1,0:T(8,128)S(1)}, f32[256,1024]{1,0:T(8,128)S(1)}, f32[256...) custom-call(s32[3]{0:T(128)S(1)} %pad_add_fusion.1.place, ...), custom_call_target="tpu_custom_call" | custom-call | flops 1024 | bytes 1024 | tf_op jit(solution)/shard_map/whole_products/pallas_call | solution.py:194
  50.2 8.3 %prepare.1 = (bf16[3,8,64,1024]{3,2,1,0:T(8,128)(2,1)S(1)}, bf16[3,8,64,1024]{3,2,1,0:T(8,128)(2,1)S(1)}) custom-call(s32[3]{0:T(128)S(1)} %pad_add_fusion.1.place, s32[4]{0:T(128)S(1)} %get-tuple-element.114.limit, f32[8,2,64,32,128]{4,3,2,1,0:T(8,128)} %bitcast.14), custom_call_target="tpu_custom_call" | custom-call | flops 1024 | bytes 1024 | tf_op jit(solution)/shard_map/prepare/pallas_call | solution.py:79
  60.4 6.0 %second_half.4 = (f32[256,1024]{1,0:T(8,128)S(1)}, f32[256,1024]{1,0:T(8,128)}) custom-call(s32[4]{0:T(128)S(1)} %get-tuple-element.156.rows_live, bf16[3,8,64,1024]{3,2,1,0:T(8,128)(2,1)S(1)} %get-tuple-element.157.b_high, bf16[3,8,64,1024]{3,2,1,0:T(8,128)(2,1)S(1)} %get-tuple-element.158.b_low, f32[4,1024,1024]{2,1,0:T(8,128)} %a_ref.7, ...), custom_call_target="tpu_custom_call" | custom-call | flops 1024 | bytes 1024 | tf_op jit(solution)/shard_map/second_half/pallas_call | solution.py:230
  67.0 5.6 %collective-permute-done.3 = f32[128,1024]{1,0:T(8,128)S(1)} collective-permute-done((f32[128,1024]{1,0:T(8,128)S(1)}, f32[128,1024]{1,0:T(8,128)S(1)}, u32[]{:S(2)}, u32[]{:S(2)}) %collective-permute-start.3) | collective-permute-done | bytes 524320 | tf_op jit(solution)/shard_map/ppermute | solution.py:351
  73.4 7.1 %second_half.5 = (f32[256,1024]{1,0:T(8,128)S(1)}, f32[256,1024]{1,0:T(8,128)}) custom-call(s32[4]{0:T(128)S(1)} %get-tuple-element.156.rows_live, bf16[3,8,64,1024]{3,2,1,0:T(8,128)(2,1)S(1)} %get-tuple-element.157.b_high, bf16[3,8,64,1024]{3,2,1,0:T(8,128)(2,1)S(1)} %get-tuple-element.158.b_low, f32[4,1024,1024]{2,1,0:T(8,128)} %a_ref.7, ...), custom_call_target="tpu_custom_call" | custom-call | flops 1024 | bytes 1024 | tf_op jit(solution)/shard_map/second_half/pallas_call | solution.py:230
  80.5 4.6 %second_half.6 = (f32[256,512]{1,0:T(8,128)S(1)}, f32[256,512]{1,0:T(8,128)}) custom-call(s32[4]{0:T(128)S(1)} %get-tuple-element.156.rows_live, bf16[3,8,64,1024]{3,2,1,0:T(8,128)(2,1)S(1)} %get-tuple-element.157.b_high, bf16[3,8,64,1024]{3,2,1,0:T(8,128)(2,1)S(1)} %get-tuple-element.158.b_low, f32[4,1024,1024]{2,1,0:T(8,128)} %a_ref.7, ...), custom_call_target="tpu_custom_call" | custom-call | flops 1024 | bytes 1024 | tf_op jit(solution)/shard_map/second_half/pallas_call | solution.py:230
  87.5 1.9 %copy-done.1 = bf16[3,8,64,1024]{3,2,1,0:T(8,128)(2,1)S(1)} copy-done((bf16[3,8,64,1024]{3,2,1,0:T(8,128)(2,1)S(1)}, bf16[3,8,64,1024]{3,2,1,0:T(8,128)(2,1)}, u32[]{:S(2)}) %copy-start.1) | copy-done | bytes 3145752
  89.4 4.3 %second_half.7 = (f32[256,512]{1,0:T(8,128)S(1)}, f32[256,512]{1,0:T(8,128)S(1)}) custom-call(s32[4]{0:T(128)S(1)} %get-tuple-element.156.rows_live, bf16[3,8,64,1024]{3,2,1,0:T(8,128)(2,1)S(1)} %get-tuple-element.157.b_high, bf16[3,8,64,1024]{3,2,1,0:T(8,128)(2,1)S(1)} %copy-done.1, f32[4,1024,1024]{2,1,0:T(8,128)} %a_ref.7, ...), custom_call_target="tpu_custom_call" | custom-call | flops 1024 | bytes 1024 | tf_op jit(solution)/shard_map/second_half/pallas_call | solution.py:230
  93.7 2.1 %collective-permute-start.19 = (f32[256,512]{1,0:T(8,128)S(1)}, f32[256,512]{1,0:T(8,128)S(1)}, u32[]{:S(2)}, u32[]{:S(2)}) collective-permute-start(f32[256,512]{1,0:T(8,128)S(1)} %get-tuple-element.176), channel_id=1, source_target_pairs={{0,4},{2,6},{4,0},{6,2},{8,12},{10,14},{12,8},{14,10},{16,20},{18,... | collective-permute-start | bytes 1572872 | tf_op jit(solution)/shard_map/ppermute | solution.py:351
  97.2 9.3 %collective-permute-done.11 = f32[256,512]{1,0:T(8,128)} collective-permute-done((f32[256,512]{1,0:T(8,128)}, f32[256,512]{1,0:T(8,128)}, u32[]{:S(2)}, u32[]{:S(2)}) %collective-permute-start.11) | collective-permute-done | bytes 524320 | tf_op jit(solution)/shard_map/ppermute | solution.py:351
  109.7 5.6 %collective-permute-done.16 = f32[256,1024]{1,0:T(8,128)} collective-permute-done((f32[256,1024]{1,0:T(8,128)}, f32[256,1024]{1,0:T(8,128)}, u32[]{:S(2)}, u32[]{:S(2)}) %collective-permute-start.16) | collective-permute-done | bytes 1048608 | tf_op jit(solution)/shard_map/ppermute | solution.py:351
  116.7 6.3 %collective-permute-done.15 = f32[128,1024]{1,0:T(8,128)S(1)} collective-permute-done((f32[128,1024]{1,0:T(8,128)S(1)}, f32[128,1024]{1,0:T(8,128)S(1)}, u32[]{:S(2)}, u32[]{:S(2)}) %collective-permute-start.15) | collective-permute-done | bytes 524320 | tf_op jit(solution)/shard_map/ppermute | solution.py:351
  123.2 2.0 %collective-permute-done.19 = f32[256,512]{1,0:T(8,128)S(1)} collective-permute-done((f32[256,512]{1,0:T(8,128)S(1)}, f32[256,512]{1,0:T(8,128)S(1)}, u32[]{:S(2)}, u32[]{:S(2)}) %collective-permute-start.19) | collective-permute-done | bytes 524320 | tf_op jit(solution)/shard_map/ppermute | solution.py:351
  125.8 17.5 %collective-permute-done.18 = f32[128,1024]{1,0:T(8,128)S(1)} collective-permute-done((f32[128,1024]{1,0:T(8,128)S(1)}, f32[128,1024]{1,0:T(8,128)S(1)}, u32[]{:S(2)}, u32[]{:S(2)}) %collective-permute-start.18) | collective-permute-done | bytes 524320 | tf_op jit(solution)/shard_map/ppermute | solution.py:351
  144.9 3.0 %collective-permute-done.23 = f32[128,512]{1,0:T(8,128)S(1)} collective-permute-done((f32[128,512]{1,0:T(8,128)S(1)}, f32[128,512]{1,0:T(8,128)S(1)}, u32[]{:S(2)}, u32[]{:S(2)}) %collective-permute-start.23) | collective-permute-done | bytes 262176 | tf_op jit(solution)/shard_map/ppermute | solution.py:351
  149.5 9.3 %collective-permute-done.22 = f32[64,1024]{1,0:T(8,128)S(1)} collective-permute-done((f32[64,1024]{1,0:T(8,128)S(1)}, f32[64,1024]{1,0:T(8,128)S(1)}, u32[]{:S(2)}, u32[]{:S(2)}) %collective-permute-start.22) | collective-permute-done | bytes 262176 | tf_op jit(solution)/shard_map/ppermute | solution.py:351
  158.8 2.8 %collective-permute-start.27 = (f32[64,512]{1,0:T(8,128)S(1)}, f32[64,512]{1,0:T(8,128)S(1)}, u32[]{:S(2)}, u32[]{:S(2)}) collective-permute-start(f32[64,512]{1,0:T(8,128)S(1)} %get-tuple-element.223), channel_id=1, source_target_pairs={{0,1},{1,0},{2,3},{3,2},{4,5},{5,4},{6,7},{7,6},{8,9},{9,8},{10,11... | collective-permute-start | bytes 393224 | tf_op jit(solution)/shard_map/ppermute | solution.py:378
  161.7 2.9 %collective-permute-done.27.refs_6_ = f32[64,512]{1,0:T(8,128)S(1)} collective-permute-done((f32[64,512]{1,0:T(8,128)S(1)}, f32[64,512]{1,0:T(8,128)S(1)}, u32[]{:S(2)}, u32[]{:S(2)}) %collective-permute-start.27) | collective-permute-done | bytes 131104 | tf_op jit(solution)/shard_map/ppermute | solution.py:378
  164.6 2.0 %collective-permute-done.25 = f32[64,512]{1,0:T(8,128)S(1)} collective-permute-done((f32[64,512]{1,0:T(8,128)S(1)}, f32[64,512]{1,0:T(8,128)S(1)}, u32[]{:S(2)}, u32[]{:S(2)}) %collective-permute-start.25) | collective-permute-done | bytes 131104 | tf_op jit(solution)/shard_map/ppermute | solution.py:351
  166.9 4.8 %collective-permute-done.28.refs_7_ = f32[64,512]{1,0:T(8,128)S(1)} collective-permute-done((f32[64,512]{1,0:T(8,128)S(1)}, f32[64,512]{1,0:T(8,128)S(1)}, u32[]{:S(2)}, u32[]{:S(2)}) %collective-permute-start.28) | collective-permute-done | bytes 131104 | tf_op jit(solution)/shard_map/ppermute | solution.py:378
  (88 shorter events, 21.7 us)
Async XLA Ops:
  24.0 34.5 %collective-permute-start.2 = (f32[256,1024]{1,0:T(8,128)S(1)}, f32[256,1024]{1,0:T(8,128)S(1)}, u32[]{:S(2)}, u32[]{:S(2)}) collective-permute-start(f32[256,1024]{1,0:T(8,128)S(1)} %get-tuple-element.112), channel_id=1, source_target_pairs={{0,4},{2,6},{4,0},{6,2},{8,12},{10,14},{12,8},{14,10},{16,20},{18,... | collective-permute-start | bytes 3145736 | tf_op jit(solution)/shard_map/ppermute | solution.py:351
  49.2 11.2 %collective-permute-start.4 = (f32[256,1024]{1,0:T(8,128)S(1)}, f32[256,1024]{1,0:T(8,128)S(1)}, u32[]{:S(2)}, u32[]{:S(2)}) collective-permute-start(f32[256,1024]{1,0:T(8,128)S(1)} %get-tuple-element.118), channel_id=1, source_target_pairs={{0,2},{2,0},{4,6},{6,4},{8,10},{10,8},{12,14},{14,12},{16,18},{18,... | collective-permute-start | bytes 3145736 | tf_op jit(solution)/shard_map/ppermute | solution.py:335
  49.2 11.2 %collective-permute-start.5 = (f32[256,1024]{1,0:T(8,128)S(1)}, f32[256,1024]{1,0:T(8,128)S(1)}, u32[]{:S(2)}, u32[]{:S(2)}) collective-permute-start(f32[256,1024]{1,0:T(8,128)S(1)} %get-tuple-element.124), channel_id=1, source_target_pairs={{0,2},{2,0},{4,6},{6,4},{8,10},{10,8},{12,14},{14,12},{16,18},{18,... | collective-permute-start | bytes 3145736 | tf_op jit(solution)/shard_map/ppermute | solution.py:335
  49.7 16.8 %collective-permute-start.9 = (f32[256,1024]{1,0:T(8,128)S(1)}, f32[256,1024]{1,0:T(8,128)S(1)}, u32[]{:S(2)}, u32[]{:S(2)}) collective-permute-start(f32[256,1024]{1,0:T(8,128)S(1)} %get-tuple-element.136), channel_id=1, source_target_pairs={{0,2},{2,0},{4,6},{6,4},{8,10},{10,8},{12,14},{14,12},{16,18},{18,... | collective-permute-start | bytes 3145736 | tf_op jit(solution)/shard_map/ppermute | solution.py:335
  49.7 17.3 %collective-permute-start.10 = (f32[256,1024]{1,0:T(8,128)S(1)}, f32[256,1024]{1,0:T(8,128)S(1)}, u32[]{:S(2)}, u32[]{:S(2)}) collective-permute-start(f32[256,1024]{1,0:T(8,128)S(1)} %get-tuple-element.137), channel_id=1, source_target_pairs={{0,2},{2,0},{4,6},{6,4},{8,10},{10,8},{12,14},{14,12},{16,18},{18,... | collective-permute-start | bytes 3145736 | tf_op jit(solution)/shard_map/ppermute | solution.py:335
  58.8 13.9 %collective-permute-start.3 = (f32[128,1024]{1,0:T(8,128)S(1)}, f32[128,1024]{1,0:T(8,128)S(1)}, u32[]{:S(2)}, u32[]{:S(2)}) collective-permute-start(f32[128,1024]{1,0:T(8,128)S(1)} %get-tuple-element.205), channel_id=1, source_target_pairs={{0,8},{2,10},{4,12},{6,14},{8,0},{10,2},{12,4},{14,6},{16,24},{18,... | collective-permute-start | bytes 1572872 | tf_op jit(solution)/shard_map/ppermute | solution.py:351
  66.4 29.4 %collective-permute-start.12 = (f32[256,1024]{1,0:T(8,128)}, f32[256,1024]{1,0:T(8,128)}, u32[]{:S(2)}, u32[]{:S(2)}) collective-permute-start(f32[256,1024]{1,0:T(8,128)} %get-tuple-element.153), channel_id=1, source_target_pairs={{0,4},{2,6},{4,0},{6,2},{8,12},{10,14},{12,8},{14,10},{16,20},{18,... | collective-permute-start | bytes 3145736 | tf_op jit(solution)/shard_map/ppermute | solution.py:351
  66.4 14.1 %collective-permute-start.7 = (f32[256,512]{1,0:T(8,128)S(1)}, f32[256,512]{1,0:T(8,128)S(1)}, u32[]{:S(2)}, u32[]{:S(2)}) collective-permute-start(f32[256,512]{1,0:T(8,128)S(1)} %get-tuple-element.134), channel_id=1, source_target_pairs={{0,2},{2,0},{4,6},{6,4},{8,10},{10,8},{12,14},{14,12},{16,18},{18,... | collective-permute-start | bytes 1572872 | tf_op jit(solution)/shard_map/ppermute | solution.py:335
  66.5 14.0 %collective-permute-start.8 = (f32[256,512]{1,0:T(8,128)S(1)}, f32[256,512]{1,0:T(8,128)S(1)}, u32[]{:S(2)}, u32[]{:S(2)}) collective-permute-start(f32[256,512]{1,0:T(8,128)S(1)} %get-tuple-element.135), channel_id=1, source_target_pairs={{0,2},{2,0},{4,6},{6,4},{8,10},{10,8},{12,14},{14,12},{16,18},{18,... | collective-permute-start | bytes 1572872 | tf_op jit(solution)/shard_map/ppermute | solution.py:335
  67.0 20.5 %collective-permute-start.13 = (f32[256,512]{1,0:T(8,128)}, f32[256,512]{1,0:T(8,128)}, u32[]{:S(2)}, u32[]{:S(2)}) collective-permute-start(f32[256,512]{1,0:T(8,128)} %get-tuple-element.154), channel_id=1, source_target_pairs={{0,2},{2,0},{4,6},{6,4},{8,10},{10,8},{12,14},{14,12},{16,18},{18,... | collective-permute-start | bytes 1572872 | tf_op jit(solution)/shard_map/ppermute | solution.py:335
  72.7 14.9 %collective-permute-start.14 = (f32[256,512]{1,0:T(8,128)}, f32[256,512]{1,0:T(8,128)}, u32[]{:S(2)}, u32[]{:S(2)}) collective-permute-start(f32[256,512]{1,0:T(8,128)} %get-tuple-element.155), channel_id=1, source_target_pairs={{0,2},{2,0},{4,6},{6,4},{8,10},{10,8},{12,14},{14,12},{16,18},{18,... | collective-permute-start | bytes 1572872 | tf_op jit(solution)/shard_map/ppermute | solution.py:335
  85.9 20.7 %collective-permute-start.11 = (f32[256,512]{1,0:T(8,128)}, f32[256,512]{1,0:T(8,128)}, u32[]{:S(2)}, u32[]{:S(2)}) collective-permute-start(f32[256,512]{1,0:T(8,128)} %get-tuple-element.152), channel_id=1, source_target_pairs={{0,8},{2,10},{4,12},{6,14},{8,0},{10,2},{12,4},{14,6},{16,24},{18,... | collective-permute-start | bytes 1572872 | tf_op jit(solution)/shard_map/ppermute | solution.py:351
  87.5 27.8 %collective-permute-start.16 = (f32[256,1024]{1,0:T(8,128)}, f32[256,1024]{1,0:T(8,128)}, u32[]{:S(2)}, u32[]{:S(2)}) collective-permute-start(f32[256,1024]{1,0:T(8,128)} %get-tuple-element.171), channel_id=1, source_target_pairs={{0,4},{2,6},{4,0},{6,2},{8,12},{10,14},{12,8},{14,10},{16,20},{18,... | collective-permute-start | bytes 3145736 | tf_op jit(solution)/shard_map/ppermute | solution.py:351
  87.5 20.2 %collective-permute-start.6 = (f32[64,1024]{1,0:T(8,128)}, f32[64,1024]{1,0:T(8,128)S(1)}, u32[]{:S(2)}, u32[]{:S(2)}) collective-permute-start(f32[64,1024]{1,0:T(8,128)} %get-tuple-element.215), channel_id=1, source_target_pairs={{0,16},{2,18},{4,20},{6,22},{8,24},{10,26},{12,28},{14,30},{16,0},... | collective-permute-start | bytes 786440 | tf_op jit(solution)/shard_map/ppermute | solution.py:351
  93.7 31.4 %collective-permute-start.19 = (f32[256,512]{1,0:T(8,128)S(1)}, f32[256,512]{1,0:T(8,128)S(1)}, u32[]{:S(2)}, u32[]{:S(2)}) collective-permute-start(f32[256,512]{1,0:T(8,128)S(1)} %get-tuple-element.176), channel_id=1, source_target_pairs={{0,4},{2,6},{4,0},{6,2},{8,12},{10,14},{12,8},{14,10},{16,20},{18,... | collective-permute-start | bytes 1572872 | tf_op jit(solution)/shard_map/ppermute | solution.py:351
  97.2 25.8 %collective-permute-start.15 = (f32[128,1024]{1,0:T(8,128)S(1)}, f32[128,1024]{1,0:T(8,128)S(1)}, u32[]{:S(2)}, u32[]{:S(2)}) collective-permute-start(f32[128,1024]{1,0:T(8,128)S(1)} %get-tuple-element.203), channel_id=1, source_target_pairs={{0,8},{2,10},{4,12},{6,14},{8,0},{10,2},{12,4},{14,6},{16,24},{18,... | collective-permute-start | bytes 1572872 | tf_op jit(solution)/shard_map/ppermute | solution.py:351
  107.8 15.3 %collective-permute-start.20 = (f32[128,512]{1,0:T(8,128)S(1)}, f32[128,512]{1,0:T(8,128)S(1)}, u32[]{:S(2)}, u32[]{:S(2)}) collective-permute-start(f32[128,512]{1,0:T(8,128)S(1)} %get-tuple-element.211), channel_id=1, source_target_pairs={{0,16},{2,18},{4,20},{6,22},{8,24},{10,26},{12,28},{14,30},{16,0},... | collective-permute-start | bytes 786440 | tf_op jit(solution)/shard_map/ppermute | solution.py:351
  109.2 13.8 %collective-permute-start.21 = (f32[64,512]{1,0:T(8,128)S(1)}, f32[64,512]{1,0:T(8,128)S(1)}, u32[]{:S(2)}, u32[]{:S(2)}) collective-permute-start(f32[64,512]{1,0:T(8,128)S(1)} %get-tuple-element.231), channel_id=1, source_target_pairs={{0,1},{1,0},{2,3},{3,2},{4,5},{5,4},{6,7},{7,6},{8,9},{9,8},{10,11... | collective-permute-start | bytes 393224 | tf_op jit(solution)/shard_map/ppermute | solution.py:378
  122.9 20.3 %collective-permute-start.18 = (f32[128,1024]{1,0:T(8,128)S(1)}, f32[128,1024]{1,0:T(8,128)S(1)}, u32[]{:S(2)}, u32[]{:S(2)}) collective-permute-start(f32[128,1024]{1,0:T(8,128)S(1)} %get-tuple-element.201), channel_id=1, source_target_pairs={{0,8},{2,10},{4,12},{6,14},{8,0},{10,2},{12,4},{14,6},{16,24},{18,... | collective-permute-start | bytes 1572872 | tf_op jit(solution)/shard_map/ppermute | solution.py:351
  123.0 20.3 %collective-permute-start.17 = (f32[64,1024]{1,0:T(8,128)S(1)}, f32[64,1024]{1,0:T(8,128)S(1)}, u32[]{:S(2)}, u32[]{:S(2)}) collective-permute-start(f32[64,1024]{1,0:T(8,128)S(1)} %get-tuple-element.213), channel_id=1, source_target_pairs={{0,16},{2,18},{4,20},{6,22},{8,24},{10,26},{12,28},{14,30},{16,0},... | collective-permute-start | bytes 786440 | tf_op jit(solution)/shard_map/ppermute | solution.py:351
  125.2 22.8 %collective-permute-start.23 = (f32[128,512]{1,0:T(8,128)S(1)}, f32[128,512]{1,0:T(8,128)S(1)}, u32[]{:S(2)}, u32[]{:S(2)}) collective-permute-start(f32[128,512]{1,0:T(8,128)S(1)} %get-tuple-element.207), channel_id=1, source_target_pairs={{0,8},{2,10},{4,12},{6,14},{8,0},{10,2},{12,4},{14,6},{16,24},{18,... | collective-permute-start | bytes 786440 | tf_op jit(solution)/shard_map/ppermute | solution.py:351
  144.1 14.7 %collective-permute-start.22 = (f32[64,1024]{1,0:T(8,128)S(1)}, f32[64,1024]{1,0:T(8,128)S(1)}, u32[]{:S(2)}, u32[]{:S(2)}) collective-permute-start(f32[64,1024]{1,0:T(8,128)S(1)} %get-tuple-element.209), channel_id=1, source_target_pairs={{0,16},{2,18},{4,20},{6,22},{8,24},{10,26},{12,28},{14,30},{16,0},... | collective-permute-start | bytes 786440 | tf_op jit(solution)/shard_map/ppermute | solution.py:351
  148.5 13.1 %collective-permute-start.26 = (f32[64,512]{1,0:T(8,128)S(1)}, f32[64,512]{1,0:T(8,128)S(1)}, u32[]{:S(2)}, u32[]{:S(2)}) collective-permute-start(f32[64,512]{1,0:T(8,128)S(1)} %get-tuple-element.217), channel_id=1, source_target_pairs={{0,16},{2,18},{4,20},{6,22},{8,24},{10,26},{12,28},{14,30},{16,0},... | collective-permute-start | bytes 393224 | tf_op jit(solution)/shard_map/ppermute | solution.py:351
  158.8 5.8 %collective-permute-start.27 = (f32[64,512]{1,0:T(8,128)S(1)}, f32[64,512]{1,0:T(8,128)S(1)}, u32[]{:S(2)}, u32[]{:S(2)}) collective-permute-start(f32[64,512]{1,0:T(8,128)S(1)} %get-tuple-element.223), channel_id=1, source_target_pairs={{0,1},{1,0},{2,3},{3,2},{4,5},{5,4},{6,7},{7,6},{8,9},{9,8},{10,11... | collective-permute-start | bytes 393224 | tf_op jit(solution)/shard_map/ppermute | solution.py:378
  (15 other events, 271.9 us)

commit v4 on v3

v4 whole, which is shorter than its diff:
```python
import functools

import jax
import jax.numpy as jnp
from jax import lax
from jax.experimental import pallas as pl
from jax.experimental.pallas import tpu as pltpu
from jax.sharding import PartitionSpec as P

OUTER = 4
CORES = 2
LANES = 128
TILE = 256
VMEM_BYTES = 40 * 1024 * 1024
F32 = jnp.float32
BF16 = jnp.bfloat16


def params():
    return pltpu.CompilerParams(vmem_limit_bytes=VMEM_BYTES)


def cost():
    return pl.CostEstimate(flops=1024, bytes_accessed=1024, transcendentals=0)


def split(value):
    high = value.astype(BF16)
    return high, (value - high.astype(F32)).astype(BF16)


def reversed_bits(value, count):
    result, bit = 0, 1
    while bit < count:
        result = 2 * result + (value // bit) % 2
        bit *= 2
    return result


def put_split(group, limit, first, b_ref, high_ref, low_ref, place):
    used = high_ref.shape[0]
    cols, depth = high_ref.shape[-2:]
    tiles = depth // LANES
    blocks = b_ref.shape[3] // tiles
    lane = lax.broadcasted_iota(jnp.int32, (1, LANES), 1)
    for h in range(used):
        rows = pl.ds(first + h, tiles, stride=blocks) if blocks > 1 else slice(None)
        turned = jnp.swapaxes(b_ref[group, 0, :, rows, :], 0, 1)
        for t in range(tiles):
            value = jnp.where(lane < limit[first + h] - t * LANES, turned[t], F32(0.0))
            high, low = split(value)
            high_ref[(h, *place, slice(None), slice(t * LANES, (t + 1) * LANES))] = high
            low_ref[(h, *place, slice(None), slice(t * LANES, (t + 1) * LANES))] = low


def slot(group, place, inner):
    x = reversed_bits((group % inner) ^ place[1], inner)
    z = reversed_bits((group // inner) ^ place[0], OUTER)
    return x * OUTER + z


def halves_put(total, outs, inner, cols, outer_first):
    groups = total.shape[0] // cols
    for x in range(inner):
        for z in range(groups // inner):
            row = (x * OUTER + z) * cols
            place = z * inner + x if outer_first else x * OUTER + z
            at = place % (groups // 2) * cols
            outs[place // (groups // 2)][at:at + cols, :] = total[row:row + cols]


def both(refs):
    return jnp.concatenate([ref[...] for ref in refs], axis=0)


def dot3(left_high, left_low, a_ref):
    high, low = split(a_ref[0])
    dot = functools.partial(jnp.dot, preferred_element_type=F32)
    return dot(left_high, high) + (dot(left_high, low) + dot(left_low, high))


def products_kernel(first, inner, step, chunks, pieces, adds, place, limit, rows_live, b_ref, a_ref, *refs):
    taken = sum(pieces) if adds else 0
    received, outs, (high_ref, low_ref) = refs[:taken], refs[taken:-2], refs[-2:]
    tile = a_ref.shape[2]
    groups, cols, depth = high_ref.shape[1:]
    loads = groups // step
    now = pl.program_id(0)

    @pl.when(now < loads)
    def _():
        for i in range(step):
            group = now * step + i
            put_split(i, limit, first, b_ref, high_ref, low_ref, (slot(group, place, inner),))

    at = loads
    for (h, start, count, outer_first), parts in zip(chunks, pieces):
        size = count // tile
        mine = (now >= at) & (now < at + size)
        live = start + (now - at) * tile < rows_live[h]
        got, received = received[:parts], received[parts:]
        out, outs = outs[:2 if adds else parts], outs[2 if adds else parts:]

        def put(total):
            if adds:
                halves_put(total, out, inner, cols, outer_first)
                return
            part = total.shape[0] // parts
            for i, ref in enumerate(out):
                ref[...] = total[i * part:(i + 1) * part]

        @pl.when(mine & live)
        def _():
            left = (r[h - first].reshape(groups * cols, depth) for r in (high_ref, low_ref))
            total = dot3(*left, a_ref)
            put(total + both(got) if adds else total)

        @pl.when(mine & jnp.logical_not(live))
        def _():
            put(both(got) if adds else jnp.zeros((groups * cols, tile), F32))

        at += size


def products(place, limit, rows_live, parts_of_b, amplitudes, chunks, shift, inner, pieces, received):
    groups, _, cols, rows_b, _ = parts_of_b.shape
    blocks, depth, rows = amplitudes.shape
    tile = min(rows, TILE)
    step = min(groups, 2)
    loads = groups // step
    first, last = chunks[0][0], chunks[-1][0]
    sizes = [chunk[2] // tile for chunk in chunks]
    offset = chunks[0][1] // tile
    total = sum(sizes)
    per_block = rows // tile
    height = groups * cols
    adds = bool(received)

    def b_map(n, place, *_):
        return (jnp.minimum(n, loads - 1), lax.rem(place[2] + shift, CORES), 0, 0, 0)

    def a_map(n, *_):
        t = jnp.maximum(n - loads, 0) + offset
        return (first + t // per_block, 0, t % per_block)

    def tiles_of(counts):
        result, at = [], 0
        for size, count in zip(sizes, counts):
            result += [pl.BlockSpec(
                (height // count, tile),
                lambda n, *_, at=at, size=size: (0, jnp.clip(n - loads - at, 0, size - 1)),
            )] * count
            at += size
        return result

    counts = [2] * len(chunks) if adds else pieces
    part = pltpu.VMEM((last - first + 1, groups, cols, depth), BF16)
    return pl.pallas_call(
        functools.partial(products_kernel, first, inner, step, chunks, pieces, adds),
        grid_spec=pltpu.PrefetchScalarGridSpec(
            num_scalar_prefetch=3,
            grid=(loads + total,),
            in_specs=[pl.BlockSpec((step, 1, cols, rows_b, LANES), b_map),
                      pl.BlockSpec((1, depth, tile), a_map)] + (tiles_of(pieces) if adds else []),
            out_specs=tiles_of(counts),
            scratch_shapes=[part, part],
        ),
        out_shape=[jax.ShapeDtypeStruct((height // count, chunk[2]), F32)
                   for chunk, count in zip(chunks, counts) for _ in range(count)],
        cost_estimate=cost(),
        compiler_params=params(),
        name="second_halves" if adds else "first_halves",
    )(place, limit, rows_live, parts_of_b, amplitudes, *received)


def place_kernel(side_ref, base, row_count, col_count, *refs):
    *parts, out_ref = refs
    side = side_ref[0]
    blocks = len(parts) // 2
    cols, rows = parts[0].shape
    col = base[0] + lax.broadcasted_iota(jnp.int32, (cols, rows), 0)
    row = base[1] + lax.broadcasted_iota(jnp.int32, (cols, rows), 1)
    for here in range(2):
        @pl.when(side == here)
        def _():
            order = parts[blocks:] + parts[:blocks] if here else parts
            kept = [
                jnp.where((col < col_count[h]) & (row < row_count[h]), part[...], F32(0.0))
                for h, part in enumerate(order)
            ]
            out_ref[...] = jnp.swapaxes(jnp.stack(kept), 0, 1)


def place_blocks(side, base, row_count, col_count, mine, other):
    cols, rows = mine[0].shape
    blocks = 2 * len(mine)
    vmem = pl.BlockSpec(memory_space=pltpu.VMEM)
    return pl.pallas_call(
        place_kernel,
        grid_spec=pltpu.PrefetchScalarGridSpec(
            num_scalar_prefetch=4, grid=(), in_specs=[vmem] * blocks, out_specs=vmem,
        ),
        out_shape=jax.ShapeDtypeStruct((cols, blocks, rows), F32),
        cost_estimate=cost(),
        compiler_params=params(),
        name="place_blocks",
    )(side, base, row_count, col_count, *mine, *other)


class Chain:
    def __init__(self):
        self.last = None

    def run(self, step, *args):
        if self.last is not None:
            args, _ = lax.optimization_barrier((args, self.last))
        result = step(*args)
        self.last = jax.tree.leaves(result)[0]
        return result


def local(inner, amplitudes, integrals, row_count, pair_count, col_count):
    blocks, depth, rows = amplitudes.shape
    all_cols = integrals.shape[0]
    tensor, rep = lax.axis_size("tensor"), lax.axis_size("rep")
    cols, row_local = all_cols // tensor, rows // rep
    me, side = lax.axis_index("tensor"), lax.axis_index("rep")
    z, x, core = me // (inner * CORES), me // CORES % inner, me % CORES
    place = jnp.stack([z, x, core]).astype(jnp.int32)

    pairs_here = lax.dynamic_slice_in_dim(pair_count, side * blocks, blocks) - me * depth
    rows_here = lax.dynamic_slice_in_dim(row_count, side * blocks, blocks)
    rows_here = jnp.where(pairs_here > 0, rows_here, 0)
    parts_of_b = integrals.reshape(all_cols, blocks, depth // LANES, LANES).transpose(0, 2, 1, 3)
    parts_of_b = parts_of_b.reshape(inner * OUTER, CORES, cols, blocks * depth // LANES, LANES)

    def index(z, x, core):
        return (z * inner + x) * CORES + core

    across = [(index(z, x, c), index(z, x, 1 - c))
              for z in range(OUTER) for x in range(inner) for c in range(CORES)]

    def along_inner(bit):
        return [(index(z, x, c), index(z, x ^ bit, c))
                for z in range(OUTER) for x in range(inner) for c in range(CORES)]

    def along_outer(bit):
        return [(index(z, x, c), index(z ^ bit, x, c))
                for z in range(OUTER) for x in range(inner) for c in range(CORES)]

    chain = Chain()
    received, split_in, totals, gens = {}, {}, {}, {}

    def run_products(chunks, shift, pieces, *got):
        return chain.run(
            lambda p, l, r, b, a, *g: products(p, l, r, b, a, chunks, shift, inner, pieces, g),
            place, pairs_here, rows_here, parts_of_b, amplitudes, *got,
        )

    def first_halves(names, pieces):
        sent = run_products([chunks[i] for i in names], 1, pieces)
        for i, count in zip(names, pieces):
            received[i] = [lax.ppermute(part, "tensor", across) for part in sent[:count]]
            sent = sent[count:]

    def second_halves(names):
        got = [part for i in names for part in received[i]]
        outs = run_products([chunks[i] for i in names], 0, [len(received[i]) for i in names], *got)
        for at, i in enumerate(names):
            gens[i] = work(*chunks[i], *outs[2 * at:2 * at + 2])

    def work(h, start, count, outer_first, keep, send):
        steps = [along_inner(1 << i) for i in range(inner.bit_length() - 1)]
        more = [along_outer(1 << i) for i in range(OUTER.bit_length() - 1)]
        for pairs in more + steps if outer_first else steps + more:
            got = lax.ppermute(send, "tensor", pairs)
            half = keep.shape[0] // 2
            if half < cols:
                total = chain.run(jnp.add, keep, got)
            else:
                keep, send = chain.run(
                    lambda a, b: (a[:half] + b[:half], a[half:] + b[half:]), keep, got
                )
            yield
        totals[h, start] = total

    mine, other = {}, {}

    def exchange(h):
        for i, chunk in enumerate(chunks):
            if chunk[0] == h:
                for _ in gens[i]:
                    pass
        if rep != 2:
            mine[h] = totals[h, 0]
            return
        if (h, row_local) in totals:
            first, second = totals[h, 0], totals[h, row_local]
        else:
            first, second = totals[h, 0][:, :row_local], totals[h, 0][:, row_local:]
        mine[h], away = chain.run(
            lambda a, b: (jnp.where(side == 0, a, b), jnp.where(side == 0, b, a)), first, second
        )
        other[h] = lax.ppermute(away, "rep", [(0, 1), (1, 0)])

    if inner == 2 and rep == 2 and blocks == 4:
        half = rows // 2
        chunks = [(0, 0, rows, False), (1, 0, half, True), (1, half, half, False),
                  (2, 0, rows, False), (3, 0, half, False), (3, half, half, False)]
        firsts = {"p": ([0, 1, 2], [2, 2, 2]), "q": ([3, 4, 5], [4, 2, 2])}
        seconds = {"w": [0], "x": [1, 2], "y": [3], "z": [4, 5]}
        plan = "pwxq01y21z020a3A21b4353cB45Cd"
    else:
        chunks = [(h, 0, rows, False) for h in range(blocks)]
        firsts = {"p": (list(range(blocks)), [2] * blocks)}
        seconds = {"w": list(range(blocks))}
        plan = "pw" + "abcdefgh"[:blocks]
    for move in plan:
        if move in firsts:
            first_halves(*firsts[move])
        elif move in seconds:
            second_halves(seconds[move])
        elif move in "ABCDEFGH":
            chain.last = chain.last, other["ABCDEFGH".index(move)]
        elif move in "abcdefgh":
            exchange("abcdefgh".index(move))
        else:
            next(gens[int(move)])

    if rep == 2:
        base = jnp.stack([me * cols, side * row_local]).astype(jnp.int32)
        return place_blocks(
            jnp.reshape(side, (1,)).astype(jnp.int32), base, row_count, col_count,
            [mine[h] for h in range(blocks)], [other[h] for h in range(blocks)],
        )
    arranged = lax.all_to_all(
        jnp.stack([mine[h] for h in range(blocks)], axis=1), "rep",
        split_axis=2, concat_axis=1, tiled=True,
    )
    col_index = me * cols + lax.broadcasted_iota(jnp.int32, (cols, 1, 1), 0)
    row_index = side * row_local + lax.broadcasted_iota(jnp.int32, (1, 1, row_local), 2)
    keep = (col_index < col_count[None, :, None]) & (row_index < row_count[None, :, None])
    return jnp.where(keep, arranged, F32(0.0))


def solution(mesh):
    inner = mesh.shape["tensor"] // (OUTER * CORES)
    in_specs = (P("rep", "tensor", None), P(None, "rep", "tensor"), P(), P(), P())
    out_specs = P("tensor", None, "rep")
    return jax.shard_map(
        functools.partial(local, inner), mesh=mesh, in_specs=in_specs, out_specs=out_specs,
        check_vma=False,
    )
```

time: 174 us -> 180 us (1.034)
  starting transfers between devices: 18.5 us -> 32 us
  Pallas kernels: 73.3 us -> 68.4 us
  waiting for transfers between devices: 72.5 us -> 69.9 us
    ppermute x15 -> x18, starting transfers between devices: 12.2 us -> 18.3 us  [work(): got = lax.ppermute(send, 'tensor', pairs)]
    ppermute x4, starting transfers between devices: 4.03 us -> 9.77 us  [exchange(): other[h] = lax.ppermute(away, 'rep', [(0, 1), (1, 0)])]
    pallas_call x8 -> x6, Pallas kernels: 71.4 us -> 66.5 us  [products(): pl.pallas_call(functools.partial(products_kernel, first, inner, step, chu...]
    ppermute x4, waiting for transfers between devices: 8.24 us -> 5.84 us  [exchange(): other[h] = lax.ppermute(away, 'rep', [(0, 1), (1, 0)])]
    ppermute x10 -> x14, starting transfers between devices: 2.2 us -> 4.01 us  [first_halves(): lax.ppermute(part, 'tensor', across)]
    ppermute x10 -> x14, waiting for transfers between devices: 3.73 us -> 2.42 us  [first_halves(): lax.ppermute(part, 'tensor', across)]
    ppermute x15 -> x18, waiting for transfers between devices: 60.6 us -> 61.6 us  [work(): got = lax.ppermute(send, 'tensor', pairs)]
    add x10 -> x12, other arithmetic: 5.06 us -> 5.26 us  [work(): a[half:] + b[half:]]
  transfers between devices with their start and end apart: 29 -> 36, of which waited for: 14 -> 13; matrix products, arithmetic and copies ran while one was open for 3% -> 4% of each run, Pallas kernels for 30% -> 29%
where the time goes in v4:
time: 180 us
  waiting for transfers between devices  69.9 us (39%)
  Pallas kernels  68.4 us (38%)
  starting transfers between devices  32 us (18%)
  other arithmetic  7.42 us (4%)
    pallas_call x6, Pallas kernels, products(): pl.pallas_call(functools.partial(products_kernel, first, inner, step, chu...  66.5 us
    ppermute x18, waiting for transfers between devices, work(): got = lax.ppermute(send, 'tensor', pairs)  61.6 us
    ppermute x18, starting transfers between devices, work(): got = lax.ppermute(send, 'tensor', pairs)  18.3 us
    ppermute x4, starting transfers between devices, exchange(): other[h] = lax.ppermute(away, 'rep', [(0, 1), (1, 0)])  9.77 us
    ppermute x4, waiting for transfers between devices, exchange(): other[h] = lax.ppermute(away, 'rep', [(0, 1), (1, 0)])  5.84 us
    add x12, other arithmetic, work(): a[half:] + b[half:]  5.26 us
    ppermute x14, starting transfers between devices, first_halves(): lax.ppermute(part, 'tensor', across)  4.01 us
  transfers between devices with their start and end apart: 36, of which 13 were waited for; matrix products, arithmetic and copies ran while one was open for 4% of the time, Pallas kernels for 29%

profile of v4, /device:TPU:0, one launch (start us, length us, event | category | flops | bytes accessed | tf_op | source)
XLA Modules:
  0.0 179.6 jit_solution(590446079903243886)
XLA Ops:
  0.8 13.7 %first_halves.2 = (f32[256,1024]{1,0:T(8,128)S(1)}, f32[256,1024]{1,0:T(8,128)S(1)}, f32[256,512]{1,0:T(8,128)S(1)}, f32[256,512]{1,0:T(8,128)S(1)}, f32[256,512]{1,0:T(8,128)S(1)}, /*index=5*/f32[256,512]{1,0:T(8,128)S(1)}) custom-call(s32[3]{0:T(128)S(1)} %pad_add_fusion.1.place, s32[4]{0:T(128)S(1)} %get-tuple-element.174.limit, ...), custom_call_target="tpu_custom_call" | custom-call | flops 1024 | bytes 1024 | tf_op jit(solution)/shard_map/first_halves/pallas_call | solution.py:158
  18.9 9.1 %second_halves.4 = (f32[256,1024]{1,0:T(8,128)S(1)}, f32[256,1024]{1,0:T(8,128)S(1)}) custom-call(s32[3]{0:T(128)S(1)} %pad_add_fusion.1.place, s32[4]{0:T(128)S(1)} %get-tuple-element.174.limit, s32[4]{0:T(128)S(1)} %get-tuple-element.175.rows_live, f32[8,2,64,32,128]{4,3,2,1,0:T(8,128)} %bitcast.12, f32[4,1024,1024]{2,1,0:T(8,128)} %a_ref.6, ...), custom_call_target="tpu_custom_call" | custom-call | flops 1024 | bytes 1024 | tf_op jit(solution)/shard_map/second_halves/pallas_call | solution.py:158
  28.0 2.9 %collective-permute-start.2 = (f32[256,1024]{1,0:T(8,128)S(1)}, f32[256,1024]{1,0:T(8,128)S(1)}, u32[]{:S(2)}, u32[]{:S(2)}) collective-permute-start(f32[256,1024]{1,0:T(8,128)S(1)} %get-tuple-element.124), channel_id=1, source_target_pairs={{0,4},{2,6},{4,0},{6,2},{8,12},{10,14},{12,8},{14,10},{16,20},{18,... | collective-permute-start | bytes 3145736 | tf_op jit(solution)/shard_map/ppermute | solution.py:276
  31.0 9.3 %second_halves.5 = (f32[256,512]{1,0:T(8,128)S(1)}, f32[256,512]{1,0:T(8,128)S(1)}, f32[256,512]{1,0:T(8,128)S(1)}, f32[256,512]{1,0:T(8,128)S(1)}) custom-call(s32[3]{0:T(128)S(1)} %pad_add_fusion.1.place, s32[4]{0:T(128)S(1)} %get-tuple-element.174.limit, s32[4]{0:T(128)S(1)} %get-tuple-element.175.rows_live, f32[8,2,64,32,128]{4,3,2,1,0:T(8,128)} %bitcast.13, ...), custom_call_target="tpu_custom_call" | custom-call | flops 1024 | bytes 1024 | tf_op jit(solution)/shard_map/second_halves/pallas_call | solution.py:158
  40.7 14.8 %first_halves.3 = (f32[128,1024]{1,0:T(8,128)S(1)}, f32[128,1024]{1,0:T(8,128)S(1)}, f32[128,1024]{1,0:T(8,128)S(1)}, f32[128,1024]{1,0:T(8,128)S(1)}, f32[256,5...) custom-call(s32[3]{0:T(128)S(1)} %pad_add_fusion.1.place, ...), custom_call_target="tpu_custom_call" | custom-call | flops 1024 | bytes 1024 | tf_op jit(solution)/shard_map/first_halves/pallas_call | solution.py:158
  56.8 7.9 %collective-permute-done.14 = f32[256,512]{1,0:T(8,128)S(1)} collective-permute-done((f32[256,512]{1,0:T(8,128)S(1)}, f32[256,512]{1,0:T(8,128)S(1)}, u32[]{:S(2)}, u32[]{:S(2)}) %collective-permute-start.14) | collective-permute-done | bytes 524320 | tf_op jit(solution)/shard_map/ppermute | solution.py:276
  66.7 11.4 %collective-permute-done.13 = f32[128,512]{1,0:T(8,128)S(1)} collective-permute-done((f32[128,512]{1,0:T(8,128)S(1)}, f32[128,512]{1,0:T(8,128)S(1)}, u32[]{:S(2)}, u32[]{:S(2)}) %collective-permute-start.13) | collective-permute-done | bytes 262176 | tf_op jit(solution)/shard_map/ppermute | solution.py:276
  78.1 9.3 %second_halves.6 = (f32[256,1024]{1,0:T(8,128)S(1)}, f32[256,1024]{1,0:T(8,128)S(1)}) custom-call(s32[3]{0:T(128)S(1)} %pad_add_fusion.1.place, s32[4]{0:T(128)S(1)} %get-tuple-element.174.limit, s32[4]{0:T(128)S(1)} %get-tuple-element.175.rows_live, f32[8,2,64,32,128]{4,3,2,1,0:T(8,128)} %bitcast.15, f32[4,1024,1024]{2,1,0:T(8,128)} %a_ref.6, ...), custom_call_target="tpu_custom_call" | custom-call | flops 1024 | bytes 1024 | tf_op jit(solution)/shard_map/second_halves/pallas_call | solution.py:158
  88.2 1.4 collective-permute-start.23
  90.3 2.0 %collective-permute-start.20 = (f32[128,512]{1,0:T(8,128)}, f32[128,512]{1,0:T(8,128)}, u32[]{:S(2)}, u32[]{:S(2)}) collective-permute-start(f32[128,512]{1,0:T(8,128)} %get-tuple-element.235), channel_id=1, source_target_pairs={{0,8},{2,10},{4,12},{6,14},{8,0},{10,2},{12,4},{14,6},{16,24},{18,... | collective-permute-start | bytes 786440 | tf_op jit(solution)/shard_map/ppermute | solution.py:276
  92.3 10.3 %second_halves.7 = (f32[256,512]{1,0:T(8,128)S(1)}, f32[256,512]{1,0:T(8,128)S(1)}, f32[256,512]{1,0:T(8,128)S(1)}, f32[256,512]{1,0:T(8,128)S(1)}) custom-call(s32[3]{0:T(128)S(1)} %pad_add_fusion.1.place, s32[4]{0:T(128)S(1)} %get-tuple-element.174.limit, s32[4]{0:T(128)S(1)} %get-tuple-element.175.rows_live, f32[8,2,64,32,128]{4,3,2,1,0:T(8,128)} %bitcast.16, ...), custom_call_target="tpu_custom_call" | custom-call | flops 1024 | bytes 1024 | tf_op jit(solution)/shard_map/second_halves/pallas_call | solution.py:158
  108.1 3.0 %collective-permute-start.22 = (f32[64,512]{1,0:T(8,128)S(1)}, f32[64,512]{1,0:T(8,128)S(1)}, u32[]{:S(2)}, u32[]{:S(2)}) collective-permute-start(f32[64,512]{1,0:T(8,128)S(1)} %get-tuple-element.245), channel_id=1, source_target_pairs={{0,16},{2,18},{4,20},{6,22},{8,24},{10,26},{12,28},{14,30},{16,0},... | collective-permute-start | bytes 393224 | tf_op jit(solution)/shard_map/ppermute | solution.py:276
  111.1 9.1 %collective-permute-done.19 = f32[64,1024]{1,0:T(8,128)} collective-permute-done((f32[64,1024]{1,0:T(8,128)}, f32[64,1024]{1,0:T(8,128)}, u32[]{:S(2)}, u32[]{:S(2)}) %collective-permute-start.19) | collective-permute-done | bytes 262176 | tf_op jit(solution)/shard_map/ppermute | solution.py:276
  121.3 7.8 %collective-permute-start.24 = (f32[64,512]{1,0:T(8,128)S(1)}, f32[64,512]{1,0:T(8,128)S(1)}, u32[]{:S(2)}, u32[]{:S(2)}) collective-permute-start(f32[64,512]{1,0:T(8,128)S(1)} %get-tuple-element.257), channel_id=1, source_target_pairs={{0,1},{1,0},{2,3},{3,2},{4,5},{5,4},{6,7},{7,6},{8,9},{9,8},{10,11... | collective-permute-start | bytes 393224 | tf_op jit(solution)/shard_map/ppermute | solution.py:304
  131.2 1.6 collective-permute-done.24.refs_4_
  132.9 11.1 %collective-permute-done.25 = f32[128,1024]{1,0:T(8,128)S(1)} collective-permute-done((f32[128,1024]{1,0:T(8,128)S(1)}, f32[128,1024]{1,0:T(8,128)S(1)}, u32[]{:S(2)}, u32[]{:S(2)}) %collective-permute-start.25) | collective-permute-done | bytes 524320 | tf_op jit(solution)/shard_map/ppermute | solution.py:276
  144.4 1.7 collective-permute-start.29
  146.9 10.9 %collective-permute-done.27 = f32[64,1024]{1,0:T(8,128)S(1)} collective-permute-done((f32[64,1024]{1,0:T(8,128)S(1)}, f32[64,1024]{1,0:T(8,128)S(1)}, u32[]{:S(2)}, u32[]{:S(2)}) %collective-permute-start.27) | collective-permute-done | bytes 262176 | tf_op jit(solution)/shard_map/ppermute | solution.py:276
  160.4 3.3 %collective-permute-done.32 = f32[128,512]{1,0:T(8,128)S(1)} collective-permute-done((f32[128,512]{1,0:T(8,128)S(1)}, f32[128,512]{1,0:T(8,128)S(1)}, u32[]{:S(2)}, u32[]{:S(2)}) %collective-permute-start.32) | collective-permute-done | bytes 262176 | tf_op jit(solution)/shard_map/ppermute | solution.py:276
  164.6 1.5 collective-permute-start.34
  166.1 4.7 %collective-permute-done.31 = f32[64,512]{1,0:T(8,128)S(1)} collective-permute-done((f32[64,512]{1,0:T(8,128)S(1)}, f32[64,512]{1,0:T(8,128)S(1)}, u32[]{:S(2)}, u32[]{:S(2)}) %collective-permute-start.31) | collective-permute-done | bytes 131104 | tf_op jit(solution)/shard_map/ppermute | solution.py:276
  170.8 1.8 %collective-permute-done.34 = f32[64,512]{1,0:T(8,128)S(1)} collective-permute-done((f32[64,512]{1,0:T(8,128)S(1)}, f32[64,512]{1,0:T(8,128)S(1)}, u32[]{:S(2)}, u32[]{:S(2)}) %collective-permute-start.34) | collective-permute-done | bytes 131104 | tf_op jit(solution)/shard_map/ppermute | solution.py:276
  173.5 4.3 %collective-permute-done.35.refs_7_ = f32[64,512]{1,0:T(8,128)S(1)} collective-permute-done((f32[64,512]{1,0:T(8,128)S(1)}, f32[64,512]{1,0:T(8,128)S(1)}, u32[]{:S(2)}, u32[]{:S(2)}) %collective-permute-start.35) | collective-permute-done | bytes 131104 | tf_op jit(solution)/shard_map/ppermute | solution.py:304
  177.7 1.9 %place_blocks.1 = f32[64,8,512]{2,1,0:T(8,128)} custom-call(s32[1]{0:T(128)} %bitcast.side_ref, s32[2]{0:T(128)S(1)} %pad_add_fusion.base, s32[8]{0:T(128)S(1)} %copy-done, s32[8]{0:T(128)S(1)} %copy-done.1, f32[64,512]{1,0:T(8,128)S(1)} %get-tuple-element.258.refs_0_, f32[64,512]{1,0:T(8,128)S(1)} %get-tuple-element.254.refs_1_, ...), custom_call_target="tpu_custom_call" | custom-call | flops 1024 | bytes 1024 | tf_op jit(solution)/shard_map/place_blocks/pallas_call | solution.py:198
  (90 shorter events, 24.4 us)
Async XLA Ops:
  15.2 15.8 %collective-permute-start.3 = (f32[256,512]{1,0:T(8,128)S(1)}, f32[256,512]{1,0:T(8,128)S(1)}, u32[]{:S(2)}, u32[]{:S(2)}) collective-permute-start(f32[256,512]{1,0:T(8,128)S(1)} %get-tuple-element.125), channel_id=1, source_target_pairs={{0,2},{2,0},{4,6},{6,4},{8,10},{10,8},{12,14},{14,12},{16,18},{18,... | collective-permute-start | bytes 1572872 | tf_op jit(solution)/shard_map/ppermute | solution.py:263
  15.6 15.3 %collective-permute-start.4 = (f32[256,512]{1,0:T(8,128)S(1)}, f32[256,512]{1,0:T(8,128)S(1)}, u32[]{:S(2)}, u32[]{:S(2)}) collective-permute-start(f32[256,512]{1,0:T(8,128)S(1)} %get-tuple-element.126), channel_id=1, source_target_pairs={{0,2},{2,0},{4,6},{6,4},{8,10},{10,8},{12,14},{14,12},{16,18},{18,... | collective-permute-start | bytes 1572872 | tf_op jit(solution)/shard_map/ppermute | solution.py:263
  15.7 15.3 %collective-permute-start.5 = (f32[256,512]{1,0:T(8,128)S(1)}, f32[256,512]{1,0:T(8,128)S(1)}, u32[]{:S(2)}, u32[]{:S(2)}) collective-permute-start(f32[256,512]{1,0:T(8,128)S(1)} %get-tuple-element.127), channel_id=1, source_target_pairs={{0,2},{2,0},{4,6},{6,4},{8,10},{10,8},{12,14},{14,12},{16,18},{18,... | collective-permute-start | bytes 1572872 | tf_op jit(solution)/shard_map/ppermute | solution.py:263
  17.4 13.6 %collective-permute-start.6 = (f32[256,512]{1,0:T(8,128)S(1)}, f32[256,512]{1,0:T(8,128)S(1)}, u32[]{:S(2)}, u32[]{:S(2)}) collective-permute-start(f32[256,512]{1,0:T(8,128)S(1)} %get-tuple-element.128), channel_id=1, source_target_pairs={{0,2},{2,0},{4,6},{6,4},{8,10},{10,8},{12,14},{14,12},{16,18},{18,... | collective-permute-start | bytes 1572872 | tf_op jit(solution)/shard_map/ppermute | solution.py:263
  28.0 28.0 %collective-permute-start.2 = (f32[256,1024]{1,0:T(8,128)S(1)}, f32[256,1024]{1,0:T(8,128)S(1)}, u32[]{:S(2)}, u32[]{:S(2)}) collective-permute-start(f32[256,1024]{1,0:T(8,128)S(1)} %get-tuple-element.124), channel_id=1, source_target_pairs={{0,4},{2,6},{4,0},{6,2},{8,12},{10,14},{12,8},{14,10},{16,20},{18,... | collective-permute-start | bytes 3145736 | tf_op jit(solution)/shard_map/ppermute | solution.py:276
  40.3 15.8 %collective-permute-start.12 = (f32[256,512]{1,0:T(8,128)S(1)}, f32[256,512]{1,0:T(8,128)S(1)}, u32[]{:S(2)}, u32[]{:S(2)}) collective-permute-start(f32[256,512]{1,0:T(8,128)S(1)} %get-tuple-element.151), channel_id=1, source_target_pairs={{0,8},{2,10},{4,12},{6,14},{8,0},{10,2},{12,4},{14,6},{16,24},{18,... | collective-permute-start | bytes 1572872 | tf_op jit(solution)/shard_map/ppermute | solution.py:276
  40.4 24.4 %collective-permute-start.14 = (f32[256,512]{1,0:T(8,128)S(1)}, f32[256,512]{1,0:T(8,128)S(1)}, u32[]{:S(2)}, u32[]{:S(2)}) collective-permute-start(f32[256,512]{1,0:T(8,128)S(1)} %get-tuple-element.155), channel_id=1, source_target_pairs={{0,4},{2,6},{4,0},{6,2},{8,12},{10,14},{12,8},{14,10},{16,20},{18,... | collective-permute-start | bytes 1572872 | tf_op jit(solution)/shard_map/ppermute | solution.py:276
  64.8 13.3 %collective-permute-start.13 = (f32[128,512]{1,0:T(8,128)S(1)}, f32[128,512]{1,0:T(8,128)S(1)}, u32[]{:S(2)}, u32[]{:S(2)}) collective-permute-start(f32[128,512]{1,0:T(8,128)S(1)} %get-tuple-element.239), channel_id=1, source_target_pairs={{0,16},{2,18},{4,20},{6,22},{8,24},{10,26},{12,28},{14,30},{16,0},... | collective-permute-start | bytes 786440 | tf_op jit(solution)/shard_map/ppermute | solution.py:276
  65.6 22.6 %collective-permute-start.8 = (f32[256,512]{1,0:T(8,128)S(1)}, f32[256,512]{1,0:T(8,128)S(1)}, u32[]{:S(2)}, u32[]{:S(2)}) collective-permute-start(f32[256,512]{1,0:T(8,128)S(1)} %get-tuple-element.147), channel_id=1, source_target_pairs={{0,2},{2,0},{4,6},{6,4},{8,10},{10,8},{12,14},{14,12},{16,18},{18,... | collective-permute-start | bytes 1572872 | tf_op jit(solution)/shard_map/ppermute | solution.py:263
  65.6 24.7 %collective-permute-start.9 = (f32[256,512]{1,0:T(8,128)S(1)}, f32[256,512]{1,0:T(8,128)S(1)}, u32[]{:S(2)}, u32[]{:S(2)}) collective-permute-start(f32[256,512]{1,0:T(8,128)S(1)} %get-tuple-element.148), channel_id=1, source_target_pairs={{0,2},{2,0},{4,6},{6,4},{8,10},{10,8},{12,14},{14,12},{16,18},{18,... | collective-permute-start | bytes 1572872 | tf_op jit(solution)/shard_map/ppermute | solution.py:263
  66.1 26.2 %collective-permute-start.10 = (f32[256,512]{1,0:T(8,128)S(1)}, f32[256,512]{1,0:T(8,128)S(1)}, u32[]{:S(2)}, u32[]{:S(2)}) collective-permute-start(f32[256,512]{1,0:T(8,128)S(1)} %get-tuple-element.149), channel_id=1, source_target_pairs={{0,2},{2,0},{4,6},{6,4},{8,10},{10,8},{12,14},{14,12},{16,18},{18,... | collective-permute-start | bytes 1572872 | tf_op jit(solution)/shard_map/ppermute | solution.py:263
  66.2 26.1 %collective-permute-start.11 = (f32[256,512]{1,0:T(8,128)S(1)}, f32[256,512]{1,0:T(8,128)S(1)}, u32[]{:S(2)}, u32[]{:S(2)}) collective-permute-start(f32[256,512]{1,0:T(8,128)S(1)} %get-tuple-element.150), channel_id=1, source_target_pairs={{0,2},{2,0},{4,6},{6,4},{8,10},{10,8},{12,14},{14,12},{16,18},{18,... | collective-permute-start | bytes 1572872 | tf_op jit(solution)/shard_map/ppermute | solution.py:263
  78.1 26.1 %collective-permute-start.7 = (f32[128,1024]{1,0:T(8,128)S(1)}, f32[128,1024]{1,0:T(8,128)S(1)}, u32[]{:S(2)}, u32[]{:S(2)}) collective-permute-start(f32[128,1024]{1,0:T(8,128)S(1)} %get-tuple-element.227), channel_id=1, source_target_pairs={{0,8},{2,10},{4,12},{6,14},{8,0},{10,2},{12,4},{14,6},{16,24},{18,... | collective-permute-start | bytes 1572872 | tf_op jit(solution)/shard_map/ppermute | solution.py:276
  88.2 40.9 %collective-permute-start.23 = (f32[256,1024]{1,0:T(8,128)S(1)}, f32[256,1024]{1,0:T(8,128)}, u32[]{:S(2)}, u32[]{:S(2)}) collective-permute-start(f32[256,1024]{1,0:T(8,128)S(1)} %get-tuple-element.191), channel_id=1, source_target_pairs={{0,4},{2,6},{4,0},{6,2},{8,12},{10,14},{12,8},{14,10},{16,20},{18,... | collective-permute-start | bytes 3145736 | tf_op jit(solution)/shard_map/ppermute | solution.py:276
  90.3 16.8 %collective-permute-start.20 = (f32[128,512]{1,0:T(8,128)}, f32[128,512]{1,0:T(8,128)}, u32[]{:S(2)}, u32[]{:S(2)}) collective-permute-start(f32[128,512]{1,0:T(8,128)} %get-tuple-element.235), channel_id=1, source_target_pairs={{0,8},{2,10},{4,12},{6,14},{8,0},{10,2},{12,4},{14,6},{16,24},{18,... | collective-permute-start | bytes 786440 | tf_op jit(solution)/shard_map/ppermute | solution.py:276
  105.0 15.2 %collective-permute-start.19 = (f32[64,1024]{1,0:T(8,128)}, f32[64,1024]{1,0:T(8,128)}, u32[]{:S(2)}, u32[]{:S(2)}) collective-permute-start(f32[64,1024]{1,0:T(8,128)} %get-tuple-element.237), channel_id=1, source_target_pairs={{0,16},{2,18},{4,20},{6,22},{8,24},{10,26},{12,28},{14,30},{16,0},... | collective-permute-start | bytes 786440 | tf_op jit(solution)/shard_map/ppermute | solution.py:276
  105.0 27.7 %collective-permute-start.21 = (f32[64,512]{1,0:T(8,128)}, f32[64,512]{1,0:T(8,128)S(1)}, u32[]{:S(2)}, u32[]{:S(2)}) collective-permute-start(f32[64,512]{1,0:T(8,128)} %get-tuple-element.247), channel_id=1, source_target_pairs={{0,4},{2,6},{4,0},{6,2},{8,12},{10,14},{12,8},{14,10},{16,20},{18,... | collective-permute-start | bytes 393224 | tf_op jit(solution)/shard_map/ppermute | solution.py:276
  105.7 27.2 %collective-permute-start.26 = (f32[256,512]{1,0:T(8,128)}, f32[256,512]{1,0:T(8,128)S(1)}, u32[]{:S(2)}, u32[]{:S(2)}) collective-permute-start(f32[256,512]{1,0:T(8,128)} %copy-done.3), channel_id=1, source_target_pairs={{0,4},{2,6},{4,0},{6,2},{8,12},{10,14},{12,8},{14,10},{16,20},{18,... | collective-permute-start | bytes 1572872 | tf_op jit(solution)/shard_map/ppermute | solution.py:276
  108.1 22.5 %collective-permute-start.22 = (f32[64,512]{1,0:T(8,128)S(1)}, f32[64,512]{1,0:T(8,128)S(1)}, u32[]{:S(2)}, u32[]{:S(2)}) collective-permute-start(f32[64,512]{1,0:T(8,128)S(1)} %get-tuple-element.245), channel_id=1, source_target_pairs={{0,16},{2,18},{4,20},{6,22},{8,24},{10,26},{12,28},{14,30},{16,0},... | collective-permute-start | bytes 393224 | tf_op jit(solution)/shard_map/ppermute | solution.py:276
  130.5 13.5 %collective-permute-start.25 = (f32[128,1024]{1,0:T(8,128)S(1)}, f32[128,1024]{1,0:T(8,128)S(1)}, u32[]{:S(2)}, u32[]{:S(2)}) collective-permute-start(f32[128,1024]{1,0:T(8,128)S(1)} %get-tuple-element.225), channel_id=1, source_target_pairs={{0,8},{2,10},{4,12},{6,14},{8,0},{10,2},{12,4},{14,6},{16,24},{18,... | collective-permute-start | bytes 1572872 | tf_op jit(solution)/shard_map/ppermute | solution.py:276
  130.6 15.8 %collective-permute-start.28 = (f32[256,512]{1,0:T(8,128)}, f32[256,512]{1,0:T(8,128)S(1)}, u32[]{:S(2)}, u32[]{:S(2)}) collective-permute-start(f32[256,512]{1,0:T(8,128)} %copy-done.2), channel_id=1, source_target_pairs={{0,4},{2,6},{4,0},{6,2},{8,12},{10,14},{12,8},{14,10},{16,20},{18,... | collective-permute-start | bytes 1572872 | tf_op jit(solution)/shard_map/ppermute | solution.py:276
  144.1 13.6 %collective-permute-start.27 = (f32[64,1024]{1,0:T(8,128)S(1)}, f32[64,1024]{1,0:T(8,128)S(1)}, u32[]{:S(2)}, u32[]{:S(2)}) collective-permute-start(f32[64,1024]{1,0:T(8,128)S(1)} %get-tuple-element.233), channel_id=1, source_target_pairs={{0,16},{2,18},{4,20},{6,22},{8,24},{10,26},{12,28},{14,30},{16,0},... | collective-permute-start | bytes 786440 | tf_op jit(solution)/shard_map/ppermute | solution.py:276
  144.4 14.7 %collective-permute-start.29 = (f32[128,512]{1,0:T(8,128)S(1)}, f32[128,512]{1,0:T(8,128)S(1)}, u32[]{:S(2)}, u32[]{:S(2)}) collective-permute-start(f32[128,512]{1,0:T(8,128)S(1)} %get-tuple-element.231), channel_id=1, source_target_pairs={{0,8},{2,10},{4,12},{6,14},{8,0},{10,2},{12,4},{14,6},{16,24},{18,... | collective-permute-start | bytes 786440 | tf_op jit(solution)/shard_map/ppermute | solution.py:276
  146.5 17.1 %collective-permute-start.32 = (f32[128,512]{1,0:T(8,128)S(1)}, f32[128,512]{1,0:T(8,128)S(1)}, u32[]{:S(2)}, u32[]{:S(2)}) collective-permute-start(f32[128,512]{1,0:T(8,128)S(1)} %get-tuple-element.229), channel_id=1, source_target_pairs={{0,8},{2,10},{4,12},{6,14},{8,0},{10,2},{12,4},{14,6},{16,24},{18,... | collective-permute-start | bytes 786440 | tf_op jit(solution)/shard_map/ppermute | solution.py:276
  (16 other events, 251.0 us)

commit v5 on v4

--- a/solution.py
+++ b/solution.py
@@ -11,6 +11,7 @@
 CORES = 2
 LANES = 128
 TILE = 256
+PIECES = 2
 VMEM_BYTES = 40 * 1024 * 1024
 F32 = jnp.float32
 BF16 = jnp.bfloat16
@@ -69,7 +70,7 @@
             outs[place // (groups // 2)][at:at + cols, :] = total[row:row + cols]
 
 
-def both(refs):
+def joined(refs):
     return jnp.concatenate([ref[...] for ref in refs], axis=0)
 
 
@@ -80,8 +81,7 @@
 
 
 def products_kernel(first, inner, step, chunks, pieces, adds, place, limit, rows_live, b_ref, a_ref, *refs):
-    taken = sum(pieces) if adds else 0
-    received, outs, (high_ref, low_ref) = refs[:taken], refs[taken:-2], refs[-2:]
+    received, outs, (high_ref, low_ref) = refs[:adds], refs[adds:-2], refs[-2:]
     tile = a_ref.shape[2]
     groups, cols, depth = high_ref.shape[1:]
     loads = groups // step
@@ -94,18 +94,18 @@
             put_split(i, limit, first, b_ref, high_ref, low_ref, (slot(group, place, inner),))
 
     at = loads
-    for (h, start, count, outer_first), parts in zip(chunks, pieces):
+    for h, start, count, outer_first in chunks:
         size = count // tile
         mine = (now >= at) & (now < at + size)
         live = start + (now - at) * tile < rows_live[h]
-        got, received = received[:parts], received[parts:]
-        out, outs = outs[:2 if adds else parts], outs[2 if adds else parts:]
+        got = received[(h - first) * pieces:(h - first + 1) * pieces]
+        out, outs = outs[:2 if adds else pieces], outs[2 if adds else pieces:]
 
         def put(total):
             if adds:
                 halves_put(total, out, inner, cols, outer_first)
                 return
-            part = total.shape[0] // parts
+            part = total.shape[0] // pieces
             for i, ref in enumerate(out):
                 ref[...] = total[i * part:(i + 1) * part]
 
@@ -113,16 +113,16 @@
         def _():
             left = (r[h - first].reshape(groups * cols, depth) for r in (high_ref, low_ref))
             total = dot3(*left, a_ref)
-            put(total + both(got) if adds else total)
+            put(total + joined(got) if adds else total)
 
         @pl.when(mine & jnp.logical_not(live))
         def _():
-            put(both(got) if adds else jnp.zeros((groups * cols, tile), F32))
+            put(joined(got) if adds else jnp.zeros((groups * cols, tile), F32))
 
         at += size
 
 
-def products(place, limit, rows_live, parts_of_b, amplitudes, chunks, shift, inner, pieces, received):
+def products(place, limit, rows_live, parts_of_b, amplitudes, chunks, shift, inner, received):
     groups, _, cols, rows_b, _ = parts_of_b.shape
     blocks, depth, rows = amplitudes.shape
     tile = min(rows, TILE)
@@ -153,15 +153,24 @@
             at += size
         return result
 
-    counts = [2] * len(chunks) if adds else pieces
+    counts = [2 if adds else PIECES] * len(chunks)
+    got_specs = []
+    for h in range(first, last + 1) if adds else []:
+        mine = [i for i, chunk in enumerate(chunks) if chunk[0] == h]
+        at, size = sum(sizes[:mine[0]]), sum(sizes[i] for i in mine)
+        begin = chunks[mine[0]][1] // tile
+        got_specs += [pl.BlockSpec(
+            (height // PIECES, tile),
+            lambda n, *_, at=at, size=size, begin=begin: (0, begin + jnp.clip(n - loads - at, 0, size - 1)),
+        )] * PIECES
     part = pltpu.VMEM((last - first + 1, groups, cols, depth), BF16)
     return pl.pallas_call(
-        functools.partial(products_kernel, first, inner, step, chunks, pieces, adds),
+        functools.partial(products_kernel, first, inner, step, chunks, PIECES, len(received)),
         grid_spec=pltpu.PrefetchScalarGridSpec(
             num_scalar_prefetch=3,
             grid=(loads + total,),
             in_specs=[pl.BlockSpec((step, 1, cols, rows_b, LANES), b_map),
-                      pl.BlockSpec((1, depth, tile), a_map)] + (tiles_of(pieces) if adds else []),
+                      pl.BlockSpec((1, depth, tile), a_map)] + got_specs,
             out_specs=tiles_of(counts),
             scratch_shapes=[part, part],
         ),
@@ -251,21 +260,21 @@
     chain = Chain()
     received, split_in, totals, gens = {}, {}, {}, {}
 
-    def run_products(chunks, shift, pieces, *got):
+    def run_products(chunks, shift, *got):
         return chain.run(
-            lambda p, l, r, b, a, *g: products(p, l, r, b, a, chunks, shift, inner, pieces, g),
+            lambda p, l, r, b, a, *g: products(p, l, r, b, a, chunks, shift, inner, g),
             place, pairs_here, rows_here, parts_of_b, amplitudes, *got,
         )
 
-    def first_halves(names, pieces):
-        sent = run_products([chunks[i] for i in names], 1, pieces)
-        for i, count in zip(names, pieces):
-            received[i] = [lax.ppermute(part, "tensor", across) for part in sent[:count]]
-            sent = sent[count:]
+    def first_halves(names):
+        sent = run_products([(h, 0, rows, False) for h in names], 1)
+        for i, h in enumerate(names):
+            received[h] = [lax.ppermute(part, "tensor", across)
+                           for part in sent[i * PIECES:(i + 1) * PIECES]]
 
     def second_halves(names):
-        got = [part for i in names for part in received[i]]
-        outs = run_products([chunks[i] for i in names], 0, [len(received[i]) for i in names], *got)
+        got = [part for h in sorted({chunks[i][0] for i in names}) for part in received[h]]
+        outs = run_products([chunks[i] for i in names], 0, *got)
         for at, i in enumerate(names):
             gens[i] = work(*chunks[i], *outs[2 * at:2 * at + 2])
 
@@ -305,19 +314,19 @@
 
     if inner == 2 and rep == 2 and blocks == 4:
         half = rows // 2
-        chunks = [(0, 0, rows, False), (1, 0, half, True), (1, half, half, False),
-                  (2, 0, rows, False), (3, 0, half, False), (3, half, half, False)]
-        firsts = {"p": ([0, 1, 2], [2, 2, 2]), "q": ([3, 4, 5], [4, 2, 2])}
-        seconds = {"w": [0], "x": [1, 2], "y": [3], "z": [4, 5]}
-        plan = "pwxq01y21z020a3A21b4353cB45Cd"
+        chunks = [(0, 0, rows, False), (1, 0, rows, False), (2, 0, rows, False),
+                  (3, 0, half, False), (3, half, half, False)]
+        firsts = {"p": [0, 1], "q": [2, 3]}
+        seconds = {"w": [0, 1], "z": [2, 3, 4]}
+        plan = "pwq0z01a213Ab24B3c4Cd"
     else:
         chunks = [(h, 0, rows, False) for h in range(blocks)]
-        firsts = {"p": (list(range(blocks)), [2] * blocks)}
+        firsts = {"p": list(range(blocks))}
         seconds = {"w": list(range(blocks))}
         plan = "pw" + "abcdefgh"[:blocks]
     for move in plan:
         if move in firsts:
-            first_halves(*firsts[move])
+            first_halves(firsts[move])
         elif move in seconds:
             second_halves(seconds[move])
         elif move in "ABCDEFGH":

time: 180 us -> 172 us (0.956)
  Pallas kernels: 68.4 us -> 61.3 us
    pallas_call x6 -> x4, Pallas kernels: 66.5 us -> 59.5 us  [products(): pl.pallas_call(functools.partial(products_kernel, first, inner, step, chu...]
    ppermute x18 -> x15, waiting for transfers between devices: 61.6 us -> 55.2 us  [work(): got = lax.ppermute(send, 'tensor', pairs)]
    ppermute x14 -> x8, waiting for transfers between devices: 2.42 us -> 6.2 us  [first_halves(): lax.ppermute(part, 'tensor', across)]
    ppermute x4, waiting for transfers between devices: 5.84 us -> 7.83 us  [exchange(): other[h] = lax.ppermute(away, 'rep', [(0, 1), (1, 0)])]
    ppermute x14 -> x8, starting transfers between devices: 4.01 us -> 2.18 us  [first_halves(): lax.ppermute(part, 'tensor', across)]
    ppermute x18 -> x15, starting transfers between devices: 18.3 us -> 19.6 us  [work(): got = lax.ppermute(send, 'tensor', pairs)]
    add x12 -> x10, other arithmetic: 5.26 us -> 5.49 us  [work(): a[half:] + b[half:]]
  transfers between devices with their start and end apart: 36 -> 27, of which waited for: 13 -> 17; matrix products, arithmetic and copies ran while one was open for 4% -> 3% of each run, Pallas kernels for 29% -> 17%
where the time goes in v5:
time: 172 us; the launch traced here: 171 us
  waiting for transfers between devices  69.2 us (40%)
  Pallas kernels  61.3 us (36%)
  starting transfers between devices  32.1 us (19%)
  other arithmetic  6.6 us (4%)
    pallas_call x4, Pallas kernels, products(): pl.pallas_call(functools.partial(products_kernel, first, inner, step, chu...  59.5 us
    ppermute x15, waiting for transfers between devices, work(): got = lax.ppermute(send, 'tensor', pairs)  55.2 us
    ppermute x15, starting transfers between devices, work(): got = lax.ppermute(send, 'tensor', pairs)  19.6 us
    ppermute x4, starting transfers between devices, exchange(): other[h] = lax.ppermute(away, 'rep', [(0, 1), (1, 0)])  10.3 us
    ppermute x4, waiting for transfers between devices, exchange(): other[h] = lax.ppermute(away, 'rep', [(0, 1), (1, 0)])  7.83 us
    ppermute x8, waiting for transfers between devices, first_halves(): lax.ppermute(part, 'tensor', across)  6.2 us
    add x10, other arithmetic, work(): a[half:] + b[half:]  5.49 us
  transfers between devices with their start and end apart: 27, of which 17 were waited for; matrix products, arithmetic and copies ran while one was open for 3% of the time, Pallas kernels for 17%

profile of v5, /device:TPU:0, one launch (start us, length us, event | category | flops | bytes accessed | tf_op | source)
XLA Modules:
  0.0 171.1 jit_solution(15805839635347877200)
XLA Ops:
  0.8 14.4 %first_halves.2 = (f32[256,1024]{1,0:T(8,128)S(1)}, f32[256,1024]{1,0:T(8,128)S(1)}, f32[256,1024]{1,0:T(8,128)S(1)}, f32[256,1024]{1,0:T(8,128)S(1)}) custom-call(s32[3]{0:T(128)S(1)} %pad_add_fusion.1.place, s32[4]{0:T(128)S(1)} %get-tuple-element.111.limit, s32[4]{0:T(128)S(1)} %get-tuple-element.112.rows_live, f32[8,2,64,32,128]{4,3,2,1,0:T(8,128)} %bitcast.11, ...), custom_call_target="tpu_custom_call" | custom-call | flops 1024 | bytes 1024 | tf_op jit(solution)/shard_map/first_halves/pallas_call | solution.py:167
  22.5 15.2 %second_halves.2 = (f32[256,1024]{1,0:T(8,128)S(1)}, f32[256,1024]{1,0:T(8,128)S(1)}, f32[256,1024]{1,0:T(8,128)S(1)}, f32[256,1024]{1,0:T(8,128)}) custom-call(s32[3]{0:T(128)S(1)} %pad_add_fusion.1.place, s32[4]{0:T(128)S(1)} %get-tuple-element.111.limit, s32[4]{0:T(128)S(1)} %get-tuple-element.112.rows_live, f32[8,2,64,32,128]{4,3,2,1,0:T(8,128)} %bitcast.12, ...), custom_call_target="tpu_custom_call" | custom-call | flops 1024 | bytes 1024 | tf_op jit(solution)/shard_map/second_halves/pallas_call | solution.py:167
  37.7 2.9 %collective-permute-start.4 = (f32[256,1024]{1,0:T(8,128)S(1)}, f32[256,1024]{1,0:T(8,128)S(1)}, u32[]{:S(2)}, u32[]{:S(2)}) collective-permute-start(f32[256,1024]{1,0:T(8,128)S(1)} %get-tuple-element.98), channel_id=1, source_target_pairs={{0,4},{2,6},{4,0},{6,2},{8,12},{10,14},{12,8},{14,10},{16,20},{18,... | collective-permute-start | bytes 3145736 | tf_op jit(solution)/shard_map/ppermute | solution.py:285
  40.6 14.4 %first_halves.3 = (f32[256,1024]{1,0:T(8,128)S(1)}, f32[256,1024]{1,0:T(8,128)S(1)}, f32[256,1024]{1,0:T(8,128)S(1)}, f32[256,1024]{1,0:T(8,128)S(1)}) custom-call(s32[3]{0:T(128)S(1)} %pad_add_fusion.1.place, s32[4]{0:T(128)S(1)} %get-tuple-element.111.limit, s32[4]{0:T(128)S(1)} %get-tuple-element.112.rows_live, f32[8,2,64,32,128]{4,3,2,1,0:T(8,128)} %bitcast.13, ...), custom_call_target="tpu_custom_call" | custom-call | flops 1024 | bytes 1024 | tf_op jit(solution)/shard_map/first_halves/pallas_call | solution.py:167
  56.1 8.0 %collective-permute-done.4 = f32[256,1024]{1,0:T(8,128)S(1)} collective-permute-done((f32[256,1024]{1,0:T(8,128)S(1)}, f32[256,1024]{1,0:T(8,128)S(1)}, u32[]{:S(2)}, u32[]{:S(2)}) %collective-permute-start.4) | collective-permute-done | bytes 1048608 | tf_op jit(solution)/shard_map/ppermute | solution.py:285
  67.7 15.5 %second_halves.3 = (f32[256,1024]{1,0:T(8,128)S(1)}, f32[256,1024]{1,0:T(8,128)}, f32[256,512]{1,0:T(8,128)S(1)}, f32[256,512]{1,0:T(8,128)S(1)}, f32[256,512]{1,0:T(8,128)S(1)}, /*index=5*/f32[256,512]{1,0:T(8,128)S(1)}) custom-call(s32[3]{0:T(128)S(1)} %pad_add_fusion.1.place, s32[4]{0:T(128)S(1)} %get-tuple-element.111.limit, ...), custom_call_target="tpu_custom_call" | custom-call | flops 1024 | bytes 1024 | tf_op jit(solution)/shard_map/second_halves/pallas_call | solution.py:167
  84.9 2.0 %collective-permute-start.15 = (f32[256,512]{1,0:T(8,128)}, f32[256,512]{1,0:T(8,128)S(1)}, u32[]{:S(2)}, u32[]{:S(2)}) collective-permute-start(f32[256,512]{1,0:T(8,128)} %copy-done.3), channel_id=1, source_target_pairs={{0,4},{2,6},{4,0},{6,2},{8,12},{10,14},{12,8},{14,10},{16,20},{18,... | collective-permute-start | bytes 1572872 | tf_op jit(solution)/shard_map/ppermute | solution.py:285
  88.2 2.2 %collective-permute-done.11 = f32[256,1024]{1,0:T(8,128)} collective-permute-done((f32[256,1024]{1,0:T(8,128)}, f32[256,1024]{1,0:T(8,128)}, u32[]{:S(2)}, u32[]{:S(2)}) %collective-permute-start.11) | collective-permute-done | bytes 1048608 | tf_op jit(solution)/shard_map/ppermute | solution.py:285
  91.8 1.9 %collective-permute-start.12 = (f32[128,1024]{1,0:T(8,128)S(1)}, f32[128,1024]{1,0:T(8,128)S(1)}, u32[]{:S(2)}, u32[]{:S(2)}) collective-permute-start(f32[128,1024]{1,0:T(8,128)S(1)} %get-tuple-element.167), channel_id=1, source_target_pairs={{0,8},{2,10},{4,12},{6,14},{8,0},{10,2},{12,4},{14,6},{16,24},{18,... | collective-permute-start | bytes 1572872 | tf_op jit(solution)/shard_map/ppermute | solution.py:285
  93.7 6.7 %collective-permute-done.10 = f32[64,1024]{1,0:T(8,128)S(1)} collective-permute-done((f32[64,1024]{1,0:T(8,128)S(1)}, f32[64,1024]{1,0:T(8,128)S(1)}, u32[]{:S(2)}, u32[]{:S(2)}) %collective-permute-start.10) | collective-permute-done | bytes 262176 | tf_op jit(solution)/shard_map/ppermute | solution.py:285
  100.5 12.4 %collective-permute-done.13 = f32[256,1024]{1,0:T(8,128)} collective-permute-done((f32[256,1024]{1,0:T(8,128)}, f32[256,1024]{1,0:T(8,128)}, u32[]{:S(2)}, u32[]{:S(2)}) %collective-permute-start.13) | collective-permute-done | bytes 1048608 | tf_op jit(solution)/shard_map/ppermute | solution.py:285
  117.1 5.1 %collective-permute-start.16 = (f32[64,512]{1,0:T(8,128)S(1)}, f32[64,512]{1,0:T(8,128)S(1)}, u32[]{:S(2)}, u32[]{:S(2)}) collective-permute-start(f32[64,512]{1,0:T(8,128)S(1)} %get-tuple-element.195), channel_id=1, source_target_pairs={{0,1},{1,0},{2,3},{3,2},{4,5},{5,4},{6,7},{7,6},{8,9},{9,8},{10,11... | collective-permute-start | bytes 393224 | tf_op jit(solution)/shard_map/ppermute | solution.py:313
  124.1 1.9 %collective-permute-start.19 = (f32[128,512]{1,0:T(8,128)S(1)}, f32[128,512]{1,0:T(8,128)S(1)}, u32[]{:S(2)}, u32[]{:S(2)}) collective-permute-start(f32[128,512]{1,0:T(8,128)S(1)} %get-tuple-element.173), channel_id=1, source_target_pairs={{0,8},{2,10},{4,12},{6,14},{8,0},{10,2},{12,4},{14,6},{16,24},{18,... | collective-permute-start | bytes 786440 | tf_op jit(solution)/shard_map/ppermute | solution.py:285
  126.7 3.2 %collective-permute-start.21 = (f32[64,512]{1,0:T(8,128)S(1)}, f32[64,512]{1,0:T(8,128)S(1)}, u32[]{:S(2)}, u32[]{:S(2)}) collective-permute-start(f32[64,512]{1,0:T(8,128)S(1)} %get-tuple-element.191), channel_id=1, source_target_pairs={{0,1},{1,0},{2,3},{3,2},{4,5},{5,4},{6,7},{7,6},{8,9},{9,8},{10,11... | collective-permute-start | bytes 393224 | tf_op jit(solution)/shard_map/ppermute | solution.py:313
  129.9 10.4 %collective-permute-done.17 = f32[128,1024]{1,0:T(8,128)S(1)} collective-permute-done((f32[128,1024]{1,0:T(8,128)S(1)}, f32[128,1024]{1,0:T(8,128)S(1)}, u32[]{:S(2)}, u32[]{:S(2)}) %collective-permute-start.17) | collective-permute-done | bytes 524320 | tf_op jit(solution)/shard_map/ppermute | solution.py:285
  140.5 3.2 %collective-permute-done.19 = f32[128,512]{1,0:T(8,128)S(1)} collective-permute-done((f32[128,512]{1,0:T(8,128)S(1)}, f32[128,512]{1,0:T(8,128)S(1)}, u32[]{:S(2)}, u32[]{:S(2)}) %collective-permute-start.19) | collective-permute-done | bytes 262176 | tf_op jit(solution)/shard_map/ppermute | solution.py:285
  143.7 2.9 %collective-permute-start.22 = (f32[64,512]{1,0:T(8,128)S(1)}, f32[64,512]{1,0:T(8,128)S(1)}, u32[]{:S(2)}, u32[]{:S(2)}) collective-permute-start(f32[64,512]{1,0:T(8,128)S(1)} %get-tuple-element.183), channel_id=1, source_target_pairs={{0,16},{2,18},{4,20},{6,22},{8,24},{10,26},{12,28},{14,30},{16,0},... | collective-permute-start | bytes 393224 | tf_op jit(solution)/shard_map/ppermute | solution.py:285
  146.6 2.5 %collective-permute-start.23 = (f32[128,512]{1,0:T(8,128)S(1)}, f32[128,512]{1,0:T(8,128)S(1)}, u32[]{:S(2)}, u32[]{:S(2)}) collective-permute-start(f32[128,512]{1,0:T(8,128)S(1)} %get-tuple-element.171), channel_id=1, source_target_pairs={{0,8},{2,10},{4,12},{6,14},{8,0},{10,2},{12,4},{14,6},{16,24},{18,... | collective-permute-start | bytes 786440 | tf_op jit(solution)/shard_map/ppermute | solution.py:285
  149.1 4.2 %collective-permute-done.18 = f32[64,1024]{1,0:T(8,128)S(1)} collective-permute-done((f32[64,1024]{1,0:T(8,128)S(1)}, f32[64,1024]{1,0:T(8,128)S(1)}, u32[]{:S(2)}, u32[]{:S(2)}) %collective-permute-start.18) | collective-permute-done | bytes 262176 | tf_op jit(solution)/shard_map/ppermute | solution.py:285
  153.4 4.3 %collective-permute-done.23 = f32[128,512]{1,0:T(8,128)S(1)} collective-permute-done((f32[128,512]{1,0:T(8,128)S(1)}, f32[128,512]{1,0:T(8,128)S(1)}, u32[]{:S(2)}, u32[]{:S(2)}) %collective-permute-start.23) | collective-permute-done | bytes 262176 | tf_op jit(solution)/shard_map/ppermute | solution.py:285
  157.8 4.8 %collective-permute-done.24.refs_6_ = f32[64,512]{1,0:T(8,128)S(1)} collective-permute-done((f32[64,512]{1,0:T(8,128)S(1)}, f32[64,512]{1,0:T(8,128)S(1)}, u32[]{:S(2)}, u32[]{:S(2)}) %collective-permute-start.24) | collective-permute-done | bytes 131104 | tf_op jit(solution)/shard_map/ppermute | solution.py:313
  164.2 2.0 %collective-permute-start.26 = (f32[64,512]{1,0:T(8,128)S(1)}, f32[64,512]{1,0:T(8,128)S(1)}, u32[]{:S(2)}, u32[]{:S(2)}) collective-permute-start(f32[64,512]{1,0:T(8,128)S(1)} %get-tuple-element.185), channel_id=1, source_target_pairs={{0,1},{1,0},{2,3},{3,2},{4,5},{5,4},{6,7},{7,6},{8,9},{9,8},{10,11... | collective-permute-start | bytes 393224 | tf_op jit(solution)/shard_map/ppermute | solution.py:313
  166.2 3.0 %collective-permute-done.26.refs_7_ = f32[64,512]{1,0:T(8,128)S(1)} collective-permute-done((f32[64,512]{1,0:T(8,128)S(1)}, f32[64,512]{1,0:T(8,128)S(1)}, u32[]{:S(2)}, u32[]{:S(2)}) %collective-permute-start.26) | collective-permute-done | bytes 131104 | tf_op jit(solution)/shard_map/ppermute | solution.py:313
  169.2 1.9 %place_blocks.1 = f32[64,8,512]{2,1,0:T(8,128)} custom-call(s32[1]{0:T(128)} %bitcast.side_ref, s32[2]{0:T(128)S(1)} %pad_add_fusion.base, s32[8]{0:T(128)S(1)} %copy-done, s32[8]{0:T(128)S(1)} %copy-done.1, f32[64,512]{1,0:T(8,128)S(1)} %get-tuple-element.196.refs_0_, f32[64,512]{1,0:T(8,128)S(1)} %get-tuple-element.192.refs_1_, ...), custom_call_target="tpu_custom_call" | custom-call | flops 1024 | bytes 1024 | tf_op jit(solution)/shard_map/place_blocks/pallas_call | solution.py:207
  (68 shorter events, 26.0 us)
Async XLA Ops:
  15.8 5.2 %collective-permute-start.2 = (f32[256,1024]{1,0:T(8,128)S(1)}, f32[256,1024]{1,0:T(8,128)S(1)}, u32[]{:S(2)}, u32[]{:S(2)}) collective-permute-start(f32[256,1024]{1,0:T(8,128)S(1)} %get-tuple-element.86), channel_id=1, source_target_pairs={{0,2},{2,0},{4,6},{6,4},{8,10},{10,8},{12,14},{14,12},{16,18},{18,... | collective-permute-start | bytes 3145736 | tf_op jit(solution)/shard_map/ppermute | solution.py:272
  16.2 6.3 %collective-permute-start.3 = (f32[256,1024]{1,0:T(8,128)S(1)}, f32[256,1024]{1,0:T(8,128)S(1)}, u32[]{:S(2)}, u32[]{:S(2)}) collective-permute-start(f32[256,1024]{1,0:T(8,128)S(1)} %get-tuple-element.87), channel_id=1, source_target_pairs={{0,2},{2,0},{4,6},{6,4},{8,10},{10,8},{12,14},{14,12},{16,18},{18,... | collective-permute-start | bytes 3145736 | tf_op jit(solution)/shard_map/ppermute | solution.py:272
  37.7 26.3 %collective-permute-start.4 = (f32[256,1024]{1,0:T(8,128)S(1)}, f32[256,1024]{1,0:T(8,128)S(1)}, u32[]{:S(2)}, u32[]{:S(2)}) collective-permute-start(f32[256,1024]{1,0:T(8,128)S(1)} %get-tuple-element.98), channel_id=1, source_target_pairs={{0,4},{2,6},{4,0},{6,2},{8,12},{10,14},{12,8},{14,10},{16,20},{18,... | collective-permute-start | bytes 3145736 | tf_op jit(solution)/shard_map/ppermute | solution.py:285
  55.0 12.0 %collective-permute-start.6 = (f32[256,1024]{1,0:T(8,128)S(1)}, f32[256,1024]{1,0:T(8,128)S(1)}, u32[]{:S(2)}, u32[]{:S(2)}) collective-permute-start(f32[256,1024]{1,0:T(8,128)S(1)} %get-tuple-element.104), channel_id=1, source_target_pairs={{0,2},{2,0},{4,6},{6,4},{8,10},{10,8},{12,14},{14,12},{16,18},{18,... | collective-permute-start | bytes 3145736 | tf_op jit(solution)/shard_map/ppermute | solution.py:272
  55.1 12.7 %collective-permute-start.7 = (f32[256,1024]{1,0:T(8,128)S(1)}, f32[256,1024]{1,0:T(8,128)S(1)}, u32[]{:S(2)}, u32[]{:S(2)}) collective-permute-start(f32[256,1024]{1,0:T(8,128)S(1)} %get-tuple-element.107), channel_id=1, source_target_pairs={{0,2},{2,0},{4,6},{6,4},{8,10},{10,8},{12,14},{14,12},{16,18},{18,... | collective-permute-start | bytes 3145736 | tf_op jit(solution)/shard_map/ppermute | solution.py:272
  55.6 12.2 %collective-permute-start.8 = (f32[256,1024]{1,0:T(8,128)S(1)}, f32[256,1024]{1,0:T(8,128)S(1)}, u32[]{:S(2)}, u32[]{:S(2)}) collective-permute-start(f32[256,1024]{1,0:T(8,128)S(1)} %get-tuple-element.108), channel_id=1, source_target_pairs={{0,2},{2,0},{4,6},{6,4},{8,10},{10,8},{12,14},{14,12},{16,18},{18,... | collective-permute-start | bytes 3145736 | tf_op jit(solution)/shard_map/ppermute | solution.py:272
  55.6 12.1 %collective-permute-start.9 = (f32[256,1024]{1,0:T(8,128)S(1)}, f32[256,1024]{1,0:T(8,128)S(1)}, u32[]{:S(2)}, u32[]{:S(2)}) collective-permute-start(f32[256,1024]{1,0:T(8,128)S(1)} %get-tuple-element.109), channel_id=1, source_target_pairs={{0,2},{2,0},{4,6},{6,4},{8,10},{10,8},{12,14},{14,12},{16,18},{18,... | collective-permute-start | bytes 3145736 | tf_op jit(solution)/shard_map/ppermute | solution.py:272
  64.1 26.4 %collective-permute-start.11 = (f32[256,1024]{1,0:T(8,128)}, f32[256,1024]{1,0:T(8,128)}, u32[]{:S(2)}, u32[]{:S(2)}) collective-permute-start(f32[256,1024]{1,0:T(8,128)} %get-tuple-element.123), channel_id=1, source_target_pairs={{0,4},{2,6},{4,0},{6,2},{8,12},{10,14},{12,8},{14,10},{16,20},{18,... | collective-permute-start | bytes 3145736 | tf_op jit(solution)/shard_map/ppermute | solution.py:285
  66.9 20.0 %collective-permute-start.5 = (f32[128,1024]{1,0:T(8,128)}, f32[128,1024]{1,0:T(8,128)}, u32[]{:S(2)}, u32[]{:S(2)}) collective-permute-start(f32[128,1024]{1,0:T(8,128)} %get-tuple-element.169), channel_id=1, source_target_pairs={{0,8},{2,10},{4,12},{6,14},{8,0},{10,2},{12,4},{14,6},{16,24},{18,... | collective-permute-start | bytes 1572872 | tf_op jit(solution)/shard_map/ppermute | solution.py:285
  84.9 28.1 %collective-permute-start.13 = (f32[256,1024]{1,0:T(8,128)}, f32[256,1024]{1,0:T(8,128)}, u32[]{:S(2)}, u32[]{:S(2)}) collective-permute-start(f32[256,1024]{1,0:T(8,128)} %get-tuple-element.130), channel_id=1, source_target_pairs={{0,4},{2,6},{4,0},{6,2},{8,12},{10,14},{12,8},{14,10},{16,20},{18,... | collective-permute-start | bytes 3145736 | tf_op jit(solution)/shard_map/ppermute | solution.py:285
  84.9 39.2 %collective-permute-start.15 = (f32[256,512]{1,0:T(8,128)}, f32[256,512]{1,0:T(8,128)S(1)}, u32[]{:S(2)}, u32[]{:S(2)}) collective-permute-start(f32[256,512]{1,0:T(8,128)} %copy-done.3), channel_id=1, source_target_pairs={{0,4},{2,6},{4,0},{6,2},{8,12},{10,14},{12,8},{14,10},{16,20},{18,... | collective-permute-start | bytes 1572872 | tf_op jit(solution)/shard_map/ppermute | solution.py:285
  88.1 12.2 %collective-permute-start.10 = (f32[64,1024]{1,0:T(8,128)S(1)}, f32[64,1024]{1,0:T(8,128)S(1)}, u32[]{:S(2)}, u32[]{:S(2)}) collective-permute-start(f32[64,1024]{1,0:T(8,128)S(1)} %get-tuple-element.179), channel_id=1, source_target_pairs={{0,16},{2,18},{4,20},{6,22},{8,24},{10,26},{12,28},{14,30},{16,0},... | collective-permute-start | bytes 786440 | tf_op jit(solution)/shard_map/ppermute | solution.py:285
  91.8 22.5 %collective-permute-start.12 = (f32[128,1024]{1,0:T(8,128)S(1)}, f32[128,1024]{1,0:T(8,128)S(1)}, u32[]{:S(2)}, u32[]{:S(2)}) collective-permute-start(f32[128,1024]{1,0:T(8,128)S(1)} %get-tuple-element.167), channel_id=1, source_target_pairs={{0,8},{2,10},{4,12},{6,14},{8,0},{10,2},{12,4},{14,6},{16,24},{18,... | collective-permute-start | bytes 1572872 | tf_op jit(solution)/shard_map/ppermute | solution.py:285
  114.4 12.2 %collective-permute-start.14 = (f32[64,1024]{1,0:T(8,128)S(1)}, f32[64,1024]{1,0:T(8,128)S(1)}, u32[]{:S(2)}, u32[]{:S(2)}) collective-permute-start(f32[64,1024]{1,0:T(8,128)S(1)} %get-tuple-element.177), channel_id=1, source_target_pairs={{0,16},{2,18},{4,20},{6,22},{8,24},{10,26},{12,28},{14,30},{16,0},... | collective-permute-start | bytes 786440 | tf_op jit(solution)/shard_map/ppermute | solution.py:285
  115.6 24.8 %collective-permute-start.20 = (f32[256,512]{1,0:T(8,128)}, f32[256,512]{1,0:T(8,128)S(1)}, u32[]{:S(2)}, u32[]{:S(2)}) collective-permute-start(f32[256,512]{1,0:T(8,128)} %copy-done.2), channel_id=1, source_target_pairs={{0,4},{2,6},{4,0},{6,2},{8,12},{10,14},{12,8},{14,10},{16,20},{18,... | collective-permute-start | bytes 1572872 | tf_op jit(solution)/shard_map/ppermute | solution.py:285
  117.1 9.0 %collective-permute-start.16 = (f32[64,512]{1,0:T(8,128)S(1)}, f32[64,512]{1,0:T(8,128)S(1)}, u32[]{:S(2)}, u32[]{:S(2)}) collective-permute-start(f32[64,512]{1,0:T(8,128)S(1)} %get-tuple-element.195), channel_id=1, source_target_pairs={{0,1},{1,0},{2,3},{3,2},{4,5},{5,4},{6,7},{7,6},{8,9},{9,8},{10,11... | collective-permute-start | bytes 393224 | tf_op jit(solution)/shard_map/ppermute | solution.py:313
  122.2 18.0 %collective-permute-start.17 = (f32[128,1024]{1,0:T(8,128)S(1)}, f32[128,1024]{1,0:T(8,128)S(1)}, u32[]{:S(2)}, u32[]{:S(2)}) collective-permute-start(f32[128,1024]{1,0:T(8,128)S(1)} %get-tuple-element.165), channel_id=1, source_target_pairs={{0,8},{2,10},{4,12},{6,14},{8,0},{10,2},{12,4},{14,6},{16,24},{18,... | collective-permute-start | bytes 1572872 | tf_op jit(solution)/shard_map/ppermute | solution.py:285
  124.1 19.5 %collective-permute-start.19 = (f32[128,512]{1,0:T(8,128)S(1)}, f32[128,512]{1,0:T(8,128)S(1)}, u32[]{:S(2)}, u32[]{:S(2)}) collective-permute-start(f32[128,512]{1,0:T(8,128)S(1)} %get-tuple-element.173), channel_id=1, source_target_pairs={{0,8},{2,10},{4,12},{6,14},{8,0},{10,2},{12,4},{14,6},{16,24},{18,... | collective-permute-start | bytes 786440 | tf_op jit(solution)/shard_map/ppermute | solution.py:285
  126.7 17.0 %collective-permute-start.21 = (f32[64,512]{1,0:T(8,128)S(1)}, f32[64,512]{1,0:T(8,128)S(1)}, u32[]{:S(2)}, u32[]{:S(2)}) collective-permute-start(f32[64,512]{1,0:T(8,128)S(1)} %get-tuple-element.191), channel_id=1, source_target_pairs={{0,1},{1,0},{2,3},{3,2},{4,5},{5,4},{6,7},{7,6},{8,9},{9,8},{10,11... | collective-permute-start | bytes 393224 | tf_op jit(solution)/shard_map/ppermute | solution.py:313
  140.3 12.9 %collective-permute-start.18 = (f32[64,1024]{1,0:T(8,128)S(1)}, f32[64,1024]{1,0:T(8,128)S(1)}, u32[]{:S(2)}, u32[]{:S(2)}) collective-permute-start(f32[64,1024]{1,0:T(8,128)S(1)} %get-tuple-element.175), channel_id=1, source_target_pairs={{0,16},{2,18},{4,20},{6,22},{8,24},{10,26},{12,28},{14,30},{16,0},... | collective-permute-start | bytes 786440 | tf_op jit(solution)/shard_map/ppermute | solution.py:285
  143.7 14.0 %collective-permute-start.22 = (f32[64,512]{1,0:T(8,128)S(1)}, f32[64,512]{1,0:T(8,128)S(1)}, u32[]{:S(2)}, u32[]{:S(2)}) collective-permute-start(f32[64,512]{1,0:T(8,128)S(1)} %get-tuple-element.183), channel_id=1, source_target_pairs={{0,16},{2,18},{4,20},{6,22},{8,24},{10,26},{12,28},{14,30},{16,0},... | collective-permute-start | bytes 393224 | tf_op jit(solution)/shard_map/ppermute | solution.py:285
  146.6 11.0 %collective-permute-start.23 = (f32[128,512]{1,0:T(8,128)S(1)}, f32[128,512]{1,0:T(8,128)S(1)}, u32[]{:S(2)}, u32[]{:S(2)}) collective-permute-start(f32[128,512]{1,0:T(8,128)S(1)} %get-tuple-element.171), channel_id=1, source_target_pairs={{0,8},{2,10},{4,12},{6,14},{8,0},{10,2},{12,4},{14,6},{16,24},{18,... | collective-permute-start | bytes 786440 | tf_op jit(solution)/shard_map/ppermute | solution.py:285
  157.7 6.4 %collective-permute-start.25 = (f32[64,512]{1,0:T(8,128)S(1)}, f32[64,512]{1,0:T(8,128)S(1)}, u32[]{:S(2)}, u32[]{:S(2)}) collective-permute-start(f32[64,512]{1,0:T(8,128)S(1)} %get-tuple-element.181), channel_id=1, source_target_pairs={{0,16},{2,18},{4,20},{6,22},{8,24},{10,26},{12,28},{14,30},{16,0},... | collective-permute-start | bytes 393224 | tf_op jit(solution)/shard_map/ppermute | solution.py:285
  164.2 5.0 %collective-permute-start.26 = (f32[64,512]{1,0:T(8,128)S(1)}, f32[64,512]{1,0:T(8,128)S(1)}, u32[]{:S(2)}, u32[]{:S(2)}) collective-permute-start(f32[64,512]{1,0:T(8,128)S(1)} %get-tuple-element.185), channel_id=1, source_target_pairs={{0,1},{1,0},{2,3},{3,2},{4,5},{5,4},{6,7},{7,6},{8,9},{9,8},{10,11... | collective-permute-start | bytes 393224 | tf_op jit(solution)/shard_map/ppermute | solution.py:313
  (7 other events, 181.8 us)

commit v6 on v5

--- a/solution.py
+++ b/solution.py
@@ -12,7 +12,7 @@
 LANES = 128
 TILE = 256
 PIECES = 2
-VMEM_BYTES = 40 * 1024 * 1024
+VMEM_BYTES = 44 * 1024 * 1024
 F32 = jnp.float32
 BF16 = jnp.bfloat16
 
@@ -42,11 +42,11 @@
     used = high_ref.shape[0]
     cols, depth = high_ref.shape[-2:]
     tiles = depth // LANES
-    blocks = b_ref.shape[3] // tiles
+    blocks = b_ref.shape[2] // tiles
     lane = lax.broadcasted_iota(jnp.int32, (1, LANES), 1)
     for h in range(used):
         rows = pl.ds(first + h, tiles, stride=blocks) if blocks > 1 else slice(None)
-        turned = jnp.swapaxes(b_ref[group, 0, :, rows, :], 0, 1)
+        turned = jnp.swapaxes(b_ref[group, :, rows, :], 0, 1)
         for t in range(tiles):
             value = jnp.where(lane < limit[first + h] - t * LANES, turned[t], F32(0.0))
             high, low = split(value)
@@ -60,125 +60,143 @@
     return x * OUTER + z
 
 
-def halves_put(total, outs, inner, cols, outer_first):
-    groups = total.shape[0] // cols
-    for x in range(inner):
-        for z in range(groups // inner):
-            row = (x * OUTER + z) * cols
-            place = z * inner + x if outer_first else x * OUTER + z
-            at = place % (groups // 2) * cols
-            outs[place // (groups // 2)][at:at + cols, :] = total[row:row + cols]
-
-
-def joined(refs):
-    return jnp.concatenate([ref[...] for ref in refs], axis=0)
-
-
 def dot3(left_high, left_low, a_ref):
-    high, low = split(a_ref[0])
+    high, low = split(a_ref[...])
     dot = functools.partial(jnp.dot, preferred_element_type=F32)
     return dot(left_high, high) + (dot(left_high, low) + dot(left_low, high))
 
 
-def products_kernel(first, inner, step, chunks, pieces, adds, place, limit, rows_live, b_ref, a_ref, *refs):
-    received, outs, (high_ref, low_ref) = refs[:adds], refs[adds:-2], refs[-2:]
-    tile = a_ref.shape[2]
+def products_kernel(first, inner, chunks, adds, place, limit, rows_live, b_hbm, a_hbm, *refs):
+    received, (*outs, b_buf, a_buf, sums, high_ref, low_ref, b_sem, a_sem, in_sem, out_sem) = (
+        refs[:adds], refs[adds:]
+    )
     groups, cols, depth = high_ref.shape[1:]
-    loads = groups // step
-    now = pl.program_id(0)
-
-    @pl.when(now < loads)
-    def _():
-        for i in range(step):
-            group = now * step + i
-            put_split(i, limit, first, b_ref, high_ref, low_ref, (slot(group, place, inner),))
-
-    at = loads
-    for h, start, count, outer_first in chunks:
-        size = count // tile
-        mine = (now >= at) & (now < at + size)
-        live = start + (now - at) * tile < rows_live[h]
-        got = received[(h - first) * pieces:(h - first + 1) * pieces]
-        out, outs = outs[:2 if adds else pieces], outs[2 if adds else pieces:]
-
-        def put(total):
-            if adds:
-                halves_put(total, out, inner, cols, outer_first)
-                return
-            part = total.shape[0] // pieces
-            for i, ref in enumerate(out):
-                ref[...] = total[i * part:(i + 1) * part]
-
-        @pl.when(mine & live)
-        def _():
-            left = (r[h - first].reshape(groups * cols, depth) for r in (high_ref, low_ref))
-            total = dot3(*left, a_ref)
-            put(total + joined(got) if adds else total)
-
-        @pl.when(mine & jnp.logical_not(live))
-        def _():
-            put(joined(got) if adds else jnp.zeros((groups * cols, tile), F32))
-
-        at += size
-
-
-def products(place, limit, rows_live, parts_of_b, amplitudes, chunks, shift, inner, received):
+    tile = a_buf.shape[2]
+    height = groups * cols
+    per_chunk = 2 if adds else PIECES
+    side = lax.rem(place[2] + (0 if adds else 1), CORES)
+    tiles = []
+    at = 0
+    for i, (h, start, count, outer_first) in enumerate(chunks):
+        tiles.append((at, count // tile, h, start, outer_first, outs[i * per_chunk:(i + 1) * per_chunk]))
+        at += count // tile
+
+    def columns(n, start=0):
+        return pl.ds(pl.multiple_of(start + n * tile, tile), tile)
+
+    def load_b(g):
+        return pltpu.make_async_copy(b_hbm.at[g, side], b_buf.at[g], b_sem.at[g])
+
+    def load_a(at, n, h, start):
+        return pltpu.make_async_copy(
+            a_hbm.at[h, :, columns(n, start)], a_buf.at[at + n], a_sem.at[at + n]
+        )
+
+    def loads(at, n, h, start):
+        part = height // PIECES
+        return [pltpu.make_async_copy(
+            received[(h - first) * PIECES + i].at[:, columns(n, start)],
+            sums.at[at + n, pl.ds(i * part, part)], in_sem.at[at + n, i],
+        ) for i in range(PIECES if adds else 0)]
+
+    def stores(at, n, outer_first, out):
+        copies = []
+        part = height // len(out)
+        pieces = groups if outer_first else len(out)
+        for i in range(pieces):
+            if outer_first:
+                x, z = i // OUTER, i % OUTER
+                to, row = divmod((z * inner + x) * cols, part)
+            else:
+                to, row = i, 0
+            size = height // pieces
+            copies.append(pltpu.make_async_copy(
+                sums.at[at + n, pl.ds(i * size, size)],
+                out[to].at[pl.ds(row, size), columns(n)], out_sem.at[at + n, i],
+            ))
+        return copies
+
+    def live(n, h, start):
+        return start + n * tile < rows_live[h]
+
+    for g in range(groups):
+        load_b(g).start()
+    for at, count, h, start, _, _ in tiles:
+        @pl.loop(0, count)
+        def _(n):
+            @pl.when(live(n, h, start))
+            def _():
+                load_a(at, n, h, start).start()
+            for copy in loads(at, n, h, start):
+                copy.start()
+
+    @pl.loop(0, groups)
+    def _(g):
+        load_b(g).wait()
+        put_split(g, limit, first, b_buf, high_ref, low_ref, (slot(g, place, inner),))
+
+    for at, count, h, start, outer_first, out in tiles:
+        @pl.loop(0, count)
+        def _(n):
+            for copy in loads(at, n, h, start):
+                copy.wait()
+
+            @pl.when(live(n, h, start))
+            def _():
+                load_a(at, n, h, start).wait()
+                left = (r[h - first].reshape(height, depth) for r in (high_ref, low_ref))
+                total = dot3(*left, a_buf.at[at + n])
+                sums[at + n] = sums[at + n] + total if adds else total
+
+            if not adds:
+                @pl.when(jnp.logical_not(live(n, h, start)))
+                def _():
+                    sums[at + n] = jnp.zeros((height, tile), F32)
+
+            for copy in stores(at, n, outer_first, out):
+                copy.start()
+
+    for at, count, _, _, outer_first, out in tiles:
+        @pl.loop(0, count)
+        def _(n):
+            for copy in stores(at, n, outer_first, out):
+                copy.wait()
+
+
+def products(place, limit, rows_live, parts_of_b, amplitudes, chunks, inner, received):
     groups, _, cols, rows_b, _ = parts_of_b.shape
     blocks, depth, rows = amplitudes.shape
     tile = min(rows, TILE)
-    step = min(groups, 2)
-    loads = groups // step
     first, last = chunks[0][0], chunks[-1][0]
-    sizes = [chunk[2] // tile for chunk in chunks]
-    offset = chunks[0][1] // tile
-    total = sum(sizes)
-    per_block = rows // tile
+    total = sum(chunk[2] for chunk in chunks) // tile
     height = groups * cols
-    adds = bool(received)
-
-    def b_map(n, place, *_):
-        return (jnp.minimum(n, loads - 1), lax.rem(place[2] + shift, CORES), 0, 0, 0)
-
-    def a_map(n, *_):
-        t = jnp.maximum(n - loads, 0) + offset
-        return (first + t // per_block, 0, t % per_block)
-
-    def tiles_of(counts):
-        result, at = [], 0
-        for size, count in zip(sizes, counts):
-            result += [pl.BlockSpec(
-                (height // count, tile),
-                lambda n, *_, at=at, size=size: (0, jnp.clip(n - loads - at, 0, size - 1)),
-            )] * count
-            at += size
-        return result
-
-    counts = [2 if adds else PIECES] * len(chunks)
-    got_specs = []
-    for h in range(first, last + 1) if adds else []:
-        mine = [i for i, chunk in enumerate(chunks) if chunk[0] == h]
-        at, size = sum(sizes[:mine[0]]), sum(sizes[i] for i in mine)
-        begin = chunks[mine[0]][1] // tile
-        got_specs += [pl.BlockSpec(
-            (height // PIECES, tile),
-            lambda n, *_, at=at, size=size, begin=begin: (0, begin + jnp.clip(n - loads - at, 0, size - 1)),
-        )] * PIECES
+    count = 2 if received else PIECES
+    anywhere = pl.BlockSpec(memory_space=pl.ANY)
     part = pltpu.VMEM((last - first + 1, groups, cols, depth), BF16)
     return pl.pallas_call(
-        functools.partial(products_kernel, first, inner, step, chunks, PIECES, len(received)),
+        functools.partial(products_kernel, first, inner, chunks, len(received)),
         grid_spec=pltpu.PrefetchScalarGridSpec(
             num_scalar_prefetch=3,
-            grid=(loads + total,),
-            in_specs=[pl.BlockSpec((step, 1, cols, rows_b, LANES), b_map),
-                      pl.BlockSpec((1, depth, tile), a_map)] + got_specs,
-            out_specs=tiles_of(counts),
-            scratch_shapes=[part, part],
+            grid=(),
+            in_specs=[anywhere] * (2 + len(received)),
+            out_specs=[anywhere] * (count * len(chunks)),
+            scratch_shapes=[
+                pltpu.VMEM((groups, cols, rows_b, LANES), F32),
+                pltpu.VMEM((total, depth, tile), F32),
+                pltpu.VMEM((total, height, tile), F32),
+                part,
+                part,
+                pltpu.SemaphoreType.DMA((groups,)),
+                pltpu.SemaphoreType.DMA((total,)),
+                pltpu.SemaphoreType.DMA((total, PIECES)),
+                pltpu.SemaphoreType.DMA((total, groups)),
+            ],
         ),
         out_shape=[jax.ShapeDtypeStruct((height // count, chunk[2]), F32)
-                   for chunk, count in zip(chunks, counts) for _ in range(count)],
+                   for chunk in chunks for _ in range(count)],
         cost_estimate=cost(),
         compiler_params=params(),
-        name="second_halves" if adds else "first_halves",
+        name="second_halves" if received else "first_halves",
     )(place, limit, rows_live, parts_of_b, amplitudes, *received)
 
 
@@ -260,21 +278,21 @@
     chain = Chain()
     received, split_in, totals, gens = {}, {}, {}, {}
 
-    def run_products(chunks, shift, *got):
+    def run_products(chunks, *got):
         return chain.run(
-            lambda p, l, r, b, a, *g: products(p, l, r, b, a, chunks, shift, inner, g),
+            lambda p, l, r, b, a, *g: products(p, l, r, b, a, chunks, inner, g),
             place, pairs_here, rows_here, parts_of_b, amplitudes, *got,
         )
 
     def first_halves(names):
-        sent = run_products([(h, 0, rows, False) for h in names], 1)
+        sent = run_products([(h, 0, rows, False) for h in names])
         for i, h in enumerate(names):
             received[h] = [lax.ppermute(part, "tensor", across)
                            for part in sent[i * PIECES:(i + 1) * PIECES]]
 
     def second_halves(names):
         got = [part for h in sorted({chunks[i][0] for i in names}) for part in received[h]]
-        outs = run_products([chunks[i] for i in names], 0, *got)
+        outs = run_products([chunks[i] for i in names], *got)
         for at, i in enumerate(names):
             gens[i] = work(*chunks[i], *outs[2 * at:2 * at + 2])
 
@@ -315,10 +333,10 @@
     if inner == 2 and rep == 2 and blocks == 4:
         half = rows // 2
         chunks = [(0, 0, rows, False), (1, 0, rows, False), (2, 0, rows, False),
-                  (3, 0, half, False), (3, half, half, False)]
+                  (3, 0, half, True), (3, half, half, False)]
         firsts = {"p": [0, 1], "q": [2, 3]}
-        seconds = {"w": [0, 1], "z": [2, 3, 4]}
-        plan = "pwq0z01a213Ab24B3c4Cd"
+        seconds = {"w": [0], "x": [1], "z": [2, 3, 4]}
+        plan = "pwxq0z013a132A42bB4cCd"
     else:
         chunks = [(h, 0, rows, False) for h in range(blocks)]
         firsts = {"p": list(range(blocks))}

time: 172 us -> 159 us (0.924)
  Pallas kernels: 61.3 us -> 56 us
  starting transfers between devices: 32.1 us -> 29 us
    pallas_call x4 -> x5, Pallas kernels: 59.5 us -> 54.1 us  [products(): pl.pallas_call(functools.partial(products_kernel, first, inner, chunks, l...]
    ppermute x4, starting transfers between devices: 10.3 us -> 6.58 us  [exchange(): other[h] = lax.ppermute(away, 'rep', [(0, 1), (1, 0)])]
    ppermute x4, waiting for transfers between devices: 7.83 us -> 11.1 us  [exchange(): other[h] = lax.ppermute(away, 'rep', [(0, 1), (1, 0)])]
    ppermute x8, waiting for transfers between devices: 6.2 us -> 3.77 us  [first_halves(): lax.ppermute(part, 'tensor', across)]
    ppermute x15, waiting for transfers between devices: 55.2 us -> 53.2 us  [work(): got = lax.ppermute(send, 'tensor', pairs)]
  transfers between devices with their start and end apart: 27 -> 27, of which waited for: 17 -> 14; matrix products, arithmetic and copies ran while one was open for 3% -> 3% of each run, Pallas kernels for 17% -> 26%
where the time goes in v6:
time: 159 us
  waiting for transfers between devices  68 us (43%)
  Pallas kernels  56 us (35%)
  starting transfers between devices  29 us (18%)
  other arithmetic  5.22 us (3%)
    pallas_call x5, Pallas kernels, products(): pl.pallas_call(functools.partial(products_kernel, first, inner, chunks, l...  54.1 us
    ppermute x15, waiting for transfers between devices, work(): got = lax.ppermute(send, 'tensor', pairs)  53.2 us
    ppermute x15, starting transfers between devices, work(): got = lax.ppermute(send, 'tensor', pairs)  20.3 us
    ppermute x4, waiting for transfers between devices, exchange(): other[h] = lax.ppermute(away, 'rep', [(0, 1), (1, 0)])  11.1 us
    ppermute x4, starting transfers between devices, exchange(): other[h] = lax.ppermute(away, 'rep', [(0, 1), (1, 0)])  6.58 us
    add x10, other arithmetic, work(): a[half:] + b[half:]  4.08 us
    ppermute x8, waiting for transfers between devices, first_halves(): lax.ppermute(part, 'tensor', across)  3.77 us
  transfers between devices with their start and end apart: 27, of which 14 were waited for; matrix products, arithmetic and copies ran while one was open for 3% of the time, Pallas kernels for 26%

profile of v6, /device:TPU:0, one launch (start us, length us, event | category | flops | bytes accessed | tf_op | source)
XLA Modules:
  0.0 158.5 jit_solution(4885426814346447730)
XLA Ops:
  0.8 12.6 %first_halves.2 = (f32[256,1024]{1,0:T(8,128)S(1)}, f32[256,1024]{1,0:T(8,128)S(1)}, f32[256,1024]{1,0:T(8,128)S(1)}, f32[256,1024]{1,0:T(8,128)S(1)}) custom-call(s32[3]{0:T(128)S(1)} %pad_add_fusion.1.place, s32[4]{0:T(128)S(1)} %get-tuple-element.122.limit, s32[4]{0:T(128)S(1)} %get-tuple-element.123.rows_live, f32[8,2,64,32,128]{4,3,2,1,0:T(8,128)} %bitcast.11, ...), custom_call_target="tpu_custom_call" | custom-call | flops 1024 | bytes 1024 | tf_op jit(solution)/shard_map/first_halves/pallas_call | solution.py:176
  14.5 1.7 %collective-permute-done.refs_0_ = f32[256,1024]{1,0:T(8,128)S(1)} collective-permute-done((f32[256,1024]{1,0:T(8,128)S(1)}, f32[256,1024]{1,0:T(8,128)S(1)}, u32[]{:S(2)}, u32[]{:S(2)}) %collective-permute-start) | collective-permute-done | bytes 1048608 | tf_op jit(solution)/shard_map/ppermute | solution.py:290
  17.7 8.9 %second_halves.3 = (f32[256,1024]{1,0:T(8,128)S(1)}, f32[256,1024]{1,0:T(8,128)S(1)}) custom-call(s32[3]{0:T(128)S(1)} %pad_add_fusion.1.place, s32[4]{0:T(128)S(1)} %get-tuple-element.122.limit, s32[4]{0:T(128)S(1)} %get-tuple-element.123.rows_live, f32[8,2,64,32,128]{4,3,2,1,0:T(8,128)} %bitcast.12, f32[4,1024,1024]{2,1,0:T(8,128)} %a_hbm.5, ...), custom_call_target="tpu_custom_call" | custom-call | flops 1024 | bytes 1024 | tf_op jit(solution)/shard_map/second_halves/pallas_call | solution.py:176
  26.6 2.9 %collective-permute-start.2 = (f32[256,1024]{1,0:T(8,128)S(1)}, f32[256,1024]{1,0:T(8,128)S(1)}, u32[]{:S(2)}, u32[]{:S(2)}) collective-permute-start(f32[256,1024]{1,0:T(8,128)S(1)} %get-tuple-element.99), channel_id=1, source_target_pairs={{0,4},{2,6},{4,0},{6,2},{8,12},{10,14},{12,8},{14,10},{16,20},{18,... | collective-permute-start | bytes 3145736 | tf_op jit(solution)/shard_map/ppermute | solution.py:303
  29.5 8.6 %second_halves.4 = (f32[256,1024]{1,0:T(8,128)S(1)}, f32[256,1024]{1,0:T(8,128)}) custom-call(s32[3]{0:T(128)S(1)} %pad_add_fusion.1.place, s32[4]{0:T(128)S(1)} %get-tuple-element.122.limit, s32[4]{0:T(128)S(1)} %get-tuple-element.123.rows_live, f32[8,2,64,32,128]{4,3,2,1,0:T(8,128)} %bitcast.13, f32[4,1024,1024]{2,1,0:T(8,128)} %a_hbm.5, ...), custom_call_target="tpu_custom_call" | custom-call | flops 1024 | bytes 1024 | tf_op jit(solution)/shard_map/second_halves/pallas_call | solution.py:176
  38.1 12.3 %first_halves.3 = (f32[256,1024]{1,0:T(8,128)S(1)}, f32[256,1024]{1,0:T(8,128)}, f32[256,1024]{1,0:T(8,128)}, f32[256,1024]{1,0:T(8,128)}) custom-call(s32[3]{0:T(128)S(1)} %pad_add_fusion.1.place, s32[4]{0:T(128)S(1)} %get-tuple-element.122.limit, s32[4]{0:T(128)S(1)} %get-tuple-element.123.rows_live, f32[8,2,64,32,128]{4,3,2,1,0:T(8,128)} %bitcast.14, ...), custom_call_target="tpu_custom_call" | custom-call | flops 1024 | bytes 1024 | tf_op jit(solution)/shard_map/first_halves/pallas_call | solution.py:176
  53.0 1.7 %collective-permute-start.12 = (f32[256,1024]{1,0:T(8,128)}, f32[256,1024]{1,0:T(8,128)}, u32[]{:S(2)}, u32[]{:S(2)}) collective-permute-start(f32[256,1024]{1,0:T(8,128)} %get-tuple-element.135), channel_id=1, source_target_pairs={{0,4},{2,6},{4,0},{6,2},{8,12},{10,14},{12,8},{14,10},{16,20},{18,... | collective-permute-start | bytes 3145736 | tf_op jit(solution)/shard_map/ppermute | solution.py:303
  55.8 1.6 collective-permute-start.5
  58.0 11.8 %second_halves.5 = (f32[256,1024]{1,0:T(8,128)S(1)}, f32[256,1024]{1,0:T(8,128)S(1)}, f32[256,512]{1,0:T(8,128)S(1)}, f32[256,512]{1,0:T(8,128)S(1)}, f32[256,512]{1,0:T(8,128)S(1)}, /*index=5*/f32[256,512]{1,0:T(8,128)S(1)}) custom-call(s32[3]{0:T(128)S(1)} %pad_add_fusion.1.place, s32[4]{0:T(128)S(1)} %get-tuple-element.122.limit, ...), custom_call_target="tpu_custom_call" | custom-call | flops 1024 | bytes 1024 | tf_op jit(solution)/shard_map/second_halves/pallas_call | solution.py:176
  69.8 1.6 %collective-permute-start.11 = (f32[256,512]{1,0:T(8,128)S(1)}, f32[256,512]{1,0:T(8,128)S(1)}, u32[]{:S(2)}, u32[]{:S(2)}) collective-permute-start(f32[256,512]{1,0:T(8,128)S(1)} %get-tuple-element.134), channel_id=1, source_target_pairs={{0,8},{2,10},{4,12},{6,14},{8,0},{10,2},{12,4},{14,6},{16,24},{18,... | collective-permute-start | bytes 1572872 | tf_op jit(solution)/shard_map/ppermute | solution.py:303
  75.8 3.6 %collective-permute-done.12 = f32[256,1024]{1,0:T(8,128)} collective-permute-done((f32[256,1024]{1,0:T(8,128)}, f32[256,1024]{1,0:T(8,128)}, u32[]{:S(2)}, u32[]{:S(2)}) %collective-permute-start.12) | collective-permute-done | bytes 1048608 | tf_op jit(solution)/shard_map/ppermute | solution.py:303
  80.7 8.8 %collective-permute-done.11 = f32[256,512]{1,0:T(8,128)S(1)} collective-permute-done((f32[256,512]{1,0:T(8,128)S(1)}, f32[256,512]{1,0:T(8,128)S(1)}, u32[]{:S(2)}, u32[]{:S(2)}) %collective-permute-start.11) | collective-permute-done | bytes 524320 | tf_op jit(solution)/shard_map/ppermute | solution.py:303
  89.6 2.9 %collective-permute-start.16 = (f32[128,512]{1,0:T(8,128)S(1)}, f32[128,512]{1,0:T(8,128)S(1)}, u32[]{:S(2)}, u32[]{:S(2)}) collective-permute-start(f32[128,512]{1,0:T(8,128)S(1)} %get-tuple-element.185), channel_id=1, source_target_pairs={{0,16},{2,18},{4,20},{6,22},{8,24},{10,26},{12,28},{14,30},{16,0},... | collective-permute-start | bytes 786440 | tf_op jit(solution)/shard_map/ppermute | solution.py:303
  92.6 15.6 %collective-permute-done.13 = f32[128,1024]{1,0:T(8,128)S(1)} collective-permute-done((f32[128,1024]{1,0:T(8,128)S(1)}, f32[128,1024]{1,0:T(8,128)S(1)}, u32[]{:S(2)}, u32[]{:S(2)}) %collective-permute-start.13) | collective-permute-done | bytes 524320 | tf_op jit(solution)/shard_map/ppermute | solution.py:303
  110.0 2.0 %collective-permute-start.19 = (f32[64,512]{1,0:T(8,128)S(1)}, f32[64,512]{1,0:T(8,128)S(1)}, u32[]{:S(2)}, u32[]{:S(2)}) collective-permute-start(f32[64,512]{1,0:T(8,128)S(1)} %get-tuple-element.205), channel_id=1, source_target_pairs={{0,1},{1,0},{2,3},{3,2},{4,5},{5,4},{6,7},{7,6},{8,9},{9,8},{10,11... | collective-permute-start | bytes 393224 | tf_op jit(solution)/shard_map/ppermute | solution.py:331
  113.1 1.9 %collective-permute-done.19.refs_4_ = f32[64,512]{1,0:T(8,128)S(1)} collective-permute-done((f32[64,512]{1,0:T(8,128)S(1)}, f32[64,512]{1,0:T(8,128)S(1)}, u32[]{:S(2)}, u32[]{:S(2)}) %collective-permute-start.19) | collective-permute-done | bytes 131104 | tf_op jit(solution)/shard_map/ppermute | solution.py:331
  115.0 2.0 %collective-permute-start.21 = (f32[128,512]{1,0:T(8,128)S(1)}, f32[128,512]{1,0:T(8,128)S(1)}, u32[]{:S(2)}, u32[]{:S(2)}) collective-permute-start(f32[128,512]{1,0:T(8,128)S(1)} %get-tuple-element.181), channel_id=1, source_target_pairs={{0,8},{2,10},{4,12},{6,14},{8,0},{10,2},{12,4},{14,6},{16,24},{18,... | collective-permute-start | bytes 786440 | tf_op jit(solution)/shard_map/ppermute | solution.py:303
  117.0 12.1 %collective-permute-done.17 = f32[128,1024]{1,0:T(8,128)S(1)} collective-permute-done((f32[128,1024]{1,0:T(8,128)S(1)}, f32[128,1024]{1,0:T(8,128)S(1)}, u32[]{:S(2)}, u32[]{:S(2)}) %collective-permute-start.17) | collective-permute-done | bytes 524320 | tf_op jit(solution)/shard_map/ppermute | solution.py:303
  129.3 2.4 %collective-permute-start.22 = (f32[64,512]{1,0:T(8,128)S(1)}, f32[64,512]{1,0:T(8,128)S(1)}, u32[]{:S(2)}, u32[]{:S(2)}) collective-permute-start(f32[64,512]{1,0:T(8,128)S(1)} %get-tuple-element.201), channel_id=1, source_target_pairs={{0,1},{1,0},{2,3},{3,2},{4,5},{5,4},{6,7},{7,6},{8,9},{9,8},{10,11... | collective-permute-start | bytes 393224 | tf_op jit(solution)/shard_map/ppermute | solution.py:331
  131.7 1.7 %collective-permute-start.20 = (f32[64,1024]{1,0:T(8,128)S(1)}, f32[64,1024]{1,0:T(8,128)S(1)}, u32[]{:S(2)}, u32[]{:S(2)}) collective-permute-start(f32[64,1024]{1,0:T(8,128)S(1)} %get-tuple-element.183), channel_id=1, source_target_pairs={{0,16},{2,18},{4,20},{6,22},{8,24},{10,26},{12,28},{14,30},{16,0},... | collective-permute-start | bytes 786440 | tf_op jit(solution)/shard_map/ppermute | solution.py:303
  134.7 10.1 %collective-permute-done.20 = f32[64,1024]{1,0:T(8,128)S(1)} collective-permute-done((f32[64,1024]{1,0:T(8,128)S(1)}, f32[64,1024]{1,0:T(8,128)S(1)}, u32[]{:S(2)}, u32[]{:S(2)}) %collective-permute-start.20) | collective-permute-done | bytes 262176 | tf_op jit(solution)/shard_map/ppermute | solution.py:303
  145.8 4.4 %collective-permute-done.24.refs_6_ = f32[64,512]{1,0:T(8,128)S(1)} collective-permute-done((f32[64,512]{1,0:T(8,128)S(1)}, f32[64,512]{1,0:T(8,128)S(1)}, u32[]{:S(2)}, u32[]{:S(2)}) %collective-permute-start.24) | collective-permute-done | bytes 131104 | tf_op jit(solution)/shard_map/ppermute | solution.py:331
  153.0 3.7 %collective-permute-done.26.refs_7_ = f32[64,512]{1,0:T(8,128)S(1)} collective-permute-done((f32[64,512]{1,0:T(8,128)S(1)}, f32[64,512]{1,0:T(8,128)S(1)}, u32[]{:S(2)}, u32[]{:S(2)}) %collective-permute-start.26) | collective-permute-done | bytes 131104 | tf_op jit(solution)/shard_map/ppermute | solution.py:331
  156.7 1.8 %place_blocks.1 = f32[64,8,512]{2,1,0:T(8,128)} custom-call(s32[1]{0:T(128)} %bitcast.side_ref, s32[2]{0:T(128)S(1)} %pad_add_fusion.base, s32[8]{0:T(128)S(1)} %copy-done, s32[8]{0:T(128)S(1)} %copy-done.1, f32[64,512]{1,0:T(8,128)S(1)} %get-tuple-element.206.refs_0_, f32[64,512]{1,0:T(8,128)S(1)} %get-tuple-element.202.refs_1_, ...), custom_call_target="tpu_custom_call" | custom-call | flops 1024 | bytes 1024 | tf_op jit(solution)/shard_map/place_blocks/pallas_call | solution.py:225
  (67 shorter events, 21.6 us)
Async XLA Ops:
  14.0 15.5 %collective-permute-start.3 = (f32[256,1024]{1,0:T(8,128)S(1)}, f32[256,1024]{1,0:T(8,128)S(1)}, u32[]{:S(2)}, u32[]{:S(2)}) collective-permute-start(f32[256,1024]{1,0:T(8,128)S(1)} %get-tuple-element.100), channel_id=1, source_target_pairs={{0,2},{2,0},{4,6},{6,4},{8,10},{10,8},{12,14},{14,12},{16,18},{18,... | collective-permute-start | bytes 3145736 | tf_op jit(solution)/shard_map/ppermute | solution.py:290
  14.4 15.1 %collective-permute-start.4 = (f32[256,1024]{1,0:T(8,128)S(1)}, f32[256,1024]{1,0:T(8,128)S(1)}, u32[]{:S(2)}, u32[]{:S(2)}) collective-permute-start(f32[256,1024]{1,0:T(8,128)S(1)} %get-tuple-element.101), channel_id=1, source_target_pairs={{0,2},{2,0},{4,6},{6,4},{8,10},{10,8},{12,14},{14,12},{16,18},{18,... | collective-permute-start | bytes 3145736 | tf_op jit(solution)/shard_map/ppermute | solution.py:290
  26.6 26.4 %collective-permute-start.2 = (f32[256,1024]{1,0:T(8,128)S(1)}, f32[256,1024]{1,0:T(8,128)S(1)}, u32[]{:S(2)}, u32[]{:S(2)}) collective-permute-start(f32[256,1024]{1,0:T(8,128)S(1)} %get-tuple-element.99), channel_id=1, source_target_pairs={{0,4},{2,6},{4,0},{6,2},{8,12},{10,14},{12,8},{14,10},{16,20},{18,... | collective-permute-start | bytes 3145736 | tf_op jit(solution)/shard_map/ppermute | solution.py:303
  50.4 5.4 %collective-permute-start.6 = (f32[256,1024]{1,0:T(8,128)S(1)}, f32[256,1024]{1,0:T(8,128)S(1)}, u32[]{:S(2)}, u32[]{:S(2)}) collective-permute-start(f32[256,1024]{1,0:T(8,128)S(1)} %get-tuple-element.115), channel_id=1, source_target_pairs={{0,2},{2,0},{4,6},{6,4},{8,10},{10,8},{12,14},{14,12},{16,18},{18,... | collective-permute-start | bytes 3145736 | tf_op jit(solution)/shard_map/ppermute | solution.py:290
  50.5 6.9 %collective-permute-start.7 = (f32[256,1024]{1,0:T(8,128)}, f32[256,1024]{1,0:T(8,128)S(1)}, u32[]{:S(2)}, u32[]{:S(2)}) collective-permute-start(f32[256,1024]{1,0:T(8,128)} %get-tuple-element.118), channel_id=1, source_target_pairs={{0,2},{2,0},{4,6},{6,4},{8,10},{10,8},{12,14},{14,12},{16,18},{18,... | collective-permute-start | bytes 3145736 | tf_op jit(solution)/shard_map/ppermute | solution.py:290
  51.0 6.4 %collective-permute-start.8 = (f32[256,1024]{1,0:T(8,128)}, f32[256,1024]{1,0:T(8,128)}, u32[]{:S(2)}, u32[]{:S(2)}) collective-permute-start(f32[256,1024]{1,0:T(8,128)} %get-tuple-element.119), channel_id=1, source_target_pairs={{0,2},{2,0},{4,6},{6,4},{8,10},{10,8},{12,14},{14,12},{16,18},{18,... | collective-permute-start | bytes 3145736 | tf_op jit(solution)/shard_map/ppermute | solution.py:290
  51.1 6.9 %collective-permute-start.9 = (f32[256,1024]{1,0:T(8,128)}, f32[256,1024]{1,0:T(8,128)}, u32[]{:S(2)}, u32[]{:S(2)}) collective-permute-start(f32[256,1024]{1,0:T(8,128)} %get-tuple-element.120), channel_id=1, source_target_pairs={{0,2},{2,0},{4,6},{6,4},{8,10},{10,8},{12,14},{14,12},{16,18},{18,... | collective-permute-start | bytes 3145736 | tf_op jit(solution)/shard_map/ppermute | solution.py:290
  53.0 26.4 %collective-permute-start.12 = (f32[256,1024]{1,0:T(8,128)}, f32[256,1024]{1,0:T(8,128)}, u32[]{:S(2)}, u32[]{:S(2)}) collective-permute-start(f32[256,1024]{1,0:T(8,128)} %get-tuple-element.135), channel_id=1, source_target_pairs={{0,4},{2,6},{4,0},{6,2},{8,12},{10,14},{12,8},{14,10},{16,20},{18,... | collective-permute-start | bytes 3145736 | tf_op jit(solution)/shard_map/ppermute | solution.py:303
  55.8 17.7 %collective-permute-start.5 = (f32[128,1024]{1,0:T(8,128)}, f32[128,1024]{1,0:T(8,128)}, u32[]{:S(2)}, u32[]{:S(2)}) collective-permute-start(f32[128,1024]{1,0:T(8,128)} %get-tuple-element.179), channel_id=1, source_target_pairs={{0,8},{2,10},{4,12},{6,14},{8,0},{10,2},{12,4},{14,6},{16,24},{18,... | collective-permute-start | bytes 1572872 | tf_op jit(solution)/shard_map/ppermute | solution.py:303
  69.8 19.6 %collective-permute-start.11 = (f32[256,512]{1,0:T(8,128)S(1)}, f32[256,512]{1,0:T(8,128)S(1)}, u32[]{:S(2)}, u32[]{:S(2)}) collective-permute-start(f32[256,512]{1,0:T(8,128)S(1)} %get-tuple-element.134), channel_id=1, source_target_pairs={{0,8},{2,10},{4,12},{6,14},{8,0},{10,2},{12,4},{14,6},{16,24},{18,... | collective-permute-start | bytes 1572872 | tf_op jit(solution)/shard_map/ppermute | solution.py:303
  71.5 36.9 %collective-permute-start.15 = (f32[256,1024]{1,0:T(8,128)S(1)}, f32[256,1024]{1,0:T(8,128)S(1)}, u32[]{:S(2)}, u32[]{:S(2)}) collective-permute-start(f32[256,1024]{1,0:T(8,128)S(1)} %get-tuple-element.146), channel_id=1, source_target_pairs={{0,4},{2,6},{4,0},{6,2},{8,12},{10,14},{12,8},{14,10},{16,20},{18,... | collective-permute-start | bytes 3145736 | tf_op jit(solution)/shard_map/ppermute | solution.py:303
  72.0 41.1 %collective-permute-start.18 = (f32[256,512]{1,0:T(8,128)S(1)}, f32[256,512]{1,0:T(8,128)S(1)}, u32[]{:S(2)}, u32[]{:S(2)}) collective-permute-start(f32[256,512]{1,0:T(8,128)S(1)} %get-tuple-element.152), channel_id=1, source_target_pairs={{0,4},{2,6},{4,0},{6,2},{8,12},{10,14},{12,8},{14,10},{16,20},{18,... | collective-permute-start | bytes 1572872 | tf_op jit(solution)/shard_map/ppermute | solution.py:303
  74.6 17.9 %collective-permute-start.10 = (f32[64,1024]{1,0:T(8,128)S(1)}, f32[64,1024]{1,0:T(8,128)S(1)}, u32[]{:S(2)}, u32[]{:S(2)}) collective-permute-start(f32[64,1024]{1,0:T(8,128)S(1)} %get-tuple-element.189), channel_id=1, source_target_pairs={{0,16},{2,18},{4,20},{6,22},{8,24},{10,26},{12,28},{14,30},{16,0},... | collective-permute-start | bytes 786440 | tf_op jit(solution)/shard_map/ppermute | solution.py:303
  89.5 18.8 %collective-permute-start.13 = (f32[128,1024]{1,0:T(8,128)S(1)}, f32[128,1024]{1,0:T(8,128)S(1)}, u32[]{:S(2)}, u32[]{:S(2)}) collective-permute-start(f32[128,1024]{1,0:T(8,128)S(1)} %get-tuple-element.177), channel_id=1, source_target_pairs={{0,8},{2,10},{4,12},{6,14},{8,0},{10,2},{12,4},{14,6},{16,24},{18,... | collective-permute-start | bytes 1572872 | tf_op jit(solution)/shard_map/ppermute | solution.py:303
  89.6 18.7 %collective-permute-start.16 = (f32[128,512]{1,0:T(8,128)S(1)}, f32[128,512]{1,0:T(8,128)S(1)}, u32[]{:S(2)}, u32[]{:S(2)}) collective-permute-start(f32[128,512]{1,0:T(8,128)S(1)} %get-tuple-element.185), channel_id=1, source_target_pairs={{0,16},{2,18},{4,20},{6,22},{8,24},{10,26},{12,28},{14,30},{16,0},... | collective-permute-start | bytes 786440 | tf_op jit(solution)/shard_map/ppermute | solution.py:303
  108.6 20.5 %collective-permute-start.17 = (f32[128,1024]{1,0:T(8,128)S(1)}, f32[128,1024]{1,0:T(8,128)S(1)}, u32[]{:S(2)}, u32[]{:S(2)}) collective-permute-start(f32[128,1024]{1,0:T(8,128)S(1)} %get-tuple-element.175), channel_id=1, source_target_pairs={{0,8},{2,10},{4,12},{6,14},{8,0},{10,2},{12,4},{14,6},{16,24},{18,... | collective-permute-start | bytes 1572872 | tf_op jit(solution)/shard_map/ppermute | solution.py:303
  112.0 17.2 %collective-permute-start.14 = (f32[64,1024]{1,0:T(8,128)S(1)}, f32[64,1024]{1,0:T(8,128)S(1)}, u32[]{:S(2)}, u32[]{:S(2)}) collective-permute-start(f32[64,1024]{1,0:T(8,128)S(1)} %get-tuple-element.187), channel_id=1, source_target_pairs={{0,16},{2,18},{4,20},{6,22},{8,24},{10,26},{12,28},{14,30},{16,0},... | collective-permute-start | bytes 786440 | tf_op jit(solution)/shard_map/ppermute | solution.py:303
  115.0 18.4 %collective-permute-start.21 = (f32[128,512]{1,0:T(8,128)S(1)}, f32[128,512]{1,0:T(8,128)S(1)}, u32[]{:S(2)}, u32[]{:S(2)}) collective-permute-start(f32[128,512]{1,0:T(8,128)S(1)} %get-tuple-element.181), channel_id=1, source_target_pairs={{0,8},{2,10},{4,12},{6,14},{8,0},{10,2},{12,4},{14,6},{16,24},{18,... | collective-permute-start | bytes 786440 | tf_op jit(solution)/shard_map/ppermute | solution.py:303
  129.3 5.4 %collective-permute-start.22 = (f32[64,512]{1,0:T(8,128)S(1)}, f32[64,512]{1,0:T(8,128)S(1)}, u32[]{:S(2)}, u32[]{:S(2)}) collective-permute-start(f32[64,512]{1,0:T(8,128)S(1)} %get-tuple-element.201), channel_id=1, source_target_pairs={{0,1},{1,0},{2,3},{3,2},{4,5},{5,4},{6,7},{7,6},{8,9},{9,8},{10,11... | collective-permute-start | bytes 393224 | tf_op jit(solution)/shard_map/ppermute | solution.py:331
  131.7 13.1 %collective-permute-start.20 = (f32[64,1024]{1,0:T(8,128)S(1)}, f32[64,1024]{1,0:T(8,128)S(1)}, u32[]{:S(2)}, u32[]{:S(2)}) collective-permute-start(f32[64,1024]{1,0:T(8,128)S(1)} %get-tuple-element.183), channel_id=1, source_target_pairs={{0,16},{2,18},{4,20},{6,22},{8,24},{10,26},{12,28},{14,30},{16,0},... | collective-permute-start | bytes 786440 | tf_op jit(solution)/shard_map/ppermute | solution.py:303
  133.4 12.3 %collective-permute-start.23 = (f32[64,512]{1,0:T(8,128)S(1)}, f32[64,512]{1,0:T(8,128)S(1)}, u32[]{:S(2)}, u32[]{:S(2)}) collective-permute-start(f32[64,512]{1,0:T(8,128)S(1)} %get-tuple-element.193), channel_id=1, source_target_pairs={{0,4},{2,6},{4,0},{6,2},{8,12},{10,14},{12,8},{14,10},{16,20},{18,... | collective-permute-start | bytes 393224 | tf_op jit(solution)/shard_map/ppermute | solution.py:303
  144.9 5.2 %collective-permute-start.24 = (f32[64,512]{1,0:T(8,128)S(1)}, f32[64,512]{1,0:T(8,128)S(1)}, u32[]{:S(2)}, u32[]{:S(2)}) collective-permute-start(f32[64,512]{1,0:T(8,128)S(1)} %get-tuple-element.197), channel_id=1, source_target_pairs={{0,1},{1,0},{2,3},{3,2},{4,5},{5,4},{6,7},{7,6},{8,9},{9,8},{10,11... | collective-permute-start | bytes 393224 | tf_op jit(solution)/shard_map/ppermute | solution.py:331
  145.7 5.9 %collective-permute-start.25 = (f32[64,512]{1,0:T(8,128)S(1)}, f32[64,512]{1,0:T(8,128)S(1)}, u32[]{:S(2)}, u32[]{:S(2)}) collective-permute-start(f32[64,512]{1,0:T(8,128)S(1)} %get-tuple-element.191), channel_id=1, source_target_pairs={{0,16},{2,18},{4,20},{6,22},{8,24},{10,26},{12,28},{14,30},{16,0},... | collective-permute-start | bytes 393224 | tf_op jit(solution)/shard_map/ppermute | solution.py:303
  151.7 5.0 %collective-permute-start.26 = (f32[64,512]{1,0:T(8,128)S(1)}, f32[64,512]{1,0:T(8,128)S(1)}, u32[]{:S(2)}, u32[]{:S(2)}) collective-permute-start(f32[64,512]{1,0:T(8,128)S(1)} %get-tuple-element.195), channel_id=1, source_target_pairs={{0,1},{1,0},{2,3},{3,2},{4,5},{5,4},{6,7},{7,6},{8,9},{9,8},{10,11... | collective-permute-start | bytes 393224 | tf_op jit(solution)/shard_map/ppermute | solution.py:331
  (6 other events, 200.9 us)

commit v7 on v6

--- a/solution.py
+++ b/solution.py
@@ -276,7 +276,7 @@
                 for z in range(OUTER) for x in range(inner) for c in range(CORES)]
 
     chain = Chain()
-    received, split_in, totals, gens = {}, {}, {}, {}
+    received, totals, gens = {}, {}, {}
 
     def run_products(chunks, *got):
         return chain.run(
@@ -303,54 +303,61 @@
             got = lax.ppermute(send, "tensor", pairs)
             half = keep.shape[0] // 2
             if half < cols:
-                total = chain.run(jnp.add, keep, got)
+                totals[h, start] = chain.run(jnp.add, keep, got)
             else:
                 keep, send = chain.run(
                     lambda a, b: (a[:half] + b[:half], a[half:] + b[half:]), keep, got
                 )
             yield
-        totals[h, start] = total
-
-    mine, other = {}, {}
-
-    def exchange(h):
-        for i, chunk in enumerate(chunks):
-            if chunk[0] == h:
-                for _ in gens[i]:
-                    pass
+
+    mine, other, arriving = {}, {}, []
+
+    def exchange(group):
         if rep != 2:
-            mine[h] = totals[h, 0]
+            for h in group:
+                mine[h] = totals[h, 0]
             return
-        if (h, row_local) in totals:
-            first, second = totals[h, 0], totals[h, row_local]
-        else:
-            first, second = totals[h, 0][:, :row_local], totals[h, 0][:, row_local:]
-        mine[h], away = chain.run(
-            lambda a, b: (jnp.where(side == 0, a, b), jnp.where(side == 0, b, a)), first, second
-        )
-        other[h] = lax.ppermute(away, "rep", [(0, 1), (1, 0)])
+        pairs = []
+        for h in group:
+            if (h, row_local) in totals:
+                pairs.append((totals[h, 0], totals[h, row_local]))
+            else:
+                pairs.append((totals[h, 0][:, :row_local], totals[h, 0][:, row_local:]))
+
+        def choose(pairs):
+            kept = [jnp.where(side == 0, a, b) for a, b in pairs]
+            return kept, jnp.concatenate([jnp.where(side == 0, b, a) for a, b in pairs])
+
+        kept, away = chain.run(choose, pairs)
+        got = lax.ppermute(away, "rep", [(0, 1), (1, 0)])
+        for i, h in enumerate(group):
+            mine[h], other[h] = kept[i], got[i * cols:(i + 1) * cols]
+        arriving.append(got)
 
     if inner == 2 and rep == 2 and blocks == 4:
         half = rows // 2
         chunks = [(0, 0, rows, False), (1, 0, rows, False), (2, 0, rows, False),
-                  (3, 0, half, True), (3, half, half, False)]
+                  (3, 0, half, False), (3, half, half, False)]
         firsts = {"p": [0, 1], "q": [2, 3]}
-        seconds = {"w": [0], "x": [1], "z": [2, 3, 4]}
-        plan = "pwxq0z013a132A42bB4cCd"
+        seconds = {"w": [0], "x": [1], "y": [2], "z": [3, 4]}
+        groups = {"a": [0, 1, 2], "d": [3]}
+        plan = "pwxq0y0z1012132432a434Ad"
     else:
         chunks = [(h, 0, rows, False) for h in range(blocks)]
         firsts = {"p": list(range(blocks))}
         seconds = {"w": list(range(blocks))}
-        plan = "pw" + "abcdefgh"[:blocks]
+        groups = {"a": list(range(blocks))}
+        steps = (inner * OUTER).bit_length() - 1
+        plan = "pw" + "".join(str(h) * steps for h in range(blocks)) + "a"
     for move in plan:
         if move in firsts:
             first_halves(firsts[move])
         elif move in seconds:
             second_halves(seconds[move])
-        elif move in "ABCDEFGH":
-            chain.last = chain.last, other["ABCDEFGH".index(move)]
-        elif move in "abcdefgh":
-            exchange("abcdefgh".index(move))
+        elif move == "A":
+            chain.last = chain.last, arriving[-1]
+        elif move in groups:
+            exchange(groups[move])
         else:
             next(gens[int(move)])
 

time: 159 us -> 155 us (0.975)
  waiting for transfers between devices: 68 us -> 62.6 us
  starting transfers between devices: 29 us -> 23.9 us
  Pallas kernels: 56 us -> 60.8 us
    ppermute x4 -> x2, waiting for transfers between devices: 11.1 us -> 2.92 us  [exchange(): got = lax.ppermute(away, 'rep', [(0, 1), (1, 0)])]
    ppermute x15, starting transfers between devices: 20.3 us -> 14.2 us  [work(): got = lax.ppermute(send, 'tensor', pairs)]
    pallas_call x5 -> x6, Pallas kernels: 54.1 us -> 58.9 us  [products(): pl.pallas_call(functools.partial(products_kernel, first, inner, chunks, l...]
    ppermute x15, waiting for transfers between devices: 53.2 us -> 56.4 us  [work(): got = lax.ppermute(send, 'tensor', pairs)]
    ppermute x4 -> x2, starting transfers between devices: 6.58 us -> 7.99 us  [exchange(): got = lax.ppermute(away, 'rep', [(0, 1), (1, 0)])]
  transfers between devices with their start and end apart: 27 -> 25, of which waited for: 14 -> 12; matrix products, arithmetic and copies ran while one was open for 3% -> 3% of each run, Pallas kernels for 26% -> 31%
where the time goes in v7:
time: 155 us; the launch traced here: 153 us
  waiting for transfers between devices  62.6 us (40%)
  Pallas kernels  60.8 us (39%)
  starting transfers between devices  23.9 us (15%)
  other arithmetic  5.64 us (4%)
    pallas_call x6, Pallas kernels, products(): pl.pallas_call(functools.partial(products_kernel, first, inner, chunks, l...  58.9 us
    ppermute x15, waiting for transfers between devices, work(): got = lax.ppermute(send, 'tensor', pairs)  56.4 us
    ppermute x15, starting transfers between devices, work(): got = lax.ppermute(send, 'tensor', pairs)  14.2 us
    ppermute x2, starting transfers between devices, exchange(): got = lax.ppermute(away, 'rep', [(0, 1), (1, 0)])  7.99 us
    add x10, other arithmetic, work(): a[half:] + b[half:]  4.48 us
    ppermute x8, waiting for transfers between devices, first_halves(): lax.ppermute(part, 'tensor', across)  3.21 us
  transfers between devices with their start and end apart: 25, of which 12 were waited for; matrix products, arithmetic and copies ran while one was open for 3% of the time, Pallas kernels for 31%

profile of v7, /device:TPU:0, one launch (start us, length us, event | category | flops | bytes accessed | tf_op | source)
XLA Modules:
  0.0 153.2 jit_solution(6089496701067967324)
XLA Ops:
  0.8 11.6 %first_halves.2 = (f32[256,1024]{1,0:T(8,128)S(1)}, f32[256,1024]{1,0:T(8,128)S(1)}, f32[256,1024]{1,0:T(8,128)S(1)}, f32[256,1024]{1,0:T(8,128)S(1)}) custom-call(s32[3]{0:T(128)S(1)} %pad_add_fusion.1.place, s32[4]{0:T(128)S(1)} %get-tuple-element.138.limit, s32[4]{0:T(128)S(1)} %get-tuple-element.139.rows_live, f32[8,2,64,32,128]{4,3,2,1,0:T(8,128)} %bitcast.11, ...), custom_call_target="tpu_custom_call" | custom-call | flops 1024 | bytes 1024 | tf_op jit(solution)/shard_map/first_halves/pallas_call | solution.py:176
  13.5 1.7 %collective-permute-done.refs_0_ = f32[256,1024]{1,0:T(8,128)S(1)} collective-permute-done((f32[256,1024]{1,0:T(8,128)S(1)}, f32[256,1024]{1,0:T(8,128)S(1)}, u32[]{:S(2)}, u32[]{:S(2)}) %collective-permute-start) | collective-permute-done | bytes 1048608 | tf_op jit(solution)/shard_map/ppermute | solution.py:290
  15.2 1.5 collective-permute-done.1.refs_1_
  16.7 7.9 %second_halves.4 = (f32[256,1024]{1,0:T(8,128)S(1)}, f32[256,1024]{1,0:T(8,128)S(1)}) custom-call(s32[3]{0:T(128)S(1)} %pad_add_fusion.1.place, s32[4]{0:T(128)S(1)} %get-tuple-element.138.limit, s32[4]{0:T(128)S(1)} %get-tuple-element.139.rows_live, f32[8,2,64,32,128]{4,3,2,1,0:T(8,128)} %bitcast.12, f32[4,1024,1024]{2,1,0:T(8,128)} %a_hbm.6, ...), custom_call_target="tpu_custom_call" | custom-call | flops 1024 | bytes 1024 | tf_op jit(solution)/shard_map/second_halves/pallas_call | solution.py:176
  24.8 7.9 %second_halves.5 = (f32[256,1024]{1,0:T(8,128)S(1)}, f32[256,1024]{1,0:T(8,128)S(1)}) custom-call(s32[3]{0:T(128)S(1)} %pad_add_fusion.1.place, s32[4]{0:T(128)S(1)} %get-tuple-element.138.limit, s32[4]{0:T(128)S(1)} %get-tuple-element.139.rows_live, f32[8,2,64,32,128]{4,3,2,1,0:T(8,128)} %bitcast.13, f32[4,1024,1024]{2,1,0:T(8,128)} %a_hbm.6, ...), custom_call_target="tpu_custom_call" | custom-call | flops 1024 | bytes 1024 | tf_op jit(solution)/shard_map/second_halves/pallas_call | solution.py:176
  32.7 13.5 %first_halves.3 = (f32[256,1024]{1,0:T(8,128)S(1)}, f32[256,1024]{1,0:T(8,128)S(1)}, f32[256,1024]{1,0:T(8,128)S(1)}, f32[256,1024]{1,0:T(8,128)S(1)}) custom-call(s32[3]{0:T(128)S(1)} %pad_add_fusion.1.place, s32[4]{0:T(128)S(1)} %get-tuple-element.138.limit, s32[4]{0:T(128)S(1)} %get-tuple-element.139.rows_live, f32[8,2,64,32,128]{4,3,2,1,0:T(8,128)} %bitcast.14, ...), custom_call_target="tpu_custom_call" | custom-call | flops 1024 | bytes 1024 | tf_op jit(solution)/shard_map/first_halves/pallas_call | solution.py:176
  46.8 2.0 %collective-permute-start.9 = (f32[256,1024]{1,0:T(8,128)S(1)}, f32[256,1024]{1,0:T(8,128)S(1)}, u32[]{:S(2)}, u32[]{:S(2)}) collective-permute-start(f32[256,1024]{1,0:T(8,128)S(1)} %get-tuple-element.134), channel_id=1, source_target_pairs={{0,4},{2,6},{4,0},{6,2},{8,12},{10,14},{12,8},{14,10},{16,20},{18,... | collective-permute-start | bytes 3145736 | tf_op jit(solution)/shard_map/ppermute | solution.py:303
  48.8 1.7 %collective-permute-done.2 = f32[256,1024]{1,0:T(8,128)S(1)} collective-permute-done((f32[256,1024]{1,0:T(8,128)S(1)}, f32[256,1024]{1,0:T(8,128)S(1)}, u32[]{:S(2)}, u32[]{:S(2)}) %collective-permute-start.2) | collective-permute-done | bytes 1048608 | tf_op jit(solution)/shard_map/ppermute | solution.py:303
  50.8 8.9 %second_halves.6 = (f32[256,1024]{1,0:T(8,128)S(1)}, f32[256,1024]{1,0:T(8,128)S(1)}) custom-call(s32[3]{0:T(128)S(1)} %pad_add_fusion.1.place, s32[4]{0:T(128)S(1)} %get-tuple-element.138.limit, s32[4]{0:T(128)S(1)} %get-tuple-element.139.rows_live, f32[8,2,64,32,128]{4,3,2,1,0:T(8,128)} %bitcast.15, f32[4,1024,1024]{2,1,0:T(8,128)} %a_hbm.6, ...), custom_call_target="tpu_custom_call" | custom-call | flops 1024 | bytes 1024 | tf_op jit(solution)/shard_map/second_halves/pallas_call | solution.py:176
  59.7 1.7 %collective-permute-start.14 = (f32[256,1024]{1,0:T(8,128)S(1)}, f32[256,1024]{1,0:T(8,128)S(1)}, u32[]{:S(2)}, u32[]{:S(2)}) collective-permute-start(f32[256,1024]{1,0:T(8,128)S(1)} %get-tuple-element.151), channel_id=1, source_target_pairs={{0,4},{2,6},{4,0},{6,2},{8,12},{10,14},{12,8},{14,10},{16,20},{18,... | collective-permute-start | bytes 3145736 | tf_op jit(solution)/shard_map/ppermute | solution.py:303
  61.4 3.7 %collective-permute-done.5 = f32[128,1024]{1,0:T(8,128)S(1)} collective-permute-done((f32[128,1024]{1,0:T(8,128)S(1)}, f32[128,1024]{1,0:T(8,128)S(1)}, u32[]{:S(2)}, u32[]{:S(2)}) %collective-permute-start.5) | collective-permute-done | bytes 524320 | tf_op jit(solution)/shard_map/ppermute | solution.py:303
  65.2 9.1 %second_halves.7 = (f32[256,512]{1,0:T(8,128)S(1)}, f32[256,512]{1,0:T(8,128)S(1)}, f32[256,512]{1,0:T(8,128)S(1)}, f32[256,512]{1,0:T(8,128)S(1)}) custom-call(s32[3]{0:T(128)S(1)} %pad_add_fusion.1.place, s32[4]{0:T(128)S(1)} %get-tuple-element.138.limit, s32[4]{0:T(128)S(1)} %get-tuple-element.139.rows_live, f32[8,2,64,32,128]{4,3,2,1,0:T(8,128)} %bitcast.16, ...), custom_call_target="tpu_custom_call" | custom-call | flops 1024 | bytes 1024 | tf_op jit(solution)/shard_map/second_halves/pallas_call | solution.py:176
  75.2 16.5 %collective-permute-done.8 = f32[64,1024]{1,0:T(8,128)S(1)} collective-permute-done((f32[64,1024]{1,0:T(8,128)S(1)}, f32[64,1024]{1,0:T(8,128)S(1)}, u32[]{:S(2)}, u32[]{:S(2)}) %collective-permute-start.8) | collective-permute-done | bytes 262176 | tf_op jit(solution)/shard_map/ppermute | solution.py:303
  91.8 2.0 %collective-permute-done.12 = f32[128,1024]{1,0:T(8,128)S(1)} collective-permute-done((f32[128,1024]{1,0:T(8,128)S(1)}, f32[128,1024]{1,0:T(8,128)S(1)}, u32[]{:S(2)}, u32[]{:S(2)}) %collective-permute-start.12) | collective-permute-done | bytes 524320 | tf_op jit(solution)/shard_map/ppermute | solution.py:303
  98.2 15.1 %collective-permute-done.13 = f32[64,1024]{1,0:T(8,128)S(1)} collective-permute-done((f32[64,1024]{1,0:T(8,128)}, f32[64,1024]{1,0:T(8,128)S(1)}, u32[]{:S(2)}, u32[]{:S(2)}) %collective-permute-start.13) | collective-permute-done | bytes 262176 | tf_op jit(solution)/shard_map/ppermute | solution.py:303
  114.5 2.3 %collective-permute-start.18 = (f32[128,512]{1,0:T(8,128)S(1)}, f32[128,512]{1,0:T(8,128)S(1)}, u32[]{:S(2)}, u32[]{:S(2)}) collective-permute-start(f32[128,512]{1,0:T(8,128)S(1)} %get-tuple-element.193), channel_id=1, source_target_pairs={{0,8},{2,10},{4,12},{6,14},{8,0},{10,2},{12,4},{14,6},{16,24},{18,... | collective-permute-start | bytes 786440 | tf_op jit(solution)/shard_map/ppermute | solution.py:303
  119.2 10.2 %collective-permute-done.18 = f32[128,512]{1,0:T(8,128)S(1)} collective-permute-done((f32[128,512]{1,0:T(8,128)S(1)}, f32[128,512]{1,0:T(8,128)S(1)}, u32[]{:S(2)}, u32[]{:S(2)}) %collective-permute-start.18) | collective-permute-done | bytes 262176 | tf_op jit(solution)/shard_map/ppermute | solution.py:303
  129.6 4.5 %collective-permute-start.23 = (f32[192,512]{1,0:T(8,128)S(1)}, f32[192,512]{1,0:T(8,128)S(1)}, u32[]{:S(2)}, u32[]{:S(2)}) collective-permute-start(f32[192,512]{1,0:T(8,128)S(1)} %pad_maximum_fusion), channel_id=1, source_target_pairs={{0,1},{1,0},{2,3},{3,2},{4,5},{5,4},{6,7},{7,6},{8,9},{9,8},{10,11... | collective-permute-start | bytes 1179656 | tf_op jit(solution)/shard_map/ppermute | solution.py:332
  134.1 3.5 %collective-permute-start.20 = (f32[64,512]{1,0:T(8,128)S(1)}, f32[64,512]{1,0:T(8,128)S(1)}, u32[]{:S(2)}, u32[]{:S(2)}) collective-permute-start(f32[64,512]{1,0:T(8,128)S(1)} %get-tuple-element.203), channel_id=1, source_target_pairs={{0,16},{2,18},{4,20},{6,22},{8,24},{10,26},{12,28},{14,30},{16,0},... | collective-permute-start | bytes 393224 | tf_op jit(solution)/shard_map/ppermute | solution.py:303
  138.6 4.9 %collective-permute-done.20 = f32[64,512]{1,0:T(8,128)S(1)} collective-permute-done((f32[64,512]{1,0:T(8,128)S(1)}, f32[64,512]{1,0:T(8,128)S(1)}, u32[]{:S(2)}, u32[]{:S(2)}) %collective-permute-start.20) | collective-permute-done | bytes 131104 | tf_op jit(solution)/shard_map/ppermute | solution.py:303
  143.5 1.4 collective-permute-done.22
  144.9 3.5 %collective-permute-start.24 = (f32[64,512]{1,0:T(8,128)S(1)}, f32[64,512]{1,0:T(8,128)S(1)}, u32[]{:S(2)}, u32[]{:S(2)}) collective-permute-start(f32[64,512]{1,0:T(8,128)S(1)} %get-tuple-element.208), channel_id=1, source_target_pairs={{0,1},{1,0},{2,3},{3,2},{4,5},{5,4},{6,7},{7,6},{8,9},{9,8},{10,11... | collective-permute-start | bytes 393224 | tf_op jit(solution)/shard_map/ppermute | solution.py:332
  148.5 2.9 %collective-permute-done.24.refs_7_ = f32[64,512]{1,0:T(8,128)S(1)} collective-permute-done((f32[64,512]{1,0:T(8,128)S(1)}, f32[64,512]{1,0:T(8,128)S(1)}, u32[]{:S(2)}, u32[]{:S(2)}) %collective-permute-start.24) | collective-permute-done | bytes 131104 | tf_op jit(solution)/shard_map/ppermute | solution.py:332
  151.4 1.8 %place_blocks.1 = f32[64,8,512]{2,1,0:T(8,128)} custom-call(s32[1]{0:T(128)} %bitcast.side_ref, s32[2]{0:T(128)S(1)} %pad_add_fusion.base, s32[8]{0:T(128)S(1)} %copy-done, s32[8]{0:T(128)S(1)} %copy-done.1, f32[64,512]{1,0:T(8,128)S(1)} %get-tuple-element.211.refs_0_, f32[64,512]{1,0:T(8,128)S(1)} %get-tuple-element.213.refs_1_, ...), custom_call_target="tpu_custom_call" | custom-call | flops 1024 | bytes 1024 | tf_op jit(solution)/shard_map/place_blocks/pallas_call | solution.py:225
  (63 shorter events, 13.1 us)
Async XLA Ops:
  13.0 3.8 %collective-permute-start.1 = (f32[256,1024]{1,0:T(8,128)S(1)}, f32[256,1024]{1,0:T(8,128)S(1)}, u32[]{:S(2)}, u32[]{:S(2)}) collective-permute-start(f32[256,1024]{1,0:T(8,128)S(1)} %get-tuple-element.95), channel_id=1, source_target_pairs={{0,2},{2,0},{4,6},{6,4},{8,10},{10,8},{12,14},{14,12},{16,18},{18,... | collective-permute-start | bytes 3145736 | tf_op jit(solution)/shard_map/ppermute | solution.py:290
  13.0 11.7 %collective-permute-start.3 = (f32[256,1024]{1,0:T(8,128)S(1)}, f32[256,1024]{1,0:T(8,128)S(1)}, u32[]{:S(2)}, u32[]{:S(2)}) collective-permute-start(f32[256,1024]{1,0:T(8,128)S(1)} %get-tuple-element.105), channel_id=1, source_target_pairs={{0,2},{2,0},{4,6},{6,4},{8,10},{10,8},{12,14},{14,12},{16,18},{18,... | collective-permute-start | bytes 3145736 | tf_op jit(solution)/shard_map/ppermute | solution.py:290
  13.5 11.3 %collective-permute-start.4 = (f32[256,1024]{1,0:T(8,128)S(1)}, f32[256,1024]{1,0:T(8,128)S(1)}, u32[]{:S(2)}, u32[]{:S(2)}) collective-permute-start(f32[256,1024]{1,0:T(8,128)S(1)} %get-tuple-element.106), channel_id=1, source_target_pairs={{0,2},{2,0},{4,6},{6,4},{8,10},{10,8},{12,14},{14,12},{16,18},{18,... | collective-permute-start | bytes 3145736 | tf_op jit(solution)/shard_map/ppermute | solution.py:290
  24.7 25.8 %collective-permute-start.2 = (f32[256,1024]{1,0:T(8,128)S(1)}, f32[256,1024]{1,0:T(8,128)S(1)}, u32[]{:S(2)}, u32[]{:S(2)}) collective-permute-start(f32[256,1024]{1,0:T(8,128)S(1)} %get-tuple-element.104), channel_id=1, source_target_pairs={{0,4},{2,6},{4,0},{6,2},{8,12},{10,14},{12,8},{14,10},{16,20},{18,... | collective-permute-start | bytes 3145736 | tf_op jit(solution)/shard_map/ppermute | solution.py:303
  46.2 4.5 %collective-permute-start.6 = (f32[256,1024]{1,0:T(8,128)S(1)}, f32[256,1024]{1,0:T(8,128)S(1)}, u32[]{:S(2)}, u32[]{:S(2)}) collective-permute-start(f32[256,1024]{1,0:T(8,128)S(1)} %get-tuple-element.120), channel_id=1, source_target_pairs={{0,2},{2,0},{4,6},{6,4},{8,10},{10,8},{12,14},{14,12},{16,18},{18,... | collective-permute-start | bytes 3145736 | tf_op jit(solution)/shard_map/ppermute | solution.py:290
  46.7 4.1 %collective-permute-start.7 = (f32[256,1024]{1,0:T(8,128)S(1)}, f32[256,1024]{1,0:T(8,128)S(1)}, u32[]{:S(2)}, u32[]{:S(2)}) collective-permute-start(f32[256,1024]{1,0:T(8,128)S(1)} %get-tuple-element.123), channel_id=1, source_target_pairs={{0,2},{2,0},{4,6},{6,4},{8,10},{10,8},{12,14},{14,12},{16,18},{18,... | collective-permute-start | bytes 3145736 | tf_op jit(solution)/shard_map/ppermute | solution.py:290
  46.8 27.5 %collective-permute-start.9 = (f32[256,1024]{1,0:T(8,128)S(1)}, f32[256,1024]{1,0:T(8,128)S(1)}, u32[]{:S(2)}, u32[]{:S(2)}) collective-permute-start(f32[256,1024]{1,0:T(8,128)S(1)} %get-tuple-element.134), channel_id=1, source_target_pairs={{0,4},{2,6},{4,0},{6,2},{8,12},{10,14},{12,8},{14,10},{16,20},{18,... | collective-permute-start | bytes 3145736 | tf_op jit(solution)/shard_map/ppermute | solution.py:303
  48.8 16.4 %collective-permute-start.10 = (f32[256,1024]{1,0:T(8,128)S(1)}, f32[256,1024]{1,0:T(8,128)S(1)}, u32[]{:S(2)}, u32[]{:S(2)}) collective-permute-start(f32[256,1024]{1,0:T(8,128)S(1)} %get-tuple-element.135), channel_id=1, source_target_pairs={{0,2},{2,0},{4,6},{6,4},{8,10},{10,8},{12,14},{14,12},{16,18},{18,... | collective-permute-start | bytes 3145736 | tf_op jit(solution)/shard_map/ppermute | solution.py:290
  50.5 14.7 %collective-permute-start.11 = (f32[256,1024]{1,0:T(8,128)S(1)}, f32[256,1024]{1,0:T(8,128)S(1)}, u32[]{:S(2)}, u32[]{:S(2)}) collective-permute-start(f32[256,1024]{1,0:T(8,128)S(1)} %get-tuple-element.136), channel_id=1, source_target_pairs={{0,2},{2,0},{4,6},{6,4},{8,10},{10,8},{12,14},{14,12},{16,18},{18,... | collective-permute-start | bytes 3145736 | tf_op jit(solution)/shard_map/ppermute | solution.py:290
  50.7 14.4 %collective-permute-start.5 = (f32[128,1024]{1,0:T(8,128)S(1)}, f32[128,1024]{1,0:T(8,128)S(1)}, u32[]{:S(2)}, u32[]{:S(2)}) collective-permute-start(f32[128,1024]{1,0:T(8,128)S(1)} %get-tuple-element.189), channel_id=1, source_target_pairs={{0,8},{2,10},{4,12},{6,14},{8,0},{10,2},{12,4},{14,6},{16,24},{18,... | collective-permute-start | bytes 1572872 | tf_op jit(solution)/shard_map/ppermute | solution.py:303
  59.7 35.7 %collective-permute-start.14 = (f32[256,1024]{1,0:T(8,128)S(1)}, f32[256,1024]{1,0:T(8,128)S(1)}, u32[]{:S(2)}, u32[]{:S(2)}) collective-permute-start(f32[256,1024]{1,0:T(8,128)S(1)} %get-tuple-element.151), channel_id=1, source_target_pairs={{0,4},{2,6},{4,0},{6,2},{8,12},{10,14},{12,8},{14,10},{16,20},{18,... | collective-permute-start | bytes 3145736 | tf_op jit(solution)/shard_map/ppermute | solution.py:303
  74.5 19.2 %collective-permute-start.12 = (f32[128,1024]{1,0:T(8,128)S(1)}, f32[128,1024]{1,0:T(8,128)S(1)}, u32[]{:S(2)}, u32[]{:S(2)}) collective-permute-start(f32[128,1024]{1,0:T(8,128)S(1)} %get-tuple-element.187), channel_id=1, source_target_pairs={{0,8},{2,10},{4,12},{6,14},{8,0},{10,2},{12,4},{14,6},{16,24},{18,... | collective-permute-start | bytes 1572872 | tf_op jit(solution)/shard_map/ppermute | solution.py:303
  74.8 16.9 %collective-permute-start.8 = (f32[64,1024]{1,0:T(8,128)S(1)}, f32[64,1024]{1,0:T(8,128)S(1)}, u32[]{:S(2)}, u32[]{:S(2)}) collective-permute-start(f32[64,1024]{1,0:T(8,128)S(1)} %get-tuple-element.199), channel_id=1, source_target_pairs={{0,16},{2,18},{4,20},{6,22},{8,24},{10,26},{12,28},{14,30},{16,0},... | collective-permute-start | bytes 786440 | tf_op jit(solution)/shard_map/ppermute | solution.py:303
  74.8 38.6 %collective-permute-start.16 = (f32[256,512]{1,0:T(8,128)S(1)}, f32[256,512]{1,0:T(8,128)}, u32[]{:S(2)}, u32[]{:S(2)}) collective-permute-start(f32[256,512]{1,0:T(8,128)S(1)} %get-tuple-element.156), channel_id=1, source_target_pairs={{0,4},{2,6},{4,0},{6,2},{8,12},{10,14},{12,8},{14,10},{16,20},{18,... | collective-permute-start | bytes 1572872 | tf_op jit(solution)/shard_map/ppermute | solution.py:303
  96.4 20.4 %collective-permute-start.15 = (f32[128,1024]{1,0:T(8,128)}, f32[128,1024]{1,0:T(8,128)}, u32[]{:S(2)}, u32[]{:S(2)}) collective-permute-start(f32[128,1024]{1,0:T(8,128)} %get-tuple-element.185), channel_id=1, source_target_pairs={{0,8},{2,10},{4,12},{6,14},{8,0},{10,2},{12,4},{14,6},{16,24},{18,... | collective-permute-start | bytes 1572872 | tf_op jit(solution)/shard_map/ppermute | solution.py:303
  96.4 17.0 %collective-permute-start.13 = (f32[64,1024]{1,0:T(8,128)}, f32[64,1024]{1,0:T(8,128)S(1)}, u32[]{:S(2)}, u32[]{:S(2)}) collective-permute-start(f32[64,1024]{1,0:T(8,128)} %get-tuple-element.197), channel_id=1, source_target_pairs={{0,16},{2,18},{4,20},{6,22},{8,24},{10,26},{12,28},{14,30},{16,0},... | collective-permute-start | bytes 786440 | tf_op jit(solution)/shard_map/ppermute | solution.py:303
  96.9 22.2 %collective-permute-start.19 = (f32[256,512]{1,0:T(8,128)S(1)}, f32[256,512]{1,0:T(8,128)S(1)}, u32[]{:S(2)}, u32[]{:S(2)}) collective-permute-start(f32[256,512]{1,0:T(8,128)S(1)} %get-tuple-element.162), channel_id=1, source_target_pairs={{0,4},{2,6},{4,0},{6,2},{8,12},{10,14},{12,8},{14,10},{16,20},{18,... | collective-permute-start | bytes 1572872 | tf_op jit(solution)/shard_map/ppermute | solution.py:303
  114.5 14.8 %collective-permute-start.18 = (f32[128,512]{1,0:T(8,128)S(1)}, f32[128,512]{1,0:T(8,128)S(1)}, u32[]{:S(2)}, u32[]{:S(2)}) collective-permute-start(f32[128,512]{1,0:T(8,128)S(1)} %get-tuple-element.193), channel_id=1, source_target_pairs={{0,8},{2,10},{4,12},{6,14},{8,0},{10,2},{12,4},{14,6},{16,24},{18,... | collective-permute-start | bytes 786440 | tf_op jit(solution)/shard_map/ppermute | solution.py:303
  117.9 11.5 %collective-permute-start.17 = (f32[64,1024]{1,0:T(8,128)S(1)}, f32[64,1024]{1,0:T(8,128)S(1)}, u32[]{:S(2)}, u32[]{:S(2)}) collective-permute-start(f32[64,1024]{1,0:T(8,128)S(1)} %get-tuple-element.195), channel_id=1, source_target_pairs={{0,16},{2,18},{4,20},{6,22},{8,24},{10,26},{12,28},{14,30},{16,0},... | collective-permute-start | bytes 786440 | tf_op jit(solution)/shard_map/ppermute | solution.py:303
  129.4 8.2 %collective-permute-start.21 = (f32[128,512]{1,0:T(8,128)S(1)}, f32[128,512]{1,0:T(8,128)S(1)}, u32[]{:S(2)}, u32[]{:S(2)}) collective-permute-start(f32[128,512]{1,0:T(8,128)S(1)} %get-tuple-element.191), channel_id=1, source_target_pairs={{0,8},{2,10},{4,12},{6,14},{8,0},{10,2},{12,4},{14,6},{16,24},{18,... | collective-permute-start | bytes 786440 | tf_op jit(solution)/shard_map/ppermute | solution.py:303
  129.6 15.3 %collective-permute-start.23 = (f32[192,512]{1,0:T(8,128)S(1)}, f32[192,512]{1,0:T(8,128)S(1)}, u32[]{:S(2)}, u32[]{:S(2)}) collective-permute-start(f32[192,512]{1,0:T(8,128)S(1)} %pad_maximum_fusion), channel_id=1, source_target_pairs={{0,1},{1,0},{2,3},{3,2},{4,5},{5,4},{6,7},{7,6},{8,9},{9,8},{10,11... | collective-permute-start | bytes 1179656 | tf_op jit(solution)/shard_map/ppermute | solution.py:332
  134.1 9.3 %collective-permute-start.20 = (f32[64,512]{1,0:T(8,128)S(1)}, f32[64,512]{1,0:T(8,128)S(1)}, u32[]{:S(2)}, u32[]{:S(2)}) collective-permute-start(f32[64,512]{1,0:T(8,128)S(1)} %get-tuple-element.203), channel_id=1, source_target_pairs={{0,16},{2,18},{4,20},{6,22},{8,24},{10,26},{12,28},{14,30},{16,0},... | collective-permute-start | bytes 393224 | tf_op jit(solution)/shard_map/ppermute | solution.py:303
  137.6 7.2 %collective-permute-start.22 = (f32[64,512]{1,0:T(8,128)S(1)}, f32[64,512]{1,0:T(8,128)S(1)}, u32[]{:S(2)}, u32[]{:S(2)}) collective-permute-start(f32[64,512]{1,0:T(8,128)S(1)} %get-tuple-element.201), channel_id=1, source_target_pairs={{0,16},{2,18},{4,20},{6,22},{8,24},{10,26},{12,28},{14,30},{16,0},... | collective-permute-start | bytes 393224 | tf_op jit(solution)/shard_map/ppermute | solution.py:303
  144.9 6.4 %collective-permute-start.24 = (f32[64,512]{1,0:T(8,128)S(1)}, f32[64,512]{1,0:T(8,128)S(1)}, u32[]{:S(2)}, u32[]{:S(2)}) collective-permute-start(f32[64,512]{1,0:T(8,128)S(1)} %get-tuple-element.208), channel_id=1, source_target_pairs={{0,1},{1,0},{2,3},{3,2},{4,5},{5,4},{6,7},{7,6},{8,9},{9,8},{10,11... | collective-permute-start | bytes 393224 | tf_op jit(solution)/shard_map/ppermute | solution.py:332
  (3 other events, 157.0 us)

commit v8 on v7

--- a/solution.py
+++ b/solution.py
@@ -336,12 +336,12 @@
 
     if inner == 2 and rep == 2 and blocks == 4:
         half = rows // 2
-        chunks = [(0, 0, rows, False), (1, 0, rows, False), (2, 0, rows, False),
-                  (3, 0, half, False), (3, half, half, False)]
+        chunks = [(0, 0, rows, False), (1, 0, rows, False), (2, 0, half, True),
+                  (2, half, half, False), (3, 0, half, False), (3, half, half, False)]
         firsts = {"p": [0, 1], "q": [2, 3]}
-        seconds = {"w": [0], "x": [1], "y": [2], "z": [3, 4]}
+        seconds = {"w": [0], "x": [1], "y": [2, 3], "z": [4, 5]}
         groups = {"a": [0, 1, 2], "d": [3]}
-        plan = "pwxq0y0z1012132432a434Ad"
+        plan = "pwxq0yz01203214135243a545Ad"
     else:
         chunks = [(h, 0, rows, False) for h in range(blocks)]
         firsts = {"p": list(range(blocks))}

time: 155 us -> 147 us (0.948); the launches traced: 153 us -> 147 us
  waiting for transfers between devices: 62.6 us -> 43 us
  starting transfers between devices: 23.9 us -> 37.8 us
  Pallas kernels: 60.8 us -> 59 us
    ppermute x15 -> x18, waiting for transfers between devices: 56.4 us -> 36.9 us  [work(): got = lax.ppermute(send, 'tensor', pairs)]
    ppermute x15 -> x18, starting transfers between devices: 14.2 us -> 25.2 us  [work(): got = lax.ppermute(send, 'tensor', pairs)]
    ppermute x2, starting transfers between devices: 7.99 us -> 10.4 us  [exchange(): got = lax.ppermute(away, 'rep', [(0, 1), (1, 0)])]
    pallas_call x6, Pallas kernels: 58.9 us -> 57.1 us  [products(): pl.pallas_call(functools.partial(products_kernel, first, inner, chunks, l...]
    add x10 -> x12, other arithmetic: 4.48 us -> 4.99 us  [work(): a[half:] + b[half:]]
  transfers between devices with their start and end apart: 25 -> 28, of which waited for: 12 -> 14; matrix products, arithmetic and copies ran while one was open for 3% -> 4% of each run, Pallas kernels for 31% -> 32%
where the time goes in v8:
time: 147 us
  Pallas kernels  59 us (40%)
  waiting for transfers between devices  43 us (29%)
  starting transfers between devices  37.8 us (26%)
  other arithmetic  7.1 us (5%)
    pallas_call x6, Pallas kernels, products(): pl.pallas_call(functools.partial(products_kernel, first, inner, chunks, l...  57.1 us
    ppermute x18, waiting for transfers between devices, work(): got = lax.ppermute(send, 'tensor', pairs)  36.9 us
    ppermute x18, starting transfers between devices, work(): got = lax.ppermute(send, 'tensor', pairs)  25.2 us
    ppermute x2, starting transfers between devices, exchange(): got = lax.ppermute(away, 'rep', [(0, 1), (1, 0)])  10.4 us
    add x12, other arithmetic, work(): a[half:] + b[half:]  4.99 us
    ppermute x8, waiting for transfers between devices, first_halves(): lax.ppermute(part, 'tensor', across)  3.21 us
  transfers between devices with their start and end apart: 28, of which 14 were waited for; matrix products, arithmetic and copies ran while one was open for 4% of the time, Pallas kernels for 32%

profile of v8, /device:TPU:0, one launch (start us, length us, event | category | flops | bytes accessed | tf_op | source)
XLA Modules:
  0.0 147.2 jit_solution(13865459512345733828)
XLA Ops:
  0.8 10.7 %first_halves.2 = (f32[256,1024]{1,0:T(8,128)S(1)}, f32[256,1024]{1,0:T(8,128)S(1)}, f32[256,1024]{1,0:T(8,128)S(1)}, f32[256,1024]{1,0:T(8,128)S(1)}) custom-call(s32[3]{0:T(128)S(1)} %pad_add_fusion.1.place, s32[4]{0:T(128)S(1)} %get-tuple-element.143.limit, s32[4]{0:T(128)S(1)} %get-tuple-element.144.rows_live, f32[8,2,64,32,128]{4,3,2,1,0:T(8,128)} %bitcast.11, ...), custom_call_target="tpu_custom_call" | custom-call | flops 1024 | bytes 1024 | tf_op jit(solution)/shard_map/first_halves/pallas_call | solution.py:176
  15.8 7.9 %second_halves.4 = (f32[256,1024]{1,0:T(8,128)S(1)}, f32[256,1024]{1,0:T(8,128)S(1)}) custom-call(s32[3]{0:T(128)S(1)} %pad_add_fusion.1.place, s32[4]{0:T(128)S(1)} %get-tuple-element.143.limit, s32[4]{0:T(128)S(1)} %get-tuple-element.144.rows_live, f32[8,2,64,32,128]{4,3,2,1,0:T(8,128)} %bitcast.12, f32[4,1024,1024]{2,1,0:T(8,128)} %a_hbm.6, ...), custom_call_target="tpu_custom_call" | custom-call | flops 1024 | bytes 1024 | tf_op jit(solution)/shard_map/second_halves/pallas_call | solution.py:176
  23.7 2.9 %collective-permute-start.2 = (f32[256,1024]{1,0:T(8,128)S(1)}, f32[256,1024]{1,0:T(8,128)S(1)}, u32[]{:S(2)}, u32[]{:S(2)}) collective-permute-start(f32[256,1024]{1,0:T(8,128)S(1)} %get-tuple-element.112), channel_id=1, source_target_pairs={{0,4},{2,6},{4,0},{6,2},{8,12},{10,14},{12,8},{14,10},{16,20},{18,... | collective-permute-start | bytes 3145736 | tf_op jit(solution)/shard_map/ppermute | solution.py:303
  26.6 6.9 %second_halves.5 = (f32[256,1024]{1,0:T(8,128)S(1)}, f32[256,1024]{1,0:T(8,128)S(1)}) custom-call(s32[3]{0:T(128)S(1)} %pad_add_fusion.1.place, s32[4]{0:T(128)S(1)} %get-tuple-element.143.limit, s32[4]{0:T(128)S(1)} %get-tuple-element.144.rows_live, f32[8,2,64,32,128]{4,3,2,1,0:T(8,128)} %bitcast.13, f32[4,1024,1024]{2,1,0:T(8,128)} %a_hbm.6, ...), custom_call_target="tpu_custom_call" | custom-call | flops 1024 | bytes 1024 | tf_op jit(solution)/shard_map/second_halves/pallas_call | solution.py:176
  33.6 13.5 %first_halves.3 = (f32[256,1024]{1,0:T(8,128)S(1)}, f32[256,1024]{1,0:T(8,128)S(1)}, f32[256,1024]{1,0:T(8,128)S(1)}, f32[256,1024]{1,0:T(8,128)S(1)}) custom-call(s32[3]{0:T(128)S(1)} %pad_add_fusion.1.place, s32[4]{0:T(128)S(1)} %get-tuple-element.143.limit, s32[4]{0:T(128)S(1)} %get-tuple-element.144.rows_live, f32[8,2,64,32,128]{4,3,2,1,0:T(8,128)} %bitcast.14, ...), custom_call_target="tpu_custom_call" | custom-call | flops 1024 | bytes 1024 | tf_op jit(solution)/shard_map/first_halves/pallas_call | solution.py:176
  48.2 1.9 %collective-permute-done.2 = f32[256,1024]{1,0:T(8,128)S(1)} collective-permute-done((f32[256,1024]{1,0:T(8,128)S(1)}, f32[256,1024]{1,0:T(8,128)S(1)}, u32[]{:S(2)}, u32[]{:S(2)}) %collective-permute-start.2) | collective-permute-done | bytes 1048608 | tf_op jit(solution)/shard_map/ppermute | solution.py:303
  50.1 1.7 %collective-permute-start.12 = (f32[256,1024]{1,0:T(8,128)S(1)}, f32[256,1024]{1,0:T(8,128)S(1)}, u32[]{:S(2)}, u32[]{:S(2)}) collective-permute-start(f32[256,1024]{1,0:T(8,128)S(1)} %get-tuple-element.153), channel_id=1, source_target_pairs={{0,4},{2,6},{4,0},{6,2},{8,12},{10,14},{12,8},{14,10},{16,20},{18,... | collective-permute-start | bytes 3145736 | tf_op jit(solution)/shard_map/ppermute | solution.py:303
  53.7 9.0 %second_halves.6 = (f32[256,512]{1,0:T(8,128)S(1)}, f32[256,512]{1,0:T(8,128)S(1)}, f32[256,512]{1,0:T(8,128)S(1)}, f32[256,512]{1,0:T(8,128)S(1)}) custom-call(s32[3]{0:T(128)S(1)} %pad_add_fusion.1.place, s32[4]{0:T(128)S(1)} %get-tuple-element.143.limit, s32[4]{0:T(128)S(1)} %get-tuple-element.144.rows_live, f32[8,2,64,32,128]{4,3,2,1,0:T(8,128)} %bitcast.15, ...), custom_call_target="tpu_custom_call" | custom-call | flops 1024 | bytes 1024 | tf_op jit(solution)/shard_map/second_halves/pallas_call | solution.py:176
  63.4 9.1 %second_halves.7 = (f32[256,512]{1,0:T(8,128)S(1)}, f32[256,512]{1,0:T(8,128)S(1)}, f32[256,512]{1,0:T(8,128)S(1)}, f32[256,512]{1,0:T(8,128)S(1)}) custom-call(s32[3]{0:T(128)S(1)} %pad_add_fusion.1.place, s32[4]{0:T(128)S(1)} %get-tuple-element.143.limit, s32[4]{0:T(128)S(1)} %get-tuple-element.144.rows_live, f32[8,2,64,32,128]{4,3,2,1,0:T(8,128)} %bitcast.16, ...), custom_call_target="tpu_custom_call" | custom-call | flops 1024 | bytes 1024 | tf_op jit(solution)/shard_map/second_halves/pallas_call | solution.py:176
  72.6 3.6 %collective-permute-done.12 = f32[256,1024]{1,0:T(8,128)S(1)} collective-permute-done((f32[256,1024]{1,0:T(8,128)S(1)}, f32[256,1024]{1,0:T(8,128)S(1)}, u32[]{:S(2)}, u32[]{:S(2)}) %collective-permute-start.12) | collective-permute-done | bytes 1048608 | tf_op jit(solution)/shard_map/ppermute | solution.py:303
  78.4 3.0 %collective-permute-start.14 = (f32[128,512]{1,0:T(8,128)S(1)}, f32[128,512]{1,0:T(8,128)S(1)}, u32[]{:S(2)}, u32[]{:S(2)}) collective-permute-start(f32[128,512]{1,0:T(8,128)S(1)} %get-tuple-element.213), channel_id=1, source_target_pairs={{0,16},{2,18},{4,20},{6,22},{8,24},{10,26},{12,28},{14,30},{16,0},... | collective-permute-start | bytes 786440 | tf_op jit(solution)/shard_map/ppermute | solution.py:303
  82.8 6.4 %collective-permute-done.10 = f32[64,1024]{1,0:T(8,128)S(1)} collective-permute-done((f32[64,1024]{1,0:T(8,128)S(1)}, f32[64,1024]{1,0:T(8,128)S(1)}, u32[]{:S(2)}, u32[]{:S(2)}) %collective-permute-start.10) | collective-permute-done | bytes 262176 | tf_op jit(solution)/shard_map/ppermute | solution.py:303
  89.2 1.8 %collective-permute-start.19 = (f32[256,512]{1,0:T(8,128)S(1)}, f32[256,512]{1,0:T(8,128)S(1)}, u32[]{:S(2)}, u32[]{:S(2)}) collective-permute-start(f32[256,512]{1,0:T(8,128)S(1)} %get-tuple-element.174), channel_id=1, source_target_pairs={{0,4},{2,6},{4,0},{6,2},{8,12},{10,14},{12,8},{14,10},{16,20},{18,... | collective-permute-start | bytes 1572872 | tf_op jit(solution)/shard_map/ppermute | solution.py:303
  91.8 6.0 %collective-permute-done.14 = f32[128,512]{1,0:T(8,128)S(1)} collective-permute-done((f32[128,512]{1,0:T(8,128)S(1)}, f32[128,512]{1,0:T(8,128)S(1)}, u32[]{:S(2)}, u32[]{:S(2)}) %collective-permute-start.14) | collective-permute-done | bytes 262176 | tf_op jit(solution)/shard_map/ppermute | solution.py:303
  99.6 3.0 %collective-permute-start.16 = (f32[64,1024]{1,0:T(8,128)}, f32[64,1024]{1,0:T(8,128)}, u32[]{:S(2)}, u32[]{:S(2)}) collective-permute-start(f32[64,1024]{1,0:T(8,128)} %get-tuple-element.211), channel_id=1, source_target_pairs={{0,16},{2,18},{4,20},{6,22},{8,24},{10,26},{12,28},{14,30},{16,0},... | collective-permute-start | bytes 786440 | tf_op jit(solution)/shard_map/ppermute | solution.py:303
  106.4 5.8 %collective-permute-done.16 = f32[64,1024]{1,0:T(8,128)} collective-permute-done((f32[64,1024]{1,0:T(8,128)}, f32[64,1024]{1,0:T(8,128)}, u32[]{:S(2)}, u32[]{:S(2)}) %collective-permute-start.16) | collective-permute-done | bytes 262176 | tf_op jit(solution)/shard_map/ppermute | solution.py:303
  113.1 1.9 %collective-permute-done.20 = f32[128,512]{1,0:T(8,128)} collective-permute-done((f32[128,512]{1,0:T(8,128)}, f32[128,512]{1,0:T(8,128)}, u32[]{:S(2)}, u32[]{:S(2)}) %collective-permute-start.20) | collective-permute-done | bytes 262176 | tf_op jit(solution)/shard_map/ppermute | solution.py:303
  117.3 2.9 %collective-permute-done.22 = f32[128,512]{1,0:T(8,128)S(1)} collective-permute-done((f32[128,512]{1,0:T(8,128)S(1)}, f32[128,512]{1,0:T(8,128)S(1)}, u32[]{:S(2)}, u32[]{:S(2)}) %collective-permute-start.22) | collective-permute-done | bytes 262176 | tf_op jit(solution)/shard_map/ppermute | solution.py:303
  122.4 8.2 %collective-permute-start.26 = (f32[192,512]{1,0:T(8,128)S(1)}, f32[192,512]{1,0:T(8,128)S(1)}, u32[]{:S(2)}, u32[]{:S(2)}) collective-permute-start(f32[192,512]{1,0:T(8,128)S(1)} %pad_maximum_fusion), channel_id=1, source_target_pairs={{0,1},{1,0},{2,3},{3,2},{4,5},{5,4},{6,7},{7,6},{8,9},{9,8},{10,11... | collective-permute-start | bytes 1179656 | tf_op jit(solution)/shard_map/ppermute | solution.py:332
  130.6 3.0 %collective-permute-start.25 = (f32[64,512]{1,0:T(8,128)S(1)}, f32[64,512]{1,0:T(8,128)S(1)}, u32[]{:S(2)}, u32[]{:S(2)}) collective-permute-start(f32[64,512]{1,0:T(8,128)S(1)} %get-tuple-element.217), channel_id=1, source_target_pairs={{0,16},{2,18},{4,20},{6,22},{8,24},{10,26},{12,28},{14,30},{16,0},... | collective-permute-start | bytes 393224 | tf_op jit(solution)/shard_map/ppermute | solution.py:303
  133.7 5.1 %collective-permute-done.23 = f32[64,512]{1,0:T(8,128)S(1)} collective-permute-done((f32[64,512]{1,0:T(8,128)S(1)}, f32[64,512]{1,0:T(8,128)S(1)}, u32[]{:S(2)}, u32[]{:S(2)}) %collective-permute-start.23) | collective-permute-done | bytes 131104 | tf_op jit(solution)/shard_map/ppermute | solution.py:303
  140.3 2.2 %collective-permute-start.27 = (f32[64,512]{1,0:T(8,128)S(1)}, f32[64,512]{1,0:T(8,128)S(1)}, u32[]{:S(2)}, u32[]{:S(2)}) collective-permute-start(f32[64,512]{1,0:T(8,128)S(1)} %get-tuple-element.228), channel_id=1, source_target_pairs={{0,1},{1,0},{2,3},{3,2},{4,5},{5,4},{6,7},{7,6},{8,9},{9,8},{10,11... | collective-permute-start | bytes 393224 | tf_op jit(solution)/shard_map/ppermute | solution.py:332
  142.4 2.9 %collective-permute-done.27.refs_7_ = f32[64,512]{1,0:T(8,128)S(1)} collective-permute-done((f32[64,512]{1,0:T(8,128)S(1)}, f32[64,512]{1,0:T(8,128)S(1)}, u32[]{:S(2)}, u32[]{:S(2)}) %collective-permute-start.27) | collective-permute-done | bytes 131104 | tf_op jit(solution)/shard_map/ppermute | solution.py:332
  145.4 1.9 %place_blocks.1 = f32[64,8,512]{2,1,0:T(8,128)} custom-call(s32[1]{0:T(128)} %bitcast.side_ref, s32[2]{0:T(128)S(1)} %pad_add_fusion.base, s32[8]{0:T(128)S(1)} %copy-done, s32[8]{0:T(128)S(1)} %copy-done.1, f32[64,512]{1,0:T(8,128)S(1)} %get-tuple-element.231.refs_0_, f32[64,512]{1,0:T(8,128)S(1)} %get-tuple-element.233.refs_1_, ...), custom_call_target="tpu_custom_call" | custom-call | flops 1024 | bytes 1024 | tf_op jit(solution)/shard_map/place_blocks/pallas_call | solution.py:225
  (71 shorter events, 25.7 us)
Async XLA Ops:
  12.1 14.6 %collective-permute-start.3 = (f32[256,1024]{1,0:T(8,128)S(1)}, f32[256,1024]{1,0:T(8,128)S(1)}, u32[]{:S(2)}, u32[]{:S(2)}) collective-permute-start(f32[256,1024]{1,0:T(8,128)S(1)} %get-tuple-element.113), channel_id=1, source_target_pairs={{0,2},{2,0},{4,6},{6,4},{8,10},{10,8},{12,14},{14,12},{16,18},{18,... | collective-permute-start | bytes 3145736 | tf_op jit(solution)/shard_map/ppermute | solution.py:290
  12.5 14.1 %collective-permute-start.4 = (f32[256,1024]{1,0:T(8,128)S(1)}, f32[256,1024]{1,0:T(8,128)S(1)}, u32[]{:S(2)}, u32[]{:S(2)}) collective-permute-start(f32[256,1024]{1,0:T(8,128)S(1)} %get-tuple-element.114), channel_id=1, source_target_pairs={{0,2},{2,0},{4,6},{6,4},{8,10},{10,8},{12,14},{14,12},{16,18},{18,... | collective-permute-start | bytes 3145736 | tf_op jit(solution)/shard_map/ppermute | solution.py:290
  23.7 26.4 %collective-permute-start.2 = (f32[256,1024]{1,0:T(8,128)S(1)}, f32[256,1024]{1,0:T(8,128)S(1)}, u32[]{:S(2)}, u32[]{:S(2)}) collective-permute-start(f32[256,1024]{1,0:T(8,128)S(1)} %get-tuple-element.112), channel_id=1, source_target_pairs={{0,4},{2,6},{4,0},{6,2},{8,12},{10,14},{12,8},{14,10},{16,20},{18,... | collective-permute-start | bytes 3145736 | tf_op jit(solution)/shard_map/ppermute | solution.py:303
  47.2 6.5 %collective-permute-start.9 = (f32[256,1024]{1,0:T(8,128)S(1)}, f32[256,1024]{1,0:T(8,128)S(1)}, u32[]{:S(2)}, u32[]{:S(2)}) collective-permute-start(f32[256,1024]{1,0:T(8,128)S(1)} %get-tuple-element.133), channel_id=1, source_target_pairs={{0,2},{2,0},{4,6},{6,4},{8,10},{10,8},{12,14},{14,12},{16,18},{18,... | collective-permute-start | bytes 3145736 | tf_op jit(solution)/shard_map/ppermute | solution.py:290
  47.7 15.0 %collective-permute-start.6 = (f32[256,1024]{1,0:T(8,128)S(1)}, f32[256,1024]{1,0:T(8,128)S(1)}, u32[]{:S(2)}, u32[]{:S(2)}) collective-permute-start(f32[256,1024]{1,0:T(8,128)S(1)} %get-tuple-element.131), channel_id=1, source_target_pairs={{0,2},{2,0},{4,6},{6,4},{8,10},{10,8},{12,14},{14,12},{16,18},{18,... | collective-permute-start | bytes 3145736 | tf_op jit(solution)/shard_map/ppermute | solution.py:290
  47.8 14.9 %collective-permute-start.7 = (f32[256,1024]{1,0:T(8,128)S(1)}, f32[256,1024]{1,0:T(8,128)S(1)}, u32[]{:S(2)}, u32[]{:S(2)}) collective-permute-start(f32[256,1024]{1,0:T(8,128)S(1)} %get-tuple-element.132), channel_id=1, source_target_pairs={{0,2},{2,0},{4,6},{6,4},{8,10},{10,8},{12,14},{14,12},{16,18},{18,... | collective-permute-start | bytes 3145736 | tf_op jit(solution)/shard_map/ppermute | solution.py:290
  50.1 26.1 %collective-permute-start.12 = (f32[256,1024]{1,0:T(8,128)S(1)}, f32[256,1024]{1,0:T(8,128)S(1)}, u32[]{:S(2)}, u32[]{:S(2)}) collective-permute-start(f32[256,1024]{1,0:T(8,128)S(1)} %get-tuple-element.153), channel_id=1, source_target_pairs={{0,4},{2,6},{4,0},{6,2},{8,12},{10,14},{12,8},{14,10},{16,20},{18,... | collective-permute-start | bytes 3145736 | tf_op jit(solution)/shard_map/ppermute | solution.py:303
  52.0 20.5 %collective-permute-start.5 = (f32[128,1024]{1,0:T(8,128)S(1)}, f32[128,1024]{1,0:T(8,128)S(1)}, u32[]{:S(2)}, u32[]{:S(2)}) collective-permute-start(f32[128,1024]{1,0:T(8,128)S(1)} %get-tuple-element.203), channel_id=1, source_target_pairs={{0,8},{2,10},{4,12},{6,14},{8,0},{10,2},{12,4},{14,6},{16,24},{18,... | collective-permute-start | bytes 1572872 | tf_op jit(solution)/shard_map/ppermute | solution.py:303
  62.7 15.6 %collective-permute-start.11 = (f32[256,512]{1,0:T(8,128)S(1)}, f32[256,512]{1,0:T(8,128)S(1)}, u32[]{:S(2)}, u32[]{:S(2)}) collective-permute-start(f32[256,512]{1,0:T(8,128)S(1)} %get-tuple-element.152), channel_id=1, source_target_pairs={{0,8},{2,10},{4,12},{6,14},{8,0},{10,2},{12,4},{14,6},{16,24},{18,... | collective-permute-start | bytes 1572872 | tf_op jit(solution)/shard_map/ppermute | solution.py:303
  62.8 28.2 %collective-permute-start.15 = (f32[256,512]{1,0:T(8,128)S(1)}, f32[256,512]{1,0:T(8,128)S(1)}, u32[]{:S(2)}, u32[]{:S(2)}) collective-permute-start(f32[256,512]{1,0:T(8,128)S(1)} %get-tuple-element.161), channel_id=1, source_target_pairs={{0,4},{2,6},{4,0},{6,2},{8,12},{10,14},{12,8},{14,10},{16,20},{18,... | collective-permute-start | bytes 1572872 | tf_op jit(solution)/shard_map/ppermute | solution.py:303
  76.2 13.0 %collective-permute-start.10 = (f32[64,1024]{1,0:T(8,128)S(1)}, f32[64,1024]{1,0:T(8,128)S(1)}, u32[]{:S(2)}, u32[]{:S(2)}) collective-permute-start(f32[64,1024]{1,0:T(8,128)S(1)} %get-tuple-element.215), channel_id=1, source_target_pairs={{0,16},{2,18},{4,20},{6,22},{8,24},{10,26},{12,28},{14,30},{16,0},... | collective-permute-start | bytes 786440 | tf_op jit(solution)/shard_map/ppermute | solution.py:303
  77.3 21.5 %collective-permute-start.13 = (f32[128,1024]{1,0:T(8,128)S(1)}, f32[128,1024]{1,0:T(8,128)S(1)}, u32[]{:S(2)}, u32[]{:S(2)}) collective-permute-start(f32[128,1024]{1,0:T(8,128)S(1)} %get-tuple-element.201), channel_id=1, source_target_pairs={{0,8},{2,10},{4,12},{6,14},{8,0},{10,2},{12,4},{14,6},{16,24},{18,... | collective-permute-start | bytes 1572872 | tf_op jit(solution)/shard_map/ppermute | solution.py:303
  78.4 19.4 %collective-permute-start.14 = (f32[128,512]{1,0:T(8,128)S(1)}, f32[128,512]{1,0:T(8,128)S(1)}, u32[]{:S(2)}, u32[]{:S(2)}) collective-permute-start(f32[128,512]{1,0:T(8,128)S(1)} %get-tuple-element.213), channel_id=1, source_target_pairs={{0,16},{2,18},{4,20},{6,22},{8,24},{10,26},{12,28},{14,30},{16,0},... | collective-permute-start | bytes 786440 | tf_op jit(solution)/shard_map/ppermute | solution.py:303
  81.3 22.8 %collective-permute-start.17 = (f32[256,512]{1,0:T(8,128)S(1)}, f32[256,512]{1,0:T(8,128)}, u32[]{:S(2)}, u32[]{:S(2)}) collective-permute-start(f32[256,512]{1,0:T(8,128)S(1)} %get-tuple-element.168), channel_id=1, source_target_pairs={{0,4},{2,6},{4,0},{6,2},{8,12},{10,14},{12,8},{14,10},{16,20},{18,... | collective-permute-start | bytes 1572872 | tf_op jit(solution)/shard_map/ppermute | solution.py:303
  89.2 26.9 %collective-permute-start.19 = (f32[256,512]{1,0:T(8,128)S(1)}, f32[256,512]{1,0:T(8,128)S(1)}, u32[]{:S(2)}, u32[]{:S(2)}) collective-permute-start(f32[256,512]{1,0:T(8,128)S(1)} %get-tuple-element.174), channel_id=1, source_target_pairs={{0,4},{2,6},{4,0},{6,2},{8,12},{10,14},{12,8},{14,10},{16,20},{18,... | collective-permute-start | bytes 1572872 | tf_op jit(solution)/shard_map/ppermute | solution.py:303
  99.6 12.6 %collective-permute-start.16 = (f32[64,1024]{1,0:T(8,128)}, f32[64,1024]{1,0:T(8,128)}, u32[]{:S(2)}, u32[]{:S(2)}) collective-permute-start(f32[64,1024]{1,0:T(8,128)} %get-tuple-element.211), channel_id=1, source_target_pairs={{0,16},{2,18},{4,20},{6,22},{8,24},{10,26},{12,28},{14,30},{16,0},... | collective-permute-start | bytes 786440 | tf_op jit(solution)/shard_map/ppermute | solution.py:303
  102.6 12.4 %collective-permute-start.20 = (f32[128,512]{1,0:T(8,128)}, f32[128,512]{1,0:T(8,128)}, u32[]{:S(2)}, u32[]{:S(2)}) collective-permute-start(f32[128,512]{1,0:T(8,128)} %get-tuple-element.209), channel_id=1, source_target_pairs={{0,8},{2,10},{4,12},{6,14},{8,0},{10,2},{12,4},{14,6},{16,24},{18,... | collective-permute-start | bytes 786440 | tf_op jit(solution)/shard_map/ppermute | solution.py:303
  102.6 13.5 %collective-permute-start.18 = (f32[64,512]{1,0:T(8,128)}, f32[64,512]{1,0:T(8,128)S(1)}, u32[]{:S(2)}, u32[]{:S(2)}) collective-permute-start(f32[64,512]{1,0:T(8,128)} %get-tuple-element.223), channel_id=1, source_target_pairs={{0,4},{2,6},{4,0},{6,2},{8,12},{10,14},{12,8},{14,10},{16,20},{18,... | collective-permute-start | bytes 393224 | tf_op jit(solution)/shard_map/ppermute | solution.py:303
  105.2 15.0 %collective-permute-start.22 = (f32[128,512]{1,0:T(8,128)S(1)}, f32[128,512]{1,0:T(8,128)S(1)}, u32[]{:S(2)}, u32[]{:S(2)}) collective-permute-start(f32[128,512]{1,0:T(8,128)S(1)} %get-tuple-element.207), channel_id=1, source_target_pairs={{0,8},{2,10},{4,12},{6,14},{8,0},{10,2},{12,4},{14,6},{16,24},{18,... | collective-permute-start | bytes 786440 | tf_op jit(solution)/shard_map/ppermute | solution.py:303
  116.2 6.0 %collective-permute-start.21 = (f32[64,512]{1,0:T(8,128)S(1)}, f32[64,512]{1,0:T(8,128)S(1)}, u32[]{:S(2)}, u32[]{:S(2)}) collective-permute-start(f32[64,512]{1,0:T(8,128)S(1)} %get-tuple-element.221), channel_id=1, source_target_pairs={{0,16},{2,18},{4,20},{6,22},{8,24},{10,26},{12,28},{14,30},{16,0},... | collective-permute-start | bytes 393224 | tf_op jit(solution)/shard_map/ppermute | solution.py:303
  120.2 10.4 %collective-permute-start.24 = (f32[128,512]{1,0:T(8,128)S(1)}, f32[128,512]{1,0:T(8,128)S(1)}, u32[]{:S(2)}, u32[]{:S(2)}) collective-permute-start(f32[128,512]{1,0:T(8,128)S(1)} %get-tuple-element.205), channel_id=1, source_target_pairs={{0,8},{2,10},{4,12},{6,14},{8,0},{10,2},{12,4},{14,6},{16,24},{18,... | collective-permute-start | bytes 786440 | tf_op jit(solution)/shard_map/ppermute | solution.py:303
  122.4 17.8 %collective-permute-start.26 = (f32[192,512]{1,0:T(8,128)S(1)}, f32[192,512]{1,0:T(8,128)S(1)}, u32[]{:S(2)}, u32[]{:S(2)}) collective-permute-start(f32[192,512]{1,0:T(8,128)S(1)} %pad_maximum_fusion), channel_id=1, source_target_pairs={{0,1},{1,0},{2,3},{3,2},{4,5},{5,4},{6,7},{7,6},{8,9},{9,8},{10,11... | collective-permute-start | bytes 1179656 | tf_op jit(solution)/shard_map/ppermute | solution.py:332
  130.6 8.2 %collective-permute-start.23 = (f32[64,512]{1,0:T(8,128)S(1)}, f32[64,512]{1,0:T(8,128)S(1)}, u32[]{:S(2)}, u32[]{:S(2)}) collective-permute-start(f32[64,512]{1,0:T(8,128)S(1)} %get-tuple-element.219), channel_id=1, source_target_pairs={{0,16},{2,18},{4,20},{6,22},{8,24},{10,26},{12,28},{14,30},{16,0},... | collective-permute-start | bytes 393224 | tf_op jit(solution)/shard_map/ppermute | solution.py:303
  130.6 9.6 %collective-permute-start.25 = (f32[64,512]{1,0:T(8,128)S(1)}, f32[64,512]{1,0:T(8,128)S(1)}, u32[]{:S(2)}, u32[]{:S(2)}) collective-permute-start(f32[64,512]{1,0:T(8,128)S(1)} %get-tuple-element.217), channel_id=1, source_target_pairs={{0,16},{2,18},{4,20},{6,22},{8,24},{10,26},{12,28},{14,30},{16,0},... | collective-permute-start | bytes 393224 | tf_op jit(solution)/shard_map/ppermute | solution.py:303
  (6 other events, 162.4 us)

commit v9 on v8

--- a/solution.py
+++ b/solution.py
@@ -336,12 +336,12 @@
 
     if inner == 2 and rep == 2 and blocks == 4:
         half = rows // 2
-        chunks = [(0, 0, rows, False), (1, 0, rows, False), (2, 0, half, True),
-                  (2, half, half, False), (3, 0, half, False), (3, half, half, False)]
+        chunks = [(0, 0, rows, False), (1, 0, half, True), (1, half, half, False),
+                  (2, 0, rows, False), (3, 0, half, False), (3, half, half, False)]
         firsts = {"p": [0, 1], "q": [2, 3]}
-        seconds = {"w": [0], "x": [1], "y": [2, 3], "z": [4, 5]}
+        seconds = {"w": [0], "x": [1, 2], "y": [3], "z": [4, 5]}
         groups = {"a": [0, 1, 2], "d": [3]}
-        plan = "pwxq0yz01203214135243a545Ad"
+        plan = "pwxq0y12z012032143543a545Ad"
     else:
         chunks = [(h, 0, rows, False) for h in range(blocks)]
         firsts = {"p": list(range(blocks))}

time: 147 us -> 151 us (1.027)
  waiting for transfers between devices: 43 us -> 52.3 us
  starting transfers between devices: 37.8 us -> 30.3 us
    ppermute x18, waiting for transfers between devices: 36.9 us -> 46.2 us  [work(): got = lax.ppermute(send, 'tensor', pairs)]
    ppermute x18, starting transfers between devices: 25.2 us -> 20.8 us  [work(): got = lax.ppermute(send, 'tensor', pairs)]
    ppermute x2, starting transfers between devices: 10.4 us -> 7.34 us  [exchange(): got = lax.ppermute(away, 'rep', [(0, 1), (1, 0)])]
  transfers between devices with their start and end apart: 28 -> 28, of which waited for: 14 -> 13; matrix products, arithmetic and copies ran while one was open for 4% -> 5% of each run, Pallas kernels for 32% -> 30%
where the time goes in v9:
time: 151 us; the launch traced here: 150 us
  Pallas kernels  58.9 us (39%)
  waiting for transfers between devices  52.3 us (35%)
  starting transfers between devices  30.3 us (20%)
  other arithmetic  8.2 us (5%)
    pallas_call x6, Pallas kernels, products(): pl.pallas_call(functools.partial(products_kernel, first, inner, chunks, l...  57.1 us
    ppermute x18, waiting for transfers between devices, work(): got = lax.ppermute(send, 'tensor', pairs)  46.2 us
    ppermute x18, starting transfers between devices, work(): got = lax.ppermute(send, 'tensor', pairs)  20.8 us
    ppermute x2, starting transfers between devices, exchange(): got = lax.ppermute(away, 'rep', [(0, 1), (1, 0)])  7.34 us
    add x12, other arithmetic, work(): a[half:] + b[half:]  5.17 us
    ppermute x8, waiting for transfers between devices, first_halves(): lax.ppermute(part, 'tensor', across)  3.21 us
  transfers between devices with their start and end apart: 28, of which 13 were waited for; matrix products, arithmetic and copies ran while one was open for 5% of the time, Pallas kernels for 30%

profile of v9, /device:TPU:0, one launch (start us, length us, event | category | flops | bytes accessed | tf_op | source)
XLA Modules:
  0.0 150.2 jit_solution(13725162974333551464)
XLA Ops:
  0.8 12.6 %first_halves.2 = (f32[256,1024]{1,0:T(8,128)S(1)}, f32[256,1024]{1,0:T(8,128)S(1)}, f32[256,1024]{1,0:T(8,128)S(1)}, f32[256,1024]{1,0:T(8,128)S(1)}) custom-call(s32[3]{0:T(128)S(1)} %pad_add_fusion.1.place, s32[4]{0:T(128)S(1)} %get-tuple-element.150.limit, s32[4]{0:T(128)S(1)} %get-tuple-element.151.rows_live, f32[8,2,64,32,128]{4,3,2,1,0:T(8,128)} %bitcast.11, ...), custom_call_target="tpu_custom_call" | custom-call | flops 1024 | bytes 1024 | tf_op jit(solution)/shard_map/first_halves/pallas_call | solution.py:176
  17.7 8.9 %second_halves.4 = (f32[256,1024]{1,0:T(8,128)S(1)}, f32[256,1024]{1,0:T(8,128)S(1)}) custom-call(s32[3]{0:T(128)S(1)} %pad_add_fusion.1.place, s32[4]{0:T(128)S(1)} %get-tuple-element.150.limit, s32[4]{0:T(128)S(1)} %get-tuple-element.151.rows_live, f32[8,2,64,32,128]{4,3,2,1,0:T(8,128)} %bitcast.12, f32[4,1024,1024]{2,1,0:T(8,128)} %a_hbm.6, ...), custom_call_target="tpu_custom_call" | custom-call | flops 1024 | bytes 1024 | tf_op jit(solution)/shard_map/second_halves/pallas_call | solution.py:176
  26.6 2.9 %collective-permute-start.2 = (f32[256,1024]{1,0:T(8,128)S(1)}, f32[256,1024]{1,0:T(8,128)S(1)}, u32[]{:S(2)}, u32[]{:S(2)}) collective-permute-start(f32[256,1024]{1,0:T(8,128)S(1)} %get-tuple-element.112), channel_id=1, source_target_pairs={{0,4},{2,6},{4,0},{6,2},{8,12},{10,14},{12,8},{14,10},{16,20},{18,... | collective-permute-start | bytes 3145736 | tf_op jit(solution)/shard_map/ppermute | solution.py:303
  29.5 8.0 %second_halves.5 = (f32[256,512]{1,0:T(8,128)S(1)}, f32[256,512]{1,0:T(8,128)S(1)}, f32[256,512]{1,0:T(8,128)S(1)}, f32[256,512]{1,0:T(8,128)S(1)}) custom-call(s32[3]{0:T(128)S(1)} %pad_add_fusion.1.place, s32[4]{0:T(128)S(1)} %get-tuple-element.150.limit, s32[4]{0:T(128)S(1)} %get-tuple-element.151.rows_live, f32[8,2,64,32,128]{4,3,2,1,0:T(8,128)} %bitcast.13, ...), custom_call_target="tpu_custom_call" | custom-call | flops 1024 | bytes 1024 | tf_op jit(solution)/shard_map/second_halves/pallas_call | solution.py:176
  37.6 11.6 %first_halves.3 = (f32[256,1024]{1,0:T(8,128)S(1)}, f32[256,1024]{1,0:T(8,128)S(1)}, f32[256,1024]{1,0:T(8,128)S(1)}, f32[256,1024]{1,0:T(8,128)S(1)}) custom-call(s32[3]{0:T(128)S(1)} %pad_add_fusion.1.place, s32[4]{0:T(128)S(1)} %get-tuple-element.150.limit, s32[4]{0:T(128)S(1)} %get-tuple-element.151.rows_live, f32[8,2,64,32,128]{4,3,2,1,0:T(8,128)} %bitcast.14, ...), custom_call_target="tpu_custom_call" | custom-call | flops 1024 | bytes 1024 | tf_op jit(solution)/shard_map/first_halves/pallas_call | solution.py:176
  50.3 2.7 %collective-permute-done.2 = f32[256,1024]{1,0:T(8,128)S(1)} collective-permute-done((f32[256,1024]{1,0:T(8,128)S(1)}, f32[256,1024]{1,0:T(8,128)S(1)}, u32[]{:S(2)}, u32[]{:S(2)}) %collective-permute-start.2) | collective-permute-done | bytes 1048608 | tf_op jit(solution)/shard_map/ppermute | solution.py:303
  54.9 2.1 %collective-permute-start.5 = (f32[128,1024]{1,0:T(8,128)S(1)}, f32[128,1024]{1,0:T(8,128)S(1)}, u32[]{:S(2)}, u32[]{:S(2)}) collective-permute-start(f32[128,1024]{1,0:T(8,128)S(1)} %get-tuple-element.203), channel_id=1, source_target_pairs={{0,8},{2,10},{4,12},{6,14},{8,0},{10,2},{12,4},{14,6},{16,24},{18,... | collective-permute-start | bytes 1572872 | tf_op jit(solution)/shard_map/ppermute | solution.py:303
  57.0 7.9 %second_halves.6 = (f32[256,1024]{1,0:T(8,128)S(1)}, f32[256,1024]{1,0:T(8,128)S(1)}) custom-call(s32[3]{0:T(128)S(1)} %pad_add_fusion.1.place, s32[4]{0:T(128)S(1)} %get-tuple-element.150.limit, s32[4]{0:T(128)S(1)} %get-tuple-element.151.rows_live, f32[8,2,64,32,128]{4,3,2,1,0:T(8,128)} %bitcast.15, f32[4,1024,1024]{2,1,0:T(8,128)} %a_hbm.6, ...), custom_call_target="tpu_custom_call" | custom-call | flops 1024 | bytes 1024 | tf_op jit(solution)/shard_map/second_halves/pallas_call | solution.py:176
  64.9 2.9 %collective-permute-done.9 = f32[256,512]{1,0:T(8,128)S(1)} collective-permute-done((f32[256,512]{1,0:T(8,128)S(1)}, f32[256,512]{1,0:T(8,128)S(1)}, u32[]{:S(2)}, u32[]{:S(2)}) %collective-permute-start.9) | collective-permute-done | bytes 524320 | tf_op jit(solution)/shard_map/ppermute | solution.py:303
  67.8 1.8 %collective-permute-start.17 = (f32[256,1024]{1,0:T(8,128)S(1)}, f32[256,1024]{1,0:T(8,128)S(1)}, u32[]{:S(2)}, u32[]{:S(2)}) collective-permute-start(f32[256,1024]{1,0:T(8,128)S(1)} %get-tuple-element.165), channel_id=1, source_target_pairs={{0,4},{2,6},{4,0},{6,2},{8,12},{10,14},{12,8},{14,10},{16,20},{18,... | collective-permute-start | bytes 3145736 | tf_op jit(solution)/shard_map/ppermute | solution.py:303
  69.9 8.1 %second_halves.7 = (f32[256,512]{1,0:T(8,128)S(1)}, f32[256,512]{1,0:T(8,128)S(1)}, f32[256,512]{1,0:T(8,128)S(1)}, f32[256,512]{1,0:T(8,128)S(1)}) custom-call(s32[3]{0:T(128)S(1)} %pad_add_fusion.1.place, s32[4]{0:T(128)S(1)} %get-tuple-element.150.limit, s32[4]{0:T(128)S(1)} %get-tuple-element.151.rows_live, f32[8,2,64,32,128]{4,3,2,1,0:T(8,128)} %bitcast.16, ...), custom_call_target="tpu_custom_call" | custom-call | flops 1024 | bytes 1024 | tf_op jit(solution)/shard_map/second_halves/pallas_call | solution.py:176
  78.4 6.3 %collective-permute-done.5 = f32[128,1024]{1,0:T(8,128)S(1)} collective-permute-done((f32[128,1024]{1,0:T(8,128)S(1)}, f32[128,1024]{1,0:T(8,128)S(1)}, u32[]{:S(2)}, u32[]{:S(2)}) %collective-permute-start.5) | collective-permute-done | bytes 524320 | tf_op jit(solution)/shard_map/ppermute | solution.py:303
  85.6 4.3 %collective-permute-done.13 = f32[128,512]{1,0:T(8,128)S(1)} collective-permute-done((f32[128,512]{1,0:T(8,128)S(1)}, f32[128,512]{1,0:T(8,128)S(1)}, u32[]{:S(2)}, u32[]{:S(2)}) %collective-permute-start.13) | collective-permute-done | bytes 262176 | tf_op jit(solution)/shard_map/ppermute | solution.py:303
  90.6 5.3 %collective-permute-done.12 = f32[64,1024]{1,0:T(8,128)S(1)} collective-permute-done((f32[64,1024]{1,0:T(8,128)S(1)}, f32[64,1024]{1,0:T(8,128)S(1)}, u32[]{:S(2)}, u32[]{:S(2)}) %collective-permute-start.12) | collective-permute-done | bytes 262176 | tf_op jit(solution)/shard_map/ppermute | solution.py:303
  100.5 10.2 %collective-permute-done.16 = f32[64,512]{1,0:T(8,128)} collective-permute-done((f32[64,512]{1,0:T(8,128)}, f32[64,512]{1,0:T(8,128)}, u32[]{:S(2)}, u32[]{:S(2)}) %collective-permute-start.16) | collective-permute-done | bytes 131104 | tf_op jit(solution)/shard_map/ppermute | solution.py:303
  112.7 2.1 %collective-permute-start.21 = (f32[128,512]{1,0:T(8,128)S(1)}, f32[128,512]{1,0:T(8,128)S(1)}, u32[]{:S(2)}, u32[]{:S(2)}) collective-permute-start(f32[128,512]{1,0:T(8,128)S(1)} %get-tuple-element.207), channel_id=1, source_target_pairs={{0,8},{2,10},{4,12},{6,14},{8,0},{10,2},{12,4},{14,6},{16,24},{18,... | collective-permute-start | bytes 786440 | tf_op jit(solution)/shard_map/ppermute | solution.py:303
  118.5 8.8 %collective-permute-done.21 = f32[128,512]{1,0:T(8,128)S(1)} collective-permute-done((f32[128,512]{1,0:T(8,128)S(1)}, f32[128,512]{1,0:T(8,128)S(1)}, u32[]{:S(2)}, u32[]{:S(2)}) %collective-permute-start.21) | collective-permute-done | bytes 262176 | tf_op jit(solution)/shard_map/ppermute | solution.py:303
  127.5 3.5 %collective-permute-start.26 = (f32[192,512]{1,0:T(8,128)S(1)}, f32[192,512]{1,0:T(8,128)S(1)}, u32[]{:S(2)}, u32[]{:S(2)}) collective-permute-start(f32[192,512]{1,0:T(8,128)S(1)} %pad_maximum_fusion), channel_id=1, source_target_pairs={{0,1},{1,0},{2,3},{3,2},{4,5},{5,4},{6,7},{7,6},{8,9},{9,8},{10,11... | collective-permute-start | bytes 1179656 | tf_op jit(solution)/shard_map/ppermute | solution.py:332
  131.0 2.9 %collective-permute-start.23 = (f32[64,512]{1,0:T(8,128)S(1)}, f32[64,512]{1,0:T(8,128)S(1)}, u32[]{:S(2)}, u32[]{:S(2)}) collective-permute-start(f32[64,512]{1,0:T(8,128)S(1)} %get-tuple-element.219), channel_id=1, source_target_pairs={{0,16},{2,18},{4,20},{6,22},{8,24},{10,26},{12,28},{14,30},{16,0},... | collective-permute-start | bytes 393224 | tf_op jit(solution)/shard_map/ppermute | solution.py:303
  136.8 1.8 %collective-permute-done.23 = f32[64,512]{1,0:T(8,128)S(1)} collective-permute-done((f32[64,512]{1,0:T(8,128)S(1)}, f32[64,512]{1,0:T(8,128)S(1)}, u32[]{:S(2)}, u32[]{:S(2)}) %collective-permute-start.23) | collective-permute-done | bytes 131104 | tf_op jit(solution)/shard_map/ppermute | solution.py:303
  138.6 2.9 %collective-permute-done.25 = f32[64,512]{1,0:T(8,128)S(1)} collective-permute-done((f32[64,512]{1,0:T(8,128)S(1)}, f32[64,512]{1,0:T(8,128)S(1)}, u32[]{:S(2)}, u32[]{:S(2)}) %collective-permute-start.25) | collective-permute-done | bytes 131104 | tf_op jit(solution)/shard_map/ppermute | solution.py:303
  141.5 3.9 %collective-permute-start.27 = (f32[64,512]{1,0:T(8,128)S(1)}, f32[64,512]{1,0:T(8,128)S(1)}, u32[]{:S(2)}, u32[]{:S(2)}) collective-permute-start(f32[64,512]{1,0:T(8,128)S(1)} %get-tuple-element.228), channel_id=1, source_target_pairs={{0,1},{1,0},{2,3},{3,2},{4,5},{5,4},{6,7},{7,6},{8,9},{9,8},{10,11... | collective-permute-start | bytes 393224 | tf_op jit(solution)/shard_map/ppermute | solution.py:332
  145.4 2.9 %collective-permute-done.27.refs_7_ = f32[64,512]{1,0:T(8,128)S(1)} collective-permute-done((f32[64,512]{1,0:T(8,128)S(1)}, f32[64,512]{1,0:T(8,128)S(1)}, u32[]{:S(2)}, u32[]{:S(2)}) %collective-permute-start.27) | collective-permute-done | bytes 131104 | tf_op jit(solution)/shard_map/ppermute | solution.py:332
  148.4 1.9 %place_blocks.1 = f32[64,8,512]{2,1,0:T(8,128)} custom-call(s32[1]{0:T(128)} %bitcast.side_ref, s32[2]{0:T(128)S(1)} %pad_add_fusion.base, s32[8]{0:T(128)S(1)} %copy-done, s32[8]{0:T(128)S(1)} %copy-done.1, f32[64,512]{1,0:T(8,128)S(1)} %get-tuple-element.231.refs_0_, f32[64,512]{1,0:T(8,128)S(1)} %get-tuple-element.233.refs_1_, ...), custom_call_target="tpu_custom_call" | custom-call | flops 1024 | bytes 1024 | tf_op jit(solution)/shard_map/place_blocks/pallas_call | solution.py:225
  (71 shorter events, 23.8 us)
Async XLA Ops:
  14.0 15.5 %collective-permute-start.3 = (f32[256,1024]{1,0:T(8,128)S(1)}, f32[256,1024]{1,0:T(8,128)S(1)}, u32[]{:S(2)}, u32[]{:S(2)}) collective-permute-start(f32[256,1024]{1,0:T(8,128)S(1)} %get-tuple-element.113), channel_id=1, source_target_pairs={{0,2},{2,0},{4,6},{6,4},{8,10},{10,8},{12,14},{14,12},{16,18},{18,... | collective-permute-start | bytes 3145736 | tf_op jit(solution)/shard_map/ppermute | solution.py:290
  14.4 15.1 %collective-permute-start.4 = (f32[256,1024]{1,0:T(8,128)S(1)}, f32[256,1024]{1,0:T(8,128)S(1)}, u32[]{:S(2)}, u32[]{:S(2)}) collective-permute-start(f32[256,1024]{1,0:T(8,128)S(1)} %get-tuple-element.114), channel_id=1, source_target_pairs={{0,2},{2,0},{4,6},{6,4},{8,10},{10,8},{12,14},{14,12},{16,18},{18,... | collective-permute-start | bytes 3145736 | tf_op jit(solution)/shard_map/ppermute | solution.py:290
  26.6 26.4 %collective-permute-start.2 = (f32[256,1024]{1,0:T(8,128)S(1)}, f32[256,1024]{1,0:T(8,128)S(1)}, u32[]{:S(2)}, u32[]{:S(2)}) collective-permute-start(f32[256,1024]{1,0:T(8,128)S(1)} %get-tuple-element.112), channel_id=1, source_target_pairs={{0,4},{2,6},{4,0},{6,2},{8,12},{10,14},{12,8},{14,10},{16,20},{18,... | collective-permute-start | bytes 3145736 | tf_op jit(solution)/shard_map/ppermute | solution.py:303
  49.8 20.1 %collective-permute-start.6 = (f32[256,1024]{1,0:T(8,128)S(1)}, f32[256,1024]{1,0:T(8,128)S(1)}, u32[]{:S(2)}, u32[]{:S(2)}) collective-permute-start(f32[256,1024]{1,0:T(8,128)S(1)} %get-tuple-element.131), channel_id=1, source_target_pairs={{0,2},{2,0},{4,6},{6,4},{8,10},{10,8},{12,14},{14,12},{16,18},{18,... | collective-permute-start | bytes 3145736 | tf_op jit(solution)/shard_map/ppermute | solution.py:290
  49.8 20.0 %collective-permute-start.7 = (f32[256,1024]{1,0:T(8,128)S(1)}, f32[256,1024]{1,0:T(8,128)S(1)}, u32[]{:S(2)}, u32[]{:S(2)}) collective-permute-start(f32[256,1024]{1,0:T(8,128)S(1)} %get-tuple-element.132), channel_id=1, source_target_pairs={{0,2},{2,0},{4,6},{6,4},{8,10},{10,8},{12,14},{14,12},{16,18},{18,... | collective-permute-start | bytes 3145736 | tf_op jit(solution)/shard_map/ppermute | solution.py:290
  53.0 14.8 %collective-permute-start.9 = (f32[256,512]{1,0:T(8,128)S(1)}, f32[256,512]{1,0:T(8,128)S(1)}, u32[]{:S(2)}, u32[]{:S(2)}) collective-permute-start(f32[256,512]{1,0:T(8,128)S(1)} %get-tuple-element.135), channel_id=1, source_target_pairs={{0,8},{2,10},{4,12},{6,14},{8,0},{10,2},{12,4},{14,6},{16,24},{18,... | collective-permute-start | bytes 1572872 | tf_op jit(solution)/shard_map/ppermute | solution.py:303
  53.0 16.7 %collective-permute-start.8 = (f32[256,512]{1,0:T(8,128)S(1)}, f32[256,512]{1,0:T(8,128)S(1)}, u32[]{:S(2)}, u32[]{:S(2)}) collective-permute-start(f32[256,512]{1,0:T(8,128)S(1)} %get-tuple-element.134), channel_id=1, source_target_pairs={{0,4},{2,6},{4,0},{6,2},{8,12},{10,14},{12,8},{14,10},{16,20},{18,... | collective-permute-start | bytes 1572872 | tf_op jit(solution)/shard_map/ppermute | solution.py:303
  54.9 29.8 %collective-permute-start.5 = (f32[128,1024]{1,0:T(8,128)S(1)}, f32[128,1024]{1,0:T(8,128)S(1)}, u32[]{:S(2)}, u32[]{:S(2)}) collective-permute-start(f32[128,1024]{1,0:T(8,128)S(1)} %get-tuple-element.203), channel_id=1, source_target_pairs={{0,8},{2,10},{4,12},{6,14},{8,0},{10,2},{12,4},{14,6},{16,24},{18,... | collective-permute-start | bytes 1572872 | tf_op jit(solution)/shard_map/ppermute | solution.py:303
  67.8 28.1 %collective-permute-start.17 = (f32[256,1024]{1,0:T(8,128)S(1)}, f32[256,1024]{1,0:T(8,128)S(1)}, u32[]{:S(2)}, u32[]{:S(2)}) collective-permute-start(f32[256,1024]{1,0:T(8,128)S(1)} %get-tuple-element.165), channel_id=1, source_target_pairs={{0,4},{2,6},{4,0},{6,2},{8,12},{10,14},{12,8},{14,10},{16,20},{18,... | collective-permute-start | bytes 3145736 | tf_op jit(solution)/shard_map/ppermute | solution.py:303
  69.7 15.2 %collective-permute-start.14 = (f32[128,512]{1,0:T(8,128)S(1)}, f32[128,512]{1,0:T(8,128)S(1)}, u32[]{:S(2)}, u32[]{:S(2)}) collective-permute-start(f32[128,512]{1,0:T(8,128)S(1)} %get-tuple-element.211), channel_id=1, source_target_pairs={{0,16},{2,18},{4,20},{6,22},{8,24},{10,26},{12,28},{14,30},{16,0},... | collective-permute-start | bytes 786440 | tf_op jit(solution)/shard_map/ppermute | solution.py:303
  69.9 20.0 %collective-permute-start.13 = (f32[128,512]{1,0:T(8,128)S(1)}, f32[128,512]{1,0:T(8,128)S(1)}, u32[]{:S(2)}, u32[]{:S(2)}) collective-permute-start(f32[128,512]{1,0:T(8,128)S(1)} %get-tuple-element.213), channel_id=1, source_target_pairs={{0,8},{2,10},{4,12},{6,14},{8,0},{10,2},{12,4},{14,6},{16,24},{18,... | collective-permute-start | bytes 786440 | tf_op jit(solution)/shard_map/ppermute | solution.py:303
  78.1 34.6 %collective-permute-start.19 = (f32[256,512]{1,0:T(8,128)S(1)}, f32[256,512]{1,0:T(8,128)S(1)}, u32[]{:S(2)}, u32[]{:S(2)}) collective-permute-start(f32[256,512]{1,0:T(8,128)S(1)} %get-tuple-element.172), channel_id=1, source_target_pairs={{0,4},{2,6},{4,0},{6,2},{8,12},{10,14},{12,8},{14,10},{16,20},{18,... | collective-permute-start | bytes 1572872 | tf_op jit(solution)/shard_map/ppermute | solution.py:303
  84.7 11.1 %collective-permute-start.12 = (f32[64,1024]{1,0:T(8,128)S(1)}, f32[64,1024]{1,0:T(8,128)S(1)}, u32[]{:S(2)}, u32[]{:S(2)}) collective-permute-start(f32[64,1024]{1,0:T(8,128)S(1)} %get-tuple-element.215), channel_id=1, source_target_pairs={{0,16},{2,18},{4,20},{6,22},{8,24},{10,26},{12,28},{14,30},{16,0},... | collective-permute-start | bytes 786440 | tf_op jit(solution)/shard_map/ppermute | solution.py:303
  96.8 18.0 %collective-permute-start.18 = (f32[128,1024]{1,0:T(8,128)}, f32[128,1024]{1,0:T(8,128)}, u32[]{:S(2)}, u32[]{:S(2)}) collective-permute-start(f32[128,1024]{1,0:T(8,128)} %get-tuple-element.201), channel_id=1, source_target_pairs={{0,8},{2,10},{4,12},{6,14},{8,0},{10,2},{12,4},{14,6},{16,24},{18,... | collective-permute-start | bytes 1572872 | tf_op jit(solution)/shard_map/ppermute | solution.py:303
  96.8 13.9 %collective-permute-start.16 = (f32[64,512]{1,0:T(8,128)}, f32[64,512]{1,0:T(8,128)}, u32[]{:S(2)}, u32[]{:S(2)}) collective-permute-start(f32[64,512]{1,0:T(8,128)} %get-tuple-element.221), channel_id=1, source_target_pairs={{0,16},{2,18},{4,20},{6,22},{8,24},{10,26},{12,28},{14,30},{16,0},... | collective-permute-start | bytes 393224 | tf_op jit(solution)/shard_map/ppermute | solution.py:303
  98.5 13.3 %collective-permute-start.15 = (f32[64,512]{1,0:T(8,128)}, f32[64,512]{1,0:T(8,128)}, u32[]{:S(2)}, u32[]{:S(2)}) collective-permute-start(f32[64,512]{1,0:T(8,128)} %get-tuple-element.223), channel_id=1, source_target_pairs={{0,4},{2,6},{4,0},{6,2},{8,12},{10,14},{12,8},{14,10},{16,20},{18,... | collective-permute-start | bytes 393224 | tf_op jit(solution)/shard_map/ppermute | solution.py:303
  100.0 15.9 %collective-permute-start.22 = (f32[256,512]{1,0:T(8,128)S(1)}, f32[256,512]{1,0:T(8,128)}, u32[]{:S(2)}, u32[]{:S(2)}) collective-permute-start(f32[256,512]{1,0:T(8,128)S(1)} %get-tuple-element.178), channel_id=1, source_target_pairs={{0,4},{2,6},{4,0},{6,2},{8,12},{10,14},{12,8},{14,10},{16,20},{18,... | collective-permute-start | bytes 1572872 | tf_op jit(solution)/shard_map/ppermute | solution.py:303
  112.7 14.5 %collective-permute-start.21 = (f32[128,512]{1,0:T(8,128)S(1)}, f32[128,512]{1,0:T(8,128)S(1)}, u32[]{:S(2)}, u32[]{:S(2)}) collective-permute-start(f32[128,512]{1,0:T(8,128)S(1)} %get-tuple-element.207), channel_id=1, source_target_pairs={{0,8},{2,10},{4,12},{6,14},{8,0},{10,2},{12,4},{14,6},{16,24},{18,... | collective-permute-start | bytes 786440 | tf_op jit(solution)/shard_map/ppermute | solution.py:303
  115.9 11.4 %collective-permute-start.20 = (f32[64,1024]{1,0:T(8,128)S(1)}, f32[64,1024]{1,0:T(8,128)S(1)}, u32[]{:S(2)}, u32[]{:S(2)}) collective-permute-start(f32[64,1024]{1,0:T(8,128)S(1)} %get-tuple-element.209), channel_id=1, source_target_pairs={{0,16},{2,18},{4,20},{6,22},{8,24},{10,26},{12,28},{14,30},{16,0},... | collective-permute-start | bytes 786440 | tf_op jit(solution)/shard_map/ppermute | solution.py:303
  127.3 7.8 %collective-permute-start.24 = (f32[128,512]{1,0:T(8,128)S(1)}, f32[128,512]{1,0:T(8,128)S(1)}, u32[]{:S(2)}, u32[]{:S(2)}) collective-permute-start(f32[128,512]{1,0:T(8,128)S(1)} %get-tuple-element.205), channel_id=1, source_target_pairs={{0,8},{2,10},{4,12},{6,14},{8,0},{10,2},{12,4},{14,6},{16,24},{18,... | collective-permute-start | bytes 786440 | tf_op jit(solution)/shard_map/ppermute | solution.py:303
  127.5 13.9 %collective-permute-start.26 = (f32[192,512]{1,0:T(8,128)S(1)}, f32[192,512]{1,0:T(8,128)S(1)}, u32[]{:S(2)}, u32[]{:S(2)}) collective-permute-start(f32[192,512]{1,0:T(8,128)S(1)} %pad_maximum_fusion), channel_id=1, source_target_pairs={{0,1},{1,0},{2,3},{3,2},{4,5},{5,4},{6,7},{7,6},{8,9},{9,8},{10,11... | collective-permute-start | bytes 1179656 | tf_op jit(solution)/shard_map/ppermute | solution.py:332
  131.0 7.6 %collective-permute-start.23 = (f32[64,512]{1,0:T(8,128)S(1)}, f32[64,512]{1,0:T(8,128)S(1)}, u32[]{:S(2)}, u32[]{:S(2)}) collective-permute-start(f32[64,512]{1,0:T(8,128)S(1)} %get-tuple-element.219), channel_id=1, source_target_pairs={{0,16},{2,18},{4,20},{6,22},{8,24},{10,26},{12,28},{14,30},{16,0},... | collective-permute-start | bytes 393224 | tf_op jit(solution)/shard_map/ppermute | solution.py:303
  135.1 6.3 %collective-permute-start.25 = (f32[64,512]{1,0:T(8,128)S(1)}, f32[64,512]{1,0:T(8,128)S(1)}, u32[]{:S(2)}, u32[]{:S(2)}) collective-permute-start(f32[64,512]{1,0:T(8,128)S(1)} %get-tuple-element.217), channel_id=1, source_target_pairs={{0,16},{2,18},{4,20},{6,22},{8,24},{10,26},{12,28},{14,30},{16,0},... | collective-permute-start | bytes 393224 | tf_op jit(solution)/shard_map/ppermute | solution.py:303
  141.5 6.8 %collective-permute-start.27 = (f32[64,512]{1,0:T(8,128)S(1)}, f32[64,512]{1,0:T(8,128)S(1)}, u32[]{:S(2)}, u32[]{:S(2)}) collective-permute-start(f32[64,512]{1,0:T(8,128)S(1)} %get-tuple-element.228), channel_id=1, source_target_pairs={{0,1},{1,0},{2,3},{3,2},{4,5},{5,4},{6,7},{7,6},{8,9},{9,8},{10,11... | collective-permute-start | bytes 393224 | tf_op jit(solution)/shard_map/ppermute | solution.py:332
  (6 other events, 156.7 us)

commit v10 on v8

--- a/solution.py
+++ b/solution.py
@@ -340,8 +340,8 @@
                   (2, half, half, False), (3, 0, half, False), (3, half, half, False)]
         firsts = {"p": [0, 1], "q": [2, 3]}
         seconds = {"w": [0], "x": [1], "y": [2, 3], "z": [4, 5]}
-        groups = {"a": [0, 1, 2], "d": [3]}
-        plan = "pwxq0yz01203214135243a545Ad"
+        groups = {"a": [0, 1], "d": [2, 3]}
+        plan = "pwxq0yz012032141352a45345Ad"
     else:
         chunks = [(h, 0, rows, False) for h in range(blocks)]
         firsts = {"p": list(range(blocks))}

time: 147 us -> 150 us (1.020)
  starting transfers between devices: 37.8 us -> 26.5 us
  waiting for transfers between devices: 43 us -> 53.4 us
  Pallas kernels: 59 us -> 62.8 us
    ppermute x2, starting transfers between devices: 10.4 us -> 0.57 us  [exchange(): got = lax.ppermute(away, 'rep', [(0, 1), (1, 0)])]
    ppermute x18, waiting for transfers between devices: 36.9 us -> 43.1 us  [work(): got = lax.ppermute(send, 'tensor', pairs)]
    ppermute x2, waiting for transfers between devices: 2.92 us -> 7.08 us  [exchange(): got = lax.ppermute(away, 'rep', [(0, 1), (1, 0)])]
    pallas_call x6, Pallas kernels: 57.1 us -> 60.9 us  [products(): pl.pallas_call(functools.partial(products_kernel, first, inner, chunks, l...]
    ppermute x18, starting transfers between devices: 25.2 us -> 23.7 us  [work(): got = lax.ppermute(send, 'tensor', pairs)]
  transfers between devices with their start and end apart: 28 -> 28, of which waited for: 14 -> 13; matrix products, arithmetic and copies ran while one was open for 4% -> 4% of each run, Pallas kernels for 32% -> 32%
where the time goes in v10:
time: 150 us
  Pallas kernels  62.8 us (42%)
  waiting for transfers between devices  53.4 us (36%)
  starting transfers between devices  26.5 us (18%)
  other arithmetic  7.1 us (5%)
    pallas_call x6, Pallas kernels, products(): pl.pallas_call(functools.partial(products_kernel, first, inner, chunks, l...  60.9 us
    ppermute x18, waiting for transfers between devices, work(): got = lax.ppermute(send, 'tensor', pairs)  43.1 us
    ppermute x18, starting transfers between devices, work(): got = lax.ppermute(send, 'tensor', pairs)  23.7 us
    ppermute x2, waiting for transfers between devices, exchange(): got = lax.ppermute(away, 'rep', [(0, 1), (1, 0)])  7.08 us
    add x12, other arithmetic, work(): a[half:] + b[half:]  4.98 us
    ppermute x8, waiting for transfers between devices, first_halves(): lax.ppermute(part, 'tensor', across)  3.21 us
  transfers between devices with their start and end apart: 28, of which 13 were waited for; matrix products, arithmetic and copies ran while one was open for 4% of the time, Pallas kernels for 32%

profile of v10, /device:TPU:0, one launch (start us, length us, event | category | flops | bytes accessed | tf_op | source)
XLA Modules:
  0.0 150.2 jit_solution(7945636598009224533)
XLA Ops:
  0.8 12.6 %first_halves.2 = (f32[256,1024]{1,0:T(8,128)S(1)}, f32[256,1024]{1,0:T(8,128)S(1)}, f32[256,1024]{1,0:T(8,128)S(1)}, f32[256,1024]{1,0:T(8,128)S(1)}) custom-call(s32[3]{0:T(128)S(1)} %pad_add_fusion.1.place, s32[4]{0:T(128)S(1)} %get-tuple-element.143.limit, s32[4]{0:T(128)S(1)} %get-tuple-element.144.rows_live, f32[8,2,64,32,128]{4,3,2,1,0:T(8,128)} %bitcast.11, ...), custom_call_target="tpu_custom_call" | custom-call | flops 1024 | bytes 1024 | tf_op jit(solution)/shard_map/first_halves/pallas_call | solution.py:176
  14.5 1.7 %collective-permute-done.refs_0_ = f32[256,1024]{1,0:T(8,128)S(1)} collective-permute-done((f32[256,1024]{1,0:T(8,128)S(1)}, f32[256,1024]{1,0:T(8,128)S(1)}, u32[]{:S(2)}, u32[]{:S(2)}) %collective-permute-start) | collective-permute-done | bytes 1048608 | tf_op jit(solution)/shard_map/ppermute | solution.py:290
  17.7 8.9 %second_halves.4 = (f32[256,1024]{1,0:T(8,128)S(1)}, f32[256,1024]{1,0:T(8,128)S(1)}) custom-call(s32[3]{0:T(128)S(1)} %pad_add_fusion.1.place, s32[4]{0:T(128)S(1)} %get-tuple-element.143.limit, s32[4]{0:T(128)S(1)} %get-tuple-element.144.rows_live, f32[8,2,64,32,128]{4,3,2,1,0:T(8,128)} %bitcast.12, f32[4,1024,1024]{2,1,0:T(8,128)} %a_hbm.6, ...), custom_call_target="tpu_custom_call" | custom-call | flops 1024 | bytes 1024 | tf_op jit(solution)/shard_map/second_halves/pallas_call | solution.py:176
  26.6 2.9 %collective-permute-start.2 = (f32[256,1024]{1,0:T(8,128)S(1)}, f32[256,1024]{1,0:T(8,128)S(1)}, u32[]{:S(2)}, u32[]{:S(2)}) collective-permute-start(f32[256,1024]{1,0:T(8,128)S(1)} %get-tuple-element.112), channel_id=1, source_target_pairs={{0,4},{2,6},{4,0},{6,2},{8,12},{10,14},{12,8},{14,10},{16,20},{18,... | collective-permute-start | bytes 3145736 | tf_op jit(solution)/shard_map/ppermute | solution.py:303
  29.5 7.9 %second_halves.5 = (f32[256,1024]{1,0:T(8,128)S(1)}, f32[256,1024]{1,0:T(8,128)S(1)}) custom-call(s32[3]{0:T(128)S(1)} %pad_add_fusion.1.place, s32[4]{0:T(128)S(1)} %get-tuple-element.143.limit, s32[4]{0:T(128)S(1)} %get-tuple-element.144.rows_live, f32[8,2,64,32,128]{4,3,2,1,0:T(8,128)} %bitcast.13, f32[4,1024,1024]{2,1,0:T(8,128)} %a_hbm.6, ...), custom_call_target="tpu_custom_call" | custom-call | flops 1024 | bytes 1024 | tf_op jit(solution)/shard_map/second_halves/pallas_call | solution.py:176
  37.5 13.5 %first_halves.3 = (f32[256,1024]{1,0:T(8,128)S(1)}, f32[256,1024]{1,0:T(8,128)S(1)}, f32[256,1024]{1,0:T(8,128)S(1)}, f32[256,1024]{1,0:T(8,128)S(1)}) custom-call(s32[3]{0:T(128)S(1)} %pad_add_fusion.1.place, s32[4]{0:T(128)S(1)} %get-tuple-element.143.limit, s32[4]{0:T(128)S(1)} %get-tuple-element.144.rows_live, f32[8,2,64,32,128]{4,3,2,1,0:T(8,128)} %bitcast.14, ...), custom_call_target="tpu_custom_call" | custom-call | flops 1024 | bytes 1024 | tf_op jit(solution)/shard_map/first_halves/pallas_call | solution.py:176
  53.0 1.7 %collective-permute-start.12 = (f32[256,1024]{1,0:T(8,128)S(1)}, f32[256,1024]{1,0:T(8,128)S(1)}, u32[]{:S(2)}, u32[]{:S(2)}) collective-permute-start(f32[256,1024]{1,0:T(8,128)S(1)} %get-tuple-element.153), channel_id=1, source_target_pairs={{0,4},{2,6},{4,0},{6,2},{8,12},{10,14},{12,8},{14,10},{16,20},{18,... | collective-permute-start | bytes 3145736 | tf_op jit(solution)/shard_map/ppermute | solution.py:303
  56.6 9.0 %second_halves.6 = (f32[256,512]{1,0:T(8,128)S(1)}, f32[256,512]{1,0:T(8,128)S(1)}, f32[256,512]{1,0:T(8,128)S(1)}, f32[256,512]{1,0:T(8,128)S(1)}) custom-call(s32[3]{0:T(128)S(1)} %pad_add_fusion.1.place, s32[4]{0:T(128)S(1)} %get-tuple-element.143.limit, s32[4]{0:T(128)S(1)} %get-tuple-element.144.rows_live, f32[8,2,64,32,128]{4,3,2,1,0:T(8,128)} %bitcast.15, ...), custom_call_target="tpu_custom_call" | custom-call | flops 1024 | bytes 1024 | tf_op jit(solution)/shard_map/second_halves/pallas_call | solution.py:176
  66.4 9.1 %second_halves.7 = (f32[256,512]{1,0:T(8,128)S(1)}, f32[256,512]{1,0:T(8,128)S(1)}, f32[256,512]{1,0:T(8,128)S(1)}, f32[256,512]{1,0:T(8,128)S(1)}) custom-call(s32[3]{0:T(128)S(1)} %pad_add_fusion.1.place, s32[4]{0:T(128)S(1)} %get-tuple-element.143.limit, s32[4]{0:T(128)S(1)} %get-tuple-element.144.rows_live, f32[8,2,64,32,128]{4,3,2,1,0:T(8,128)} %bitcast.16, ...), custom_call_target="tpu_custom_call" | custom-call | flops 1024 | bytes 1024 | tf_op jit(solution)/shard_map/second_halves/pallas_call | solution.py:176
  75.6 3.5 %collective-permute-done.12 = f32[256,1024]{1,0:T(8,128)S(1)} collective-permute-done((f32[256,1024]{1,0:T(8,128)S(1)}, f32[256,1024]{1,0:T(8,128)S(1)}, u32[]{:S(2)}, u32[]{:S(2)}) %collective-permute-start.12) | collective-permute-done | bytes 1048608 | tf_op jit(solution)/shard_map/ppermute | solution.py:303
  79.2 1.9 %collective-permute-start.13 = (f32[128,1024]{1,0:T(8,128)S(1)}, f32[128,1024]{1,0:T(8,128)S(1)}, u32[]{:S(2)}, u32[]{:S(2)}) collective-permute-start(f32[128,1024]{1,0:T(8,128)S(1)} %get-tuple-element.201), channel_id=1, source_target_pairs={{0,8},{2,10},{4,12},{6,14},{8,0},{10,2},{12,4},{14,6},{16,24},{18,... | collective-permute-start | bytes 1572872 | tf_op jit(solution)/shard_map/ppermute | solution.py:303
  81.2 3.0 %collective-permute-start.14 = (f32[128,512]{1,0:T(8,128)S(1)}, f32[128,512]{1,0:T(8,128)S(1)}, u32[]{:S(2)}, u32[]{:S(2)}) collective-permute-start(f32[128,512]{1,0:T(8,128)S(1)} %get-tuple-element.213), channel_id=1, source_target_pairs={{0,16},{2,18},{4,20},{6,22},{8,24},{10,26},{12,28},{14,30},{16,0},... | collective-permute-start | bytes 786440 | tf_op jit(solution)/shard_map/ppermute | solution.py:303
  85.7 6.4 %collective-permute-done.10 = f32[64,1024]{1,0:T(8,128)S(1)} collective-permute-done((f32[64,1024]{1,0:T(8,128)S(1)}, f32[64,1024]{1,0:T(8,128)S(1)}, u32[]{:S(2)}, u32[]{:S(2)}) %collective-permute-start.10) | collective-permute-done | bytes 262176 | tf_op jit(solution)/shard_map/ppermute | solution.py:303
  92.1 1.8 %collective-permute-start.19 = (f32[256,512]{1,0:T(8,128)S(1)}, f32[256,512]{1,0:T(8,128)S(1)}, u32[]{:S(2)}, u32[]{:S(2)}) collective-permute-start(f32[256,512]{1,0:T(8,128)S(1)} %get-tuple-element.174), channel_id=1, source_target_pairs={{0,4},{2,6},{4,0},{6,2},{8,12},{10,14},{12,8},{14,10},{16,20},{18,... | collective-permute-start | bytes 1572872 | tf_op jit(solution)/shard_map/ppermute | solution.py:303
  94.7 6.0 %collective-permute-done.14 = f32[128,512]{1,0:T(8,128)S(1)} collective-permute-done((f32[128,512]{1,0:T(8,128)S(1)}, f32[128,512]{1,0:T(8,128)S(1)}, u32[]{:S(2)}, u32[]{:S(2)}) %collective-permute-start.14) | collective-permute-done | bytes 262176 | tf_op jit(solution)/shard_map/ppermute | solution.py:303
  102.5 3.1 %collective-permute-start.16 = (f32[64,1024]{1,0:T(8,128)}, f32[64,1024]{1,0:T(8,128)}, u32[]{:S(2)}, u32[]{:S(2)}) collective-permute-start(f32[64,1024]{1,0:T(8,128)} %get-tuple-element.211), channel_id=1, source_target_pairs={{0,16},{2,18},{4,20},{6,22},{8,24},{10,26},{12,28},{14,30},{16,0},... | collective-permute-start | bytes 786440 | tf_op jit(solution)/shard_map/ppermute | solution.py:303
  109.3 5.8 %collective-permute-done.16 = f32[64,1024]{1,0:T(8,128)} collective-permute-done((f32[64,1024]{1,0:T(8,128)}, f32[64,1024]{1,0:T(8,128)}, u32[]{:S(2)}, u32[]{:S(2)}) %collective-permute-start.16) | collective-permute-done | bytes 262176 | tf_op jit(solution)/shard_map/ppermute | solution.py:303
  116.0 2.1 %collective-permute-done.20 = f32[128,512]{1,0:T(8,128)} collective-permute-done((f32[128,512]{1,0:T(8,128)}, f32[128,512]{1,0:T(8,128)}, u32[]{:S(2)}, u32[]{:S(2)}) %collective-permute-start.20) | collective-permute-done | bytes 262176 | tf_op jit(solution)/shard_map/ppermute | solution.py:303
  119.6 2.3 %collective-permute-start.22 = (f32[128,512]{1,0:T(8,128)S(1)}, f32[128,512]{1,0:T(8,128)S(1)}, u32[]{:S(2)}, u32[]{:S(2)}) collective-permute-start(f32[128,512]{1,0:T(8,128)S(1)} %get-tuple-element.207), channel_id=1, source_target_pairs={{0,8},{2,10},{4,12},{6,14},{8,0},{10,2},{12,4},{14,6},{16,24},{18,... | collective-permute-start | bytes 786440 | tf_op jit(solution)/shard_map/ppermute | solution.py:303
  122.0 4.3 %collective-permute-done.23 = f32[128,512]{1,0:T(8,128)S(1)} collective-permute-done((f32[128,512]{1,0:T(8,128)S(1)}, f32[128,512]{1,0:T(8,128)S(1)}, u32[]{:S(2)}, u32[]{:S(2)}) %collective-permute-start.23) | collective-permute-done | bytes 262176 | tf_op jit(solution)/shard_map/ppermute | solution.py:303
  127.0 7.2 %collective-permute-done.22 = f32[128,512]{1,0:T(8,128)S(1)} collective-permute-done((f32[128,512]{1,0:T(8,128)S(1)}, f32[128,512]{1,0:T(8,128)S(1)}, u32[]{:S(2)}, u32[]{:S(2)}) %collective-permute-start.22) | collective-permute-done | bytes 262176 | tf_op jit(solution)/shard_map/ppermute | solution.py:303
  134.3 6.6 %collective-permute-done.25 = f32[64,512]{1,0:T(8,128)S(1)} collective-permute-done((f32[64,512]{1,0:T(8,128)S(1)}, f32[64,512]{1,0:T(8,128)S(1)}, u32[]{:S(2)}, u32[]{:S(2)}) %collective-permute-start.25) | collective-permute-done | bytes 131104 | tf_op jit(solution)/shard_map/ppermute | solution.py:303
  141.3 7.1 %collective-permute-done.27 = f32[128,512]{1,0:T(8,128)S(1)} collective-permute-done((f32[128,512]{1,0:T(8,128)S(1)}, f32[128,512]{1,0:T(8,128)S(1)}, u32[]{:S(2)}, u32[]{:S(2)}) %collective-permute-start.27) | collective-permute-done | bytes 262176 | tf_op jit(solution)/shard_map/ppermute | solution.py:332
  148.4 1.9 %place_blocks.1 = f32[64,8,512]{2,1,0:T(8,128)} custom-call(s32[1]{0:T(128)} %bitcast.side_ref, s32[2]{0:T(128)S(1)} %pad_add_fusion.base, s32[8]{0:T(128)S(1)} %copy-done, s32[8]{0:T(128)S(1)} %copy-done.1, f32[64,512]{1,0:T(8,128)S(1)} %get-tuple-element.234.refs_0_, f32[64,512]{1,0:T(8,128)S(1)} %get-tuple-element.236.refs_1_, ...), custom_call_target="tpu_custom_call" | custom-call | flops 1024 | bytes 1024 | tf_op jit(solution)/shard_map/place_blocks/pallas_call | solution.py:225
  (73 shorter events, 19.7 us)
Async XLA Ops:
  14.0 15.5 %collective-permute-start.3 = (f32[256,1024]{1,0:T(8,128)S(1)}, f32[256,1024]{1,0:T(8,128)S(1)}, u32[]{:S(2)}, u32[]{:S(2)}) collective-permute-start(f32[256,1024]{1,0:T(8,128)S(1)} %get-tuple-element.113), channel_id=1, source_target_pairs={{0,2},{2,0},{4,6},{6,4},{8,10},{10,8},{12,14},{14,12},{16,18},{18,... | collective-permute-start | bytes 3145736 | tf_op jit(solution)/shard_map/ppermute | solution.py:290
  14.4 15.1 %collective-permute-start.4 = (f32[256,1024]{1,0:T(8,128)S(1)}, f32[256,1024]{1,0:T(8,128)S(1)}, u32[]{:S(2)}, u32[]{:S(2)}) collective-permute-start(f32[256,1024]{1,0:T(8,128)S(1)} %get-tuple-element.114), channel_id=1, source_target_pairs={{0,2},{2,0},{4,6},{6,4},{8,10},{10,8},{12,14},{14,12},{16,18},{18,... | collective-permute-start | bytes 3145736 | tf_op jit(solution)/shard_map/ppermute | solution.py:290
  26.6 26.4 %collective-permute-start.2 = (f32[256,1024]{1,0:T(8,128)S(1)}, f32[256,1024]{1,0:T(8,128)S(1)}, u32[]{:S(2)}, u32[]{:S(2)}) collective-permute-start(f32[256,1024]{1,0:T(8,128)S(1)} %get-tuple-element.112), channel_id=1, source_target_pairs={{0,4},{2,6},{4,0},{6,2},{8,12},{10,14},{12,8},{14,10},{16,20},{18,... | collective-permute-start | bytes 3145736 | tf_op jit(solution)/shard_map/ppermute | solution.py:303
  51.6 14.0 %collective-permute-start.6 = (f32[256,1024]{1,0:T(8,128)S(1)}, f32[256,1024]{1,0:T(8,128)S(1)}, u32[]{:S(2)}, u32[]{:S(2)}) collective-permute-start(f32[256,1024]{1,0:T(8,128)S(1)} %get-tuple-element.131), channel_id=1, source_target_pairs={{0,2},{2,0},{4,6},{6,4},{8,10},{10,8},{12,14},{14,12},{16,18},{18,... | collective-permute-start | bytes 3145736 | tf_op jit(solution)/shard_map/ppermute | solution.py:290
  51.6 13.9 %collective-permute-start.7 = (f32[256,1024]{1,0:T(8,128)S(1)}, f32[256,1024]{1,0:T(8,128)S(1)}, u32[]{:S(2)}, u32[]{:S(2)}) collective-permute-start(f32[256,1024]{1,0:T(8,128)S(1)} %get-tuple-element.132), channel_id=1, source_target_pairs={{0,2},{2,0},{4,6},{6,4},{8,10},{10,8},{12,14},{14,12},{16,18},{18,... | collective-permute-start | bytes 3145736 | tf_op jit(solution)/shard_map/ppermute | solution.py:290
  53.0 26.1 %collective-permute-start.12 = (f32[256,1024]{1,0:T(8,128)S(1)}, f32[256,1024]{1,0:T(8,128)S(1)}, u32[]{:S(2)}, u32[]{:S(2)}) collective-permute-start(f32[256,1024]{1,0:T(8,128)S(1)} %get-tuple-element.153), channel_id=1, source_target_pairs={{0,4},{2,6},{4,0},{6,2},{8,12},{10,14},{12,8},{14,10},{16,20},{18,... | collective-permute-start | bytes 3145736 | tf_op jit(solution)/shard_map/ppermute | solution.py:303
  54.9 20.6 %collective-permute-start.5 = (f32[128,1024]{1,0:T(8,128)S(1)}, f32[128,1024]{1,0:T(8,128)S(1)}, u32[]{:S(2)}, u32[]{:S(2)}) collective-permute-start(f32[128,1024]{1,0:T(8,128)S(1)} %get-tuple-element.203), channel_id=1, source_target_pairs={{0,8},{2,10},{4,12},{6,14},{8,0},{10,2},{12,4},{14,6},{16,24},{18,... | collective-permute-start | bytes 1572872 | tf_op jit(solution)/shard_map/ppermute | solution.py:303
  65.6 15.6 %collective-permute-start.11 = (f32[256,512]{1,0:T(8,128)S(1)}, f32[256,512]{1,0:T(8,128)S(1)}, u32[]{:S(2)}, u32[]{:S(2)}) collective-permute-start(f32[256,512]{1,0:T(8,128)S(1)} %get-tuple-element.152), channel_id=1, source_target_pairs={{0,8},{2,10},{4,12},{6,14},{8,0},{10,2},{12,4},{14,6},{16,24},{18,... | collective-permute-start | bytes 1572872 | tf_op jit(solution)/shard_map/ppermute | solution.py:303
  66.1 27.8 %collective-permute-start.15 = (f32[256,512]{1,0:T(8,128)S(1)}, f32[256,512]{1,0:T(8,128)S(1)}, u32[]{:S(2)}, u32[]{:S(2)}) collective-permute-start(f32[256,512]{1,0:T(8,128)S(1)} %get-tuple-element.161), channel_id=1, source_target_pairs={{0,4},{2,6},{4,0},{6,2},{8,12},{10,14},{12,8},{14,10},{16,20},{18,... | collective-permute-start | bytes 1572872 | tf_op jit(solution)/shard_map/ppermute | solution.py:303
  79.1 13.0 %collective-permute-start.10 = (f32[64,1024]{1,0:T(8,128)S(1)}, f32[64,1024]{1,0:T(8,128)S(1)}, u32[]{:S(2)}, u32[]{:S(2)}) collective-permute-start(f32[64,1024]{1,0:T(8,128)S(1)} %get-tuple-element.215), channel_id=1, source_target_pairs={{0,16},{2,18},{4,20},{6,22},{8,24},{10,26},{12,28},{14,30},{16,0},... | collective-permute-start | bytes 786440 | tf_op jit(solution)/shard_map/ppermute | solution.py:303
  79.2 22.5 %collective-permute-start.13 = (f32[128,1024]{1,0:T(8,128)S(1)}, f32[128,1024]{1,0:T(8,128)S(1)}, u32[]{:S(2)}, u32[]{:S(2)}) collective-permute-start(f32[128,1024]{1,0:T(8,128)S(1)} %get-tuple-element.201), channel_id=1, source_target_pairs={{0,8},{2,10},{4,12},{6,14},{8,0},{10,2},{12,4},{14,6},{16,24},{18,... | collective-permute-start | bytes 1572872 | tf_op jit(solution)/shard_map/ppermute | solution.py:303
  81.2 19.4 %collective-permute-start.14 = (f32[128,512]{1,0:T(8,128)S(1)}, f32[128,512]{1,0:T(8,128)S(1)}, u32[]{:S(2)}, u32[]{:S(2)}) collective-permute-start(f32[128,512]{1,0:T(8,128)S(1)} %get-tuple-element.213), channel_id=1, source_target_pairs={{0,16},{2,18},{4,20},{6,22},{8,24},{10,26},{12,28},{14,30},{16,0},... | collective-permute-start | bytes 786440 | tf_op jit(solution)/shard_map/ppermute | solution.py:303
  84.2 22.7 %collective-permute-start.17 = (f32[256,512]{1,0:T(8,128)S(1)}, f32[256,512]{1,0:T(8,128)}, u32[]{:S(2)}, u32[]{:S(2)}) collective-permute-start(f32[256,512]{1,0:T(8,128)S(1)} %get-tuple-element.168), channel_id=1, source_target_pairs={{0,4},{2,6},{4,0},{6,2},{8,12},{10,14},{12,8},{14,10},{16,20},{18,... | collective-permute-start | bytes 1572872 | tf_op jit(solution)/shard_map/ppermute | solution.py:303
  92.1 27.0 %collective-permute-start.19 = (f32[256,512]{1,0:T(8,128)S(1)}, f32[256,512]{1,0:T(8,128)S(1)}, u32[]{:S(2)}, u32[]{:S(2)}) collective-permute-start(f32[256,512]{1,0:T(8,128)S(1)} %get-tuple-element.174), channel_id=1, source_target_pairs={{0,4},{2,6},{4,0},{6,2},{8,12},{10,14},{12,8},{14,10},{16,20},{18,... | collective-permute-start | bytes 1572872 | tf_op jit(solution)/shard_map/ppermute | solution.py:303
  102.5 12.6 %collective-permute-start.16 = (f32[64,1024]{1,0:T(8,128)}, f32[64,1024]{1,0:T(8,128)}, u32[]{:S(2)}, u32[]{:S(2)}) collective-permute-start(f32[64,1024]{1,0:T(8,128)} %get-tuple-element.211), channel_id=1, source_target_pairs={{0,16},{2,18},{4,20},{6,22},{8,24},{10,26},{12,28},{14,30},{16,0},... | collective-permute-start | bytes 786440 | tf_op jit(solution)/shard_map/ppermute | solution.py:303
  105.6 12.6 %collective-permute-start.20 = (f32[128,512]{1,0:T(8,128)}, f32[128,512]{1,0:T(8,128)}, u32[]{:S(2)}, u32[]{:S(2)}) collective-permute-start(f32[128,512]{1,0:T(8,128)} %get-tuple-element.209), channel_id=1, source_target_pairs={{0,8},{2,10},{4,12},{6,14},{8,0},{10,2},{12,4},{14,6},{16,24},{18,... | collective-permute-start | bytes 786440 | tf_op jit(solution)/shard_map/ppermute | solution.py:303
  105.6 13.7 %collective-permute-start.18 = (f32[64,512]{1,0:T(8,128)}, f32[64,512]{1,0:T(8,128)S(1)}, u32[]{:S(2)}, u32[]{:S(2)}) collective-permute-start(f32[64,512]{1,0:T(8,128)} %get-tuple-element.223), channel_id=1, source_target_pairs={{0,4},{2,6},{4,0},{6,2},{8,12},{10,14},{12,8},{14,10},{16,20},{18,... | collective-permute-start | bytes 393224 | tf_op jit(solution)/shard_map/ppermute | solution.py:303
  108.1 18.2 %collective-permute-start.23 = (f32[128,512]{1,0:T(8,128)S(1)}, f32[128,512]{1,0:T(8,128)S(1)}, u32[]{:S(2)}, u32[]{:S(2)}) collective-permute-start(f32[128,512]{1,0:T(8,128)S(1)} %get-tuple-element.205), channel_id=1, source_target_pairs={{0,8},{2,10},{4,12},{6,14},{8,0},{10,2},{12,4},{14,6},{16,24},{18,... | collective-permute-start | bytes 786440 | tf_op jit(solution)/shard_map/ppermute | solution.py:303
  119.3 14.9 %collective-permute-start.21 = (f32[64,512]{1,0:T(8,128)S(1)}, f32[64,512]{1,0:T(8,128)S(1)}, u32[]{:S(2)}, u32[]{:S(2)}) collective-permute-start(f32[64,512]{1,0:T(8,128)S(1)} %get-tuple-element.221), channel_id=1, source_target_pairs={{0,16},{2,18},{4,20},{6,22},{8,24},{10,26},{12,28},{14,30},{16,0},... | collective-permute-start | bytes 393224 | tf_op jit(solution)/shard_map/ppermute | solution.py:303
  119.6 14.5 %collective-permute-start.22 = (f32[128,512]{1,0:T(8,128)S(1)}, f32[128,512]{1,0:T(8,128)S(1)}, u32[]{:S(2)}, u32[]{:S(2)}) collective-permute-start(f32[128,512]{1,0:T(8,128)S(1)} %get-tuple-element.207), channel_id=1, source_target_pairs={{0,8},{2,10},{4,12},{6,14},{8,0},{10,2},{12,4},{14,6},{16,24},{18,... | collective-permute-start | bytes 786440 | tf_op jit(solution)/shard_map/ppermute | solution.py:303
  126.3 8.0 %collective-permute-start.24 = (f32[64,512]{1,0:T(8,128)S(1)}, f32[64,512]{1,0:T(8,128)S(1)}, u32[]{:S(2)}, u32[]{:S(2)}) collective-permute-start(f32[64,512]{1,0:T(8,128)S(1)} %get-tuple-element.219), channel_id=1, source_target_pairs={{0,16},{2,18},{4,20},{6,22},{8,24},{10,26},{12,28},{14,30},{16,0},... | collective-permute-start | bytes 393224 | tf_op jit(solution)/shard_map/ppermute | solution.py:303
  126.5 14.5 %collective-permute-start.26 = (f32[128,512]{1,0:T(8,128)S(1)}, f32[128,512]{1,0:T(8,128)S(1)}, u32[]{:S(2)}, u32[]{:S(2)}) collective-permute-start(f32[128,512]{1,0:T(8,128)S(1)} %pad_maximum_fusion), channel_id=1, source_target_pairs={{0,1},{1,0},{2,3},{3,2},{4,5},{5,4},{6,7},{7,6},{8,9},{9,8},{10,11... | collective-permute-start | bytes 786440 | tf_op jit(solution)/shard_map/ppermute | solution.py:332
  134.2 6.8 %collective-permute-start.25 = (f32[64,512]{1,0:T(8,128)S(1)}, f32[64,512]{1,0:T(8,128)S(1)}, u32[]{:S(2)}, u32[]{:S(2)}) collective-permute-start(f32[64,512]{1,0:T(8,128)S(1)} %get-tuple-element.217), channel_id=1, source_target_pairs={{0,16},{2,18},{4,20},{6,22},{8,24},{10,26},{12,28},{14,30},{16,0},... | collective-permute-start | bytes 393224 | tf_op jit(solution)/shard_map/ppermute | solution.py:303
  141.1 7.3 %collective-permute-start.27 = (f32[128,512]{1,0:T(8,128)S(1)}, f32[128,512]{1,0:T(8,128)S(1)}, u32[]{:S(2)}, u32[]{:S(2)}) collective-permute-start(f32[128,512]{1,0:T(8,128)S(1)} %pad_maximum_fusion.1), channel_id=1, source_target_pairs={{0,1},{1,0},{2,3},{3,2},{4,5},{5,4},{6,7},{7,6},{8,9},{9,8},{10,11... | collective-permute-start | bytes 786440 | tf_op jit(solution)/shard_map/ppermute | solution.py:332
  (6 other events, 161.8 us)

commit v11 on v9

--- a/solution.py
+++ b/solution.py
@@ -11,7 +11,6 @@
 CORES = 2
 LANES = 128
 TILE = 256
-PIECES = 2
 VMEM_BYTES = 44 * 1024 * 1024
 F32 = jnp.float32
 BF16 = jnp.bfloat16
@@ -66,14 +65,14 @@
     return dot(left_high, high) + (dot(left_high, low) + dot(left_low, high))
 
 
-def products_kernel(first, inner, chunks, adds, place, limit, rows_live, b_hbm, a_hbm, *refs):
+def products_kernel(first, inner, chunks, pieces, adds, place, limit, rows_live, b_hbm, a_hbm, *refs):
     received, (*outs, b_buf, a_buf, sums, high_ref, low_ref, b_sem, a_sem, in_sem, out_sem) = (
         refs[:adds], refs[adds:]
     )
     groups, cols, depth = high_ref.shape[1:]
     tile = a_buf.shape[2]
     height = groups * cols
-    per_chunk = 2 if adds else PIECES
+    per_chunk = 2 if adds else pieces
     side = lax.rem(place[2] + (0 if adds else 1), CORES)
     tiles = []
     at = 0
@@ -93,23 +92,23 @@
         )
 
     def loads(at, n, h, start):
-        part = height // PIECES
+        part = height // pieces
         return [pltpu.make_async_copy(
-            received[(h - first) * PIECES + i].at[:, columns(n, start)],
+            received[(h - first) * pieces + i].at[:, columns(n, start)],
             sums.at[at + n, pl.ds(i * part, part)], in_sem.at[at + n, i],
-        ) for i in range(PIECES if adds else 0)]
+        ) for i in range(pieces if adds else 0)]
 
     def stores(at, n, outer_first, out):
         copies = []
         part = height // len(out)
-        pieces = groups if outer_first else len(out)
-        for i in range(pieces):
+        moves = groups if outer_first else len(out)
+        for i in range(moves):
             if outer_first:
                 x, z = i // OUTER, i % OUTER
                 to, row = divmod((z * inner + x) * cols, part)
             else:
                 to, row = i, 0
-            size = height // pieces
+            size = height // moves
             copies.append(pltpu.make_async_copy(
                 sums.at[at + n, pl.ds(i * size, size)],
                 out[to].at[pl.ds(row, size), columns(n)], out_sem.at[at + n, i],
@@ -163,18 +162,18 @@
                 copy.wait()
 
 
-def products(place, limit, rows_live, parts_of_b, amplitudes, chunks, inner, received):
+def products(place, limit, rows_live, parts_of_b, amplitudes, chunks, pieces, inner, received):
     groups, _, cols, rows_b, _ = parts_of_b.shape
     blocks, depth, rows = amplitudes.shape
     tile = min(rows, TILE)
     first, last = chunks[0][0], chunks[-1][0]
     total = sum(chunk[2] for chunk in chunks) // tile
     height = groups * cols
-    count = 2 if received else PIECES
+    count = 2 if received else pieces
     anywhere = pl.BlockSpec(memory_space=pl.ANY)
     part = pltpu.VMEM((last - first + 1, groups, cols, depth), BF16)
     return pl.pallas_call(
-        functools.partial(products_kernel, first, inner, chunks, len(received)),
+        functools.partial(products_kernel, first, inner, chunks, pieces, len(received)),
         grid_spec=pltpu.PrefetchScalarGridSpec(
             num_scalar_prefetch=3,
             grid=(),
@@ -188,7 +187,7 @@
                 part,
                 pltpu.SemaphoreType.DMA((groups,)),
                 pltpu.SemaphoreType.DMA((total,)),
-                pltpu.SemaphoreType.DMA((total, PIECES)),
+                pltpu.SemaphoreType.DMA((total, pieces)),
                 pltpu.SemaphoreType.DMA((total, groups)),
             ],
         ),
@@ -278,21 +277,21 @@
     chain = Chain()
     received, totals, gens = {}, {}, {}
 
-    def run_products(chunks, *got):
+    def run_products(chunks, pieces, *got):
         return chain.run(
-            lambda p, l, r, b, a, *g: products(p, l, r, b, a, chunks, inner, g),
+            lambda p, l, r, b, a, *g: products(p, l, r, b, a, chunks, pieces, inner, g),
             place, pairs_here, rows_here, parts_of_b, amplitudes, *got,
         )
 
-    def first_halves(names):
-        sent = run_products([(h, 0, rows, False) for h in names])
+    def first_halves(names, pieces):
+        sent = run_products([(h, 0, rows, False) for h in names], pieces)
         for i, h in enumerate(names):
             received[h] = [lax.ppermute(part, "tensor", across)
-                           for part in sent[i * PIECES:(i + 1) * PIECES]]
+                           for part in sent[i * pieces:(i + 1) * pieces]]
 
     def second_halves(names):
-        got = [part for h in sorted({chunks[i][0] for i in names}) for part in received[h]]
-        outs = run_products([chunks[i] for i in names], *got)
+        got = [received[h] for h in sorted({chunks[i][0] for i in names})]
+        outs = run_products([chunks[i] for i in names], len(got[0]), *sum(got, []))
         for at, i in enumerate(names):
             gens[i] = work(*chunks[i], *outs[2 * at:2 * at + 2])
 
@@ -336,22 +335,22 @@
 
     if inner == 2 and rep == 2 and blocks == 4:
         half = rows // 2
-        chunks = [(0, 0, rows, False), (1, 0, half, True), (1, half, half, False),
+        chunks = [(0, 0, half, True), (0, half, half, False), (1, 0, rows, False),
                   (2, 0, rows, False), (3, 0, half, False), (3, half, half, False)]
-        firsts = {"p": [0, 1], "q": [2, 3]}
-        seconds = {"w": [0], "x": [1, 2], "y": [3], "z": [4, 5]}
-        groups = {"a": [0, 1, 2], "d": [3]}
-        plan = "pwxq0y12z012032143543a545Ad"
+        firsts = {"p": ([0, 1], 2), "q": ([2], 4), "r": ([3], 2)}
+        seconds = {"w": [0, 1], "x": [2], "y": [3], "z": [4, 5]}
+        groups = {"a": [0, 1], "b": [2], "d": [3]}
+        plan = "pwxq10y10r2z12342350a453b45Ad"
     else:
         chunks = [(h, 0, rows, False) for h in range(blocks)]
-        firsts = {"p": list(range(blocks))}
+        firsts = {"p": (list(range(blocks)), 2)}
         seconds = {"w": list(range(blocks))}
         groups = {"a": list(range(blocks))}
         steps = (inner * OUTER).bit_length() - 1
         plan = "pw" + "".join(str(h) * steps for h in range(blocks)) + "a"
     for move in plan:
         if move in firsts:
-            first_halves(firsts[move])
+            first_halves(*firsts[move])
         elif move in seconds:
             second_halves(seconds[move])
         elif move == "A":

time: 151 us -> 167 us (1.11)
  waiting for transfers between devices: 52.3 us -> 70.9 us
  starting transfers between devices: 30.3 us -> 22.4 us
  Pallas kernels: 58.9 us -> 65.2 us
    ppermute x18, waiting for transfers between devices: 46.2 us -> 59.1 us  [work(): got = lax.ppermute(send, 'tensor', pairs)]
    pallas_call x6 -> x7, Pallas kernels: 57.1 us -> 63.4 us  [products(): pl.pallas_call(functools.partial(products_kernel, first, inner, chunks, p...]
    ppermute x2 -> x3, starting transfers between devices: 7.34 us -> 2.64 us  [exchange(): got = lax.ppermute(away, 'rep', [(0, 1), (1, 0)])]
    ppermute x18, starting transfers between devices: 20.8 us -> 17 us  [work(): got = lax.ppermute(send, 'tensor', pairs)]
    ppermute x8 -> x10, waiting for transfers between devices: 3.21 us -> 6.88 us  [first_halves(): lax.ppermute(part, 'tensor', across)]
    ppermute x2 -> x3, waiting for transfers between devices: 2.92 us -> 4.92 us  [exchange(): got = lax.ppermute(away, 'rep', [(0, 1), (1, 0)])]
  transfers between devices with their start and end apart: 28 -> 31, of which waited for: 13 -> 18; matrix products, arithmetic and copies ran while one was open for 5% -> 4% of each run, Pallas kernels for 30% -> 30%
where the time goes in v11:
time: 167 us
  waiting for transfers between devices  70.9 us (42%)
  Pallas kernels  65.2 us (39%)
  starting transfers between devices  22.4 us (13%)
  other arithmetic  8.17 us (5%)
    pallas_call x7, Pallas kernels, products(): pl.pallas_call(functools.partial(products_kernel, first, inner, chunks, p...  63.4 us
    ppermute x18, waiting for transfers between devices, work(): got = lax.ppermute(send, 'tensor', pairs)  59.1 us
    ppermute x18, starting transfers between devices, work(): got = lax.ppermute(send, 'tensor', pairs)  17 us
    ppermute x10, waiting for transfers between devices, first_halves(): lax.ppermute(part, 'tensor', across)  6.88 us
    add x12, other arithmetic, work(): a[half:] + b[half:]  5.17 us
    ppermute x3, waiting for transfers between devices, exchange(): got = lax.ppermute(away, 'rep', [(0, 1), (1, 0)])  4.92 us
  transfers between devices with their start and end apart: 31, of which 18 were waited for; matrix products, arithmetic and copies ran while one was open for 4% of the time, Pallas kernels for 30%

profile of v11, /device:TPU:0, one launch (start us, length us, event | category | flops | bytes accessed | tf_op | source)
XLA Modules:
  0.0 167.1 jit_solution(14698451510324087278)
XLA Ops:
  0.8 13.5 %first_halves.3 = (f32[256,1024]{1,0:T(8,128)S(1)}, f32[256,1024]{1,0:T(8,128)S(1)}, f32[256,1024]{1,0:T(8,128)S(1)}, f32[256,1024]{1,0:T(8,128)S(1)}) custom-call(s32[3]{0:T(128)S(1)} %pad_add_fusion.1.place, s32[4]{0:T(128)S(1)} %get-tuple-element.172.limit, s32[4]{0:T(128)S(1)} %get-tuple-element.173.rows_live, f32[8,2,64,32,128]{4,3,2,1,0:T(8,128)} %bitcast.11, ...), custom_call_target="tpu_custom_call" | custom-call | flops 1024 | bytes 1024 | tf_op jit(solution)/shard_map/first_halves/pallas_call | solution.py:175
  15.5 1.7 %collective-permute-done.1.refs_1_ = f32[256,1024]{1,0:T(8,128)S(1)} collective-permute-done((f32[256,1024]{1,0:T(8,128)S(1)}, f32[256,1024]{1,0:T(8,128)S(1)}, u32[]{:S(2)}, u32[]{:S(2)}) %collective-permute-start.1) | collective-permute-done | bytes 1048608 | tf_op jit(solution)/shard_map/ppermute | solution.py:289
  17.2 1.5 collective-permute-done.refs_0_
  18.7 9.0 %second_halves.4 = (f32[256,512]{1,0:T(8,128)S(1)}, f32[256,512]{1,0:T(8,128)S(1)}, f32[256,512]{1,0:T(8,128)S(1)}, f32[256,512]{1,0:T(8,128)S(1)}) custom-call(s32[3]{0:T(128)S(1)} %pad_add_fusion.1.place, s32[4]{0:T(128)S(1)} %get-tuple-element.172.limit, s32[4]{0:T(128)S(1)} %get-tuple-element.173.rows_live, f32[8,2,64,32,128]{4,3,2,1,0:T(8,128)} %bitcast.12, ...), custom_call_target="tpu_custom_call" | custom-call | flops 1024 | bytes 1024 | tf_op jit(solution)/shard_map/second_halves/pallas_call | solution.py:175
  27.7 2.9 %collective-permute-start.3 = (f32[256,512]{1,0:T(8,128)S(1)}, f32[256,512]{1,0:T(8,128)S(1)}, u32[]{:S(2)}, u32[]{:S(2)}) collective-permute-start(f32[256,512]{1,0:T(8,128)S(1)} %get-tuple-element.123), channel_id=1, source_target_pairs={{0,4},{2,6},{4,0},{6,2},{8,12},{10,14},{12,8},{14,10},{16,20},{18,... | collective-permute-start | bytes 1572872 | tf_op jit(solution)/shard_map/ppermute | solution.py:302
  30.6 1.6 collective-permute-start.2
  32.2 8.9 %second_halves.5 = (f32[256,1024]{1,0:T(8,128)S(1)}, f32[256,1024]{1,0:T(8,128)S(1)}) custom-call(s32[3]{0:T(128)S(1)} %pad_add_fusion.1.place, s32[4]{0:T(128)S(1)} %get-tuple-element.172.limit, s32[4]{0:T(128)S(1)} %get-tuple-element.173.rows_live, f32[8,2,64,32,128]{4,3,2,1,0:T(8,128)} %bitcast.13, f32[4,1024,1024]{2,1,0:T(8,128)} %a_hbm.7, ...), custom_call_target="tpu_custom_call" | custom-call | flops 1024 | bytes 1024 | tf_op jit(solution)/shard_map/second_halves/pallas_call | solution.py:175
  41.1 7.1 %first_halves.4 = (f32[128,1024]{1,0:T(8,128)S(1)}, f32[128,1024]{1,0:T(8,128)S(1)}, f32[128,1024]{1,0:T(8,128)S(1)}, f32[128,1024]{1,0:T(8,128)S(1)}) custom-call(s32[3]{0:T(128)S(1)} %pad_add_fusion.1.place, s32[4]{0:T(128)S(1)} %get-tuple-element.172.limit, s32[4]{0:T(128)S(1)} %get-tuple-element.173.rows_live, f32[8,2,64,32,128]{4,3,2,1,0:T(8,128)} %bitcast.14, ...), custom_call_target="tpu_custom_call" | custom-call | flops 1024 | bytes 1024 | tf_op jit(solution)/shard_map/first_halves/pallas_call | solution.py:175
  52.5 7.0 %second_halves.6 = (f32[256,1024]{1,0:T(8,128)S(1)}, f32[256,1024]{1,0:T(8,128)S(1)}) custom-call(s32[3]{0:T(128)S(1)} %pad_add_fusion.1.place, s32[4]{0:T(128)S(1)} %get-tuple-element.172.limit, s32[4]{0:T(128)S(1)} %get-tuple-element.173.rows_live, f32[8,2,64,32,128]{4,3,2,1,0:T(8,128)} %bitcast.15, f32[4,1024,1024]{2,1,0:T(8,128)} %a_hbm.7, ...), custom_call_target="tpu_custom_call" | custom-call | flops 1024 | bytes 1024 | tf_op jit(solution)/shard_map/second_halves/pallas_call | solution.py:175
  59.5 6.3 %collective-permute-done.6 = f32[128,512]{1,0:T(8,128)S(1)} collective-permute-done((f32[128,512]{1,0:T(8,128)S(1)}, f32[128,512]{1,0:T(8,128)S(1)}, u32[]{:S(2)}, u32[]{:S(2)}) %collective-permute-start.6) | collective-permute-done | bytes 262176 | tf_op jit(solution)/shard_map/ppermute | solution.py:302
  66.5 8.9 %first_halves.5 = (f32[256,1024]{1,0:T(8,128)S(1)}, f32[256,1024]{1,0:T(8,128)S(1)}) custom-call(s32[3]{0:T(128)S(1)} %pad_add_fusion.1.place, s32[4]{0:T(128)S(1)} %get-tuple-element.172.limit, s32[4]{0:T(128)S(1)} %get-tuple-element.173.rows_live, f32[8,2,64,32,128]{4,3,2,1,0:T(8,128)} %bitcast.16, f32[4,1024,1024]{2,1,0:T(8,128)} %a_hbm.7), custom_call_target="tpu_custom_call" | custom-call | flops 1024 | bytes 1024 | tf_op jit(solution)/shard_map/first_halves/pallas_call | solution.py:175
  77.0 2.0 %collective-permute-start.19 = (f32[64,512]{1,0:T(8,128)S(1)}, f32[64,512]{1,0:T(8,128)S(1)}, u32[]{:S(2)}, u32[]{:S(2)}) collective-permute-start(f32[64,512]{1,0:T(8,128)S(1)} %get-tuple-element.239), channel_id=1, source_target_pairs={{0,16},{2,18},{4,20},{6,22},{8,24},{10,26},{12,28},{14,30},{16,0},... | collective-permute-start | bytes 393224 | tf_op jit(solution)/shard_map/ppermute | solution.py:302
  79.7 8.9 %second_halves.7 = (f32[256,512]{1,0:T(8,128)S(1)}, f32[256,512]{1,0:T(8,128)S(1)}, f32[256,512]{1,0:T(8,128)S(1)}, f32[256,512]{1,0:T(8,128)S(1)}) custom-call(s32[3]{0:T(128)S(1)} %pad_add_fusion.1.place, s32[4]{0:T(128)S(1)} %get-tuple-element.172.limit, s32[4]{0:T(128)S(1)} %get-tuple-element.173.rows_live, f32[8,2,64,32,128]{4,3,2,1,0:T(8,128)} %bitcast.17, ...), custom_call_target="tpu_custom_call" | custom-call | flops 1024 | bytes 1024 | tf_op jit(solution)/shard_map/second_halves/pallas_call | solution.py:175
  88.6 2.6 %collective-permute-done.19 = f32[64,512]{1,0:T(8,128)S(1)} collective-permute-done((f32[64,512]{1,0:T(8,128)S(1)}, f32[64,512]{1,0:T(8,128)S(1)}, u32[]{:S(2)}, u32[]{:S(2)}) %collective-permute-start.19) | collective-permute-done | bytes 131104 | tf_op jit(solution)/shard_map/ppermute | solution.py:302
  91.3 2.2 %collective-permute-done.18 = f32[128,1024]{1,0:T(8,128)S(1)} collective-permute-done((f32[128,1024]{1,0:T(8,128)S(1)}, f32[128,1024]{1,0:T(8,128)S(1)}, u32[]{:S(2)}, u32[]{:S(2)}) %collective-permute-start.18) | collective-permute-done | bytes 524320 | tf_op jit(solution)/shard_map/ppermute | solution.py:302
  94.2 7.0 %collective-permute-done.17 = f32[256,1024]{1,0:T(8,128)S(1)} collective-permute-done((f32[256,1024]{1,0:T(8,128)S(1)}, f32[256,1024]{1,0:T(8,128)S(1)}, u32[]{:S(2)}, u32[]{:S(2)}) %collective-permute-start.17) | collective-permute-done | bytes 1048608 | tf_op jit(solution)/shard_map/ppermute | solution.py:302
  106.8 9.3 %collective-permute-done.22 = f32[256,512]{1,0:T(8,128)} collective-permute-done((f32[256,512]{1,0:T(8,128)S(1)}, f32[256,512]{1,0:T(8,128)}, u32[]{:S(2)}, u32[]{:S(2)}) %collective-permute-start.22) | collective-permute-done | bytes 524320 | tf_op jit(solution)/shard_map/ppermute | solution.py:302
  117.3 2.1 %collective-permute-done.21 = f32[64,1024]{1,0:T(8,128)} collective-permute-done((f32[64,1024]{1,0:T(8,128)}, f32[64,1024]{1,0:T(8,128)}, u32[]{:S(2)}, u32[]{:S(2)}) %collective-permute-start.21) | collective-permute-done | bytes 262176 | tf_op jit(solution)/shard_map/ppermute | solution.py:302
  122.6 4.2 %collective-permute-done.16 = f32[256,512]{1,0:T(8,128)S(1)} collective-permute-done((f32[256,512]{1,0:T(8,128)S(1)}, f32[256,512]{1,0:T(8,128)S(1)}, u32[]{:S(2)}, u32[]{:S(2)}) %collective-permute-start.16) | collective-permute-done | bytes 524320 | tf_op jit(solution)/shard_map/ppermute | solution.py:302
  131.4 15.7 %collective-permute-done.25 = f32[128,512]{1,0:T(8,128)S(1)} collective-permute-done((f32[128,512]{1,0:T(8,128)S(1)}, f32[128,512]{1,0:T(8,128)S(1)}, u32[]{:S(2)}, u32[]{:S(2)}) %collective-permute-start.25) | collective-permute-done | bytes 262176 | tf_op jit(solution)/shard_map/ppermute | solution.py:302
  147.2 2.9 %collective-permute-start.26 = (f32[64,512]{1,0:T(8,128)S(1)}, f32[64,512]{1,0:T(8,128)S(1)}, u32[]{:S(2)}, u32[]{:S(2)}) collective-permute-start(f32[64,512]{1,0:T(8,128)S(1)} %get-tuple-element.237), channel_id=1, source_target_pairs={{0,16},{2,18},{4,20},{6,22},{8,24},{10,26},{12,28},{14,30},{16,0},... | collective-permute-start | bytes 393224 | tf_op jit(solution)/shard_map/ppermute | solution.py:302
  152.5 7.2 %collective-permute-done.26 = f32[64,512]{1,0:T(8,128)S(1)} collective-permute-done((f32[64,512]{1,0:T(8,128)S(1)}, f32[64,512]{1,0:T(8,128)S(1)}, u32[]{:S(2)}, u32[]{:S(2)}) %collective-permute-start.26) | collective-permute-done | bytes 131104 | tf_op jit(solution)/shard_map/ppermute | solution.py:302
  160.3 4.9 %collective-permute-done.30.refs_7_ = f32[64,512]{1,0:T(8,128)S(1)} collective-permute-done((f32[64,512]{1,0:T(8,128)S(1)}, f32[64,512]{1,0:T(8,128)S(1)}, u32[]{:S(2)}, u32[]{:S(2)}) %collective-permute-start.30) | collective-permute-done | bytes 131104 | tf_op jit(solution)/shard_map/ppermute | solution.py:331
  165.2 1.8 %place_blocks.1 = f32[64,8,512]{2,1,0:T(8,128)} custom-call(s32[1]{0:T(128)} %bitcast.side_ref, s32[2]{0:T(128)S(1)} %pad_add_fusion.base, s32[8]{0:T(128)S(1)} %copy-done, s32[8]{0:T(128)S(1)} %copy-done.1, f32[64,512]{1,0:T(8,128)S(1)} %get-tuple-element.248.refs_0_, f32[64,512]{1,0:T(8,128)S(1)} %get-tuple-element.250.refs_1_, ...), custom_call_target="tpu_custom_call" | custom-call | flops 1024 | bytes 1024 | tf_op jit(solution)/shard_map/place_blocks/pallas_call | solution.py:224
  (79 shorter events, 27.5 us)
Async XLA Ops:
  14.9 17.2 %collective-permute-start.4 = (f32[256,1024]{1,0:T(8,128)S(1)}, f32[256,1024]{1,0:T(8,128)S(1)}, u32[]{:S(2)}, u32[]{:S(2)}) collective-permute-start(f32[256,1024]{1,0:T(8,128)S(1)} %get-tuple-element.124), channel_id=1, source_target_pairs={{0,2},{2,0},{4,6},{6,4},{8,10},{10,8},{12,14},{14,12},{16,18},{18,... | collective-permute-start | bytes 3145736 | tf_op jit(solution)/shard_map/ppermute | solution.py:289
  15.4 16.8 %collective-permute-start.5 = (f32[256,1024]{1,0:T(8,128)S(1)}, f32[256,1024]{1,0:T(8,128)S(1)}, u32[]{:S(2)}, u32[]{:S(2)}) collective-permute-start(f32[256,1024]{1,0:T(8,128)S(1)} %get-tuple-element.125), channel_id=1, source_target_pairs={{0,2},{2,0},{4,6},{6,4},{8,10},{10,8},{12,14},{14,12},{16,18},{18,... | collective-permute-start | bytes 3145736 | tf_op jit(solution)/shard_map/ppermute | solution.py:289
  27.7 21.1 %collective-permute-start.3 = (f32[256,512]{1,0:T(8,128)S(1)}, f32[256,512]{1,0:T(8,128)S(1)}, u32[]{:S(2)}, u32[]{:S(2)}) collective-permute-start(f32[256,512]{1,0:T(8,128)S(1)} %get-tuple-element.123), channel_id=1, source_target_pairs={{0,4},{2,6},{4,0},{6,2},{8,12},{10,14},{12,8},{14,10},{16,20},{18,... | collective-permute-start | bytes 1572872 | tf_op jit(solution)/shard_map/ppermute | solution.py:302
  30.6 18.3 %collective-permute-start.2 = (f32[256,512]{1,0:T(8,128)S(1)}, f32[256,512]{1,0:T(8,128)S(1)}, u32[]{:S(2)}, u32[]{:S(2)}) collective-permute-start(f32[256,512]{1,0:T(8,128)S(1)} %get-tuple-element.121), channel_id=1, source_target_pairs={{0,8},{2,10},{4,12},{6,14},{8,0},{10,2},{12,4},{14,6},{16,24},{18,... | collective-permute-start | bytes 1572872 | tf_op jit(solution)/shard_map/ppermute | solution.py:302
  48.8 28.0 %collective-permute-start.15 = (f32[256,1024]{1,0:T(8,128)S(1)}, f32[256,1024]{1,0:T(8,128)S(1)}, u32[]{:S(2)}, u32[]{:S(2)}) collective-permute-start(f32[256,1024]{1,0:T(8,128)S(1)} %get-tuple-element.168), channel_id=1, source_target_pairs={{0,4},{2,6},{4,0},{6,2},{8,12},{10,14},{12,8},{14,10},{16,20},{18,... | collective-permute-start | bytes 3145736 | tf_op jit(solution)/shard_map/ppermute | solution.py:302
  50.2 9.3 %collective-permute-start.7 = (f32[128,512]{1,0:T(8,128)S(1)}, f32[128,512]{1,0:T(8,128)S(1)}, u32[]{:S(2)}, u32[]{:S(2)}) collective-permute-start(f32[128,512]{1,0:T(8,128)S(1)} %get-tuple-element.231), channel_id=1, source_target_pairs={{0,8},{2,10},{4,12},{6,14},{8,0},{10,2},{12,4},{14,6},{16,24},{18,... | collective-permute-start | bytes 786440 | tf_op jit(solution)/shard_map/ppermute | solution.py:302
  51.0 14.9 %collective-permute-start.6 = (f32[128,512]{1,0:T(8,128)S(1)}, f32[128,512]{1,0:T(8,128)S(1)}, u32[]{:S(2)}, u32[]{:S(2)}) collective-permute-start(f32[128,512]{1,0:T(8,128)S(1)} %get-tuple-element.233), channel_id=1, source_target_pairs={{0,16},{2,18},{4,20},{6,22},{8,24},{10,26},{12,28},{14,30},{16,0},... | collective-permute-start | bytes 786440 | tf_op jit(solution)/shard_map/ppermute | solution.py:302
  75.5 4.1 %collective-permute-start.13 = (f32[256,1024]{1,0:T(8,128)S(1)}, f32[256,1024]{1,0:T(8,128)S(1)}, u32[]{:S(2)}, u32[]{:S(2)}) collective-permute-start(f32[256,1024]{1,0:T(8,128)S(1)} %get-tuple-element.166), channel_id=1, source_target_pairs={{0,2},{2,0},{4,6},{6,4},{8,10},{10,8},{12,14},{14,12},{16,18},{18,... | collective-permute-start | bytes 3145736 | tf_op jit(solution)/shard_map/ppermute | solution.py:289
  76.0 25.1 %collective-permute-start.17 = (f32[256,1024]{1,0:T(8,128)S(1)}, f32[256,1024]{1,0:T(8,128)S(1)}, u32[]{:S(2)}, u32[]{:S(2)}) collective-permute-start(f32[256,1024]{1,0:T(8,128)S(1)} %get-tuple-element.180), channel_id=1, source_target_pairs={{0,4},{2,6},{4,0},{6,2},{8,12},{10,14},{12,8},{14,10},{16,20},{18,... | collective-permute-start | bytes 3145736 | tf_op jit(solution)/shard_map/ppermute | solution.py:302
  76.9 16.5 %collective-permute-start.18 = (f32[128,1024]{1,0:T(8,128)S(1)}, f32[128,1024]{1,0:T(8,128)S(1)}, u32[]{:S(2)}, u32[]{:S(2)}) collective-permute-start(f32[128,1024]{1,0:T(8,128)S(1)} %get-tuple-element.221), channel_id=1, source_target_pairs={{0,8},{2,10},{4,12},{6,14},{8,0},{10,2},{12,4},{14,6},{16,24},{18,... | collective-permute-start | bytes 1572872 | tf_op jit(solution)/shard_map/ppermute | solution.py:302
  77.0 14.2 %collective-permute-start.19 = (f32[64,512]{1,0:T(8,128)S(1)}, f32[64,512]{1,0:T(8,128)S(1)}, u32[]{:S(2)}, u32[]{:S(2)}) collective-permute-start(f32[64,512]{1,0:T(8,128)S(1)} %get-tuple-element.239), channel_id=1, source_target_pairs={{0,16},{2,18},{4,20},{6,22},{8,24},{10,26},{12,28},{14,30},{16,0},... | collective-permute-start | bytes 393224 | tf_op jit(solution)/shard_map/ppermute | solution.py:302
  101.2 15.0 %collective-permute-start.22 = (f32[256,512]{1,0:T(8,128)S(1)}, f32[256,512]{1,0:T(8,128)}, u32[]{:S(2)}, u32[]{:S(2)}) collective-permute-start(f32[256,512]{1,0:T(8,128)S(1)} %get-tuple-element.188), channel_id=1, source_target_pairs={{0,4},{2,6},{4,0},{6,2},{8,12},{10,14},{12,8},{14,10},{16,20},{18,... | collective-permute-start | bytes 1572872 | tf_op jit(solution)/shard_map/ppermute | solution.py:302
  102.8 18.7 %collective-permute-start.20 = (f32[128,1024]{1,0:T(8,128)}, f32[128,1024]{1,0:T(8,128)}, u32[]{:S(2)}, u32[]{:S(2)}) collective-permute-start(f32[128,1024]{1,0:T(8,128)} %get-tuple-element.219), channel_id=1, source_target_pairs={{0,8},{2,10},{4,12},{6,14},{8,0},{10,2},{12,4},{14,6},{16,24},{18,... | collective-permute-start | bytes 1572872 | tf_op jit(solution)/shard_map/ppermute | solution.py:302
  102.8 24.1 %collective-permute-start.16 = (f32[256,512]{1,0:T(8,128)S(1)}, f32[256,512]{1,0:T(8,128)S(1)}, u32[]{:S(2)}, u32[]{:S(2)}) collective-permute-start(f32[256,512]{1,0:T(8,128)S(1)} %get-tuple-element.179), channel_id=1, source_target_pairs={{0,4},{2,6},{4,0},{6,2},{8,12},{10,14},{12,8},{14,10},{16,20},{18,... | collective-permute-start | bytes 1572872 | tf_op jit(solution)/shard_map/ppermute | solution.py:302
  104.1 15.2 %collective-permute-start.21 = (f32[64,1024]{1,0:T(8,128)}, f32[64,1024]{1,0:T(8,128)}, u32[]{:S(2)}, u32[]{:S(2)}) collective-permute-start(f32[64,1024]{1,0:T(8,128)} %get-tuple-element.229), channel_id=1, source_target_pairs={{0,16},{2,18},{4,20},{6,22},{8,24},{10,26},{12,28},{14,30},{16,0},... | collective-permute-start | bytes 786440 | tf_op jit(solution)/shard_map/ppermute | solution.py:302
  105.6 22.7 %collective-permute-start.12 = (f32[64,512]{1,0:T(8,128)}, f32[64,512]{1,0:T(8,128)S(1)}, u32[]{:S(2)}, u32[]{:S(2)}) collective-permute-start(f32[64,512]{1,0:T(8,128)} %get-tuple-element.241), channel_id=1, source_target_pairs={{0,4},{2,6},{4,0},{6,2},{8,12},{10,14},{12,8},{14,10},{16,20},{18,... | collective-permute-start | bytes 393224 | tf_op jit(solution)/shard_map/ppermute | solution.py:302
  129.2 17.9 %collective-permute-start.24 = (f32[128,512]{1,0:T(8,128)S(1)}, f32[128,512]{1,0:T(8,128)S(1)}, u32[]{:S(2)}, u32[]{:S(2)}) collective-permute-start(f32[128,512]{1,0:T(8,128)S(1)} %get-tuple-element.225), channel_id=1, source_target_pairs={{0,8},{2,10},{4,12},{6,14},{8,0},{10,2},{12,4},{14,6},{16,24},{18,... | collective-permute-start | bytes 786440 | tf_op jit(solution)/shard_map/ppermute | solution.py:302
  129.3 17.8 %collective-permute-start.23 = (f32[64,1024]{1,0:T(8,128)S(1)}, f32[64,1024]{1,0:T(8,128)S(1)}, u32[]{:S(2)}, u32[]{:S(2)}) collective-permute-start(f32[64,1024]{1,0:T(8,128)S(1)} %get-tuple-element.227), channel_id=1, source_target_pairs={{0,16},{2,18},{4,20},{6,22},{8,24},{10,26},{12,28},{14,30},{16,0},... | collective-permute-start | bytes 786440 | tf_op jit(solution)/shard_map/ppermute | solution.py:302
  130.7 16.3 %collective-permute-start.25 = (f32[128,512]{1,0:T(8,128)S(1)}, f32[128,512]{1,0:T(8,128)S(1)}, u32[]{:S(2)}, u32[]{:S(2)}) collective-permute-start(f32[128,512]{1,0:T(8,128)S(1)} %get-tuple-element.223), channel_id=1, source_target_pairs={{0,8},{2,10},{4,12},{6,14},{8,0},{10,2},{12,4},{14,6},{16,24},{18,... | collective-permute-start | bytes 786440 | tf_op jit(solution)/shard_map/ppermute | solution.py:302
  147.2 12.6 %collective-permute-start.27 = (f32[64,512]{1,0:T(8,128)S(1)}, f32[64,512]{1,0:T(8,128)S(1)}, u32[]{:S(2)}, u32[]{:S(2)}) collective-permute-start(f32[64,512]{1,0:T(8,128)S(1)} %get-tuple-element.235), channel_id=1, source_target_pairs={{0,16},{2,18},{4,20},{6,22},{8,24},{10,26},{12,28},{14,30},{16,0},... | collective-permute-start | bytes 393224 | tf_op jit(solution)/shard_map/ppermute | solution.py:302
  147.2 12.4 %collective-permute-start.26 = (f32[64,512]{1,0:T(8,128)S(1)}, f32[64,512]{1,0:T(8,128)S(1)}, u32[]{:S(2)}, u32[]{:S(2)}) collective-permute-start(f32[64,512]{1,0:T(8,128)S(1)} %get-tuple-element.237), channel_id=1, source_target_pairs={{0,16},{2,18},{4,20},{6,22},{8,24},{10,26},{12,28},{14,30},{16,0},... | collective-permute-start | bytes 393224 | tf_op jit(solution)/shard_map/ppermute | solution.py:302
  150.2 9.5 %collective-permute-start.28 = (f32[64,512]{1,0:T(8,128)S(1)}, f32[64,512]{1,0:T(8,128)S(1)}, u32[]{:S(2)}, u32[]{:S(2)}) collective-permute-start(f32[64,512]{1,0:T(8,128)S(1)} %get-tuple-element.251), channel_id=1, source_target_pairs={{0,1},{1,0},{2,3},{3,2},{4,5},{5,4},{6,7},{7,6},{8,9},{9,8},{10,11... | collective-permute-start | bytes 393224 | tf_op jit(solution)/shard_map/ppermute | solution.py:331
  150.9 9.3 %collective-permute-start.29 = (f32[128,512]{1,0:T(8,128)S(1)}, f32[128,512]{1,0:T(8,128)S(1)}, u32[]{:S(2)}, u32[]{:S(2)}) collective-permute-start(f32[128,512]{1,0:T(8,128)S(1)} %pad_maximum_fusion), channel_id=1, source_target_pairs={{0,1},{1,0},{2,3},{3,2},{4,5},{5,4},{6,7},{7,6},{8,9},{9,8},{10,11... | collective-permute-start | bytes 786440 | tf_op jit(solution)/shard_map/ppermute | solution.py:331
  159.8 5.4 %collective-permute-start.30 = (f32[64,512]{1,0:T(8,128)S(1)}, f32[64,512]{1,0:T(8,128)S(1)}, u32[]{:S(2)}, u32[]{:S(2)}) collective-permute-start(f32[64,512]{1,0:T(8,128)S(1)} %get-tuple-element.243), channel_id=1, source_target_pairs={{0,1},{1,0},{2,3},{3,2},{4,5},{5,4},{6,7},{7,6},{8,9},{9,8},{10,11... | collective-permute-start | bytes 393224 | tf_op jit(solution)/shard_map/ppermute | solution.py:331
  (9 other events, 175.1 us)

commit v12 on v10

--- a/solution.py
+++ b/solution.py
@@ -329,6 +329,7 @@
             return kept, jnp.concatenate([jnp.where(side == 0, b, a) for a, b in pairs])
 
         kept, away = chain.run(choose, pairs)
+        chain.last = away
         got = lax.ppermute(away, "rep", [(0, 1), (1, 0)])
         for i, h in enumerate(group):
             mine[h], other[h] = kept[i], got[i * cols:(i + 1) * cols]
@@ -340,8 +341,8 @@
                   (2, half, half, False), (3, 0, half, False), (3, half, half, False)]
         firsts = {"p": [0, 1], "q": [2, 3]}
         seconds = {"w": [0], "x": [1], "y": [2, 3], "z": [4, 5]}
-        groups = {"a": [0, 1], "d": [2, 3]}
-        plan = "pwxq0yz012032141352a45345Ad"
+        groups = {"a": [0, 1], "b": [2], "d": [3]}
+        plan = "pwxq0yz012032141352a453Ab45Ad"
     else:
         chunks = [(h, 0, rows, False) for h in range(blocks)]
         firsts = {"p": list(range(blocks))}

time: 150 us -> 147 us (0.980)
  waiting for transfers between devices: 53.4 us -> 40 us
  starting transfers between devices: 26.5 us -> 37.8 us
  Pallas kernels: 62.8 us -> 60.9 us
    ppermute x2 -> x3, starting transfers between devices: 0.57 us -> 15.4 us  [exchange(): got = lax.ppermute(away, 'rep', [(0, 1), (1, 0)])]
    ppermute x18, waiting for transfers between devices: 43.1 us -> 31.4 us  [work(): got = lax.ppermute(send, 'tensor', pairs)]
    ppermute x18, starting transfers between devices: 23.7 us -> 20.3 us  [work(): got = lax.ppermute(send, 'tensor', pairs)]
    ppermute x2 -> x3, waiting for transfers between devices: 7.08 us -> 4.63 us  [exchange(): got = lax.ppermute(away, 'rep', [(0, 1), (1, 0)])]
    pallas_call x6, Pallas kernels: 60.9 us -> 59 us  [products(): pl.pallas_call(functools.partial(products_kernel, first, inner, chunks, l...]
  transfers between devices with their start and end apart: 28 -> 29, of which waited for: 13 -> 15; matrix products, arithmetic and copies ran while one was open for 4% -> 4% of each run, Pallas kernels for 32% -> 32%
where the time goes in v12:
time: 147 us; the launch traced here: 146 us
  Pallas kernels  60.9 us (41%)
  waiting for transfers between devices  40 us (27%)
  starting transfers between devices  37.8 us (26%)
  other arithmetic  7.08 us (5%)
    pallas_call x6, Pallas kernels, products(): pl.pallas_call(functools.partial(products_kernel, first, inner, chunks, l...  59 us
    ppermute x18, waiting for transfers between devices, work(): got = lax.ppermute(send, 'tensor', pairs)  31.4 us
    ppermute x18, starting transfers between devices, work(): got = lax.ppermute(send, 'tensor', pairs)  20.3 us
    ppermute x3, starting transfers between devices, exchange(): got = lax.ppermute(away, 'rep', [(0, 1), (1, 0)])  15.4 us
    add x12, other arithmetic, work(): a[half:] + b[half:]  4.98 us
    ppermute x3, waiting for transfers between devices, exchange(): got = lax.ppermute(away, 'rep', [(0, 1), (1, 0)])  4.63 us
    ppermute x8, waiting for transfers between devices, first_halves(): lax.ppermute(part, 'tensor', across)  4.02 us
  transfers between devices with their start and end apart: 29, of which 15 were waited for; matrix products, arithmetic and copies ran while one was open for 4% of the time, Pallas kernels for 32%

profile of v12, /device:TPU:0, one launch (start us, length us, event | category | flops | bytes accessed | tf_op | source)
XLA Modules:
  0.0 146.2 jit_solution(10052639270278530733)
XLA Ops:
  0.8 12.6 %first_halves.2 = (f32[256,1024]{1,0:T(8,128)S(1)}, f32[256,1024]{1,0:T(8,128)S(1)}, f32[256,1024]{1,0:T(8,128)S(1)}, f32[256,1024]{1,0:T(8,128)S(1)}) custom-call(s32[3]{0:T(128)S(1)} %pad_add_fusion.1.place, s32[4]{0:T(128)S(1)} %get-tuple-element.143.limit, s32[4]{0:T(128)S(1)} %get-tuple-element.144.rows_live, f32[8,2,64,32,128]{4,3,2,1,0:T(8,128)} %bitcast.11, ...), custom_call_target="tpu_custom_call" | custom-call | flops 1024 | bytes 1024 | tf_op jit(solution)/shard_map/first_halves/pallas_call | solution.py:176
  14.5 1.6 %collective-permute-done.refs_0_ = f32[256,1024]{1,0:T(8,128)S(1)} collective-permute-done((f32[256,1024]{1,0:T(8,128)S(1)}, f32[256,1024]{1,0:T(8,128)S(1)}, u32[]{:S(2)}, u32[]{:S(2)}) %collective-permute-start) | collective-permute-done | bytes 1048608 | tf_op jit(solution)/shard_map/ppermute | solution.py:290
  17.6 7.9 %second_halves.4 = (f32[256,1024]{1,0:T(8,128)S(1)}, f32[256,1024]{1,0:T(8,128)S(1)}) custom-call(s32[3]{0:T(128)S(1)} %pad_add_fusion.1.place, s32[4]{0:T(128)S(1)} %get-tuple-element.143.limit, s32[4]{0:T(128)S(1)} %get-tuple-element.144.rows_live, f32[8,2,64,32,128]{4,3,2,1,0:T(8,128)} %bitcast.12, f32[4,1024,1024]{2,1,0:T(8,128)} %a_hbm.6, ...), custom_call_target="tpu_custom_call" | custom-call | flops 1024 | bytes 1024 | tf_op jit(solution)/shard_map/second_halves/pallas_call | solution.py:176
  25.6 8.9 %second_halves.5 = (f32[256,1024]{1,0:T(8,128)S(1)}, f32[256,1024]{1,0:T(8,128)S(1)}) custom-call(s32[3]{0:T(128)S(1)} %pad_add_fusion.1.place, s32[4]{0:T(128)S(1)} %get-tuple-element.143.limit, s32[4]{0:T(128)S(1)} %get-tuple-element.144.rows_live, f32[8,2,64,32,128]{4,3,2,1,0:T(8,128)} %bitcast.13, f32[4,1024,1024]{2,1,0:T(8,128)} %a_hbm.6, ...), custom_call_target="tpu_custom_call" | custom-call | flops 1024 | bytes 1024 | tf_op jit(solution)/shard_map/second_halves/pallas_call | solution.py:176
  34.5 12.6 %first_halves.3 = (f32[256,1024]{1,0:T(8,128)S(1)}, f32[256,1024]{1,0:T(8,128)S(1)}, f32[256,1024]{1,0:T(8,128)S(1)}, f32[256,1024]{1,0:T(8,128)S(1)}) custom-call(s32[3]{0:T(128)S(1)} %pad_add_fusion.1.place, s32[4]{0:T(128)S(1)} %get-tuple-element.143.limit, s32[4]{0:T(128)S(1)} %get-tuple-element.144.rows_live, f32[8,2,64,32,128]{4,3,2,1,0:T(8,128)} %bitcast.14, ...), custom_call_target="tpu_custom_call" | custom-call | flops 1024 | bytes 1024 | tf_op jit(solution)/shard_map/first_halves/pallas_call | solution.py:176
  48.2 2.0 %collective-permute-start.12 = (f32[256,1024]{1,0:T(8,128)S(1)}, f32[256,1024]{1,0:T(8,128)S(1)}, u32[]{:S(2)}, u32[]{:S(2)}) collective-permute-start(f32[256,1024]{1,0:T(8,128)S(1)} %get-tuple-element.153), channel_id=1, source_target_pairs={{0,4},{2,6},{4,0},{6,2},{8,12},{10,14},{12,8},{14,10},{16,20},{18,... | collective-permute-start | bytes 3145736 | tf_op jit(solution)/shard_map/ppermute | solution.py:303
  51.4 9.0 %second_halves.6 = (f32[256,512]{1,0:T(8,128)S(1)}, f32[256,512]{1,0:T(8,128)S(1)}, f32[256,512]{1,0:T(8,128)S(1)}, f32[256,512]{1,0:T(8,128)S(1)}) custom-call(s32[3]{0:T(128)S(1)} %pad_add_fusion.1.place, s32[4]{0:T(128)S(1)} %get-tuple-element.143.limit, s32[4]{0:T(128)S(1)} %get-tuple-element.144.rows_live, f32[8,2,64,32,128]{4,3,2,1,0:T(8,128)} %bitcast.15, ...), custom_call_target="tpu_custom_call" | custom-call | flops 1024 | bytes 1024 | tf_op jit(solution)/shard_map/second_halves/pallas_call | solution.py:176
  63.0 8.1 %second_halves.7 = (f32[256,512]{1,0:T(8,128)S(1)}, f32[256,512]{1,0:T(8,128)S(1)}, f32[256,512]{1,0:T(8,128)S(1)}, f32[256,512]{1,0:T(8,128)S(1)}) custom-call(s32[3]{0:T(128)S(1)} %pad_add_fusion.1.place, s32[4]{0:T(128)S(1)} %get-tuple-element.143.limit, s32[4]{0:T(128)S(1)} %get-tuple-element.144.rows_live, f32[8,2,64,32,128]{4,3,2,1,0:T(8,128)} %bitcast.16, ...), custom_call_target="tpu_custom_call" | custom-call | flops 1024 | bytes 1024 | tf_op jit(solution)/shard_map/second_halves/pallas_call | solution.py:176
  71.2 3.0 %collective-permute-done.12 = f32[256,1024]{1,0:T(8,128)S(1)} collective-permute-done((f32[256,1024]{1,0:T(8,128)S(1)}, f32[256,1024]{1,0:T(8,128)S(1)}, u32[]{:S(2)}, u32[]{:S(2)}) %collective-permute-start.12) | collective-permute-done | bytes 1048608 | tf_op jit(solution)/shard_map/ppermute | solution.py:303
  75.1 1.6 %collective-permute-start.13 = (f32[128,1024]{1,0:T(8,128)S(1)}, f32[128,1024]{1,0:T(8,128)S(1)}, u32[]{:S(2)}, u32[]{:S(2)}) collective-permute-start(f32[128,1024]{1,0:T(8,128)S(1)} %get-tuple-element.201), channel_id=1, source_target_pairs={{0,8},{2,10},{4,12},{6,14},{8,0},{10,2},{12,4},{14,6},{16,24},{18,... | collective-permute-start | bytes 1572872 | tf_op jit(solution)/shard_map/ppermute | solution.py:303
  77.5 2.0 %collective-permute-start.17 = (f32[256,512]{1,0:T(8,128)S(1)}, f32[256,512]{1,0:T(8,128)}, u32[]{:S(2)}, u32[]{:S(2)}) collective-permute-start(f32[256,512]{1,0:T(8,128)S(1)} %get-tuple-element.168), channel_id=1, source_target_pairs={{0,4},{2,6},{4,0},{6,2},{8,12},{10,14},{12,8},{14,10},{16,20},{18,... | collective-permute-start | bytes 1572872 | tf_op jit(solution)/shard_map/ppermute | solution.py:303
  79.6 7.2 %collective-permute-done.10 = f32[64,1024]{1,0:T(8,128)S(1)} collective-permute-done((f32[64,1024]{1,0:T(8,128)S(1)}, f32[64,1024]{1,0:T(8,128)S(1)}, u32[]{:S(2)}, u32[]{:S(2)}) %collective-permute-start.10) | collective-permute-done | bytes 262176 | tf_op jit(solution)/shard_map/ppermute | solution.py:303
  89.2 6.8 %collective-permute-done.14 = f32[128,512]{1,0:T(8,128)S(1)} collective-permute-done((f32[128,512]{1,0:T(8,128)S(1)}, f32[128,512]{1,0:T(8,128)S(1)}, u32[]{:S(2)}, u32[]{:S(2)}) %collective-permute-start.14) | collective-permute-done | bytes 262176 | tf_op jit(solution)/shard_map/ppermute | solution.py:303
  96.7 1.7 %collective-permute-done.13 = f32[128,1024]{1,0:T(8,128)S(1)} collective-permute-done((f32[128,1024]{1,0:T(8,128)S(1)}, f32[128,1024]{1,0:T(8,128)S(1)}, u32[]{:S(2)}, u32[]{:S(2)}) %collective-permute-start.13) | collective-permute-done | bytes 524320 | tf_op jit(solution)/shard_map/ppermute | solution.py:303
  99.2 1.7 %collective-permute-start.16 = (f32[64,1024]{1,0:T(8,128)}, f32[64,1024]{1,0:T(8,128)}, u32[]{:S(2)}, u32[]{:S(2)}) collective-permute-start(f32[64,1024]{1,0:T(8,128)} %get-tuple-element.211), channel_id=1, source_target_pairs={{0,16},{2,18},{4,20},{6,22},{8,24},{10,26},{12,28},{14,30},{16,0},... | collective-permute-start | bytes 786440 | tf_op jit(solution)/shard_map/ppermute | solution.py:303
  103.5 2.1 %collective-permute-start.23 = (f32[128,512]{1,0:T(8,128)S(1)}, f32[128,512]{1,0:T(8,128)S(1)}, u32[]{:S(2)}, u32[]{:S(2)}) collective-permute-start(f32[128,512]{1,0:T(8,128)S(1)} %get-tuple-element.205), channel_id=1, source_target_pairs={{0,8},{2,10},{4,12},{6,14},{8,0},{10,2},{12,4},{14,6},{16,24},{18,... | collective-permute-start | bytes 786440 | tf_op jit(solution)/shard_map/ppermute | solution.py:303
  105.5 6.2 %collective-permute-done.16 = f32[64,1024]{1,0:T(8,128)} collective-permute-done((f32[64,1024]{1,0:T(8,128)}, f32[64,1024]{1,0:T(8,128)}, u32[]{:S(2)}, u32[]{:S(2)}) %collective-permute-start.16) | collective-permute-done | bytes 262176 | tf_op jit(solution)/shard_map/ppermute | solution.py:303
  112.8 2.2 %collective-permute-done.20 = f32[128,512]{1,0:T(8,128)} collective-permute-done((f32[128,512]{1,0:T(8,128)}, f32[128,512]{1,0:T(8,128)}, u32[]{:S(2)}, u32[]{:S(2)}) %collective-permute-start.20) | collective-permute-done | bytes 262176 | tf_op jit(solution)/shard_map/ppermute | solution.py:303
  117.5 6.7 %collective-permute-start.24 = (f32[128,512]{1,0:T(8,128)S(1)}, f32[128,512]{1,0:T(8,128)S(1)}, u32[]{:S(2)}, u32[]{:S(2)}) collective-permute-start(f32[128,512]{1,0:T(8,128)S(1)} %pad_maximum_fusion), channel_id=1, source_target_pairs={{0,1},{1,0},{2,3},{3,2},{4,5},{5,4},{6,7},{7,6},{8,9},{9,8},{10,11... | collective-permute-start | bytes 786440 | tf_op jit(solution)/shard_map/ppermute | solution.py:333
  125.5 2.2 %collective-permute-done.22 = f32[128,512]{1,0:T(8,128)S(1)} collective-permute-done((f32[128,512]{1,0:T(8,128)S(1)}, f32[128,512]{1,0:T(8,128)S(1)}, u32[]{:S(2)}, u32[]{:S(2)}) %collective-permute-start.22) | collective-permute-done | bytes 262176 | tf_op jit(solution)/shard_map/ppermute | solution.py:303
  129.7 4.3 %collective-permute-start.27 = (f32[64,512]{1,0:T(8,128)S(1)}, f32[64,512]{1,0:T(8,128)S(1)}, u32[]{:S(2)}, u32[]{:S(2)}) collective-permute-start(f32[64,512]{1,0:T(8,128)S(1)} %get-tuple-element.229), channel_id=1, source_target_pairs={{0,1},{1,0},{2,3},{3,2},{4,5},{5,4},{6,7},{7,6},{8,9},{9,8},{10,11... | collective-permute-start | bytes 393224 | tf_op jit(solution)/shard_map/ppermute | solution.py:333
  137.0 4.4 %collective-permute-start.28 = (f32[64,512]{1,0:T(8,128)S(1)}, f32[64,512]{1,0:T(8,128)S(1)}, u32[]{:S(2)}, u32[]{:S(2)}) collective-permute-start(f32[64,512]{1,0:T(8,128)S(1)} %get-tuple-element.225), channel_id=1, source_target_pairs={{0,1},{1,0},{2,3},{3,2},{4,5},{5,4},{6,7},{7,6},{8,9},{9,8},{10,11... | collective-permute-start | bytes 393224 | tf_op jit(solution)/shard_map/ppermute | solution.py:333
  141.4 2.9 %collective-permute-done.28.refs_7_ = f32[64,512]{1,0:T(8,128)S(1)} collective-permute-done((f32[64,512]{1,0:T(8,128)S(1)}, f32[64,512]{1,0:T(8,128)S(1)}, u32[]{:S(2)}, u32[]{:S(2)}) %collective-permute-start.28) | collective-permute-done | bytes 131104 | tf_op jit(solution)/shard_map/ppermute | solution.py:333
  144.4 1.9 %place_blocks.1 = f32[64,8,512]{2,1,0:T(8,128)} custom-call(s32[1]{0:T(128)} %bitcast.side_ref, s32[2]{0:T(128)S(1)} %pad_add_fusion.base, s32[8]{0:T(128)S(1)} %copy-done, s32[8]{0:T(128)S(1)} %copy-done.1, f32[64,512]{1,0:T(8,128)S(1)} %get-tuple-element.232.refs_0_, f32[64,512]{1,0:T(8,128)S(1)} %get-tuple-element.234.refs_1_, ...), custom_call_target="tpu_custom_call" | custom-call | flops 1024 | bytes 1024 | tf_op jit(solution)/shard_map/place_blocks/pallas_call | solution.py:225
  (73 shorter events, 26.3 us)
Async XLA Ops:
  14.0 11.6 %collective-permute-start.3 = (f32[256,1024]{1,0:T(8,128)S(1)}, f32[256,1024]{1,0:T(8,128)S(1)}, u32[]{:S(2)}, u32[]{:S(2)}) collective-permute-start(f32[256,1024]{1,0:T(8,128)S(1)} %get-tuple-element.113), channel_id=1, source_target_pairs={{0,2},{2,0},{4,6},{6,4},{8,10},{10,8},{12,14},{14,12},{16,18},{18,... | collective-permute-start | bytes 3145736 | tf_op jit(solution)/shard_map/ppermute | solution.py:290
  14.1 11.6 %collective-permute-start.4 = (f32[256,1024]{1,0:T(8,128)S(1)}, f32[256,1024]{1,0:T(8,128)S(1)}, u32[]{:S(2)}, u32[]{:S(2)}) collective-permute-start(f32[256,1024]{1,0:T(8,128)S(1)} %get-tuple-element.114), channel_id=1, source_target_pairs={{0,2},{2,0},{4,6},{6,4},{8,10},{10,8},{12,14},{14,12},{16,18},{18,... | collective-permute-start | bytes 3145736 | tf_op jit(solution)/shard_map/ppermute | solution.py:290
  25.5 22.7 %collective-permute-start.2 = (f32[256,1024]{1,0:T(8,128)S(1)}, f32[256,1024]{1,0:T(8,128)S(1)}, u32[]{:S(2)}, u32[]{:S(2)}) collective-permute-start(f32[256,1024]{1,0:T(8,128)S(1)} %get-tuple-element.112), channel_id=1, source_target_pairs={{0,4},{2,6},{4,0},{6,2},{8,12},{10,14},{12,8},{14,10},{16,20},{18,... | collective-permute-start | bytes 3145736 | tf_op jit(solution)/shard_map/ppermute | solution.py:303
  47.7 12.7 %collective-permute-start.6 = (f32[256,1024]{1,0:T(8,128)S(1)}, f32[256,1024]{1,0:T(8,128)S(1)}, u32[]{:S(2)}, u32[]{:S(2)}) collective-permute-start(f32[256,1024]{1,0:T(8,128)S(1)} %get-tuple-element.131), channel_id=1, source_target_pairs={{0,2},{2,0},{4,6},{6,4},{8,10},{10,8},{12,14},{14,12},{16,18},{18,... | collective-permute-start | bytes 3145736 | tf_op jit(solution)/shard_map/ppermute | solution.py:290
  47.8 12.6 %collective-permute-start.7 = (f32[256,1024]{1,0:T(8,128)S(1)}, f32[256,1024]{1,0:T(8,128)S(1)}, u32[]{:S(2)}, u32[]{:S(2)}) collective-permute-start(f32[256,1024]{1,0:T(8,128)S(1)} %get-tuple-element.132), channel_id=1, source_target_pairs={{0,2},{2,0},{4,6},{6,4},{8,10},{10,8},{12,14},{14,12},{16,18},{18,... | collective-permute-start | bytes 3145736 | tf_op jit(solution)/shard_map/ppermute | solution.py:290
  48.2 26.0 %collective-permute-start.12 = (f32[256,1024]{1,0:T(8,128)S(1)}, f32[256,1024]{1,0:T(8,128)S(1)}, u32[]{:S(2)}, u32[]{:S(2)}) collective-permute-start(f32[256,1024]{1,0:T(8,128)S(1)} %get-tuple-element.153), channel_id=1, source_target_pairs={{0,4},{2,6},{4,0},{6,2},{8,12},{10,14},{12,8},{14,10},{16,20},{18,... | collective-permute-start | bytes 3145736 | tf_op jit(solution)/shard_map/ppermute | solution.py:303
  50.4 20.7 %collective-permute-start.5 = (f32[128,1024]{1,0:T(8,128)S(1)}, f32[128,1024]{1,0:T(8,128)S(1)}, u32[]{:S(2)}, u32[]{:S(2)}) collective-permute-start(f32[128,1024]{1,0:T(8,128)S(1)} %get-tuple-element.203), channel_id=1, source_target_pairs={{0,8},{2,10},{4,12},{6,14},{8,0},{10,2},{12,4},{14,6},{16,24},{18,... | collective-permute-start | bytes 1572872 | tf_op jit(solution)/shard_map/ppermute | solution.py:303
  60.4 16.4 %collective-permute-start.11 = (f32[256,512]{1,0:T(8,128)S(1)}, f32[256,512]{1,0:T(8,128)S(1)}, u32[]{:S(2)}, u32[]{:S(2)}) collective-permute-start(f32[256,512]{1,0:T(8,128)S(1)} %get-tuple-element.152), channel_id=1, source_target_pairs={{0,8},{2,10},{4,12},{6,14},{8,0},{10,2},{12,4},{14,6},{16,24},{18,... | collective-permute-start | bytes 1572872 | tf_op jit(solution)/shard_map/ppermute | solution.py:303
  61.6 26.9 %collective-permute-start.15 = (f32[256,512]{1,0:T(8,128)S(1)}, f32[256,512]{1,0:T(8,128)S(1)}, u32[]{:S(2)}, u32[]{:S(2)}) collective-permute-start(f32[256,512]{1,0:T(8,128)S(1)} %get-tuple-element.161), channel_id=1, source_target_pairs={{0,4},{2,6},{4,0},{6,2},{8,12},{10,14},{12,8},{14,10},{16,20},{18,... | collective-permute-start | bytes 1572872 | tf_op jit(solution)/shard_map/ppermute | solution.py:303
  74.2 12.6 %collective-permute-start.10 = (f32[64,1024]{1,0:T(8,128)S(1)}, f32[64,1024]{1,0:T(8,128)S(1)}, u32[]{:S(2)}, u32[]{:S(2)}) collective-permute-start(f32[64,1024]{1,0:T(8,128)S(1)} %get-tuple-element.215), channel_id=1, source_target_pairs={{0,16},{2,18},{4,20},{6,22},{8,24},{10,26},{12,28},{14,30},{16,0},... | collective-permute-start | bytes 786440 | tf_op jit(solution)/shard_map/ppermute | solution.py:303
  75.1 23.3 %collective-permute-start.13 = (f32[128,1024]{1,0:T(8,128)S(1)}, f32[128,1024]{1,0:T(8,128)S(1)}, u32[]{:S(2)}, u32[]{:S(2)}) collective-permute-start(f32[128,1024]{1,0:T(8,128)S(1)} %get-tuple-element.201), channel_id=1, source_target_pairs={{0,8},{2,10},{4,12},{6,14},{8,0},{10,2},{12,4},{14,6},{16,24},{18,... | collective-permute-start | bytes 1572872 | tf_op jit(solution)/shard_map/ppermute | solution.py:303
  76.8 19.2 %collective-permute-start.14 = (f32[128,512]{1,0:T(8,128)S(1)}, f32[128,512]{1,0:T(8,128)S(1)}, u32[]{:S(2)}, u32[]{:S(2)}) collective-permute-start(f32[128,512]{1,0:T(8,128)S(1)} %get-tuple-element.213), channel_id=1, source_target_pairs={{0,16},{2,18},{4,20},{6,22},{8,24},{10,26},{12,28},{14,30},{16,0},... | collective-permute-start | bytes 786440 | tf_op jit(solution)/shard_map/ppermute | solution.py:303
  77.5 24.8 %collective-permute-start.17 = (f32[256,512]{1,0:T(8,128)S(1)}, f32[256,512]{1,0:T(8,128)}, u32[]{:S(2)}, u32[]{:S(2)}) collective-permute-start(f32[256,512]{1,0:T(8,128)S(1)} %get-tuple-element.168), channel_id=1, source_target_pairs={{0,4},{2,6},{4,0},{6,2},{8,12},{10,14},{12,8},{14,10},{16,20},{18,... | collective-permute-start | bytes 1572872 | tf_op jit(solution)/shard_map/ppermute | solution.py:303
  86.8 29.1 %collective-permute-start.19 = (f32[256,512]{1,0:T(8,128)S(1)}, f32[256,512]{1,0:T(8,128)S(1)}, u32[]{:S(2)}, u32[]{:S(2)}) collective-permute-start(f32[256,512]{1,0:T(8,128)S(1)} %get-tuple-element.174), channel_id=1, source_target_pairs={{0,4},{2,6},{4,0},{6,2},{8,12},{10,14},{12,8},{14,10},{16,20},{18,... | collective-permute-start | bytes 1572872 | tf_op jit(solution)/shard_map/ppermute | solution.py:303
  99.2 12.6 %collective-permute-start.16 = (f32[64,1024]{1,0:T(8,128)}, f32[64,1024]{1,0:T(8,128)}, u32[]{:S(2)}, u32[]{:S(2)}) collective-permute-start(f32[64,1024]{1,0:T(8,128)} %get-tuple-element.211), channel_id=1, source_target_pairs={{0,16},{2,18},{4,20},{6,22},{8,24},{10,26},{12,28},{14,30},{16,0},... | collective-permute-start | bytes 786440 | tf_op jit(solution)/shard_map/ppermute | solution.py:303
  100.9 14.1 %collective-permute-start.20 = (f32[128,512]{1,0:T(8,128)}, f32[128,512]{1,0:T(8,128)}, u32[]{:S(2)}, u32[]{:S(2)}) collective-permute-start(f32[128,512]{1,0:T(8,128)} %get-tuple-element.209), channel_id=1, source_target_pairs={{0,8},{2,10},{4,12},{6,14},{8,0},{10,2},{12,4},{14,6},{16,24},{18,... | collective-permute-start | bytes 786440 | tf_op jit(solution)/shard_map/ppermute | solution.py:303
  100.9 15.2 %collective-permute-start.18 = (f32[64,512]{1,0:T(8,128)}, f32[64,512]{1,0:T(8,128)S(1)}, u32[]{:S(2)}, u32[]{:S(2)}) collective-permute-start(f32[64,512]{1,0:T(8,128)} %get-tuple-element.223), channel_id=1, source_target_pairs={{0,4},{2,6},{4,0},{6,2},{8,12},{10,14},{12,8},{14,10},{16,20},{18,... | collective-permute-start | bytes 393224 | tf_op jit(solution)/shard_map/ppermute | solution.py:303
  103.5 20.8 %collective-permute-start.23 = (f32[128,512]{1,0:T(8,128)S(1)}, f32[128,512]{1,0:T(8,128)S(1)}, u32[]{:S(2)}, u32[]{:S(2)}) collective-permute-start(f32[128,512]{1,0:T(8,128)S(1)} %get-tuple-element.205), channel_id=1, source_target_pairs={{0,8},{2,10},{4,12},{6,14},{8,0},{10,2},{12,4},{14,6},{16,24},{18,... | collective-permute-start | bytes 786440 | tf_op jit(solution)/shard_map/ppermute | solution.py:303
  116.1 11.6 %collective-permute-start.21 = (f32[64,512]{1,0:T(8,128)S(1)}, f32[64,512]{1,0:T(8,128)S(1)}, u32[]{:S(2)}, u32[]{:S(2)}) collective-permute-start(f32[64,512]{1,0:T(8,128)S(1)} %get-tuple-element.221), channel_id=1, source_target_pairs={{0,16},{2,18},{4,20},{6,22},{8,24},{10,26},{12,28},{14,30},{16,0},... | collective-permute-start | bytes 393224 | tf_op jit(solution)/shard_map/ppermute | solution.py:303
  117.1 10.5 %collective-permute-start.22 = (f32[128,512]{1,0:T(8,128)S(1)}, f32[128,512]{1,0:T(8,128)S(1)}, u32[]{:S(2)}, u32[]{:S(2)}) collective-permute-start(f32[128,512]{1,0:T(8,128)S(1)} %get-tuple-element.207), channel_id=1, source_target_pairs={{0,8},{2,10},{4,12},{6,14},{8,0},{10,2},{12,4},{14,6},{16,24},{18,... | collective-permute-start | bytes 786440 | tf_op jit(solution)/shard_map/ppermute | solution.py:303
  117.5 11.1 %collective-permute-start.24 = (f32[128,512]{1,0:T(8,128)S(1)}, f32[128,512]{1,0:T(8,128)S(1)}, u32[]{:S(2)}, u32[]{:S(2)}) collective-permute-start(f32[128,512]{1,0:T(8,128)S(1)} %pad_maximum_fusion), channel_id=1, source_target_pairs={{0,1},{1,0},{2,3},{3,2},{4,5},{5,4},{6,7},{7,6},{8,9},{9,8},{10,11... | collective-permute-start | bytes 786440 | tf_op jit(solution)/shard_map/ppermute | solution.py:333
  124.3 10.4 %collective-permute-start.25 = (f32[64,512]{1,0:T(8,128)S(1)}, f32[64,512]{1,0:T(8,128)S(1)}, u32[]{:S(2)}, u32[]{:S(2)}) collective-permute-start(f32[64,512]{1,0:T(8,128)S(1)} %get-tuple-element.219), channel_id=1, source_target_pairs={{0,16},{2,18},{4,20},{6,22},{8,24},{10,26},{12,28},{14,30},{16,0},... | collective-permute-start | bytes 393224 | tf_op jit(solution)/shard_map/ppermute | solution.py:303
  128.6 7.5 %collective-permute-start.26 = (f32[64,512]{1,0:T(8,128)S(1)}, f32[64,512]{1,0:T(8,128)S(1)}, u32[]{:S(2)}, u32[]{:S(2)}) collective-permute-start(f32[64,512]{1,0:T(8,128)S(1)} %get-tuple-element.217), channel_id=1, source_target_pairs={{0,16},{2,18},{4,20},{6,22},{8,24},{10,26},{12,28},{14,30},{16,0},... | collective-permute-start | bytes 393224 | tf_op jit(solution)/shard_map/ppermute | solution.py:303
  137.0 7.3 %collective-permute-start.28 = (f32[64,512]{1,0:T(8,128)S(1)}, f32[64,512]{1,0:T(8,128)S(1)}, u32[]{:S(2)}, u32[]{:S(2)}) collective-permute-start(f32[64,512]{1,0:T(8,128)S(1)} %get-tuple-element.225), channel_id=1, source_target_pairs={{0,1},{1,0},{2,3},{3,2},{4,5},{5,4},{6,7},{7,6},{8,9},{9,8},{10,11... | collective-permute-start | bytes 393224 | tf_op jit(solution)/shard_map/ppermute | solution.py:333
  (7 other events, 168.1 us)

commit v13 on v12

--- a/solution.py
+++ b/solution.py
@@ -319,12 +319,15 @@
             return
         pairs = []
         for h in group:
-            if (h, row_local) in totals:
-                pairs.append((totals[h, 0], totals[h, row_local]))
-            else:
-                pairs.append((totals[h, 0][:, :row_local], totals[h, 0][:, row_local:]))
-
-        def choose(pairs):
+            pairs.append([totals[at] for at in sorted(totals) if at[0] == h])
+
+        def choose(parts):
+            pairs = []
+            for part in parts:
+                if len(part) == 1 or part[0].shape[1] != row_local:
+                    whole = jnp.concatenate(part, axis=1)
+                    part = whole[:, :row_local], whole[:, row_local:]
+                pairs.append(part)
             kept = [jnp.where(side == 0, a, b) for a, b in pairs]
             return kept, jnp.concatenate([jnp.where(side == 0, b, a) for a, b in pairs])
 
@@ -338,7 +341,7 @@
     if inner == 2 and rep == 2 and blocks == 4:
         half = rows // 2
         chunks = [(0, 0, rows, False), (1, 0, rows, False), (2, 0, half, True),
-                  (2, half, half, False), (3, 0, half, False), (3, half, half, False)]
+                  (2, half, half, False), (3, 0, rows - TILE, False), (3, rows - TILE, TILE, False)]
         firsts = {"p": [0, 1], "q": [2, 3]}
         seconds = {"w": [0], "x": [1], "y": [2, 3], "z": [4, 5]}
         groups = {"a": [0, 1], "b": [2], "d": [3]}

time: 147 us -> 149 us (1.014)
  starting transfers between devices: 37.8 us -> 28.7 us
  waiting for transfers between devices: 40 us -> 48.3 us
  other arithmetic: 7.08 us -> 9.89 us
    ppermute x18, waiting for transfers between devices: 31.4 us -> 41.6 us  [work(): got = lax.ppermute(send, 'tensor', pairs)]
    ppermute x3, starting transfers between devices: 15.4 us -> 6.22 us  [exchange(): got = lax.ppermute(away, 'rep', [(0, 1), (1, 0)])]
    add x12, other arithmetic: 4.98 us -> 7.8 us  [work(): a[half:] + b[half:]]
  transfers between devices with their start and end apart: 29 -> 29, of which waited for: 15 -> 14; matrix products, arithmetic and copies ran while one was open for 4% -> 6% of each run, Pallas kernels for 32% -> 31%
where the time goes in v13:
time: 149 us; the launch traced here: 148 us
  Pallas kernels  60.9 us (41%)
  waiting for transfers between devices  48.3 us (32%)
  starting transfers between devices  28.7 us (19%)
  other arithmetic  9.89 us (7%)
    pallas_call x6, Pallas kernels, products(): pl.pallas_call(functools.partial(products_kernel, first, inner, chunks, l...  59 us
    ppermute x18, waiting for transfers between devices, work(): got = lax.ppermute(send, 'tensor', pairs)  41.6 us
    ppermute x18, starting transfers between devices, work(): got = lax.ppermute(send, 'tensor', pairs)  20.3 us
    add x12, other arithmetic, work(): a[half:] + b[half:]  7.8 us
    ppermute x3, starting transfers between devices, exchange(): got = lax.ppermute(away, 'rep', [(0, 1), (1, 0)])  6.22 us
    ppermute x3, waiting for transfers between devices, exchange(): got = lax.ppermute(away, 'rep', [(0, 1), (1, 0)])  3.45 us
    ppermute x8, waiting for transfers between devices, first_halves(): lax.ppermute(part, 'tensor', across)  3.21 us
  transfers between devices with their start and end apart: 29, of which 14 were waited for; matrix products, arithmetic and copies ran while one was open for 6% of the time, Pallas kernels for 31%

profile of v13, /device:TPU:0, one launch (start us, length us, event | category | flops | bytes accessed | tf_op | source)
XLA Modules:
  0.0 148.1 jit_solution(10398995793892991142)
XLA Ops:
  0.8 12.6 %first_halves.2 = (f32[256,1024]{1,0:T(8,128)S(1)}, f32[256,1024]{1,0:T(8,128)S(1)}, f32[256,1024]{1,0:T(8,128)S(1)}, f32[256,1024]{1,0:T(8,128)S(1)}) custom-call(s32[3]{0:T(128)S(1)} %pad_add_fusion.1.place, s32[4]{0:T(128)S(1)} %get-tuple-element.141.limit, s32[4]{0:T(128)S(1)} %get-tuple-element.142.rows_live, f32[8,2,64,32,128]{4,3,2,1,0:T(8,128)} %bitcast.11, ...), custom_call_target="tpu_custom_call" | custom-call | flops 1024 | bytes 1024 | tf_op jit(solution)/shard_map/first_halves/pallas_call | solution.py:176
  14.5 1.7 %collective-permute-done.refs_0_ = f32[256,1024]{1,0:T(8,128)S(1)} collective-permute-done((f32[256,1024]{1,0:T(8,128)S(1)}, f32[256,1024]{1,0:T(8,128)S(1)}, u32[]{:S(2)}, u32[]{:S(2)}) %collective-permute-start) | collective-permute-done | bytes 1048608 | tf_op jit(solution)/shard_map/ppermute | solution.py:290
  17.7 8.9 %second_halves.4 = (f32[256,1024]{1,0:T(8,128)S(1)}, f32[256,1024]{1,0:T(8,128)S(1)}) custom-call(s32[3]{0:T(128)S(1)} %pad_add_fusion.1.place, s32[4]{0:T(128)S(1)} %get-tuple-element.141.limit, s32[4]{0:T(128)S(1)} %get-tuple-element.142.rows_live, f32[8,2,64,32,128]{4,3,2,1,0:T(8,128)} %bitcast.12, f32[4,1024,1024]{2,1,0:T(8,128)} %a_hbm.6, ...), custom_call_target="tpu_custom_call" | custom-call | flops 1024 | bytes 1024 | tf_op jit(solution)/shard_map/second_halves/pallas_call | solution.py:176
  26.7 7.9 %second_halves.5 = (f32[256,1024]{1,0:T(8,128)S(1)}, f32[256,1024]{1,0:T(8,128)S(1)}) custom-call(s32[3]{0:T(128)S(1)} %pad_add_fusion.1.place, s32[4]{0:T(128)S(1)} %get-tuple-element.141.limit, s32[4]{0:T(128)S(1)} %get-tuple-element.142.rows_live, f32[8,2,64,32,128]{4,3,2,1,0:T(8,128)} %bitcast.13, f32[4,1024,1024]{2,1,0:T(8,128)} %a_hbm.6, ...), custom_call_target="tpu_custom_call" | custom-call | flops 1024 | bytes 1024 | tf_op jit(solution)/shard_map/second_halves/pallas_call | solution.py:176
  34.6 12.6 %first_halves.3 = (f32[256,1024]{1,0:T(8,128)S(1)}, f32[256,1024]{1,0:T(8,128)S(1)}, f32[256,1024]{1,0:T(8,128)S(1)}, f32[256,1024]{1,0:T(8,128)S(1)}) custom-call(s32[3]{0:T(128)S(1)} %pad_add_fusion.1.place, s32[4]{0:T(128)S(1)} %get-tuple-element.141.limit, s32[4]{0:T(128)S(1)} %get-tuple-element.142.rows_live, f32[8,2,64,32,128]{4,3,2,1,0:T(8,128)} %bitcast.14, ...), custom_call_target="tpu_custom_call" | custom-call | flops 1024 | bytes 1024 | tf_op jit(solution)/shard_map/first_halves/pallas_call | solution.py:176
  48.3 3.8 %collective-permute-done.2 = f32[256,1024]{1,0:T(8,128)S(1)} collective-permute-done((f32[256,1024]{1,0:T(8,128)S(1)}, f32[256,1024]{1,0:T(8,128)S(1)}, u32[]{:S(2)}, u32[]{:S(2)}) %collective-permute-start.2) | collective-permute-done | bytes 1048608 | tf_op jit(solution)/shard_map/ppermute | solution.py:303
  52.7 9.0 %second_halves.6 = (f32[256,512]{1,0:T(8,128)S(1)}, f32[256,512]{1,0:T(8,128)S(1)}, f32[256,512]{1,0:T(8,128)S(1)}, f32[256,512]{1,0:T(8,128)S(1)}) custom-call(s32[3]{0:T(128)S(1)} %pad_add_fusion.1.place, s32[4]{0:T(128)S(1)} %get-tuple-element.141.limit, s32[4]{0:T(128)S(1)} %get-tuple-element.142.rows_live, f32[8,2,64,32,128]{4,3,2,1,0:T(8,128)} %bitcast.15, ...), custom_call_target="tpu_custom_call" | custom-call | flops 1024 | bytes 1024 | tf_op jit(solution)/shard_map/second_halves/pallas_call | solution.py:176
  61.7 2.1 %collective-permute-start.11 = (f32[256,512]{1,0:T(8,128)S(1)}, f32[256,512]{1,0:T(8,128)S(1)}, u32[]{:S(2)}, u32[]{:S(2)}) collective-permute-start(f32[256,512]{1,0:T(8,128)S(1)} %get-tuple-element.150), channel_id=1, source_target_pairs={{0,8},{2,10},{4,12},{6,14},{8,0},{10,2},{12,4},{14,6},{16,24},{18,... | collective-permute-start | bytes 1572872 | tf_op jit(solution)/shard_map/ppermute | solution.py:303
  63.8 1.7 %collective-permute-start.15 = (f32[256,512]{1,0:T(8,128)S(1)}, f32[256,512]{1,0:T(8,128)}, u32[]{:S(2)}, u32[]{:S(2)}) collective-permute-start(f32[256,512]{1,0:T(8,128)S(1)} %get-tuple-element.159), channel_id=1, source_target_pairs={{0,4},{2,6},{4,0},{6,2},{8,12},{10,14},{12,8},{14,10},{16,20},{18,... | collective-permute-start | bytes 1572872 | tf_op jit(solution)/shard_map/ppermute | solution.py:303
  65.5 8.1 %second_halves.7 = (f32[256,768]{1,0:T(8,128)S(1)}, f32[256,768]{1,0:T(8,128)S(1)}, f32[256,256]{1,0:T(8,128)S(1)}, f32[256,256]{1,0:T(8,128)S(1)}) custom-call(s32[3]{0:T(128)S(1)} %pad_add_fusion.1.place, s32[4]{0:T(128)S(1)} %get-tuple-element.141.limit, s32[4]{0:T(128)S(1)} %get-tuple-element.142.rows_live, f32[8,2,64,32,128]{4,3,2,1,0:T(8,128)} %bitcast.16, ...), custom_call_target="tpu_custom_call" | custom-call | flops 1024 | bytes 1024 | tf_op jit(solution)/shard_map/second_halves/pallas_call | solution.py:176
  74.7 3.5 %collective-permute-done.12 = f32[256,1024]{1,0:T(8,128)S(1)} collective-permute-done((f32[256,1024]{1,0:T(8,128)S(1)}, f32[256,1024]{1,0:T(8,128)S(1)}, u32[]{:S(2)}, u32[]{:S(2)}) %collective-permute-start.12) | collective-permute-done | bytes 1048608 | tf_op jit(solution)/shard_map/ppermute | solution.py:303
  80.2 8.0 %collective-permute-done.10 = f32[64,1024]{1,0:T(8,128)} collective-permute-done((f32[64,1024]{1,0:T(8,128)}, f32[64,1024]{1,0:T(8,128)}, u32[]{:S(2)}, u32[]{:S(2)}) %collective-permute-start.10) | collective-permute-done | bytes 262176 | tf_op jit(solution)/shard_map/ppermute | solution.py:303
  91.8 5.9 %collective-permute-done.14 = f32[128,512]{1,0:T(8,128)} collective-permute-done((f32[128,512]{1,0:T(8,128)}, f32[128,512]{1,0:T(8,128)}, u32[]{:S(2)}, u32[]{:S(2)}) %collective-permute-start.14) | collective-permute-done | bytes 262176 | tf_op jit(solution)/shard_map/ppermute | solution.py:303
  100.4 2.1 %collective-permute-start.20 = (f32[128,512]{1,0:T(8,128)S(1)}, f32[128,512]{1,0:T(8,128)S(1)}, u32[]{:S(2)}, u32[]{:S(2)}) collective-permute-start(f32[128,512]{1,0:T(8,128)S(1)} %get-tuple-element.203), channel_id=1, source_target_pairs={{0,8},{2,10},{4,12},{6,14},{8,0},{10,2},{12,4},{14,6},{16,24},{18,... | collective-permute-start | bytes 786440 | tf_op jit(solution)/shard_map/ppermute | solution.py:303
  108.4 6.2 %collective-permute-done.16 = f32[64,1024]{1,0:T(8,128)S(1)} collective-permute-done((f32[64,1024]{1,0:T(8,128)S(1)}, f32[64,1024]{1,0:T(8,128)S(1)}, u32[]{:S(2)}, u32[]{:S(2)}) %collective-permute-start.16) | collective-permute-done | bytes 262176 | tf_op jit(solution)/shard_map/ppermute | solution.py:303
  115.5 2.8 %collective-permute-start.21 = (f32[64,512]{1,0:T(8,128)S(1)}, f32[64,512]{1,0:T(8,128)S(1)}, u32[]{:S(2)}, u32[]{:S(2)}) collective-permute-start(f32[64,512]{1,0:T(8,128)S(1)} %get-tuple-element.215), channel_id=1, source_target_pairs={{0,16},{2,18},{4,20},{6,22},{8,24},{10,26},{12,28},{14,30},{16,0},... | collective-permute-start | bytes 393224 | tf_op jit(solution)/shard_map/ppermute | solution.py:303
  118.3 2.0 %collective-permute-start.22 = (f32[128,256]{1,0:T(8,128)S(1)}, f32[128,256]{1,0:T(8,128)S(1)}, u32[]{:S(2)}, u32[]{:S(2)}) collective-permute-start(f32[128,256]{1,0:T(8,128)S(1)} %get-tuple-element.213), channel_id=1, source_target_pairs={{0,8},{2,10},{4,12},{6,14},{8,0},{10,2},{12,4},{14,6},{16,24},{18,... | collective-permute-start | bytes 393224 | tf_op jit(solution)/shard_map/ppermute | solution.py:303
  122.0 3.5 %collective-permute-done.23 = f32[128,768]{1,0:T(8,128)S(1)} collective-permute-done((f32[128,768]{1,0:T(8,128)S(1)}, f32[128,768]{1,0:T(8,128)S(1)}, u32[]{:S(2)}, u32[]{:S(2)}) %collective-permute-start.23) | collective-permute-done | bytes 393248 | tf_op jit(solution)/shard_map/ppermute | solution.py:303
  127.0 3.6 %collective-permute-start.25 = (f32[64,768]{1,0:T(8,128)S(1)}, f32[64,768]{1,0:T(8,128)S(1)}, u32[]{:S(2)}, u32[]{:S(2)}) collective-permute-start(f32[64,768]{1,0:T(8,128)S(1)} %get-tuple-element.211), channel_id=1, source_target_pairs={{0,16},{2,18},{4,20},{6,22},{8,24},{10,26},{12,28},{14,30},{16,0},... | collective-permute-start | bytes 589832 | tf_op jit(solution)/shard_map/ppermute | solution.py:303
  130.6 2.0 %collective-permute-start.27 = (f32[64,512]{1,0:T(8,128)S(1)}, f32[64,512]{1,0:T(8,128)S(1)}, u32[]{:S(2)}, u32[]{:S(2)}) collective-permute-start(f32[64,512]{1,0:T(8,128)S(1)} %get-tuple-element.225), channel_id=1, source_target_pairs={{0,1},{1,0},{2,3},{3,2},{4,5},{5,4},{6,7},{7,6},{8,9},{9,8},{10,11... | collective-permute-start | bytes 393224 | tf_op jit(solution)/shard_map/ppermute | solution.py:336
  132.7 6.7 %collective-permute-done.25 = f32[64,768]{1,0:T(8,128)S(1)} collective-permute-done((f32[64,768]{1,0:T(8,128)S(1)}, f32[64,768]{1,0:T(8,128)S(1)}, u32[]{:S(2)}, u32[]{:S(2)}) %collective-permute-start.25) | collective-permute-done | bytes 196640 | tf_op jit(solution)/shard_map/ppermute | solution.py:303
  140.1 2.6 %collective-permute-start.28 = (f32[64,512]{1,0:T(8,128)S(1)}, f32[64,512]{1,0:T(8,128)S(1)}, u32[]{:S(2)}, u32[]{:S(2)}) collective-permute-start(f32[64,512]{1,0:T(8,128)S(1)} %get-tuple-element.219), channel_id=1, source_target_pairs={{0,1},{1,0},{2,3},{3,2},{4,5},{5,4},{6,7},{7,6},{8,9},{9,8},{10,11... | collective-permute-start | bytes 393224 | tf_op jit(solution)/shard_map/ppermute | solution.py:336
  142.8 3.4 %collective-permute-done.28.refs_7_ = f32[64,512]{1,0:T(8,128)S(1)} collective-permute-done((f32[64,512]{1,0:T(8,128)S(1)}, f32[64,512]{1,0:T(8,128)S(1)}, u32[]{:S(2)}, u32[]{:S(2)}) %collective-permute-start.28) | collective-permute-done | bytes 131104 | tf_op jit(solution)/shard_map/ppermute | solution.py:336
  146.2 1.9 %place_blocks.1 = f32[64,8,512]{2,1,0:T(8,128)} custom-call(s32[1]{0:T(128)} %bitcast.side_ref, s32[2]{0:T(128)S(1)} %pad_add_fusion.base, s32[8]{0:T(128)S(1)} %copy-done, s32[8]{0:T(128)S(1)} %copy-done.1, f32[64,512]{1,0:T(8,128)S(1)} %get-tuple-element.231.refs_0_, f32[64,512]{1,0:T(8,128)S(1)} %get-tuple-element.230.refs_1_, ...), custom_call_target="tpu_custom_call" | custom-call | flops 1024 | bytes 1024 | tf_op jit(solution)/shard_map/place_blocks/pallas_call | solution.py:225
  (71 shorter events, 25.2 us)
Async XLA Ops:
  14.0 12.7 %collective-permute-start.3 = (f32[256,1024]{1,0:T(8,128)S(1)}, f32[256,1024]{1,0:T(8,128)S(1)}, u32[]{:S(2)}, u32[]{:S(2)}) collective-permute-start(f32[256,1024]{1,0:T(8,128)S(1)} %get-tuple-element.111), channel_id=1, source_target_pairs={{0,2},{2,0},{4,6},{6,4},{8,10},{10,8},{12,14},{14,12},{16,18},{18,... | collective-permute-start | bytes 3145736 | tf_op jit(solution)/shard_map/ppermute | solution.py:290
  14.4 12.3 %collective-permute-start.4 = (f32[256,1024]{1,0:T(8,128)S(1)}, f32[256,1024]{1,0:T(8,128)S(1)}, u32[]{:S(2)}, u32[]{:S(2)}) collective-permute-start(f32[256,1024]{1,0:T(8,128)S(1)} %get-tuple-element.112), channel_id=1, source_target_pairs={{0,2},{2,0},{4,6},{6,4},{8,10},{10,8},{12,14},{14,12},{16,18},{18,... | collective-permute-start | bytes 3145736 | tf_op jit(solution)/shard_map/ppermute | solution.py:290
  26.6 25.5 %collective-permute-start.2 = (f32[256,1024]{1,0:T(8,128)S(1)}, f32[256,1024]{1,0:T(8,128)S(1)}, u32[]{:S(2)}, u32[]{:S(2)}) collective-permute-start(f32[256,1024]{1,0:T(8,128)S(1)} %get-tuple-element.110), channel_id=1, source_target_pairs={{0,4},{2,6},{4,0},{6,2},{8,12},{10,14},{12,8},{14,10},{16,20},{18,... | collective-permute-start | bytes 3145736 | tf_op jit(solution)/shard_map/ppermute | solution.py:303
  47.8 13.9 %collective-permute-start.6 = (f32[256,1024]{1,0:T(8,128)S(1)}, f32[256,1024]{1,0:T(8,128)S(1)}, u32[]{:S(2)}, u32[]{:S(2)}) collective-permute-start(f32[256,1024]{1,0:T(8,128)S(1)} %get-tuple-element.129), channel_id=1, source_target_pairs={{0,2},{2,0},{4,6},{6,4},{8,10},{10,8},{12,14},{14,12},{16,18},{18,... | collective-permute-start | bytes 3145736 | tf_op jit(solution)/shard_map/ppermute | solution.py:290
  48.2 13.5 %collective-permute-start.7 = (f32[256,1024]{1,0:T(8,128)S(1)}, f32[256,1024]{1,0:T(8,128)S(1)}, u32[]{:S(2)}, u32[]{:S(2)}) collective-permute-start(f32[256,1024]{1,0:T(8,128)S(1)} %get-tuple-element.130), channel_id=1, source_target_pairs={{0,2},{2,0},{4,6},{6,4},{8,10},{10,8},{12,14},{14,12},{16,18},{18,... | collective-permute-start | bytes 3145736 | tf_op jit(solution)/shard_map/ppermute | solution.py:290
  52.1 26.1 %collective-permute-start.12 = (f32[256,1024]{1,0:T(8,128)S(1)}, f32[256,1024]{1,0:T(8,128)S(1)}, u32[]{:S(2)}, u32[]{:S(2)}) collective-permute-start(f32[256,1024]{1,0:T(8,128)S(1)} %get-tuple-element.151), channel_id=1, source_target_pairs={{0,4},{2,6},{4,0},{6,2},{8,12},{10,14},{12,8},{14,10},{16,20},{18,... | collective-permute-start | bytes 3145736 | tf_op jit(solution)/shard_map/ppermute | solution.py:303
  52.6 21.4 %collective-permute-start.5 = (f32[128,1024]{1,0:T(8,128)S(1)}, f32[128,1024]{1,0:T(8,128)S(1)}, u32[]{:S(2)}, u32[]{:S(2)}) collective-permute-start(f32[128,1024]{1,0:T(8,128)S(1)} %get-tuple-element.199), channel_id=1, source_target_pairs={{0,8},{2,10},{4,12},{6,14},{8,0},{10,2},{12,4},{14,6},{16,24},{18,... | collective-permute-start | bytes 1572872 | tf_op jit(solution)/shard_map/ppermute | solution.py:303
  61.7 17.6 %collective-permute-start.11 = (f32[256,512]{1,0:T(8,128)S(1)}, f32[256,512]{1,0:T(8,128)S(1)}, u32[]{:S(2)}, u32[]{:S(2)}) collective-permute-start(f32[256,512]{1,0:T(8,128)S(1)} %get-tuple-element.150), channel_id=1, source_target_pairs={{0,8},{2,10},{4,12},{6,14},{8,0},{10,2},{12,4},{14,6},{16,24},{18,... | collective-permute-start | bytes 1572872 | tf_op jit(solution)/shard_map/ppermute | solution.py:303
  63.8 26.9 %collective-permute-start.15 = (f32[256,512]{1,0:T(8,128)S(1)}, f32[256,512]{1,0:T(8,128)}, u32[]{:S(2)}, u32[]{:S(2)}) collective-permute-start(f32[256,512]{1,0:T(8,128)S(1)} %get-tuple-element.159), channel_id=1, source_target_pairs={{0,4},{2,6},{4,0},{6,2},{8,12},{10,14},{12,8},{14,10},{16,20},{18,... | collective-permute-start | bytes 1572872 | tf_op jit(solution)/shard_map/ppermute | solution.py:303
  73.6 32.8 %collective-permute-start.17 = (f32[256,768]{1,0:T(8,128)S(1)}, f32[256,768]{1,0:T(8,128)}, u32[]{:S(2)}, u32[]{:S(2)}) collective-permute-start(f32[256,768]{1,0:T(8,128)S(1)} %get-tuple-element.166), channel_id=1, source_target_pairs={{0,4},{2,6},{4,0},{6,2},{8,12},{10,14},{12,8},{14,10},{16,20},{18,... | collective-permute-start | bytes 2359304 | tf_op jit(solution)/shard_map/ppermute | solution.py:303
  74.7 13.4 %collective-permute-start.10 = (f32[64,1024]{1,0:T(8,128)}, f32[64,1024]{1,0:T(8,128)}, u32[]{:S(2)}, u32[]{:S(2)}) collective-permute-start(f32[64,1024]{1,0:T(8,128)} %get-tuple-element.209), channel_id=1, source_target_pairs={{0,16},{2,18},{4,20},{6,22},{8,24},{10,26},{12,28},{14,30},{16,0},... | collective-permute-start | bytes 786440 | tf_op jit(solution)/shard_map/ppermute | solution.py:303
  79.3 23.2 %collective-permute-start.13 = (f32[128,1024]{1,0:T(8,128)}, f32[128,1024]{1,0:T(8,128)}, u32[]{:S(2)}, u32[]{:S(2)}) collective-permute-start(f32[128,1024]{1,0:T(8,128)} %get-tuple-element.197), channel_id=1, source_target_pairs={{0,8},{2,10},{4,12},{6,14},{8,0},{10,2},{12,4},{14,6},{16,24},{18,... | collective-permute-start | bytes 1572872 | tf_op jit(solution)/shard_map/ppermute | solution.py:303
  80.2 17.5 %collective-permute-start.14 = (f32[128,512]{1,0:T(8,128)}, f32[128,512]{1,0:T(8,128)}, u32[]{:S(2)}, u32[]{:S(2)}) collective-permute-start(f32[128,512]{1,0:T(8,128)} %get-tuple-element.207), channel_id=1, source_target_pairs={{0,16},{2,18},{4,20},{6,22},{8,24},{10,26},{12,28},{14,30},{16,0},... | collective-permute-start | bytes 786440 | tf_op jit(solution)/shard_map/ppermute | solution.py:303
  88.2 27.2 %collective-permute-start.19 = (f32[256,256]{1,0:T(8,128)S(1)}, f32[256,256]{1,0:T(8,128)S(1)}, u32[]{:S(2)}, u32[]{:S(2)}) collective-permute-start(f32[256,256]{1,0:T(8,128)S(1)} %get-tuple-element.172), channel_id=1, source_target_pairs={{0,4},{2,6},{4,0},{6,2},{8,12},{10,14},{12,8},{14,10},{16,20},{18,... | collective-permute-start | bytes 786440 | tf_op jit(solution)/shard_map/ppermute | solution.py:303
  98.8 16.7 %collective-permute-start.18 = (f32[64,512]{1,0:T(8,128)S(1)}, f32[64,512]{1,0:T(8,128)S(1)}, u32[]{:S(2)}, u32[]{:S(2)}) collective-permute-start(f32[64,512]{1,0:T(8,128)S(1)} %get-tuple-element.217), channel_id=1, source_target_pairs={{0,4},{2,6},{4,0},{6,2},{8,12},{10,14},{12,8},{14,10},{16,20},{18,... | collective-permute-start | bytes 393224 | tf_op jit(solution)/shard_map/ppermute | solution.py:303
  100.4 15.0 %collective-permute-start.20 = (f32[128,512]{1,0:T(8,128)S(1)}, f32[128,512]{1,0:T(8,128)S(1)}, u32[]{:S(2)}, u32[]{:S(2)}) collective-permute-start(f32[128,512]{1,0:T(8,128)S(1)} %get-tuple-element.203), channel_id=1, source_target_pairs={{0,8},{2,10},{4,12},{6,14},{8,0},{10,2},{12,4},{14,6},{16,24},{18,... | collective-permute-start | bytes 786440 | tf_op jit(solution)/shard_map/ppermute | solution.py:303
  103.8 10.9 %collective-permute-start.16 = (f32[64,1024]{1,0:T(8,128)S(1)}, f32[64,1024]{1,0:T(8,128)S(1)}, u32[]{:S(2)}, u32[]{:S(2)}) collective-permute-start(f32[64,1024]{1,0:T(8,128)S(1)} %get-tuple-element.205), channel_id=1, source_target_pairs={{0,16},{2,18},{4,20},{6,22},{8,24},{10,26},{12,28},{14,30},{16,0},... | collective-permute-start | bytes 786440 | tf_op jit(solution)/shard_map/ppermute | solution.py:303
  107.6 17.9 %collective-permute-start.23 = (f32[128,768]{1,0:T(8,128)S(1)}, f32[128,768]{1,0:T(8,128)S(1)}, u32[]{:S(2)}, u32[]{:S(2)}) collective-permute-start(f32[128,768]{1,0:T(8,128)S(1)} %get-tuple-element.201), channel_id=1, source_target_pairs={{0,8},{2,10},{4,12},{6,14},{8,0},{10,2},{12,4},{14,6},{16,24},{18,... | collective-permute-start | bytes 1179656 | tf_op jit(solution)/shard_map/ppermute | solution.py:303
  115.5 11.5 %collective-permute-start.21 = (f32[64,512]{1,0:T(8,128)S(1)}, f32[64,512]{1,0:T(8,128)S(1)}, u32[]{:S(2)}, u32[]{:S(2)}) collective-permute-start(f32[64,512]{1,0:T(8,128)S(1)} %get-tuple-element.215), channel_id=1, source_target_pairs={{0,16},{2,18},{4,20},{6,22},{8,24},{10,26},{12,28},{14,30},{16,0},... | collective-permute-start | bytes 393224 | tf_op jit(solution)/shard_map/ppermute | solution.py:303
  118.3 8.7 %collective-permute-start.22 = (f32[128,256]{1,0:T(8,128)S(1)}, f32[128,256]{1,0:T(8,128)S(1)}, u32[]{:S(2)}, u32[]{:S(2)}) collective-permute-start(f32[128,256]{1,0:T(8,128)S(1)} %get-tuple-element.213), channel_id=1, source_target_pairs={{0,8},{2,10},{4,12},{6,14},{8,0},{10,2},{12,4},{14,6},{16,24},{18,... | collective-permute-start | bytes 393224 | tf_op jit(solution)/shard_map/ppermute | solution.py:303
  120.4 10.2 %collective-permute-start.24 = (f32[128,512]{1,0:T(8,128)S(1)}, f32[128,512]{1,0:T(8,128)S(1)}, u32[]{:S(2)}, u32[]{:S(2)}) collective-permute-start(f32[128,512]{1,0:T(8,128)S(1)} %pad_maximum_fusion), channel_id=1, source_target_pairs={{0,1},{1,0},{2,3},{3,2},{4,5},{5,4},{6,7},{7,6},{8,9},{9,8},{10,11... | collective-permute-start | bytes 786440 | tf_op jit(solution)/shard_map/ppermute | solution.py:336
  127.0 12.4 %collective-permute-start.25 = (f32[64,768]{1,0:T(8,128)S(1)}, f32[64,768]{1,0:T(8,128)S(1)}, u32[]{:S(2)}, u32[]{:S(2)}) collective-permute-start(f32[64,768]{1,0:T(8,128)S(1)} %get-tuple-element.211), channel_id=1, source_target_pairs={{0,16},{2,18},{4,20},{6,22},{8,24},{10,26},{12,28},{14,30},{16,0},... | collective-permute-start | bytes 589832 | tf_op jit(solution)/shard_map/ppermute | solution.py:303
  130.6 9.5 %collective-permute-start.27 = (f32[64,512]{1,0:T(8,128)S(1)}, f32[64,512]{1,0:T(8,128)S(1)}, u32[]{:S(2)}, u32[]{:S(2)}) collective-permute-start(f32[64,512]{1,0:T(8,128)S(1)} %get-tuple-element.225), channel_id=1, source_target_pairs={{0,1},{1,0},{2,3},{3,2},{4,5},{5,4},{6,7},{7,6},{8,9},{9,8},{10,11... | collective-permute-start | bytes 393224 | tf_op jit(solution)/shard_map/ppermute | solution.py:336
  132.6 7.5 %collective-permute-start.26 = (f32[64,256]{1,0:T(8,128)S(1)}, f32[64,256]{1,0:T(8,128)S(1)}, u32[]{:S(2)}, u32[]{:S(2)}) collective-permute-start(f32[64,256]{1,0:T(8,128)S(1)} %get-tuple-element.223), channel_id=1, source_target_pairs={{0,16},{2,18},{4,20},{6,22},{8,24},{10,26},{12,28},{14,30},{16,0},... | collective-permute-start | bytes 196616 | tf_op jit(solution)/shard_map/ppermute | solution.py:303
  (7 other events, 168.3 us)

commit v14 on v13

--- a/solution.py
+++ b/solution.py
@@ -340,8 +340,8 @@
 
     if inner == 2 and rep == 2 and blocks == 4:
         half = rows // 2
-        chunks = [(0, 0, rows, False), (1, 0, rows, False), (2, 0, half, True),
-                  (2, half, half, False), (3, 0, rows - TILE, False), (3, rows - TILE, TILE, False)]
+        chunks = [(0, 0, rows, False), (1, 0, rows, False), (2, 0, TILE, True),
+                  (2, TILE, rows - TILE, False), (3, 0, half, False), (3, half, half, False)]
         firsts = {"p": [0, 1], "q": [2, 3]}
         seconds = {"w": [0], "x": [1], "y": [2, 3], "z": [4, 5]}
         groups = {"a": [0, 1], "b": [2], "d": [3]}

time: 149 us -> 147 us (0.987)
  waiting for transfers between devices: 48.3 us -> 43.6 us
  starting transfers between devices: 28.7 us -> 33.3 us
  other arithmetic: 9.89 us -> 7.97 us
    ppermute x3, starting transfers between devices: 6.22 us -> 15.2 us  [exchange(): got = lax.ppermute(away, 'rep', [(0, 1), (1, 0)])]
    ppermute x18, waiting for transfers between devices: 41.6 us -> 36.2 us  [work(): got = lax.ppermute(send, 'tensor', pairs)]
    ppermute x18, starting transfers between devices: 20.3 us -> 15.9 us  [work(): got = lax.ppermute(send, 'tensor', pairs)]
    add x12, other arithmetic: 7.8 us -> 5.04 us  [work(): a[half:] + b[half:]]
  transfers between devices with their start and end apart: 29 -> 29, of which waited for: 14 -> 16; matrix products, arithmetic and copies ran while one was open for 6% -> 5% of each run, Pallas kernels for 31% -> 32%
where the time goes in v14:
time: 147 us; the launch traced here: 145 us
  Pallas kernels  59.5 us (40%)
  waiting for transfers between devices  43.6 us (30%)
  starting transfers between devices  33.3 us (23%)
  other arithmetic  7.97 us (5%)
    pallas_call x6, Pallas kernels, products(): pl.pallas_call(functools.partial(products_kernel, first, inner, chunks, l...  57.6 us
    ppermute x18, waiting for transfers between devices, work(): got = lax.ppermute(send, 'tensor', pairs)  36.2 us
    ppermute x18, starting transfers between devices, work(): got = lax.ppermute(send, 'tensor', pairs)  15.9 us
    ppermute x3, starting transfers between devices, exchange(): got = lax.ppermute(away, 'rep', [(0, 1), (1, 0)])  15.2 us
    add x12, other arithmetic, work(): a[half:] + b[half:]  5.04 us
    ppermute x3, waiting for transfers between devices, exchange(): got = lax.ppermute(away, 'rep', [(0, 1), (1, 0)])  4.23 us
    ppermute x8, waiting for transfers between devices, first_halves(): lax.ppermute(part, 'tensor', across)  3.21 us
  transfers between devices with their start and end apart: 29, of which 16 were waited for; matrix products, arithmetic and copies ran while one was open for 5% of the time, Pallas kernels for 32%

profile of v14, /device:TPU:0, one launch (start us, length us, event | category | flops | bytes accessed | tf_op | source)
XLA Modules:
  0.0 144.7 jit_solution(17234356780669537778)
XLA Ops:
  0.8 10.7 %first_halves.2 = (f32[256,1024]{1,0:T(8,128)S(1)}, f32[256,1024]{1,0:T(8,128)S(1)}, f32[256,1024]{1,0:T(8,128)S(1)}, f32[256,1024]{1,0:T(8,128)S(1)}) custom-call(s32[3]{0:T(128)S(1)} %pad_add_fusion.1.place, s32[4]{0:T(128)S(1)} %get-tuple-element.141.limit, s32[4]{0:T(128)S(1)} %get-tuple-element.142.rows_live, f32[8,2,64,32,128]{4,3,2,1,0:T(8,128)} %bitcast.11, ...), custom_call_target="tpu_custom_call" | custom-call | flops 1024 | bytes 1024 | tf_op jit(solution)/shard_map/first_halves/pallas_call | solution.py:176
  12.6 1.7 %collective-permute-done.refs_0_ = f32[256,1024]{1,0:T(8,128)S(1)} collective-permute-done((f32[256,1024]{1,0:T(8,128)S(1)}, f32[256,1024]{1,0:T(8,128)S(1)}, u32[]{:S(2)}, u32[]{:S(2)}) %collective-permute-start) | collective-permute-done | bytes 1048608 | tf_op jit(solution)/shard_map/ppermute | solution.py:290
  15.8 6.9 %second_halves.4 = (f32[256,1024]{1,0:T(8,128)S(1)}, f32[256,1024]{1,0:T(8,128)S(1)}) custom-call(s32[3]{0:T(128)S(1)} %pad_add_fusion.1.place, s32[4]{0:T(128)S(1)} %get-tuple-element.141.limit, s32[4]{0:T(128)S(1)} %get-tuple-element.142.rows_live, f32[8,2,64,32,128]{4,3,2,1,0:T(8,128)} %bitcast.12, f32[4,1024,1024]{2,1,0:T(8,128)} %a_hbm.6, ...), custom_call_target="tpu_custom_call" | custom-call | flops 1024 | bytes 1024 | tf_op jit(solution)/shard_map/second_halves/pallas_call | solution.py:176
  22.8 7.9 %second_halves.5 = (f32[256,1024]{1,0:T(8,128)S(1)}, f32[256,1024]{1,0:T(8,128)S(1)}) custom-call(s32[3]{0:T(128)S(1)} %pad_add_fusion.1.place, s32[4]{0:T(128)S(1)} %get-tuple-element.141.limit, s32[4]{0:T(128)S(1)} %get-tuple-element.142.rows_live, f32[8,2,64,32,128]{4,3,2,1,0:T(8,128)} %bitcast.13, f32[4,1024,1024]{2,1,0:T(8,128)} %a_hbm.6, ...), custom_call_target="tpu_custom_call" | custom-call | flops 1024 | bytes 1024 | tf_op jit(solution)/shard_map/second_halves/pallas_call | solution.py:176
  30.8 13.5 %first_halves.3 = (f32[256,1024]{1,0:T(8,128)S(1)}, f32[256,1024]{1,0:T(8,128)S(1)}, f32[256,1024]{1,0:T(8,128)S(1)}, f32[256,1024]{1,0:T(8,128)S(1)}) custom-call(s32[3]{0:T(128)S(1)} %pad_add_fusion.1.place, s32[4]{0:T(128)S(1)} %get-tuple-element.141.limit, s32[4]{0:T(128)S(1)} %get-tuple-element.142.rows_live, f32[8,2,64,32,128]{4,3,2,1,0:T(8,128)} %bitcast.14, ...), custom_call_target="tpu_custom_call" | custom-call | flops 1024 | bytes 1024 | tf_op jit(solution)/shard_map/first_halves/pallas_call | solution.py:176
  45.4 2.9 %collective-permute-done.2 = f32[256,1024]{1,0:T(8,128)S(1)} collective-permute-done((f32[256,1024]{1,0:T(8,128)S(1)}, f32[256,1024]{1,0:T(8,128)S(1)}, u32[]{:S(2)}, u32[]{:S(2)}) %collective-permute-start.2) | collective-permute-done | bytes 1048608 | tf_op jit(solution)/shard_map/ppermute | solution.py:303
  49.8 9.7 %second_halves.6 = (f32[256,256]{1,0:T(8,128)S(1)}, f32[256,256]{1,0:T(8,128)S(1)}, f32[256,768]{1,0:T(8,128)S(1)}, f32[256,768]{1,0:T(8,128)S(1)}) custom-call(s32[3]{0:T(128)S(1)} %pad_add_fusion.1.place, s32[4]{0:T(128)S(1)} %get-tuple-element.141.limit, s32[4]{0:T(128)S(1)} %get-tuple-element.142.rows_live, f32[8,2,64,32,128]{4,3,2,1,0:T(8,128)} %bitcast.15, ...), custom_call_target="tpu_custom_call" | custom-call | flops 1024 | bytes 1024 | tf_op jit(solution)/shard_map/second_halves/pallas_call | solution.py:176
  60.3 2.0 %collective-permute-start.11 = (f32[256,256]{1,0:T(8,128)S(1)}, f32[256,256]{1,0:T(8,128)S(1)}, u32[]{:S(2)}, u32[]{:S(2)}) collective-permute-start(f32[256,256]{1,0:T(8,128)S(1)} %get-tuple-element.150), channel_id=1, source_target_pairs={{0,8},{2,10},{4,12},{6,14},{8,0},{10,2},{12,4},{14,6},{16,24},{18,... | collective-permute-start | bytes 786440 | tf_op jit(solution)/shard_map/ppermute | solution.py:303
  62.3 8.9 %second_halves.7 = (f32[256,512]{1,0:T(8,128)S(1)}, f32[256,512]{1,0:T(8,128)S(1)}, f32[256,512]{1,0:T(8,128)S(1)}, f32[256,512]{1,0:T(8,128)S(1)}) custom-call(s32[3]{0:T(128)S(1)} %pad_add_fusion.1.place, s32[4]{0:T(128)S(1)} %get-tuple-element.141.limit, s32[4]{0:T(128)S(1)} %get-tuple-element.142.rows_live, f32[8,2,64,32,128]{4,3,2,1,0:T(8,128)} %bitcast.16, ...), custom_call_target="tpu_custom_call" | custom-call | flops 1024 | bytes 1024 | tf_op jit(solution)/shard_map/second_halves/pallas_call | solution.py:176
  71.6 1.7 %collective-permute-start.19 = (f32[256,512]{1,0:T(8,128)S(1)}, f32[256,512]{1,0:T(8,128)S(1)}, u32[]{:S(2)}, u32[]{:S(2)}) collective-permute-start(f32[256,512]{1,0:T(8,128)S(1)} %get-tuple-element.172), channel_id=1, source_target_pairs={{0,4},{2,6},{4,0},{6,2},{8,12},{10,14},{12,8},{14,10},{16,20},{18,... | collective-permute-start | bytes 1572872 | tf_op jit(solution)/shard_map/ppermute | solution.py:303
  75.5 10.4 %collective-permute-done.10 = f32[64,1024]{1,0:T(8,128)S(1)} collective-permute-done((f32[64,1024]{1,0:T(8,128)S(1)}, f32[64,1024]{1,0:T(8,128)S(1)}, u32[]{:S(2)}, u32[]{:S(2)}) %collective-permute-start.10) | collective-permute-done | bytes 262176 | tf_op jit(solution)/shard_map/ppermute | solution.py:303
  85.9 5.3 %collective-permute-done.15 = f32[256,768]{1,0:T(8,128)S(1)} collective-permute-done((f32[256,768]{1,0:T(8,128)S(1)}, f32[256,768]{1,0:T(8,128)S(1)}, u32[]{:S(2)}, u32[]{:S(2)}) %collective-permute-start.15) | collective-permute-done | bytes 786464 | tf_op jit(solution)/shard_map/ppermute | solution.py:303
  92.4 3.1 %collective-permute-start.20 = (f32[128,768]{1,0:T(8,128)}, f32[128,768]{1,0:T(8,128)}, u32[]{:S(2)}, u32[]{:S(2)}) collective-permute-start(f32[128,768]{1,0:T(8,128)} %get-tuple-element.201), channel_id=1, source_target_pairs={{0,8},{2,10},{4,12},{6,14},{8,0},{10,2},{12,4},{14,6},{16,24},{18,... | collective-permute-start | bytes 1179656 | tf_op jit(solution)/shard_map/ppermute | solution.py:303
  97.0 1.9 %collective-permute-start.18 = (f32[64,256]{1,0:T(8,128)}, f32[64,256]{1,0:T(8,128)S(1)}, u32[]{:S(2)}, u32[]{:S(2)}) collective-permute-start(f32[64,256]{1,0:T(8,128)} %get-tuple-element.229), channel_id=1, source_target_pairs={{0,4},{2,6},{4,0},{6,2},{8,12},{10,14},{12,8},{14,10},{16,20},{18,... | collective-permute-start | bytes 196616 | tf_op jit(solution)/shard_map/ppermute | solution.py:303
  98.9 3.6 %collective-permute-done.17 = f32[256,512]{1,0:T(8,128)} collective-permute-done((f32[256,512]{1,0:T(8,128)S(1)}, f32[256,512]{1,0:T(8,128)}, u32[]{:S(2)}, u32[]{:S(2)}) %collective-permute-start.17) | collective-permute-done | bytes 524320 | tf_op jit(solution)/shard_map/ppermute | solution.py:303
  103.7 5.2 %collective-permute-done.16 = f32[64,1024]{1,0:T(8,128)} collective-permute-done((f32[64,1024]{1,0:T(8,128)}, f32[64,1024]{1,0:T(8,128)}, u32[]{:S(2)}, u32[]{:S(2)}) %collective-permute-start.16) | collective-permute-done | bytes 262176 | tf_op jit(solution)/shard_map/ppermute | solution.py:303
  115.5 6.4 %collective-permute-start.24 = (f32[128,512]{1,0:T(8,128)S(1)}, f32[128,512]{1,0:T(8,128)S(1)}, u32[]{:S(2)}, u32[]{:S(2)}) collective-permute-start(f32[128,512]{1,0:T(8,128)S(1)} %pad_maximum_fusion), channel_id=1, source_target_pairs={{0,1},{1,0},{2,3},{3,2},{4,5},{5,4},{6,7},{7,6},{8,9},{9,8},{10,11... | collective-permute-start | bytes 786440 | tf_op jit(solution)/shard_map/ppermute | solution.py:336
  121.9 1.9 %collective-permute-start.25 = (f32[64,512]{1,0:T(8,128)S(1)}, f32[64,512]{1,0:T(8,128)S(1)}, u32[]{:S(2)}, u32[]{:S(2)}) collective-permute-start(f32[64,512]{1,0:T(8,128)S(1)} %get-tuple-element.215), channel_id=1, source_target_pairs={{0,16},{2,18},{4,20},{6,22},{8,24},{10,26},{12,28},{14,30},{16,0},... | collective-permute-start | bytes 393224 | tf_op jit(solution)/shard_map/ppermute | solution.py:303
  123.8 3.5 %collective-permute-done.22 = f32[128,512]{1,0:T(8,128)S(1)} collective-permute-done((f32[128,512]{1,0:T(8,128)S(1)}, f32[128,512]{1,0:T(8,128)S(1)}, u32[]{:S(2)}, u32[]{:S(2)}) %collective-permute-start.22) | collective-permute-done | bytes 262176 | tf_op jit(solution)/shard_map/ppermute | solution.py:303
  128.1 5.6 %collective-permute-start.27 = (f32[64,512]{1,0:T(8,128)S(1)}, f32[64,512]{1,0:T(8,128)S(1)}, u32[]{:S(2)}, u32[]{:S(2)}) collective-permute-start(f32[64,512]{1,0:T(8,128)S(1)} %get-tuple-element.223), channel_id=1, source_target_pairs={{0,1},{1,0},{2,3},{3,2},{4,5},{5,4},{6,7},{7,6},{8,9},{9,8},{10,11... | collective-permute-start | bytes 393224 | tf_op jit(solution)/shard_map/ppermute | solution.py:336
  133.7 1.5 %collective-permute-done.26 = f32[64,512]{1,0:T(8,128)S(1)} collective-permute-done((f32[64,512]{1,0:T(8,128)S(1)}, f32[64,512]{1,0:T(8,128)S(1)}, u32[]{:S(2)}, u32[]{:S(2)}) %collective-permute-start.26) | collective-permute-done | bytes 131104 | tf_op jit(solution)/shard_map/ppermute | solution.py:303
  136.6 3.3 %collective-permute-start.28 = (f32[64,512]{1,0:T(8,128)S(1)}, f32[64,512]{1,0:T(8,128)S(1)}, u32[]{:S(2)}, u32[]{:S(2)}) collective-permute-start(f32[64,512]{1,0:T(8,128)S(1)} %get-tuple-element.219), channel_id=1, source_target_pairs={{0,1},{1,0},{2,3},{3,2},{4,5},{5,4},{6,7},{7,6},{8,9},{9,8},{10,11... | collective-permute-start | bytes 393224 | tf_op jit(solution)/shard_map/ppermute | solution.py:336
  139.9 2.9 %collective-permute-done.28.refs_7_ = f32[64,512]{1,0:T(8,128)S(1)} collective-permute-done((f32[64,512]{1,0:T(8,128)S(1)}, f32[64,512]{1,0:T(8,128)S(1)}, u32[]{:S(2)}, u32[]{:S(2)}) %collective-permute-start.28) | collective-permute-done | bytes 131104 | tf_op jit(solution)/shard_map/ppermute | solution.py:336
  142.8 1.9 %place_blocks.1 = f32[64,8,512]{2,1,0:T(8,128)} custom-call(s32[1]{0:T(128)} %bitcast.side_ref, s32[2]{0:T(128)S(1)} %pad_add_fusion.base, s32[8]{0:T(128)S(1)} %copy-done, s32[8]{0:T(128)S(1)} %copy-done.1, f32[64,512]{1,0:T(8,128)S(1)} %get-tuple-element.231.refs_0_, f32[64,512]{1,0:T(8,128)S(1)} %get-tuple-element.228.refs_1_, ...), custom_call_target="tpu_custom_call" | custom-call | flops 1024 | bytes 1024 | tf_op jit(solution)/shard_map/place_blocks/pallas_call | solution.py:225
  (71 shorter events, 22.2 us)
Async XLA Ops:
  12.1 10.7 %collective-permute-start.3 = (f32[256,1024]{1,0:T(8,128)S(1)}, f32[256,1024]{1,0:T(8,128)S(1)}, u32[]{:S(2)}, u32[]{:S(2)}) collective-permute-start(f32[256,1024]{1,0:T(8,128)S(1)} %get-tuple-element.111), channel_id=1, source_target_pairs={{0,2},{2,0},{4,6},{6,4},{8,10},{10,8},{12,14},{14,12},{16,18},{18,... | collective-permute-start | bytes 3145736 | tf_op jit(solution)/shard_map/ppermute | solution.py:290
  12.5 10.3 %collective-permute-start.4 = (f32[256,1024]{1,0:T(8,128)S(1)}, f32[256,1024]{1,0:T(8,128)S(1)}, u32[]{:S(2)}, u32[]{:S(2)}) collective-permute-start(f32[256,1024]{1,0:T(8,128)S(1)} %get-tuple-element.112), channel_id=1, source_target_pairs={{0,2},{2,0},{4,6},{6,4},{8,10},{10,8},{12,14},{14,12},{16,18},{18,... | collective-permute-start | bytes 3145736 | tf_op jit(solution)/shard_map/ppermute | solution.py:290
  22.7 25.5 %collective-permute-start.2 = (f32[256,1024]{1,0:T(8,128)S(1)}, f32[256,1024]{1,0:T(8,128)S(1)}, u32[]{:S(2)}, u32[]{:S(2)}) collective-permute-start(f32[256,1024]{1,0:T(8,128)S(1)} %get-tuple-element.110), channel_id=1, source_target_pairs={{0,4},{2,6},{4,0},{6,2},{8,12},{10,14},{12,8},{14,10},{16,20},{18,... | collective-permute-start | bytes 3145736 | tf_op jit(solution)/shard_map/ppermute | solution.py:303
  44.9 15.5 %collective-permute-start.6 = (f32[256,1024]{1,0:T(8,128)S(1)}, f32[256,1024]{1,0:T(8,128)S(1)}, u32[]{:S(2)}, u32[]{:S(2)}) collective-permute-start(f32[256,1024]{1,0:T(8,128)S(1)} %get-tuple-element.129), channel_id=1, source_target_pairs={{0,2},{2,0},{4,6},{6,4},{8,10},{10,8},{12,14},{14,12},{16,18},{18,... | collective-permute-start | bytes 3145736 | tf_op jit(solution)/shard_map/ppermute | solution.py:290
  45.2 15.1 %collective-permute-start.7 = (f32[256,1024]{1,0:T(8,128)S(1)}, f32[256,1024]{1,0:T(8,128)S(1)}, u32[]{:S(2)}, u32[]{:S(2)}) collective-permute-start(f32[256,1024]{1,0:T(8,128)S(1)} %get-tuple-element.130), channel_id=1, source_target_pairs={{0,2},{2,0},{4,6},{6,4},{8,10},{10,8},{12,14},{14,12},{16,18},{18,... | collective-permute-start | bytes 3145736 | tf_op jit(solution)/shard_map/ppermute | solution.py:290
  48.2 26.1 %collective-permute-start.12 = (f32[256,1024]{1,0:T(8,128)S(1)}, f32[256,1024]{1,0:T(8,128)S(1)}, u32[]{:S(2)}, u32[]{:S(2)}) collective-permute-start(f32[256,1024]{1,0:T(8,128)S(1)} %get-tuple-element.151), channel_id=1, source_target_pairs={{0,4},{2,6},{4,0},{6,2},{8,12},{10,14},{12,8},{14,10},{16,20},{18,... | collective-permute-start | bytes 3145736 | tf_op jit(solution)/shard_map/ppermute | solution.py:303
  48.7 22.9 %collective-permute-start.5 = (f32[128,1024]{1,0:T(8,128)S(1)}, f32[128,1024]{1,0:T(8,128)S(1)}, u32[]{:S(2)}, u32[]{:S(2)}) collective-permute-start(f32[128,1024]{1,0:T(8,128)S(1)} %get-tuple-element.199), channel_id=1, source_target_pairs={{0,8},{2,10},{4,12},{6,14},{8,0},{10,2},{12,4},{14,6},{16,24},{18,... | collective-permute-start | bytes 1572872 | tf_op jit(solution)/shard_map/ppermute | solution.py:303
  59.5 31.6 %collective-permute-start.15 = (f32[256,768]{1,0:T(8,128)S(1)}, f32[256,768]{1,0:T(8,128)S(1)}, u32[]{:S(2)}, u32[]{:S(2)}) collective-permute-start(f32[256,768]{1,0:T(8,128)S(1)} %get-tuple-element.159), channel_id=1, source_target_pairs={{0,4},{2,6},{4,0},{6,2},{8,12},{10,14},{12,8},{14,10},{16,20},{18,... | collective-permute-start | bytes 2359304 | tf_op jit(solution)/shard_map/ppermute | solution.py:303
  60.3 15.1 %collective-permute-start.11 = (f32[256,256]{1,0:T(8,128)S(1)}, f32[256,256]{1,0:T(8,128)S(1)}, u32[]{:S(2)}, u32[]{:S(2)}) collective-permute-start(f32[256,256]{1,0:T(8,128)S(1)} %get-tuple-element.150), channel_id=1, source_target_pairs={{0,8},{2,10},{4,12},{6,14},{8,0},{10,2},{12,4},{14,6},{16,24},{18,... | collective-permute-start | bytes 786440 | tf_op jit(solution)/shard_map/ppermute | solution.py:303
  71.2 31.3 %collective-permute-start.17 = (f32[256,512]{1,0:T(8,128)S(1)}, f32[256,512]{1,0:T(8,128)}, u32[]{:S(2)}, u32[]{:S(2)}) collective-permute-start(f32[256,512]{1,0:T(8,128)S(1)} %get-tuple-element.166), channel_id=1, source_target_pairs={{0,4},{2,6},{4,0},{6,2},{8,12},{10,14},{12,8},{14,10},{16,20},{18,... | collective-permute-start | bytes 1572872 | tf_op jit(solution)/shard_map/ppermute | solution.py:303
  71.6 41.3 %collective-permute-start.19 = (f32[256,512]{1,0:T(8,128)S(1)}, f32[256,512]{1,0:T(8,128)S(1)}, u32[]{:S(2)}, u32[]{:S(2)}) collective-permute-start(f32[256,512]{1,0:T(8,128)S(1)} %get-tuple-element.172), channel_id=1, source_target_pairs={{0,4},{2,6},{4,0},{6,2},{8,12},{10,14},{12,8},{14,10},{16,20},{18,... | collective-permute-start | bytes 1572872 | tf_op jit(solution)/shard_map/ppermute | solution.py:303
  74.3 11.6 %collective-permute-start.10 = (f32[64,1024]{1,0:T(8,128)S(1)}, f32[64,1024]{1,0:T(8,128)S(1)}, u32[]{:S(2)}, u32[]{:S(2)}) collective-permute-start(f32[64,1024]{1,0:T(8,128)S(1)} %get-tuple-element.209), channel_id=1, source_target_pairs={{0,16},{2,18},{4,20},{6,22},{8,24},{10,26},{12,28},{14,30},{16,0},... | collective-permute-start | bytes 786440 | tf_op jit(solution)/shard_map/ppermute | solution.py:303
  75.4 20.8 %collective-permute-start.13 = (f32[128,1024]{1,0:T(8,128)S(1)}, f32[128,1024]{1,0:T(8,128)S(1)}, u32[]{:S(2)}, u32[]{:S(2)}) collective-permute-start(f32[128,1024]{1,0:T(8,128)S(1)} %get-tuple-element.197), channel_id=1, source_target_pairs={{0,8},{2,10},{4,12},{6,14},{8,0},{10,2},{12,4},{14,6},{16,24},{18,... | collective-permute-start | bytes 1572872 | tf_op jit(solution)/shard_map/ppermute | solution.py:303
  85.9 6.6 %collective-permute-start.14 = (f32[128,256]{1,0:T(8,128)S(1)}, f32[128,256]{1,0:T(8,128)S(1)}, u32[]{:S(2)}, u32[]{:S(2)}) collective-permute-start(f32[128,256]{1,0:T(8,128)S(1)} %get-tuple-element.217), channel_id=1, source_target_pairs={{0,16},{2,18},{4,20},{6,22},{8,24},{10,26},{12,28},{14,30},{16,0},... | collective-permute-start | bytes 393224 | tf_op jit(solution)/shard_map/ppermute | solution.py:303
  92.4 18.4 %collective-permute-start.20 = (f32[128,768]{1,0:T(8,128)}, f32[128,768]{1,0:T(8,128)}, u32[]{:S(2)}, u32[]{:S(2)}) collective-permute-start(f32[128,768]{1,0:T(8,128)} %get-tuple-element.201), channel_id=1, source_target_pairs={{0,8},{2,10},{4,12},{6,14},{8,0},{10,2},{12,4},{14,6},{16,24},{18,... | collective-permute-start | bytes 1179656 | tf_op jit(solution)/shard_map/ppermute | solution.py:303
  97.0 11.9 %collective-permute-start.16 = (f32[64,1024]{1,0:T(8,128)}, f32[64,1024]{1,0:T(8,128)}, u32[]{:S(2)}, u32[]{:S(2)}) collective-permute-start(f32[64,1024]{1,0:T(8,128)} %get-tuple-element.207), channel_id=1, source_target_pairs={{0,16},{2,18},{4,20},{6,22},{8,24},{10,26},{12,28},{14,30},{16,0},... | collective-permute-start | bytes 786440 | tf_op jit(solution)/shard_map/ppermute | solution.py:303
  97.0 16.6 %collective-permute-start.18 = (f32[64,256]{1,0:T(8,128)}, f32[64,256]{1,0:T(8,128)S(1)}, u32[]{:S(2)}, u32[]{:S(2)}) collective-permute-start(f32[64,256]{1,0:T(8,128)} %get-tuple-element.229), channel_id=1, source_target_pairs={{0,4},{2,6},{4,0},{6,2},{8,12},{10,14},{12,8},{14,10},{16,20},{18,... | collective-permute-start | bytes 196616 | tf_op jit(solution)/shard_map/ppermute | solution.py:303
  103.6 18.3 %collective-permute-start.23 = (f32[128,512]{1,0:T(8,128)S(1)}, f32[128,512]{1,0:T(8,128)S(1)}, u32[]{:S(2)}, u32[]{:S(2)}) collective-permute-start(f32[128,512]{1,0:T(8,128)S(1)} %get-tuple-element.203), channel_id=1, source_target_pairs={{0,8},{2,10},{4,12},{6,14},{8,0},{10,2},{12,4},{14,6},{16,24},{18,... | collective-permute-start | bytes 786440 | tf_op jit(solution)/shard_map/ppermute | solution.py:303
  114.4 12.9 %collective-permute-start.21 = (f32[64,768]{1,0:T(8,128)S(1)}, f32[64,768]{1,0:T(8,128)S(1)}, u32[]{:S(2)}, u32[]{:S(2)}) collective-permute-start(f32[64,768]{1,0:T(8,128)S(1)} %get-tuple-element.211), channel_id=1, source_target_pairs={{0,16},{2,18},{4,20},{6,22},{8,24},{10,26},{12,28},{14,30},{16,0},... | collective-permute-start | bytes 589832 | tf_op jit(solution)/shard_map/ppermute | solution.py:303
  115.4 11.9 %collective-permute-start.22 = (f32[128,512]{1,0:T(8,128)S(1)}, f32[128,512]{1,0:T(8,128)S(1)}, u32[]{:S(2)}, u32[]{:S(2)}) collective-permute-start(f32[128,512]{1,0:T(8,128)S(1)} %get-tuple-element.205), channel_id=1, source_target_pairs={{0,8},{2,10},{4,12},{6,14},{8,0},{10,2},{12,4},{14,6},{16,24},{18,... | collective-permute-start | bytes 786440 | tf_op jit(solution)/shard_map/ppermute | solution.py:303
  115.5 11.9 %collective-permute-start.24 = (f32[128,512]{1,0:T(8,128)S(1)}, f32[128,512]{1,0:T(8,128)S(1)}, u32[]{:S(2)}, u32[]{:S(2)}) collective-permute-start(f32[128,512]{1,0:T(8,128)S(1)} %pad_maximum_fusion), channel_id=1, source_target_pairs={{0,1},{1,0},{2,3},{3,2},{4,5},{5,4},{6,7},{7,6},{8,9},{9,8},{10,11... | collective-permute-start | bytes 786440 | tf_op jit(solution)/shard_map/ppermute | solution.py:336
  121.9 11.8 %collective-permute-start.25 = (f32[64,512]{1,0:T(8,128)S(1)}, f32[64,512]{1,0:T(8,128)S(1)}, u32[]{:S(2)}, u32[]{:S(2)}) collective-permute-start(f32[64,512]{1,0:T(8,128)S(1)} %get-tuple-element.215), channel_id=1, source_target_pairs={{0,16},{2,18},{4,20},{6,22},{8,24},{10,26},{12,28},{14,30},{16,0},... | collective-permute-start | bytes 393224 | tf_op jit(solution)/shard_map/ppermute | solution.py:303
  127.4 7.8 %collective-permute-start.26 = (f32[64,512]{1,0:T(8,128)S(1)}, f32[64,512]{1,0:T(8,128)S(1)}, u32[]{:S(2)}, u32[]{:S(2)}) collective-permute-start(f32[64,512]{1,0:T(8,128)S(1)} %get-tuple-element.213), channel_id=1, source_target_pairs={{0,16},{2,18},{4,20},{6,22},{8,24},{10,26},{12,28},{14,30},{16,0},... | collective-permute-start | bytes 393224 | tf_op jit(solution)/shard_map/ppermute | solution.py:303
  128.1 8.5 %collective-permute-start.27 = (f32[64,512]{1,0:T(8,128)S(1)}, f32[64,512]{1,0:T(8,128)S(1)}, u32[]{:S(2)}, u32[]{:S(2)}) collective-permute-start(f32[64,512]{1,0:T(8,128)S(1)} %get-tuple-element.223), channel_id=1, source_target_pairs={{0,1},{1,0},{2,3},{3,2},{4,5},{5,4},{6,7},{7,6},{8,9},{9,8},{10,11... | collective-permute-start | bytes 393224 | tf_op jit(solution)/shard_map/ppermute | solution.py:336
  (7 other events, 165.6 us)
